TPU v7x, 32 devices: a whole 2x2x4 slice. The times are simulated.
32 devices in a mesh: row: 8 (over z, y), col: 4 (over x, core).
Axes of the slice: x: 2, y: 2, z: 4, core: 2. Of those that a mesh axis runs over, the one named last changes fastest.
Arguments:
- brick_velocity_stress: float32 [128, 9, 16, 256], P(('row', 'col')), may hold values from -6 to 6
- brick_relaxation_memory: float32 [128, 18, 16, 256], P(('row', 'col')), may hold values from -2 to 2
- brick_cell_material: int32 [128, 16, 256], P(('row', 'col')), may hold values from 0 to 7
- brick_live: int32 [128], P(('row', 'col')), may hold values from 0 to 1, as said below
- water_state: float32 [4, 256, 128, 128], P(None, 'row', 'col'), may hold values from -6 to 6
- water_material: int32 [256, 128, 128], P('row', 'col'), may hold values from 0 to 7
- material_table: float32 [8, 8], replicated, may hold values from 0.01 to 0.95, as said below
Outputs:
- motion_out: float32 [128, 9, 16, 256], P(('row', 'col'))
- memory_out: float32 [128, 18, 16, 256], P(('row', 'col'))
- water_out: float32 [4, 256, 128, 128], P(None, 'row', 'col')
Inputs may be any that keep to these rules, and one draw needn't show every extreme that they name: `brick_live`: tiles j and j + 2 of one row of tiles hold 4 live bricks together; in every row some tile holds 4 or none. `material_table`: column 0 is the buoyancy, 1 the first Lame constant (the bulk modulus of water cells), 2 the shear modulus, 3 to 5 the retentions of the three mechanisms, 6 and 7 the anelastic Lame constant and shear modulus.
All inputs are finite; a program needn't handle non-finite values.
Results may differ from a plain program's by a relative error of at most 0.00011.
Values sent between devices are 32-bit elements; how exact they have to be, the bound alone decides.
No kernel may reach another device: no remote copies, remote signals or barrier semaphores. Data moves between devices by JAX's collectives and lax.ppermute only.
A program may use at most 128 MiB of HBM per device.

v0:
```python
import functools

import jax
import jax.numpy as jnp
from jax import lax
from jax.experimental import pallas as pl
from jax.experimental.pallas import tpu as pltpu
from jax.sharding import PartitionSpec as P

STEPS = 3
LANES = 128
SUB = 8
VX, VY, VZ, XX, YY, ZZ, XY, XZ, YZ = range(9)
PAD = 8
P_NEAR, P_FAR, U_NEAR, BRICKS = 0, 32, 64, 96
CORNERS = 160
ROW_CONST, COL_CONST = 160, 176
ROW_LAYERS = [("n", f) for f in (XX, YY, ZZ, XY, XZ, YZ, VX, VY, VZ)] + [("f", f) for f in (XX, XY, XZ)]
COL_LAYERS = [("n", f) for f in (XX, YY, ZZ, XY, XZ, YZ, VX, VY, VZ)] + [("f", f) for f in (XY, YY, YZ)]


def lane_ids():
    return lax.broadcasted_iota(jnp.int32, (SUB, LANES), 1)


def sub_ids():
    return lax.broadcasted_iota(jnp.int32, (SUB, LANES), 0)


def roll(value, shift):
    shift = shift % LANES
    return value if shift == 0 else pltpu.roll(value, shift, 1)


def pick(values, indices):
    return jnp.take_along_axis(values, indices, axis=1, mode="promise_in_bounds")


class Shape:
    def __init__(self, nx, ny, edge):
        self.nx, self.ny, self.edge = nx, ny, edge
        self.across = ny * edge // LANES
        self.yper = LANES // edge
        self.half = self.across // 2
        self.px = ny + 2 * PAD

    def slot(self, ti, tj):
        per = self.edge // SUB
        return 2 * (ti // per) + tj // self.half

    def place(self, ti, tj):
        per = self.edge // SUB
        row = (ti % per) * SUB
        if not isinstance(row, int):
            row = pl.multiple_of(row, SUB)
        lane = (tj % self.half) * LANES
        return pl.ds(row, SUB), pl.ds(lane, LANES)

    def layer(self, x, tj):
        return 2 * (x // self.edge) + tj // self.half, x % self.edge, (tj % self.half) * LANES


def pack(g, water, motion, live, hb_tile, row_first, row_last, col_first, col_last, edge_b=None):
    nx, ny = g.nx, g.ny
    plane = nx * ny
    lane = lane_ids()

    def scale(slot):
        return None if live is None else live[slot].astype(jnp.float32)

    for out, near, far in ((row_first, 0, 1), (row_last, nx - 1, nx - 2)):
        for first, comp, x in ((P_NEAR, 0, near), (P_FAR, 0, far), (U_NEAR, 1, near)):
            for t in range(ny // SUB):
                out[pl.ds(first + SUB * t, SUB), :] = water[pl.ds(comp * plane + x * ny + SUB * t, SUB), :]
        for tj in range(g.across):
            block = BRICKS + 16 * tj
            for k, (which, field) in enumerate(ROW_LAYERS):
                slot, row, lanes = g.layer(near if which == "n" else far, tj)
                value = motion[slot, field, pl.ds(row, 1), pl.ds(lanes, LANES)]
                factor = scale(slot)
                out[pl.ds(block + k, 1), :] = value if factor is None else value * factor
            ti = near // SUB
            value = hb_tile(ti, tj)
            out[pl.ds(block + 12, 1), :] = value[near % SUB : near % SUB + 1, :]
        if edge_b is not None:
            for t in range(ny // SUB):
                out[pl.ds(ROW_CONST + SUB * t, SUB), :] = edge_b(pl.ds(near * ny + SUB * t, SUB))
    for out, near, far, tj in ((col_first, 0, 1, 0), (col_last, ny - 1, ny - 2, g.across - 1)):
        for first, comp, y in ((P_NEAR, 0, near), (P_FAR, 0, far), (U_NEAR, 2, near)):
            for t in range(nx // SUB):
                out[pl.ds(first + SUB * t, SUB), :] = water[pl.ds(comp * plane + SUB * t * ny + y, SUB, stride=ny), :]
        for ti in range(nx // SUB):
            slot = g.slot(ti, tj)
            rows, lanes = g.place(ti, tj)
            factor = scale(slot)
            tiles = {}
            for which, field in COL_LAYERS:
                if field not in tiles:
                    value = motion[slot, field, rows, lanes]
                    tiles[field] = value if factor is None else value * factor
            pieces = [(tiles[field], near if which == "n" else far) for which, field in COL_LAYERS]
            pieces.append((hb_tile(ti, tj), near))
            for column in range(2):
                packed = None
                for k, (value, y) in enumerate(pieces[8 * column : 8 * column + 8]):
                    moved = roll(value, g.edge * k - g.edge * (y % g.yper))
                    packed = moved if packed is None else jnp.where(lane >= g.edge * k, moved, packed)
                out[pl.ds(BRICKS + 32 * column + SUB * ti, SUB), :] = packed
        if edge_b is not None:
            for t in range(nx // SUB):
                out[pl.ds(COL_CONST + SUB * t, SUB), :] = edge_b(pl.ds(SUB * t * ny + near, SUB, stride=ny))


def first_kernel(g, live, table, water, material, motion, brick_material, row_first, row_last, col_first, col_last):
    def hb_tile(ti, tj):
        slot = g.slot(ti, tj)
        rows, lanes = g.place(ti, tj)
        return pick(table[0], brick_material[slot, rows, lanes]) * live[slot].astype(jnp.float32)

    def edge_b(rows):
        return pick(table[0], material[rows, :])

    for out in (col_first, col_last):
        out[pl.ds(CORNERS, 16), :] = jnp.zeros((16, LANES), jnp.float32)
    pack(g, water, motion, live, hb_tile, row_first, row_last, col_first, col_last, edge_b)


def step_kernel(g, first, last, *refs):
    refs = list(refs)

    def take(count):
        taken = refs[:count]
        del refs[:count]
        return taken

    live, table, water, material, motion, memory, brick_material = take(7)
    row_before, row_after, col_before, col_after = take(4)
    if not first:
        (const_in,) = take(1)
    water_out, motion_out, memory_out = take(3)
    if not last:
        sends = take(4)
    if first:
        (const_out,) = take(1)
    press, uy_pad, ux_halo, bricks, hb_pad = take(5)

    nx, ny, edge, across, yper = g.nx, g.ny, g.edge, g.across, g.yper
    plane, px = nx * ny, g.px
    width = across + 2
    lane, sub = lane_ids(), sub_ids()
    depth = lane % edge
    zero = jnp.zeros((SUB, LANES), jnp.float32)
    origin = lane * 0
    top_pick = sub * edge + (edge - 1)
    ytiles, xtiles = ny // SUB, nx // SUB
    BX = 16

    def at(x, y):
        return (x + PAD) * px + y + PAD

    def const(side, t):
        if first:
            ref, start = ((row_before, ROW_CONST), (row_after, ROW_CONST), (col_before, COL_CONST), (col_after, COL_CONST))[side]
            value = ref[pl.ds(start + SUB * t, SUB), :]
            const_out[pl.ds(32 * side + SUB * t, SUB), :] = value
            return value
        return const_in[pl.ds(32 * side + SUB * t, SUB), :]

    @pl.loop(0, nx)
    def _(x):
        for t in range(ytiles):
            row = pl.multiple_of(at(x, SUB * t), SUB)
            press[pl.ds(row, SUB), :] = water[pl.ds(pl.multiple_of(x * ny + SUB * t, SUB), SUB), :]

    for ref, near, far in ((row_before, -1, -2), (row_after, nx, nx + 1)):
        for t in range(ytiles):
            press[pl.ds(at(near, SUB * t), SUB), :] = ref[pl.ds(P_NEAR + SUB * t, SUB), :]
            press[pl.ds(at(far, SUB * t), SUB), :] = ref[pl.ds(P_FAR + SUB * t, SUB), :]
    for ref, near, far in ((col_before, -1, -2), (col_after, ny, ny + 1)):
        for t in range(xtiles):
            press[pl.ds(at(SUB * t, near), SUB, stride=px), :] = ref[pl.ds(P_NEAR + SUB * t, SUB), :]
            press[pl.ds(at(SUB * t, far), SUB, stride=px), :] = ref[pl.ds(P_FAR + SUB * t, SUB), :]

    for ti in range(xtiles):
        for tj in range(across):
            slot = g.slot(ti, tj)
            rows, lanes = g.place(ti, tj)
            alive = live[slot].astype(jnp.float32)
            for field in range(9):
                value = motion[slot, field, rows, lanes]
                if first:
                    value = value * alive
                bricks[field * width + 1 + tj, pl.ds(BX + SUB * ti, SUB), :] = value
            hb_pad[1 + tj, pl.ds(BX + SUB * ti, SUB), :] = pick(table[0], brick_material[slot, rows, lanes]) * alive
    for ref, near, far in ((row_before, -1, -2), (row_after, nx, nx + 1)):
        for tj in range(across):
            block = BRICKS + 16 * tj
            for k, (which, field) in enumerate(ROW_LAYERS):
                x = near if which == "n" else far
                bricks[field * width + 1 + tj, pl.ds(BX + x, 1), :] = ref[pl.ds(block + k, 1), :]
            hb_pad[1 + tj, pl.ds(BX + near, 1), :] = ref[pl.ds(block + 12, 1), :]
    for ref, tj, near, far in ((col_before, 0, yper - 1, yper - 2), (col_after, width - 1, 0, 1)):
        for ti in range(xtiles):
            columns = [ref[pl.ds(BRICKS + 32 * c + SUB * ti, SUB), :] for c in range(2)]
            found = {}
            for k, (which, field) in enumerate(COL_LAYERS):
                y = near if which == "n" else far
                moved = roll(columns[k // 8], edge * (y - k % 8))
                if which == "n":
                    found[field] = moved
                else:
                    found[field] = jnp.where(lane // edge == far, moved, found[field])
            for field, value in found.items():
                bricks[field * width + tj, pl.ds(BX + SUB * ti, SUB), :] = value
            hb_pad[tj, pl.ds(BX + SUB * ti, SUB), :] = roll(columns[1], edge * (near - 4))
        for k, x in ((0, -1), (1, nx)):
            for c in range(6):
                bricks[(XX + c) * width + tj, pl.ds(BX + x, 1), :] = ref[pl.ds(CORNERS + 8 * k + c, 1), :]

    @pl.loop(0, nx)
    def _(x):
        for t in range(ytiles):
            own = pl.ds(pl.multiple_of(x * ny + SUB * t, SUB), SUB)
            row = at(x, SUB * t)
            here = press[pl.ds(pl.multiple_of(row, SUB), SUB), :]
            dx = press[pl.ds(pl.multiple_of(row + px, SUB), SUB), :] - press[pl.ds(pl.multiple_of(row - px, SUB), SUB), :]
            dy = press[pl.ds(row + 1, SUB), :] - press[pl.ds(row - 1, SUB), :]
            surface = jnp.broadcast_to(bricks[ZZ * width + 1 + t, pl.ds(BX + x, 1), :], (SUB, LANES))
            below = -pick(surface, top_pick)
            dz = jnp.where(lane == LANES - 1, zero, roll(here, -1)) - jnp.where(lane == 0, below, roll(here, 1))
            hb = pick(table[0], material[own, :])
            for k, change in ((1, dx), (2, dy), (3, dz)):
                place = pl.ds(pl.multiple_of(k * plane + x * ny + SUB * t, SUB), SUB)
                value = water[place, :] - hb * change
                water_out[place, :] = value
                if k == 2:
                    uy_pad[pl.ds(pl.multiple_of(x * px + PAD + SUB * t, SUB), SUB), :] = value

    for side, (ref, x) in enumerate(((row_before, -1), (row_after, nx))):
        for t in range(ytiles):
            change = press[pl.ds(at(x + 1, SUB * t), SUB), :] - press[pl.ds(at(x - 1, SUB * t), SUB), :]
            ux_halo[pl.ds(side * ny + SUB * t, SUB), :] = ref[pl.ds(U_NEAR + SUB * t, SUB), :] - const(side, t) * change
    for side, (ref, y) in enumerate(((col_before, -1), (col_after, ny))):
        for t in range(xtiles):
            change = press[pl.ds(at(SUB * t, y + 1), SUB, stride=px), :] - press[pl.ds(at(SUB * t, y - 1), SUB, stride=px), :]
            uy_pad[pl.ds(SUB * t * px + PAD + y, SUB, stride=px), :] = (
                ref[pl.ds(U_NEAR + SUB * t, SUB), :] - const(2 + side, t) * change
            )

    def beyond_top(load, ys):
        top = None
        for k, y in ys:
            value = pick(load(y), origin)
            top = value if top is None else jnp.where(lane >= edge * k, value, top)
        return top

    def tile_rows(tj):
        if tj == 0:
            return [(0, -1)]
        if tj == width - 1:
            return [(0, ny)]
        return [(k, yper * (tj - 1) + k) for k in range(yper)]

    def along_y(rolled, tj):
        ahead = rolled[tj][1] if tj == width - 1 else jnp.where(lane < LANES - edge, rolled[tj][1], rolled[tj + 1][1])
        behind = rolled[tj][0] if tj == 0 else jnp.where(lane >= edge, rolled[tj][0], rolled[tj - 1][0])
        return ahead - behind

    def along_z(value, beyond):
        return jnp.where(depth == edge - 1, beyond, roll(value, -1)) - jnp.where(depth == 0, zero, roll(value, 1))

    @pl.loop(0, xtiles + 2)
    def _(ti):
        row = pl.multiple_of(BX - SUB + SUB * ti, SUB)
        here = pl.ds(row, SUB)

        def load(field, tj):
            return bricks[field * width + tj, here, :]

        def along_x(field, tj):
            return bricks[field * width + tj, pl.ds(row + 1, SUB), :] - bricks[field * width + tj, pl.ds(row - 1, SUB), :]

        for target, fx, fy, fz in ((VX, XX, XY, XZ), (VY, XY, YY, YZ), (VZ, XZ, YZ, ZZ)):
            rolled = [(roll(value, edge), roll(value, -edge)) for value in (load(fy, tj) for tj in range(width))]
            for tj in range(width):
                beyond = zero
                if fz == ZZ:
                    beyond = -beyond_top(
                        lambda y: press[pl.ds(SUB * ti * px + y + PAD, SUB, stride=px), :], tile_rows(tj)
                    )
                change = along_x(fx, tj) + along_y(rolled, tj) + along_z(load(fz, tj), beyond)
                bricks[target * width + tj, here, :] = load(target, tj) + hb_pad[tj, here, :] * change

    def water_pressure(x, before, after):
        for t in range(ytiles):
            own = pl.ds(pl.multiple_of(x * ny + SUB * t, SUB), SUB)
            row = x * px + PAD + SUB * t
            dy = uy_pad[pl.ds(row + 1, SUB), :] - uy_pad[pl.ds(row - 1, SUB), :]
            uz = water_out[pl.ds(pl.multiple_of(3 * plane + x * ny + SUB * t, SUB), SUB), :]
            surface = jnp.broadcast_to(bricks[VZ * width + 1 + t, pl.ds(BX + x, 1), :], (SUB, LANES))
            below = pick(surface, top_pick)
            dz = jnp.where(lane == LANES - 1, zero, roll(uz, -1)) - jnp.where(lane == 0, below, roll(uz, 1))
            hk = pick(table[1], material[own, :])
            water_out[own, :] = water[own, :] - hk * ((after(t) - before(t)) + dy + dz)

    def ux_at(x):
        return lambda t: water_out[pl.ds(pl.multiple_of(plane + x * ny + SUB * t, SUB), SUB), :]

    def ux_beyond(side):
        return lambda t: ux_halo[pl.ds(side * ny + SUB * t, SUB), :]

    water_pressure(0, ux_beyond(0), ux_at(1))
    water_pressure(nx - 1, ux_at(nx - 2), ux_beyond(1))

    @pl.loop(1, nx - 1)
    def _(x):
        water_pressure(x, ux_at(x - 1), ux_at(x + 1))

    @pl.loop(0, xtiles)
    def _(ti):
        row = pl.multiple_of(BX + SUB * ti, SUB)
        here = pl.ds(row, SUB)
        rolled = []
        for field in (VX, VY, VZ):
            values = [bricks[field * width + tj, here, :] for tj in range(width)]
            rolled.append([(roll(value, edge), roll(value, -edge)) for value in values])
        for tj in range(1, across + 1):
            slot = g.slot(ti, tj - 1)
            rows, lanes = g.place(ti, tj - 1)
            alive = live[slot].astype(jnp.float32)
            dx, dy, dz = [], [], []
            for field in (VX, VY, VZ):
                key = field * width + tj
                value = bricks[key, here, :]
                motion_out[slot, field, rows, lanes] = value
                dx.append(bricks[key, pl.ds(row + 1, SUB), :] - bricks[key, pl.ds(row - 1, SUB), :])
                dy.append(along_y(rolled[field], tj))
                beyond = beyond_top(
                    lambda y: water_out[pl.ds((1 + field) * plane + SUB * ti * ny + y, SUB, stride=ny), :], tile_rows(tj)
                )
                dz.append(along_z(value, beyond))
            strain = [dx[0], dy[1], dz[2], dy[0] + dx[1], dz[0] + dx[2], dz[1] + dy[2]]
            dilation = strain[0] + strain[1] + strain[2]
            kinds = brick_material[slot, rows, lanes]
            lame = pick(table[1], kinds) * alive * dilation
            shear = pick(table[2], kinds) * alive
            retain = [pick(table[3 + l], kinds) for l in range(3)]
            spring_lame = pick(table[6], kinds) * alive * dilation
            spring_shear = pick(table[7], kinds) * alive
            half_shear, half_spring = 0.5 * shear, 0.5 * spring_shear
            for comp in range(6):
                if comp < 3:
                    elastic = shear * strain[comp] + lame
                    relaxed = spring_shear * strain[comp] + spring_lame
                else:
                    elastic = half_shear * strain[comp]
                    relaxed = half_spring * strain[comp]
                summed = None
                for l in range(3):
                    old = memory[slot, 6 * l + comp, rows, lanes]
                    if first:
                        old = old * alive
                    new = relaxed + retain[l] * (old - relaxed)
                    memory_out[slot, 6 * l + comp, rows, lanes] = new
                    summed = new if summed is None else summed + new
                motion_out[slot, XX + comp, rows, lanes] = bricks[(XX + comp) * width + tj, here, :] + elastic - summed

    if not last:
        def hb_tile(ti, tj):
            return hb_pad[1 + tj, pl.ds(BX + SUB * ti, SUB), :]

        for out in sends[2:]:
            out[pl.ds(CORNERS, 16), :] = jnp.zeros((16, LANES), jnp.float32)
        pack(g, water_out, motion_out, None, hb_tile, *sends)


def exchange(sends):
    row_first, row_last, col_first, col_last = sends

    def shift(value, axis, up):
        count = lax.axis_size(axis)
        pairs = [(i, i + 1) for i in range(count - 1)]
        return lax.ppermute(value, axis, pairs if up else [(j, i) for i, j in pairs])

    row_before = shift(row_last, "row", True)
    row_after = shift(row_first, "row", False)

    def with_corners(message, tile):
        start = BRICKS + 16 * tile
        corners = jnp.concatenate([row_before[start : start + 8], row_after[start : start + 8]])
        return lax.dynamic_update_slice(message, corners, (CORNERS, 0))

    col_before = shift(with_corners(col_last, 3), "col", True)
    col_after = shift(with_corners(col_first, 0), "col", False)
    return row_before, row_after, col_before, col_after


def body(
    brick_velocity_stress,
    brick_relaxation_memory,
    brick_cell_material,
    brick_live,
    water_state,
    water_material,
    material_table,
):
    _, nx, ny, nz = water_state.shape
    g = Shape(nx, ny, brick_cell_material.shape[1])
    halves = jnp.array([0.5, 0.5, 1.0, 1.0, 1.0, 1.0, 0.5, 1.0], jnp.float32)
    columns = (material_table * halves).T
    table = jnp.broadcast_to(
        jnp.tile(columns, (1, LANES // columns.shape[1]))[:, None, :], (columns.shape[0], SUB, LANES)
    )
    water = water_state.reshape((-1, nz))
    material = water_material.reshape((-1, nz))
    motion, memory = brick_velocity_stress, brick_relaxation_memory

    def f32(*shape):
        return jax.ShapeDtypeStruct(shape, jnp.float32)

    smem = pl.BlockSpec(memory_space=pltpu.SMEM)
    vmem = pl.BlockSpec(memory_space=pltpu.VMEM)
    params = pltpu.CompilerParams(vmem_limit_bytes=48 * 1024 * 1024)

    def messages(constants):
        extra = 32 if constants else 0
        return (f32(160 + extra, LANES), f32(160 + extra, LANES), f32(176 + extra, LANES), f32(176 + extra, LANES))

    sends = pl.pallas_call(
        functools.partial(first_kernel, g),
        out_shape=messages(True),
        in_specs=[smem] + [vmem] * 5,
        out_specs=[vmem] * 4,
        compiler_params=params,
        name="pack_edges",
    )(brick_live, table, water, material, motion, brick_cell_material)
    constants = ()
    for step in range(STEPS):
        first, last = step == 0, step == STEPS - 1
        received = exchange(sends)
        out_shape = [f32(*water.shape), f32(*motion.shape), f32(*memory.shape)]
        if not last:
            out_shape += list(messages(False))
        if first:
            out_shape += [f32(128, LANES)]
        results = pl.pallas_call(
            functools.partial(step_kernel, g, first, last),
            out_shape=out_shape,
            in_specs=[smem] + [vmem] * (10 + len(constants)),
            out_specs=[vmem] * len(out_shape),
            scratch_shapes=[
                pltpu.VMEM(((nx + 2 * PAD) * g.px, LANES), jnp.float32),
                pltpu.VMEM((nx * g.px, LANES), jnp.float32),
                pltpu.VMEM((2 * ny, LANES), jnp.float32),
                pltpu.VMEM((9 * (g.across + 2), nx + 32, LANES), jnp.float32),
                pltpu.VMEM((g.across + 2, nx + 32, LANES), jnp.float32),
            ],
            compiler_params=params,
            name="time_step",
        )(brick_live, table, water, material, motion, memory, brick_cell_material, *received, *constants)
        water, motion, memory = results[:3]
        if not last:
            sends = results[3:7]
        if first:
            constants = (results[7],)
    return motion, memory, water.reshape(water_state.shape)


def solution(mesh):
    return jax.shard_map(
        body,
        mesh=mesh,
        in_specs=(
            P(("row", "col"), None, None, None),
            P(("row", "col"), None, None, None),
            P(("row", "col"), None, None),
            P(("row", "col")),
            P(None, "row", "col", None),
            P("row", "col", None),
            P(),
        ),
        out_specs=(
            P(("row", "col"), None, None, None),
            P(("row", "col"), None, None, None),
            P(None, "row", "col", None),
        ),
        check_vma=False,
    )
```

profile of v0, /device:TPU:10, one launch (start us, length us, event | category | flops | bytes accessed | tf_op | source)
XLA Modules:
  0.0 99.2 jit_solution(15041750888934227280)
XLA Ops:
  0.6 0.0 copy-start.8
  0.6 0.7 multiply_bitcast_fusion
  1.4 0.1 copy.12
  1.4 0.1 tile.9
  1.6 0.0 copy-start
  1.6 1.0 %copy-done = s32[32,32,128]{2,1,0:T(8,128)S(1)} copy-done((s32[32,32,128]{2,1,0:T(8,128)S(1)}, s32[32,32,128]{2,1,0:T(8,128)}, u32[]{:S(2)}) %copy-start) | copy-done | bytes 524312
  2.6 0.0 copy-start.2
  2.6 1.6 %copy-done.2 = f32[4,32,32,128]{3,2,1,0:T(8,128)S(1)} copy-done((f32[4,32,32,128]{3,2,1,0:T(8,128)S(1)}, f32[4,32,32,128]{3,2,1,0:T(8,128)}, u32[]{:S(2)}) %copy-start.2) | copy-done | bytes 2097176
  4.2 0.0 copy-start.3
  4.2 1.1 %copy-done.3 = f32[4,9,16,256]{3,2,1,0:T(8,128)S(1)} copy-done((f32[4,9,16,256]{3,2,1,0:T(8,128)S(1)}, f32[4,9,16,256]{3,2,1,0:T(8,128)}, u32[]{:S(2)}) %copy-start.3) | copy-done | bytes 589848
  5.3 0.0 copy-start.7
  5.3 0.8 copy-done.7
  6.1 0.0 copy-start.9
  6.1 0.7 copy-done.9
  6.8 0.0 copy-start.1
  6.8 0.0 copy-start.4
  6.8 0.0 copy-start.6
  6.8 0.8 pack_edges.1
  7.6 3.4 %collective-permute-start = (f32[192,128]{1,0:T(8,128)S(1)}, f32[192,128]{1,0:T(8,128)S(1)}, u32[]{:S(2)}, u32[]{:S(2)}) collective-permute-start(f32[192,128]{1,0:T(8,128)S(1)} %get-tuple-element.25), channel_id=1, source_target_pairs={{0,4},{4,8},{8,12},{12,16},{16,20},{20,24},{24,28},{1,5},{5,9},{9,... | collective-permute-start | bytes 294920 | tf_op jit(solution)/shard_map/ppermute | solution.py:383
  11.0 3.3 %collective-permute-start.1 = (f32[192,128]{1,0:T(8,128)S(1)}, f32[192,128]{1,0:T(8,128)S(1)}, u32[]{:S(2)}, u32[]{:S(2)}) collective-permute-start(f32[192,128]{1,0:T(8,128)S(1)} %get-tuple-element.26), channel_id=1, source_target_pairs={{4,0},{8,4},{12,8},{16,12},{20,16},{24,20},{28,24},{5,1},{9,5},{13... | collective-permute-start | bytes 294920 | tf_op jit(solution)/shard_map/ppermute | solution.py:383
  14.4 0.7 collective-permute-done.refs_7_
  15.0 2.5 %collective-permute-done.1.refs_8_ = f32[192,128]{1,0:T(8,128)S(1)} collective-permute-done((f32[192,128]{1,0:T(8,128)S(1)}, f32[192,128]{1,0:T(8,128)S(1)}, u32[]{:S(2)}, u32[]{:S(2)}) %collective-permute-start.1) | collective-permute-done | bytes 98336 | tf_op jit(solution)/shard_map/ppermute | solution.py:383
  17.6 1.9 %collective-permute-start.3 = (f32[208,128]{1,0:T(8,128)S(1)}, f32[208,128]{1,0:T(8,128)S(1)}, u32[]{:S(2)}, u32[]{:S(2)}) collective-permute-start(f32[208,128]{1,0:T(8,128)S(1)} %maximum_dynamic-update-slice_fusion.1), channel_id=1, source_target_pairs={{1,0},{2,1},{3,2},{5,4},{6,5},{7,6},{9,8},{10,9},{11,10},{13,12},{... | collective-permute-start | bytes 319496 | tf_op jit(solution)/shard_map/ppermute | solution.py:383
  19.5 2.4 %collective-permute-start.2 = (f32[208,128]{1,0:T(8,128)S(1)}, f32[208,128]{1,0:T(8,128)S(1)}, u32[]{:S(2)}, u32[]{:S(2)}) collective-permute-start(f32[208,128]{1,0:T(8,128)S(1)} %maximum_dynamic-update-slice_fusion), channel_id=1, source_target_pairs={{0,1},{1,2},{2,3},{4,5},{5,6},{6,7},{8,9},{9,10},{10,11},{12,13},{... | collective-permute-start | bytes 319496 | tf_op jit(solution)/shard_map/ppermute | solution.py:383
  21.9 0.0 collective-permute-done.3.refs_10_
  21.9 3.6 %collective-permute-done.2.refs_9_ = f32[208,128]{1,0:T(8,128)S(1)} collective-permute-done((f32[208,128]{1,0:T(8,128)S(1)}, f32[208,128]{1,0:T(8,128)S(1)}, u32[]{:S(2)}, u32[]{:S(2)}) %collective-permute-start.2) | collective-permute-done | bytes 106528 | tf_op jit(solution)/shard_map/ppermute | solution.py:383
  25.5 0.0 copy-done.8
  25.5 0.0 copy-done.1
  25.5 0.0 copy-done.4
  25.5 0.0 copy-done.6
  25.5 12.2 %time_step.3 = (f32[4096,128]{1,0:T(8,128)}, f32[4,9,16,256]{3,2,1,0:T(8,128)S(1)}, f32[4,18,16,256]{3,2,1,0:T(8,128)S(1)}, f32[160,128]{1,0:T(8,128)S(1)}, f32[...) custom-call(s32[4]{0:T(128)S(1)} %copy-done.9, ...), custom_call_target="tpu_custom_call" | custom-call | tf_op jit(solution)/shard_map/time_step/pallas_call | solution.py:446
  37.7 4.3 %collective-permute-start.4 = (f32[160,128]{1,0:T(8,128)S(1)}, f32[160,128]{1,0:T(8,128)S(1)}, u32[]{:S(2)}, u32[]{:S(2)}) collective-permute-start(f32[160,128]{1,0:T(8,128)S(1)} %get-tuple-element.32), channel_id=1, source_target_pairs={{0,4},{4,8},{8,12},{12,16},{16,20},{20,24},{24,28},{1,5},{5,9},{9,... | collective-permute-start | bytes 245768 | tf_op jit(solution)/shard_map/ppermute | solution.py:383
  42.0 2.4 %collective-permute-start.5 = (f32[160,128]{1,0:T(8,128)S(1)}, f32[160,128]{1,0:T(8,128)S(1)}, u32[]{:S(2)}, u32[]{:S(2)}) collective-permute-start(f32[160,128]{1,0:T(8,128)S(1)} %get-tuple-element.33), channel_id=1, source_target_pairs={{4,0},{8,4},{12,8},{16,12},{20,16},{24,20},{28,24},{5,1},{9,5},{13... | collective-permute-start | bytes 245768 | tf_op jit(solution)/shard_map/ppermute | solution.py:383
  44.5 0.6 collective-permute-done.4.refs_7_
  45.0 3.3 %collective-permute-done.5.refs_8_ = f32[160,128]{1,0:T(8,128)S(1)} collective-permute-done((f32[160,128]{1,0:T(8,128)S(1)}, f32[160,128]{1,0:T(8,128)S(1)}, u32[]{:S(2)}, u32[]{:S(2)}) %collective-permute-start.5) | collective-permute-done | bytes 81952 | tf_op jit(solution)/shard_map/ppermute | solution.py:383
  48.4 1.9 %collective-permute-start.7 = (f32[176,128]{1,0:T(8,128)S(1)}, f32[176,128]{1,0:T(8,128)S(1)}, u32[]{:S(2)}, u32[]{:S(2)}) collective-permute-start(f32[176,128]{1,0:T(8,128)S(1)} %maximum_dynamic-update-slice_fusion.3), channel_id=1, source_target_pairs={{1,0},{2,1},{3,2},{5,4},{6,5},{7,6},{9,8},{10,9},{11,10},{13,12},{... | collective-permute-start | bytes 270344 | tf_op jit(solution)/shard_map/ppermute | solution.py:383
  50.3 2.4 %collective-permute-start.6 = (f32[176,128]{1,0:T(8,128)S(1)}, f32[176,128]{1,0:T(8,128)S(1)}, u32[]{:S(2)}, u32[]{:S(2)}) collective-permute-start(f32[176,128]{1,0:T(8,128)S(1)} %maximum_dynamic-update-slice_fusion.2), channel_id=1, source_target_pairs={{0,1},{1,2},{2,3},{4,5},{5,6},{6,7},{8,9},{9,10},{10,11},{12,13},{... | collective-permute-start | bytes 270344 | tf_op jit(solution)/shard_map/ppermute | solution.py:383
  52.7 0.0 collective-permute-done.7.refs_10_
  52.7 3.4 %collective-permute-done.6.refs_9_ = f32[176,128]{1,0:T(8,128)S(1)} collective-permute-done((f32[176,128]{1,0:T(8,128)S(1)}, f32[176,128]{1,0:T(8,128)S(1)}, u32[]{:S(2)}, u32[]{:S(2)}) %collective-permute-start.6) | collective-permute-done | bytes 90144 | tf_op jit(solution)/shard_map/ppermute | solution.py:383
  56.2 12.2 %time_step.4 = (f32[4096,128]{1,0:T(8,128)}, f32[4,9,16,256]{3,2,1,0:T(8,128)S(1)}, f32[4,18,16,256]{3,2,1,0:T(8,128)S(1)}, f32[160,128]{1,0:T(8,128)S(1)}, f32[...) custom-call(s32[4]{0:T(128)S(1)} %copy-done.9, ...), custom_call_target="tpu_custom_call" | custom-call | tf_op jit(solution)/shard_map/time_step/pallas_call | solution.py:446
  68.3 3.4 %collective-permute-start.8 = (f32[160,128]{1,0:T(8,128)S(1)}, f32[160,128]{1,0:T(8,128)S(1)}, u32[]{:S(2)}, u32[]{:S(2)}) collective-permute-start(f32[160,128]{1,0:T(8,128)S(1)} %get-tuple-element.40), channel_id=1, source_target_pairs={{0,4},{4,8},{8,12},{12,16},{16,20},{20,24},{24,28},{1,5},{5,9},{9,... | collective-permute-start | bytes 245768 | tf_op jit(solution)/shard_map/ppermute | solution.py:383
  71.8 3.3 %collective-permute-start.9 = (f32[160,128]{1,0:T(8,128)S(1)}, f32[160,128]{1,0:T(8,128)S(1)}, u32[]{:S(2)}, u32[]{:S(2)}) collective-permute-start(f32[160,128]{1,0:T(8,128)S(1)} %get-tuple-element.41), channel_id=1, source_target_pairs={{4,0},{8,4},{12,8},{16,12},{20,16},{24,20},{28,24},{5,1},{9,5},{13... | collective-permute-start | bytes 245768 | tf_op jit(solution)/shard_map/ppermute | solution.py:383
  75.1 0.5 collective-permute-done.8.refs_7_
  75.6 2.5 %collective-permute-done.9.refs_8_ = f32[160,128]{1,0:T(8,128)S(1)} collective-permute-done((f32[160,128]{1,0:T(8,128)S(1)}, f32[160,128]{1,0:T(8,128)S(1)}, u32[]{:S(2)}, u32[]{:S(2)}) %collective-permute-start.9) | collective-permute-done | bytes 81952 | tf_op jit(solution)/shard_map/ppermute | solution.py:383
  78.1 1.9 %collective-permute-start.11 = (f32[176,128]{1,0:T(8,128)S(1)}, f32[176,128]{1,0:T(8,128)S(1)}, u32[]{:S(2)}, u32[]{:S(2)}) collective-permute-start(f32[176,128]{1,0:T(8,128)S(1)} %maximum_dynamic-update-slice_fusion.5), channel_id=1, source_target_pairs={{1,0},{2,1},{3,2},{5,4},{6,5},{7,6},{9,8},{10,9},{11,10},{13,12},{... | collective-permute-start | bytes 270344 | tf_op jit(solution)/shard_map/ppermute | solution.py:383
  80.0 2.4 %collective-permute-start.10 = (f32[176,128]{1,0:T(8,128)S(1)}, f32[176,128]{1,0:T(8,128)S(1)}, u32[]{:S(2)}, u32[]{:S(2)}) collective-permute-start(f32[176,128]{1,0:T(8,128)S(1)} %maximum_dynamic-update-slice_fusion.4), channel_id=1, source_target_pairs={{0,1},{1,2},{2,3},{4,5},{5,6},{6,7},{8,9},{9,10},{10,11},{12,13},{... | collective-permute-start | bytes 270344 | tf_op jit(solution)/shard_map/ppermute | solution.py:383
  82.4 0.0 collective-permute-done.11.refs_10_
  82.5 3.4 %collective-permute-done.10.refs_9_ = f32[176,128]{1,0:T(8,128)S(1)} collective-permute-done((f32[176,128]{1,0:T(8,128)S(1)}, f32[176,128]{1,0:T(8,128)S(1)}, u32[]{:S(2)}, u32[]{:S(2)}) %collective-permute-start.10) | collective-permute-done | bytes 90144 | tf_op jit(solution)/shard_map/ppermute | solution.py:383
  85.9 0.0 copy-start.5
  85.9 1.6 %copy-done.5 = f32[4096,128]{1,0:T(8,128)S(1)} copy-done((f32[4096,128]{1,0:T(8,128)S(1)}, f32[4096,128]{1,0:T(8,128)}, u32[]{:S(2)}) %copy-start.5) | copy-done | bytes 2097176
  87.5 11.7 %time_step.5 = (f32[4096,128]{1,0:T(8,128)}, f32[4,9,16,256]{3,2,1,0:T(8,128)}, f32[4,18,16,256]{3,2,1,0:T(8,128)}) custom-call(s32[4]{0:T(128)S(1)} %copy-done.9, f32[8,8,128]{2,1,0:T(8,128)S(1)} %broadcast_in_dim.2.table.refs_1_, f32[4096,128]{1,0:T(8,128)S(1)} %copy-done.5, s32[1024,128]{1,0:T(8,128)S(1)} %bitcast.8, ...), custom_call_target="tpu_custom_call" | custom-call | tf_op jit(solution)/shard_map/time_step/pallas_call | solution.py:446
  (14 shorter events, 0.1 us)
Async XLA Ops:
  0.6 24.9 %copy-start.8 = (s32[4,16,256]{2,1,0:T(8,128)S(1)}, s32[4,16,256]{2,1,0:T(8,128)}, u32[]{:S(2)}) copy-start(s32[4,16,256]{2,1,0:T(8,128)} %refs_6_.5) | copy-start | bytes 196612
  1.6 1.0 %copy-start = (s32[32,32,128]{2,1,0:T(8,128)S(1)}, s32[32,32,128]{2,1,0:T(8,128)}, u32[]{:S(2)}) copy-start(s32[32,32,128]{2,1,0:T(8,128)} %param.13) | copy-start | bytes 1572868
  2.6 1.6 %copy-start.2 = (f32[4,32,32,128]{3,2,1,0:T(8,128)S(1)}, f32[4,32,32,128]{3,2,1,0:T(8,128)}, u32[]{:S(2)}) copy-start(f32[4,32,32,128]{3,2,1,0:T(8,128)} %param.12) | copy-start | bytes 6291460
  4.2 1.1 %copy-start.3 = (f32[4,9,16,256]{3,2,1,0:T(8,128)S(1)}, f32[4,9,16,256]{3,2,1,0:T(8,128)}, u32[]{:S(2)}) copy-start(f32[4,9,16,256]{3,2,1,0:T(8,128)} %refs_4_.1) | copy-start | bytes 1769476
  5.3 0.8 copy-start.7
  6.1 0.7 copy-start.9
  6.8 18.8 %copy-start.1 = (s32[32,32,128]{2,1,0:T(8,128)S(1)}, s32[32,32,128]{2,1,0:T(8,128)}, u32[]{:S(2)}) copy-start(s32[32,32,128]{2,1,0:T(8,128)} %param.13) | copy-start | bytes 1572868
  6.8 18.8 %copy-start.4 = (f32[4,9,16,256]{3,2,1,0:T(8,128)S(1)}, f32[4,9,16,256]{3,2,1,0:T(8,128)}, u32[]{:S(2)}) copy-start(f32[4,9,16,256]{3,2,1,0:T(8,128)} %refs_4_.1) | copy-start | bytes 1769476
  6.8 18.8 %copy-start.6 = (f32[4,18,16,256]{3,2,1,0:T(8,128)S(1)}, f32[4,18,16,256]{3,2,1,0:T(8,128)}, u32[]{:S(2)}) copy-start(f32[4,18,16,256]{3,2,1,0:T(8,128)} %refs_5_.1) | copy-start | bytes 3538948
  7.6 7.4 %collective-permute-start = (f32[192,128]{1,0:T(8,128)S(1)}, f32[192,128]{1,0:T(8,128)S(1)}, u32[]{:S(2)}, u32[]{:S(2)}) collective-permute-start(f32[192,128]{1,0:T(8,128)S(1)} %get-tuple-element.25), channel_id=1, source_target_pairs={{0,4},{4,8},{8,12},{12,16},{16,20},{20,24},{24,28},{1,5},{5,9},{9,... | collective-permute-start | bytes 294920 | tf_op jit(solution)/shard_map/ppermute | solution.py:383
  11.0 6.5 %collective-permute-start.1 = (f32[192,128]{1,0:T(8,128)S(1)}, f32[192,128]{1,0:T(8,128)S(1)}, u32[]{:S(2)}, u32[]{:S(2)}) collective-permute-start(f32[192,128]{1,0:T(8,128)S(1)} %get-tuple-element.26), channel_id=1, source_target_pairs={{4,0},{8,4},{12,8},{16,12},{20,16},{24,20},{28,24},{5,1},{9,5},{13... | collective-permute-start | bytes 294920 | tf_op jit(solution)/shard_map/ppermute | solution.py:383
  17.6 4.3 %collective-permute-start.3 = (f32[208,128]{1,0:T(8,128)S(1)}, f32[208,128]{1,0:T(8,128)S(1)}, u32[]{:S(2)}, u32[]{:S(2)}) collective-permute-start(f32[208,128]{1,0:T(8,128)S(1)} %maximum_dynamic-update-slice_fusion.1), channel_id=1, source_target_pairs={{1,0},{2,1},{3,2},{5,4},{6,5},{7,6},{9,8},{10,9},{11,10},{13,12},{... | collective-permute-start | bytes 319496 | tf_op jit(solution)/shard_map/ppermute | solution.py:383
  19.5 6.0 %collective-permute-start.2 = (f32[208,128]{1,0:T(8,128)S(1)}, f32[208,128]{1,0:T(8,128)S(1)}, u32[]{:S(2)}, u32[]{:S(2)}) collective-permute-start(f32[208,128]{1,0:T(8,128)S(1)} %maximum_dynamic-update-slice_fusion), channel_id=1, source_target_pairs={{0,1},{1,2},{2,3},{4,5},{5,6},{6,7},{8,9},{9,10},{10,11},{12,13},{... | collective-permute-start | bytes 319496 | tf_op jit(solution)/shard_map/ppermute | solution.py:383
  37.7 7.3 %collective-permute-start.4 = (f32[160,128]{1,0:T(8,128)S(1)}, f32[160,128]{1,0:T(8,128)S(1)}, u32[]{:S(2)}, u32[]{:S(2)}) collective-permute-start(f32[160,128]{1,0:T(8,128)S(1)} %get-tuple-element.32), channel_id=1, source_target_pairs={{0,4},{4,8},{8,12},{12,16},{16,20},{20,24},{24,28},{1,5},{5,9},{9,... | collective-permute-start | bytes 245768 | tf_op jit(solution)/shard_map/ppermute | solution.py:383
  42.0 6.3 %collective-permute-start.5 = (f32[160,128]{1,0:T(8,128)S(1)}, f32[160,128]{1,0:T(8,128)S(1)}, u32[]{:S(2)}, u32[]{:S(2)}) collective-permute-start(f32[160,128]{1,0:T(8,128)S(1)} %get-tuple-element.33), channel_id=1, source_target_pairs={{4,0},{8,4},{12,8},{16,12},{20,16},{24,20},{28,24},{5,1},{9,5},{13... | collective-permute-start | bytes 245768 | tf_op jit(solution)/shard_map/ppermute | solution.py:383
  48.4 4.3 %collective-permute-start.7 = (f32[176,128]{1,0:T(8,128)S(1)}, f32[176,128]{1,0:T(8,128)S(1)}, u32[]{:S(2)}, u32[]{:S(2)}) collective-permute-start(f32[176,128]{1,0:T(8,128)S(1)} %maximum_dynamic-update-slice_fusion.3), channel_id=1, source_target_pairs={{1,0},{2,1},{3,2},{5,4},{6,5},{7,6},{9,8},{10,9},{11,10},{13,12},{... | collective-permute-start | bytes 270344 | tf_op jit(solution)/shard_map/ppermute | solution.py:383
  50.3 5.8 %collective-permute-start.6 = (f32[176,128]{1,0:T(8,128)S(1)}, f32[176,128]{1,0:T(8,128)S(1)}, u32[]{:S(2)}, u32[]{:S(2)}) collective-permute-start(f32[176,128]{1,0:T(8,128)S(1)} %maximum_dynamic-update-slice_fusion.2), channel_id=1, source_target_pairs={{0,1},{1,2},{2,3},{4,5},{5,6},{6,7},{8,9},{9,10},{10,11},{12,13},{... | collective-permute-start | bytes 270344 | tf_op jit(solution)/shard_map/ppermute | solution.py:383
  68.3 7.2 %collective-permute-start.8 = (f32[160,128]{1,0:T(8,128)S(1)}, f32[160,128]{1,0:T(8,128)S(1)}, u32[]{:S(2)}, u32[]{:S(2)}) collective-permute-start(f32[160,128]{1,0:T(8,128)S(1)} %get-tuple-element.40), channel_id=1, source_target_pairs={{0,4},{4,8},{8,12},{12,16},{16,20},{20,24},{24,28},{1,5},{5,9},{9,... | collective-permute-start | bytes 245768 | tf_op jit(solution)/shard_map/ppermute | solution.py:383
  71.8 6.3 %collective-permute-start.9 = (f32[160,128]{1,0:T(8,128)S(1)}, f32[160,128]{1,0:T(8,128)S(1)}, u32[]{:S(2)}, u32[]{:S(2)}) collective-permute-start(f32[160,128]{1,0:T(8,128)S(1)} %get-tuple-element.41), channel_id=1, source_target_pairs={{4,0},{8,4},{12,8},{16,12},{20,16},{24,20},{28,24},{5,1},{9,5},{13... | collective-permute-start | bytes 245768 | tf_op jit(solution)/shard_map/ppermute | solution.py:383
  78.1 4.3 %collective-permute-start.11 = (f32[176,128]{1,0:T(8,128)S(1)}, f32[176,128]{1,0:T(8,128)S(1)}, u32[]{:S(2)}, u32[]{:S(2)}) collective-permute-start(f32[176,128]{1,0:T(8,128)S(1)} %maximum_dynamic-update-slice_fusion.5), channel_id=1, source_target_pairs={{1,0},{2,1},{3,2},{5,4},{6,5},{7,6},{9,8},{10,9},{11,10},{13,12},{... | collective-permute-start | bytes 270344 | tf_op jit(solution)/shard_map/ppermute | solution.py:383
  80.0 5.8 %collective-permute-start.10 = (f32[176,128]{1,0:T(8,128)S(1)}, f32[176,128]{1,0:T(8,128)S(1)}, u32[]{:S(2)}, u32[]{:S(2)}) collective-permute-start(f32[176,128]{1,0:T(8,128)S(1)} %maximum_dynamic-update-slice_fusion.4), channel_id=1, source_target_pairs={{0,1},{1,2},{2,3},{4,5},{5,6},{6,7},{8,9},{9,10},{10,11},{12,13},{... | collective-permute-start | bytes 270344 | tf_op jit(solution)/shard_map/ppermute | solution.py:383
  85.9 1.6 %copy-start.5 = (f32[4096,128]{1,0:T(8,128)S(1)}, f32[4096,128]{1,0:T(8,128)}, u32[]{:S(2)}) copy-start(f32[4096,128]{1,0:T(8,128)} %get-tuple-element.37.refs_2_) | copy-start | bytes 6291460
where the time goes:
time: 101 us; the launch traced here: 99.2 us
  Pallas kernels  36.9 us (37%)
  starting transfers between devices  33.1 us (33%)
  waiting for transfers between devices  20.6 us (20%)
  local copies, waits for them, and re-layouts  6.98 us (7%)
    pallas_call x3, Pallas kernels, body(): pl.pallas_call(functools.partial(step_kernel, g, first, last), out_shape=...  36.1 us
    ppermute x12, starting transfers between devices, shift(): lax.ppermute(value, axis, pairs if up else [(j, i) for i, j in pairs])  33.1 us
    ppermute x12, waiting for transfers between devices, shift(): lax.ppermute(value, axis, pairs if up else [(j, i) for i, j in pairs])  20.6 us
    unnamed x20, local copies, waits for them, and re-layouts  6.79 us
  transfers between devices with their start and end apart: 12, of which 9 were waited for; matrix products, arithmetic and copies ran while one was open for 0% of the time, Pallas kernels for 0%

commit v1 on v0

v1 whole, which is shorter than its diff:
```python
import functools

import jax
import jax.numpy as jnp
from jax import lax
from jax.experimental import pallas as pl
from jax.experimental.pallas import tpu as pltpu
from jax.sharding import PartitionSpec as P

STEPS = 3
LANES = 128
SUB = 8
PAD = 8
VX, VY, VZ, XX, YY, ZZ, XY, XZ, YZ = range(9)
HB, LAME, SHEAR, RETAIN, SPRING_LAME, SPRING_SHEAR = 0, 1, 2, 3, 6, 7
ALONG_X = (XX, XY, XZ)
ALONG_Y = (XY, YY, YZ)
ALONG_Z = (XZ, YZ, ZZ)
M_P, M_U, M_BRICK, M_CORNER = 0, 32, 64, 96
ROW_CONST, COL_CONST = 96, 112


def lane_ids():
    return lax.broadcasted_iota(jnp.int32, (SUB, LANES), 1)


def roll(value, shift):
    shift = shift % LANES
    return value if shift == 0 else pltpu.roll(value, shift, 1)


def roll_row(row, shift):
    shift = shift % LANES
    if shift == 0:
        return row
    return pltpu.roll(jnp.broadcast_to(row, (SUB, LANES)), shift, 1)[0:1, :]


def pick(values, indices):
    return jnp.take_along_axis(values, indices, axis=1, mode="promise_in_bounds")


def aligned(start, size=SUB):
    return pl.ds(start if isinstance(start, int) else pl.multiple_of(start, SUB), size)


class Grid:
    def __init__(self, nx, ny, edge):
        self.nx, self.ny, self.edge = nx, ny, edge
        self.plane = nx * ny
        self.across = ny * edge // LANES
        self.yper = LANES // edge
        self.half = self.across // 2
        self.xtiles, self.ytiles = nx // SUB, ny // SUB
        self.per = edge // SUB

    def slot(self, ti, tj):
        return 2 * (ti // self.per) + tj // self.half

    def place(self, ti, tj):
        return aligned((ti % self.per) * SUB), pl.ds((tj % self.half) * LANES, LANES)


def set_zero_pads(g, press, stress):
    zero = jnp.zeros((SUB, LANES), jnp.float32)
    for t in range(g.ytiles):
        press[0, pl.ds(PAD + SUB * t, SUB), :] = zero
        press[g.nx + 1, pl.ds(PAD + SUB * t, SUB), :] = zero

    @pl.loop(1, g.nx + 1)
    def _(x):
        press[x, pl.ds(0, SUB), :] = zero
        press[x, pl.ds(PAD + g.ny, SUB), :] = zero

    for field in ALONG_X:
        for tj in range(g.across):
            key = (field - XX) * g.across + tj
            stress[key, pl.ds(0, SUB), :] = zero
            stress[key, pl.ds(PAD + g.nx, SUB), :] = zero


def shifted_top(g, load, ys, lane):
    top = None
    for k, y in enumerate(ys):
        value = roll(load(y), g.edge * k + g.edge - 1)
        top = value if top is None else jnp.where(lane >= g.edge * k, value, top)
    return top


def along_y(g, rolled, tj, lane):
    zero = jnp.zeros((SUB, LANES), jnp.float32)
    after = rolled[tj + 1][1] if tj + 1 < len(rolled) else zero
    before = rolled[tj - 1][0] if tj > 0 else zero
    ahead = jnp.where(lane < LANES - g.edge, rolled[tj][1], after)
    behind = jnp.where(lane >= g.edge, rolled[tj][0], before)
    return ahead - behind


def along_z(g, value, beyond, depth):
    zero = jnp.zeros((SUB, LANES), jnp.float32)
    return jnp.where(depth == g.edge - 1, beyond, roll(value, -1)) - jnp.where(depth == 0, zero, roll(value, 1))


def water_z(g, value, below, lane):
    zero = jnp.zeros((SUB, LANES), jnp.float32)
    return jnp.where(lane == LANES - 1, zero, roll(value, -1)) - jnp.where(lane == 0, below, roll(value, 1))


def surface_pick():
    return lax.broadcasted_iota(jnp.int32, (SUB, LANES), 0)


def velocity_part(g, water_out, press, stress, hb_water, load_u, load_v, bricks_out, load_hb):
    lane = lane_ids()
    depth = lane % g.edge
    zero = jnp.zeros((SUB, LANES), jnp.float32)
    top_pick = surface_pick() * g.edge + (g.edge - 1)
    plane, ny, across = g.plane, g.ny, g.across

    def water_layer(x):
        results = []
        for t in range(g.ytiles):
            rows = pl.ds(PAD + SUB * t, SUB)
            here = press[x + 1, rows, :]
            dx = press[x + 2, rows, :] - press[x, rows, :]
            dy = press[x + 1, pl.ds(PAD + SUB * t + 1, SUB), :] - press[x + 1, pl.ds(PAD + SUB * t - 1, SUB), :]
            surface = jnp.broadcast_to(stress[(ZZ - XX) * across + t, pl.ds(PAD + x, 1), :], (SUB, LANES))
            dz = water_z(g, here, -pick(surface, top_pick), lane)
            own = x * ny + SUB * t
            hb = hb_water[aligned(own), :]
            for k, change in ((1, dx), (2, dy), (3, dz)):
                results.append((k * plane + own, load_u(k, x, t) - hb * change))
        return results

    @pl.loop(0, g.nx // 2)
    def _(pair):
        for row, value in water_layer(2 * pair) + water_layer(2 * pair + 1):
            water_out[aligned(row), :] = value

    @pl.loop(0, g.xtiles)
    def _(ti):
        row = pl.multiple_of(SUB * ti, SUB)
        here = pl.ds(pl.multiple_of(row + PAD, SUB), SUB)

        def load(field, tj):
            return stress[(field - XX) * across + tj, here, :]

        def along_x(field, tj):
            key = (field - XX) * across + tj
            return stress[key, pl.ds(row + PAD + 1, SUB), :] - stress[key, pl.ds(row + PAD - 1, SUB), :]

        results = []
        for target, fx, fy, fz in zip((VX, VY, VZ), ALONG_X, ALONG_Y, ALONG_Z):
            rolled = [(roll(value, g.edge), roll(value, -g.edge)) for value in (load(fy, tj) for tj in range(across))]
            for tj in range(across):
                beyond = zero
                if fz == ZZ:
                    ys = [g.yper * tj + k for k in range(g.yper)]
                    beyond = -shifted_top(g, lambda y: water_out[pl.ds(row * ny + y, SUB, stride=ny), :], ys, lane)
                change = along_x(fx, tj) + along_y(g, rolled, tj, lane) + along_z(g, load(fz, tj), beyond, depth)
                results.append((target * across + tj, load_v(target, ti, tj) + load_hb(ti, tj) * change))
        for key, value in results:
            bricks_out[key, pl.ds(row, SUB), :] = value


def pack(g, water, bricks, params, hb_water, row_first, row_last, col_first, col_last, first):
    nx, ny, plane, across, edge = g.nx, g.ny, g.plane, g.across, g.edge
    lane = lane_ids()
    for out, x in ((row_first, 0), (row_last, nx - 1)):
        for t in range(g.ytiles):
            own = x * ny + SUB * t
            out[pl.ds(M_P + SUB * t, SUB), :] = water[pl.ds(own, SUB), :]
            out[pl.ds(M_U + SUB * t, SUB), :] = water[pl.ds(plane + own, SUB), :]
            if first:
                out[pl.ds(ROW_CONST + SUB * t, SUB), :] = hb_water[pl.ds(own, SUB), :]
        for tj in range(across):
            block = M_BRICK + SUB * tj
            for k, field in enumerate(ALONG_X + (VX, VY, VZ)):
                out[pl.ds(block + k, 1), :] = bricks[field * across + tj, pl.ds(x, 1), :]
            out[pl.ds(block + 6, 1), :] = params[HB * across + tj, pl.ds(x, 1), :]
            spare = bricks[YY * across + tj, pl.ds(x, 1), :]
            shear = bricks[YZ * across + tj, pl.ds(x, 1), :]
            if tj == 0:
                spare = jnp.where(lane[0:1, :] < edge, spare, roll_row(shear, edge))
            elif tj == across - 1:
                spare = jnp.where(lane[0:1, :] >= LANES - edge, spare, roll_row(shear, -edge))
            out[pl.ds(block + 7, 1), :] = spare
    for out, y, tj in ((col_first, 0, 0), (col_last, ny - 1, across - 1)):
        for t in range(g.xtiles):
            own = SUB * t * ny + y
            out[pl.ds(M_P + SUB * t, SUB), :] = water[pl.ds(own, SUB, stride=ny), :]
            out[pl.ds(M_U + SUB * t, SUB), :] = water[pl.ds(2 * plane + own, SUB, stride=ny), :]
            if first:
                out[pl.ds(COL_CONST + SUB * t, SUB), :] = hb_water[pl.ds(own, SUB, stride=ny), :]
            rows = pl.ds(SUB * t, SUB)
            pieces = [bricks[field * across + tj, rows, :] for field in ALONG_Y + (VX, VY, VZ)]
            pieces.append(params[HB * across + tj, rows, :])
            packed = None
            for k, value in enumerate(pieces):
                moved = roll(value, edge * (k - y % g.yper))
                packed = moved if packed is None else jnp.where(lane >= edge * k, moved, packed)
            out[pl.ds(M_BRICK + SUB * t, SUB), :] = packed
        out[pl.ds(M_CORNER, 2 * SUB), :] = jnp.zeros((2 * SUB, LANES), jnp.float32)


def first_kernel(
    g, live, table, water_hbm, material_hbm, motion_hbm, kinds_hbm,
    water_out, bricks_out, params, hb_water, hk_water, row_first, row_last, col_first, col_last,
    press, stress, water, material, motion, kinds, sems,
):
    nx, ny, plane, across = g.nx, g.ny, g.plane, g.across
    copies = [
        pltpu.make_async_copy(motion_hbm, motion, sems.at[0]),
        pltpu.make_async_copy(kinds_hbm, kinds, sems.at[1]),
        pltpu.make_async_copy(water_hbm.at[0], press.at[pl.ds(1, nx), pl.ds(PAD, ny), :], sems.at[2]),
        pltpu.make_async_copy(material_hbm, material, sems.at[3]),
        pltpu.make_async_copy(water_hbm.at[pl.ds(1, 3)], water, sems.at[4]),
    ]
    for copy in copies:
        copy.start()
    lane = lane_ids()
    levels = table.shape[0]
    scales = (0.5, 0.5, 1.0, 1.0, 1.0, 1.0, 0.5, 1.0)
    columns = []
    for c, factor in enumerate(scales):
        column = jnp.zeros((SUB, LANES), jnp.float32)
        for level in range(levels):
            column = jnp.where(lane == level, table[level, c], column)
        columns.append(column * factor)
    set_zero_pads(g, press, stress)

    copies[0].wait()
    copies[1].wait()

    @pl.loop(0, g.xtiles)
    def _(ti):
        for tj in range(across):
            slot = g.slot(ti, tj)
            rows, lanes = g.place(ti, tj)
            alive = live[slot].astype(jnp.float32)
            here = aligned(SUB * ti)
            index = kinds[slot, rows, lanes]
            for c in range(8):
                value = pick(columns[c], index)
                params[c * across + tj, here, :] = value if 3 <= c < 6 else value * alive
            for field in range(XX, YZ + 1):
                value = motion[slot, field, rows, lanes] * alive
                bricks_out[field * across + tj, here, :] = value
                stress[(field - XX) * across + tj, aligned(PAD + SUB * ti), :] = value

    copies[2].wait()
    copies[3].wait()

    @pl.loop(0, nx)
    def _(x):
        results = []
        for t in range(g.ytiles):
            own = x * ny + SUB * t
            index = material[x, pl.ds(SUB * t, SUB), :]
            results.append((own, pick(columns[0], index), pick(columns[1], index), press[x + 1, pl.ds(PAD + SUB * t, SUB), :]))
        for own, hb, hk, p in results:
            hb_water[aligned(own), :] = hb
            hk_water[aligned(own), :] = hk
            water_out[aligned(own), :] = p

    copies[4].wait()

    def load_u(k, x, t):
        return water[k - 1, x, pl.ds(SUB * t, SUB), :]

    def load_v(field, ti, tj):
        slot = g.slot(ti, tj)
        rows, lanes = g.place(ti, tj)
        return motion[slot, field, rows, lanes] * live[slot].astype(jnp.float32)

    def load_hb(ti, tj):
        return params[HB * across + tj, aligned(SUB * ti), :]

    velocity_part(g, water_out, press, stress, hb_water, load_u, load_v, bricks_out, load_hb)
    pack(g, water_out, bricks_out, params, hb_water, row_first, row_last, col_first, col_last, True)


def step_kernel(g, first, last, *refs):
    refs = list(refs)

    def take(count):
        taken = refs[:count]
        del refs[:count]
        return taken

    if first:
        (live,) = take(1)
    water, bricks, memory, params, hb_water, hk_water = take(6)
    row_before, row_after, col_before, col_after = take(4)
    if not first:
        (const_in,) = take(1)
    water_out, bricks_out, memory_out = take(3)
    if not last:
        sends = take(4)
    if first:
        (const_out,) = take(1)
    press, stress, ux, uy, speed = take(5)

    nx, ny, edge, across, plane = g.nx, g.ny, g.edge, g.across, g.plane
    wide = across + 2
    lane = lane_ids()
    depth = lane % edge
    top_pick = surface_pick() * edge + (edge - 1)
    py = ny + 2 * PAD

    def const(side, t):
        if first:
            ref, start = ((row_before, ROW_CONST), (row_after, ROW_CONST), (col_before, COL_CONST), (col_after, COL_CONST))[side]
            value = ref[pl.ds(start + SUB * t, SUB), :]
            const_out[pl.ds(32 * side + SUB * t, SUB), :] = value
            return value
        return const_in[pl.ds(32 * side + SUB * t, SUB), :]

    if not last:
        set_zero_pads(g, press, stress)

    @pl.loop(0, nx)
    def _(x):
        for t in range(g.ytiles):
            own = x * ny + SUB * t
            ux[aligned(ny + own), :] = water[aligned(plane + own), :]
            uy[aligned(x * py + PAD + SUB * t), :] = water[aligned(2 * plane + own), :]

    for side, (ref, x, halo, sign) in enumerate(((row_before, 0, -1, 1.0), (row_after, nx - 1, nx, -1.0))):
        for t in range(g.ytiles):
            own = x * ny + SUB * t
            here = pl.ds(ny + own, SUB)
            ux[here, :] = ux[here, :] + sign * hb_water[pl.ds(own, SUB), :] * ref[pl.ds(M_P + SUB * t, SUB), :]
            ux[pl.ds((halo + 1) * ny + SUB * t, SUB), :] = (
                ref[pl.ds(M_U + SUB * t, SUB), :] - sign * const(side, t) * water[pl.ds(own, SUB), :]
            )
    for side, (ref, y, halo, sign) in enumerate(((col_before, 0, -1, 1.0), (col_after, ny - 1, ny, -1.0))):
        for t in range(g.xtiles):
            own = pl.ds(SUB * t * ny + y, SUB, stride=ny)
            here = pl.ds(SUB * t * py + PAD + y, SUB, stride=py)
            uy[here, :] = uy[here, :] + sign * hb_water[own, :] * ref[pl.ds(M_P + SUB * t, SUB), :]
            uy[pl.ds(SUB * t * py + PAD + halo, SUB, stride=py), :] = (
                ref[pl.ds(M_U + SUB * t, SUB), :] - sign * const(2 + side, t) * water[own, :]
            )

    for field in (VX, VY, VZ):
        for tj in range(across):
            for ti in range(g.xtiles):
                speed[field * wide + 1 + tj, pl.ds(PAD + SUB * ti, SUB), :] = bricks[field * across + tj, pl.ds(SUB * ti, SUB), :]
    for ref, x, halo, sign in ((row_before, 0, -1, 1.0), (row_after, nx - 1, nx, -1.0)):
        for tj in range(across):
            block = M_BRICK + SUB * tj
            own_hb = sign * params[HB * across + tj, pl.ds(x, 1), :]
            their_hb = sign * ref[pl.ds(block + 6, 1), :]
            for c in (VX, VY, VZ):
                here = pl.ds(PAD + x, 1)
                key = c * wide + 1 + tj
                speed[key, here, :] = speed[key, here, :] - own_hb * ref[pl.ds(block + c, 1), :]
                speed[key, pl.ds(PAD + halo, 1), :] = (
                    ref[pl.ds(block + 3 + c, 1), :] + their_hb * bricks[ALONG_X[c] * across + tj, pl.ds(x, 1), :]
                )
    for ref, tj, halo, sign in ((col_before, 0, 0, 1.0), (col_after, across - 1, wide - 1, -1.0)):
        near = 0 if tj == 0 else LANES - edge
        far = LANES - edge - near
        inside = (lane >= near) & (lane < near + edge)
        for ti in range(g.xtiles):
            column = ref[pl.ds(M_BRICK + SUB * ti, SUB), :]
            own_hb = jnp.where(inside, sign * params[HB * across + tj, pl.ds(SUB * ti, SUB), :], 0.0)
            their_hb = sign * roll(column, far - 6 * edge)
            here = pl.ds(PAD + SUB * ti, SUB)
            for c in (VX, VY, VZ):
                key = c * wide + 1 + tj
                speed[key, here, :] = speed[key, here, :] - own_hb * roll(column, near - c * edge)
                own = bricks[ALONG_Y[c] * across + tj, pl.ds(SUB * ti, SUB), :]
                speed[c * wide + halo, here, :] = roll(column, far - (3 + c) * edge) + their_hb * roll(own, far - near)
        for k, (row_ref, x, x_halo, x_sign) in enumerate(((row_before, 0, -1, 1.0), (row_after, nx - 1, nx, -1.0))):
            corner = M_CORNER + SUB * k
            spare = ref[pl.ds(corner + 7, 1), :]
            toward = near - far
            inward = edge if far == 0 else -edge
            along = (
                roll_row(ref[pl.ds(corner + 1, 1), :], toward),
                roll_row(spare, toward),
                roll_row(spare, toward - inward),
            )
            row_hb = jnp.where(inside[0:1, :], sign * row_ref[pl.ds(M_BRICK + SUB * tj + 6, 1), :], 0.0)
            col_hb = x_sign * roll_row(ref[pl.ds(M_BRICK + x, 1), :], far - 6 * edge)
            for c in (VX, VY, VZ):
                key, here = c * wide + 1 + tj, pl.ds(PAD + x_halo, 1)
                speed[key, here, :] = speed[key, here, :] - row_hb * along[c]
                key, here = c * wide + halo, pl.ds(PAD + x, 1)
                speed[key, here, :] = speed[key, here, :] - col_hb * ref[pl.ds(corner + c, 1), :]

    @pl.loop(0, g.xtiles)
    def _(ti):
        row = pl.multiple_of(SUB * ti, SUB)
        here = pl.ds(row, SUB)
        inner = pl.ds(pl.multiple_of(row + PAD, SUB), SUB)
        rolled = []
        for field in (VX, VY, VZ):
            values = [speed[field * wide + tj, inner, :] for tj in range(wide)]
            rolled.append([(roll(value, edge), roll(value, -edge)) for value in values])
        tops = (
            lambda y: ux[pl.ds(ny + row * ny + y, SUB, stride=ny), :],
            lambda y: uy[pl.ds(row * py + PAD + y, SUB, stride=py), :],
            lambda y: water[pl.ds(3 * plane + row * ny + y, SUB, stride=ny), :],
        )
        for tj in range(across):
            ys = [g.yper * tj + k for k in range(g.yper)]
            dx, dy, dz, speeds = [], [], [], []
            for field in (VX, VY, VZ):
                key = field * wide + 1 + tj
                value = speed[key, inner, :]
                speeds.append(value)
                dx.append(speed[key, pl.ds(row + PAD + 1, SUB), :] - speed[key, pl.ds(row + PAD - 1, SUB), :])
                dy.append(along_y(g, rolled[field], tj + 1, lane))
                dz.append(along_z(g, value, shifted_top(g, tops[field], ys, lane), depth))
            strain = [dx[0], dy[1], dz[2], dy[0] + dx[1], dz[0] + dx[2], dz[1] + dy[2]]
            dilation = strain[0] + strain[1] + strain[2]

            def param(c):
                return params[c * across + tj, here, :]

            lame, shear = param(LAME) * dilation, param(SHEAR)
            spring_lame, spring_shear = param(SPRING_LAME) * dilation, param(SPRING_SHEAR)
            retain = [param(RETAIN + l) for l in range(3)]
            half_shear, half_spring = 0.5 * shear, 0.5 * spring_shear
            slot = g.slot(ti, tj)
            rows, lanes = g.place(ti, tj)
            if first:
                alive = live[slot].astype(jnp.float32)
            stresses, memories = [], {}
            for comp in range(6):
                if comp < 3:
                    elastic = shear * strain[comp] + lame
                    relaxed = spring_shear * strain[comp] + spring_lame
                else:
                    elastic = half_shear * strain[comp]
                    relaxed = half_spring * strain[comp]
                summed = None
                for l in range(3):
                    place = 6 * l + comp
                    if first:
                        old = memory[slot, place, rows, lanes] * alive
                    else:
                        old = memory[place * across + tj, here, :]
                    new = relaxed + retain[l] * (old - relaxed)
                    memories[place] = new
                    summed = new if summed is None else summed + new
                stresses.append(bricks[(XX + comp) * across + tj, here, :] + elastic - summed)
            for place, value in memories.items():
                if last:
                    memory_out[slot, place, rows, lanes] = value
                else:
                    memory_out[place * across + tj, here, :] = value
            for comp, value in enumerate(stresses):
                if last:
                    bricks_out[slot, XX + comp, rows, lanes] = value
                else:
                    bricks_out[(XX + comp) * across + tj, here, :] = value
                    stress[comp * across + tj, inner, :] = value
            if last:
                for field in (VX, VY, VZ):
                    bricks_out[slot, field, rows, lanes] = speeds[field]

    def water_layer(x):
        results = []
        for t in range(g.ytiles):
            own = x * ny + SUB * t
            dx = ux[aligned((x + 2) * ny + SUB * t), :] - ux[aligned(x * ny + SUB * t), :]
            row = x * py + PAD + SUB * t
            dy = uy[pl.ds(row + 1, SUB), :] - uy[pl.ds(row - 1, SUB), :]
            surface = jnp.broadcast_to(speed[VZ * wide + 1 + t, pl.ds(PAD + x, 1), :], (SUB, LANES))
            uz = water[aligned(3 * plane + own), :]
            dz = water_z(g, uz, pick(surface, top_pick), lane)
            value = water[aligned(own), :] - hk_water[aligned(own), :] * (dx + dy + dz)
            results.append((own, t, value, uz, row))
        return x, results

    @pl.loop(0, nx // 2)
    def _(pair):
        for x, results in (water_layer(2 * pair), water_layer(2 * pair + 1)):
            for own, t, value, uz, row in results:
                water_out[aligned(own), :] = value
                if last:
                    water_out[aligned(plane + own), :] = ux[aligned(ny + own), :]
                    water_out[aligned(2 * plane + own), :] = uy[aligned(row), :]
                    water_out[aligned(3 * plane + own), :] = uz
                else:
                    press[x + 1, pl.ds(PAD + SUB * t, SUB), :] = value

    if not last:
        def load_u(k, x, t):
            if k == 1:
                return ux[aligned((x + 1) * ny + SUB * t), :]
            if k == 2:
                return uy[aligned(x * py + PAD + SUB * t), :]
            return water[aligned(3 * plane + x * ny + SUB * t), :]

        def load_v(field, ti, tj):
            return speed[field * wide + 1 + tj, aligned(PAD + SUB * ti), :]

        def load_hb(ti, tj):
            return params[HB * across + tj, aligned(SUB * ti), :]

        velocity_part(g, water_out, press, stress, hb_water, load_u, load_v, bricks_out, load_hb)
        pack(g, water_out, bricks_out, params, hb_water, *sends, False)


def exchange(g, sends):
    row_first, row_last, col_first, col_last = sends

    def shift(value, axis, up):
        count = lax.axis_size(axis)
        pairs = [(i, i + 1) for i in range(count - 1)]
        return lax.ppermute(value, axis, pairs if up else [(j, i) for i, j in pairs])

    row_before = shift(row_last, "row", True)
    row_after = shift(row_first, "row", False)

    def with_corners(message, tile):
        start = M_BRICK + SUB * tile
        corners = jnp.concatenate([row_before[start : start + SUB], row_after[start : start + SUB]])
        return lax.dynamic_update_slice(message, corners, (M_CORNER, 0))

    col_before = shift(with_corners(col_last, g.across - 1), "col", True)
    col_after = shift(with_corners(col_first, 0), "col", False)
    return row_before, row_after, col_before, col_after


def body(
    brick_velocity_stress,
    brick_relaxation_memory,
    brick_cell_material,
    brick_live,
    water_state,
    water_material,
    material_table,
):
    _, nx, ny, nz = water_state.shape
    g = Grid(nx, ny, brick_cell_material.shape[1])
    across, plane = g.across, g.plane

    def f32(*shape):
        return jax.ShapeDtypeStruct(shape, jnp.float32)

    smem = pl.BlockSpec(memory_space=pltpu.SMEM)
    vmem = pl.BlockSpec(memory_space=pltpu.VMEM)
    hbm = pl.BlockSpec(memory_space=pltpu.HBM)
    params = pltpu.CompilerParams(vmem_limit_bytes=24 * 1024 * 1024)
    press = pltpu.VMEM((nx + 2, ny + 2 * PAD, nz), jnp.float32)
    stress = pltpu.VMEM((6 * across, nx + 2 * PAD, LANES), jnp.float32)

    def messages(first):
        extra = 32 if first else 0
        return [f32(96 + extra, LANES)] * 2 + [f32(112 + extra, LANES)] * 2

    results = pl.pallas_call(
        functools.partial(first_kernel, g),
        out_shape=[
            f32(4 * plane, nz), f32(9 * across, nx, LANES), f32(8 * across, nx, LANES), f32(plane, nz), f32(plane, nz),
        ] + messages(True),
        in_specs=[smem] * 2 + [hbm] * 4,
        out_specs=[vmem] * 9,
        scratch_shapes=[
            press,
            stress,
            pltpu.VMEM((3, nx, ny, nz), jnp.float32),
            pltpu.VMEM(water_material.shape, jnp.int32),
            pltpu.VMEM(brick_velocity_stress.shape, jnp.float32),
            pltpu.VMEM(brick_cell_material.shape, jnp.int32),
            pltpu.SemaphoreType.DMA((5,)),
        ],
        compiler_params=params,
        name="first_velocity",
    )(brick_live, material_table, water_state, water_material, brick_velocity_stress, brick_cell_material)
    water, bricks, coefficients, hb_water, hk_water = results[:5]
    sends = results[5:]
    memory = brick_relaxation_memory
    constants = ()
    for step in range(STEPS):
        first, last = step == 0, step == STEPS - 1
        received = exchange(g, sends)
        if last:
            out_shape = [f32(4 * plane, nz), f32(*brick_velocity_stress.shape), f32(*memory_shape)]
        else:
            memory_shape = brick_relaxation_memory.shape
            out_shape = [f32(4 * plane, nz), f32(9 * across, nx, LANES), f32(18 * across, nx, LANES)] + messages(False)
        if first:
            out_shape += [f32(128, LANES)]
        alive = (brick_live,) if first else ()
        results = pl.pallas_call(
            functools.partial(step_kernel, g, first, last),
            out_shape=out_shape,
            in_specs=[smem] * len(alive) + [vmem] * (10 + len(constants)),
            out_specs=[vmem] * len(out_shape),
            scratch_shapes=[
                press,
                stress,
                pltpu.VMEM(((nx + 2) * ny, nz), jnp.float32),
                pltpu.VMEM((nx * (ny + 2 * PAD), nz), jnp.float32),
                pltpu.VMEM((3 * (across + 2), nx + 2 * PAD, LANES), jnp.float32),
            ],
            compiler_params=params,
            name="time_step",
        )(*alive, water, bricks, memory, coefficients, hb_water, hk_water, *received, *constants)
        water, bricks, memory = results[:3]
        if not last:
            sends = results[3:7]
        if first:
            constants = (results[7],)
    return bricks, memory, water.reshape(water_state.shape)


def solution(mesh):
    return jax.shard_map(
        body,
        mesh=mesh,
        in_specs=(
            P(("row", "col"), None, None, None),
            P(("row", "col"), None, None, None),
            P(("row", "col"), None, None),
            P(("row", "col")),
            P(None, "row", "col", None),
            P("row", "col", None),
            P(),
        ),
        out_specs=(
            P(("row", "col"), None, None, None),
            P(("row", "col"), None, None, None),
            P(None, "row", "col", None),
        ),
        check_vma=False,
    )
```

time: 101 us -> 84.2 us (0.83)
  Pallas kernels: 36.9 us -> 24.4 us
  waiting for transfers between devices: 20.6 us -> 18.5 us
  local copies, waits for them, and re-layouts: 6.98 us -> 5.88 us
    pallas_call x3, Pallas kernels: 36.1 us -> 17.6 us  [body(): pl.pallas_call(functools.partial(step_kernel, g, first, last), out_shape=...]
    pallas_call x1, Pallas kernels: 0.84 us -> 6.79 us  [body(): pl.pallas_call(functools.partial(first_kernel, g), out_shape=[f32(4 * pla...]
    ppermute x12, waiting for transfers between devices: 20.6 us -> 18.5 us  [shift(): lax.ppermute(value, axis, pairs if up else [(j, i) for i, j in pairs])]
    unnamed x20 -> x14, local copies, waits for them, and re-layouts: 6.79 us -> 5.87 us
where the time goes in v1:
time: 84.2 us; the launch traced here: 82.7 us
  starting transfers between devices  33.2 us (39%)
  Pallas kernels  24.4 us (29%)
  waiting for transfers between devices  18.5 us (22%)
  local copies, waits for them, and re-layouts  5.88 us (7%)
    ppermute x12, starting transfers between devices, shift(): lax.ppermute(value, axis, pairs if up else [(j, i) for i, j in pairs])  33.2 us
    ppermute x12, waiting for transfers between devices, shift(): lax.ppermute(value, axis, pairs if up else [(j, i) for i, j in pairs])  18.5 us
    pallas_call x3, Pallas kernels, body(): pl.pallas_call(functools.partial(step_kernel, g, first, last), out_shape=...  17.6 us
    pallas_call x1, Pallas kernels, body(): pl.pallas_call(functools.partial(first_kernel, g), out_shape=[f32(4 * pla...  6.79 us
    unnamed x14, local copies, waits for them, and re-layouts  5.87 us
  transfers between devices with their start and end apart: 12, of which 9 were waited for; matrix products, arithmetic and copies ran while one was open for 0% of the time, Pallas kernels for 0%

profile of v1, /device:TPU:10, one launch (start us, length us, event | category | flops | bytes accessed | tf_op | source)
XLA Modules:
  0.0 82.7 jit_solution(9421039346078178286)
XLA Ops:
  0.6 0.0 copy-start
  0.6 1.6 %copy-done = f32[4,32,32,128]{3,2,1,0:T(8,128)S(1)} copy-done((f32[4,32,32,128]{3,2,1,0:T(8,128)S(1)}, f32[4,32,32,128]{3,2,1,0:T(8,128)}, u32[]{:S(2)}) %copy-start) | copy-done | bytes 2097176
  2.2 0.0 copy-start.2
  2.2 1.1 %copy-done.2 = f32[4,9,16,256]{3,2,1,0:T(8,128)S(1)} copy-done((f32[4,9,16,256]{3,2,1,0:T(8,128)S(1)}, f32[4,9,16,256]{3,2,1,0:T(8,128)}, u32[]{:S(2)}) %copy-start.2) | copy-done | bytes 589848
  3.3 0.0 copy-start.3
  3.3 1.0 %copy-done.3 = s32[32,32,128]{2,1,0:T(8,128)S(1)} copy-done((s32[32,32,128]{2,1,0:T(8,128)S(1)}, s32[32,32,128]{2,1,0:T(8,128)}, u32[]{:S(2)}) %copy-start.3) | copy-done | bytes 524312
  4.3 0.0 copy-start.4
  4.3 0.8 %copy-done.4 = s32[4,16,256]{2,1,0:T(8,128)S(1)} copy-done((s32[4,16,256]{2,1,0:T(8,128)S(1)}, s32[4,16,256]{2,1,0:T(8,128)}, u32[]{:S(2)}) %copy-start.4) | copy-done | bytes 65560
  5.2 0.0 copy-start.5
  5.2 0.7 copy-done.5
  5.9 0.0 copy-start.6
  5.9 0.7 copy-done.6
  6.5 0.0 copy-start.1
  6.5 6.8 %first_velocity.1 = (f32[4096,128]{1,0:T(8,128)S(1)}, f32[36,32,128]{2,1,0:T(8,128)S(1)}, f32[32,32,128]{2,1,0:T(8,128)S(1)}, f32[1024,128]{1,0:T(8,128)S(1)}, f...) custom-call(s32[4]{0:T(128)S(1)} %copy-done.6, ...), custom_call_target="tpu_custom_call" | custom-call | tf_op jit(solution)/shard_map/first_velocity/pallas_call | solution.py:558
  13.3 3.4 %collective-permute-start = (f32[128,128]{1,0:T(8,128)S(1)}, f32[128,128]{1,0:T(8,128)S(1)}, u32[]{:S(2)}, u32[]{:S(2)}) collective-permute-start(f32[128,128]{1,0:T(8,128)S(1)} %get-tuple-element.35), channel_id=1, source_target_pairs={{0,4},{4,8},{8,12},{12,16},{16,20},{20,24},{24,28},{1,5},{5,9},{9,... | collective-permute-start | bytes 196616 | tf_op jit(solution)/shard_map/ppermute | solution.py:516
  16.8 3.3 %collective-permute-start.1 = (f32[128,128]{1,0:T(8,128)S(1)}, f32[128,128]{1,0:T(8,128)S(1)}, u32[]{:S(2)}, u32[]{:S(2)}) collective-permute-start(f32[128,128]{1,0:T(8,128)S(1)} %get-tuple-element.36), channel_id=1, source_target_pairs={{4,0},{8,4},{12,8},{16,12},{20,16},{24,20},{28,24},{5,1},{9,5},{13... | collective-permute-start | bytes 196616 | tf_op jit(solution)/shard_map/ppermute | solution.py:516
  20.1 0.3 collective-permute-done.refs_7_
  20.4 2.5 %collective-permute-done.1.refs_8_ = f32[128,128]{1,0:T(8,128)S(1)} collective-permute-done((f32[128,128]{1,0:T(8,128)S(1)}, f32[128,128]{1,0:T(8,128)S(1)}, u32[]{:S(2)}, u32[]{:S(2)}) %collective-permute-start.1) | collective-permute-done | bytes 65568 | tf_op jit(solution)/shard_map/ppermute | solution.py:516
  22.9 1.9 %collective-permute-start.3 = (f32[144,128]{1,0:T(8,128)S(1)}, f32[144,128]{1,0:T(8,128)S(1)}, u32[]{:S(2)}, u32[]{:S(2)}) collective-permute-start(f32[144,128]{1,0:T(8,128)S(1)} %maximum_dynamic-update-slice_fusion.1), channel_id=1, source_target_pairs={{1,0},{2,1},{3,2},{5,4},{6,5},{7,6},{9,8},{10,9},{11,10},{13,12},{... | collective-permute-start | bytes 221192 | tf_op jit(solution)/shard_map/ppermute | solution.py:516
  24.9 2.4 %collective-permute-start.2 = (f32[144,128]{1,0:T(8,128)S(1)}, f32[144,128]{1,0:T(8,128)S(1)}, u32[]{:S(2)}, u32[]{:S(2)}) collective-permute-start(f32[144,128]{1,0:T(8,128)S(1)} %maximum_dynamic-update-slice_fusion), channel_id=1, source_target_pairs={{0,1},{1,2},{2,3},{4,5},{5,6},{6,7},{8,9},{9,10},{10,11},{12,13},{... | collective-permute-start | bytes 221192 | tf_op jit(solution)/shard_map/ppermute | solution.py:516
  27.3 0.0 collective-permute-done.3.refs_10_
  27.3 3.2 %collective-permute-done.2.refs_9_ = f32[144,128]{1,0:T(8,128)S(1)} collective-permute-done((f32[144,128]{1,0:T(8,128)S(1)}, f32[144,128]{1,0:T(8,128)S(1)}, u32[]{:S(2)}, u32[]{:S(2)}) %collective-permute-start.2) | collective-permute-done | bytes 73760 | tf_op jit(solution)/shard_map/ppermute | solution.py:516
  30.5 0.0 copy-done.1
  30.5 6.5 %time_step.3 = (f32[4096,128]{1,0:T(8,128)S(1)}, f32[36,32,128]{2,1,0:T(8,128)S(1)}, f32[72,32,128]{2,1,0:T(8,128)S(1)}, f32[96,128]{1,0:T(8,128)S(1)}, f32[96,1...) custom-call(s32[4]{0:T(128)S(1)} %copy-done.6, ...), custom_call_target="tpu_custom_call" | custom-call | tf_op jit(solution)/shard_map/time_step/pallas_call | solution.py:592
  37.0 4.3 %collective-permute-start.4 = (f32[96,128]{1,0:T(8,128)S(1)}, f32[96,128]{1,0:T(8,128)S(1)}, u32[]{:S(2)}, u32[]{:S(2)}) collective-permute-start(f32[96,128]{1,0:T(8,128)S(1)} %get-tuple-element.42), channel_id=1, source_target_pairs={{0,4},{4,8},{8,12},{12,16},{16,20},{20,24},{24,28},{1,5},{5,9},{9,... | collective-permute-start | bytes 147464 | tf_op jit(solution)/shard_map/ppermute | solution.py:516
  41.3 2.4 %collective-permute-start.5 = (f32[96,128]{1,0:T(8,128)S(1)}, f32[96,128]{1,0:T(8,128)S(1)}, u32[]{:S(2)}, u32[]{:S(2)}) collective-permute-start(f32[96,128]{1,0:T(8,128)S(1)} %get-tuple-element.43), channel_id=1, source_target_pairs={{4,0},{8,4},{12,8},{16,12},{20,16},{24,20},{28,24},{5,1},{9,5},{13... | collective-permute-start | bytes 147464 | tf_op jit(solution)/shard_map/ppermute | solution.py:516
  43.7 0.2 collective-permute-done.4.refs_6_
  43.9 3.4 %collective-permute-done.5.refs_7_ = f32[96,128]{1,0:T(8,128)S(1)} collective-permute-done((f32[96,128]{1,0:T(8,128)S(1)}, f32[96,128]{1,0:T(8,128)S(1)}, u32[]{:S(2)}, u32[]{:S(2)}) %collective-permute-start.5) | collective-permute-done | bytes 49184 | tf_op jit(solution)/shard_map/ppermute | solution.py:516
  47.3 1.9 %collective-permute-start.7 = (f32[112,128]{1,0:T(8,128)S(1)}, f32[112,128]{1,0:T(8,128)S(1)}, u32[]{:S(2)}, u32[]{:S(2)}) collective-permute-start(f32[112,128]{1,0:T(8,128)S(1)} %maximum_dynamic-update-slice_fusion.3), channel_id=1, source_target_pairs={{1,0},{2,1},{3,2},{5,4},{6,5},{7,6},{9,8},{10,9},{11,10},{13,12},{... | collective-permute-start | bytes 172040 | tf_op jit(solution)/shard_map/ppermute | solution.py:516
  49.2 2.4 %collective-permute-start.6 = (f32[112,128]{1,0:T(8,128)S(1)}, f32[112,128]{1,0:T(8,128)S(1)}, u32[]{:S(2)}, u32[]{:S(2)}) collective-permute-start(f32[112,128]{1,0:T(8,128)S(1)} %maximum_dynamic-update-slice_fusion.2), channel_id=1, source_target_pairs={{0,1},{1,2},{2,3},{4,5},{5,6},{6,7},{8,9},{9,10},{10,11},{12,13},{... | collective-permute-start | bytes 172040 | tf_op jit(solution)/shard_map/ppermute | solution.py:516
  51.6 0.0 collective-permute-done.7.refs_9_
  51.7 3.1 %collective-permute-done.6.refs_8_ = f32[112,128]{1,0:T(8,128)S(1)} collective-permute-done((f32[112,128]{1,0:T(8,128)S(1)}, f32[112,128]{1,0:T(8,128)S(1)}, u32[]{:S(2)}, u32[]{:S(2)}) %collective-permute-start.6) | collective-permute-done | bytes 57376 | tf_op jit(solution)/shard_map/ppermute | solution.py:516
  54.7 5.9 %time_step.4 = (f32[4096,128]{1,0:T(8,128)S(1)}, f32[36,32,128]{2,1,0:T(8,128)S(1)}, f32[72,32,128]{2,1,0:T(8,128)S(1)}, f32[96,128]{1,0:T(8,128)S(1)}, f32[96,1...) custom-call(f32[4096,128]{1,0:T(8,128)S(1)} %get-tuple-element.39.refs_0_, ...), custom_call_target="tpu_custom_call" | custom-call | tf_op jit(solution)/shard_map/time_step/pallas_call | solution.py:592
  60.6 3.4 %collective-permute-start.8 = (f32[96,128]{1,0:T(8,128)S(1)}, f32[96,128]{1,0:T(8,128)S(1)}, u32[]{:S(2)}, u32[]{:S(2)}) collective-permute-start(f32[96,128]{1,0:T(8,128)S(1)} %get-tuple-element.50), channel_id=1, source_target_pairs={{0,4},{4,8},{8,12},{12,16},{16,20},{20,24},{24,28},{1,5},{5,9},{9,... | collective-permute-start | bytes 147464 | tf_op jit(solution)/shard_map/ppermute | solution.py:516
  64.1 3.3 %collective-permute-start.9 = (f32[96,128]{1,0:T(8,128)S(1)}, f32[96,128]{1,0:T(8,128)S(1)}, u32[]{:S(2)}, u32[]{:S(2)}) collective-permute-start(f32[96,128]{1,0:T(8,128)S(1)} %get-tuple-element.51), channel_id=1, source_target_pairs={{4,0},{8,4},{12,8},{16,12},{20,16},{24,20},{28,24},{5,1},{9,5},{13... | collective-permute-start | bytes 147464 | tf_op jit(solution)/shard_map/ppermute | solution.py:516
  67.4 0.1 collective-permute-done.8.refs_6_
  67.5 2.5 %collective-permute-done.9.refs_7_ = f32[96,128]{1,0:T(8,128)S(1)} collective-permute-done((f32[96,128]{1,0:T(8,128)S(1)}, f32[96,128]{1,0:T(8,128)S(1)}, u32[]{:S(2)}, u32[]{:S(2)}) %collective-permute-start.9) | collective-permute-done | bytes 49184 | tf_op jit(solution)/shard_map/ppermute | solution.py:516
  70.1 1.9 %collective-permute-start.11 = (f32[112,128]{1,0:T(8,128)S(1)}, f32[112,128]{1,0:T(8,128)S(1)}, u32[]{:S(2)}, u32[]{:S(2)}) collective-permute-start(f32[112,128]{1,0:T(8,128)S(1)} %maximum_dynamic-update-slice_fusion.5), channel_id=1, source_target_pairs={{1,0},{2,1},{3,2},{5,4},{6,5},{7,6},{9,8},{10,9},{11,10},{13,12},{... | collective-permute-start | bytes 172040 | tf_op jit(solution)/shard_map/ppermute | solution.py:516
  72.0 2.4 %collective-permute-start.10 = (f32[112,128]{1,0:T(8,128)S(1)}, f32[112,128]{1,0:T(8,128)S(1)}, u32[]{:S(2)}, u32[]{:S(2)}) collective-permute-start(f32[112,128]{1,0:T(8,128)S(1)} %maximum_dynamic-update-slice_fusion.4), channel_id=1, source_target_pairs={{0,1},{1,2},{2,3},{4,5},{5,6},{6,7},{8,9},{9,10},{10,11},{12,13},{... | collective-permute-start | bytes 172040 | tf_op jit(solution)/shard_map/ppermute | solution.py:516
  74.4 0.0 collective-permute-done.11.refs_9_
  74.4 3.1 %collective-permute-done.10.refs_8_ = f32[112,128]{1,0:T(8,128)S(1)} collective-permute-done((f32[112,128]{1,0:T(8,128)S(1)}, f32[112,128]{1,0:T(8,128)S(1)}, u32[]{:S(2)}, u32[]{:S(2)}) %collective-permute-start.10) | collective-permute-done | bytes 57376 | tf_op jit(solution)/shard_map/ppermute | solution.py:516
  77.5 5.2 %time_step.5 = (f32[4096,128]{1,0:T(8,128)}, f32[4,9,16,256]{3,2,1,0:T(8,128)}, f32[4,18,16,256]{3,2,1,0:T(8,128)}) custom-call(f32[4096,128]{1,0:T(8,128)S(1)} %get-tuple-element.47.refs_0_, f32[36,32,128]{2,1,0:T(8,128)S(1)} %get-tuple-element.48.refs_1_, f32[72,32,128]{2,1,0:T(8,128)S(1)} %get-tuple-element.49.refs_2_, ...), custom_call_target="tpu_custom_call" | custom-call | tf_op jit(solution)/shard_map/time_step/pallas_call | solution.py:592
  (12 shorter events, 0.0 us)
Async XLA Ops:
  0.6 1.6 %copy-start = (f32[4,32,32,128]{3,2,1,0:T(8,128)S(1)}, f32[4,32,32,128]{3,2,1,0:T(8,128)}, u32[]{:S(2)}) copy-start(f32[4,32,32,128]{3,2,1,0:T(8,128)} %water_hbm.1) | copy-start | bytes 6291460
  2.2 1.1 %copy-start.2 = (f32[4,9,16,256]{3,2,1,0:T(8,128)S(1)}, f32[4,9,16,256]{3,2,1,0:T(8,128)}, u32[]{:S(2)}) copy-start(f32[4,9,16,256]{3,2,1,0:T(8,128)} %motion_hbm.1) | copy-start | bytes 1769476
  3.3 1.0 %copy-start.3 = (s32[32,32,128]{2,1,0:T(8,128)S(1)}, s32[32,32,128]{2,1,0:T(8,128)}, u32[]{:S(2)}) copy-start(s32[32,32,128]{2,1,0:T(8,128)} %material_hbm.1) | copy-start | bytes 1572868
  4.3 0.8 %copy-start.4 = (s32[4,16,256]{2,1,0:T(8,128)S(1)}, s32[4,16,256]{2,1,0:T(8,128)}, u32[]{:S(2)}) copy-start(s32[4,16,256]{2,1,0:T(8,128)} %kinds_hbm.1) | copy-start | bytes 196612
  5.2 0.7 copy-start.5
  5.9 0.7 copy-start.6
  6.5 24.0 %copy-start.1 = (f32[4,18,16,256]{3,2,1,0:T(8,128)S(1)}, f32[4,18,16,256]{3,2,1,0:T(8,128)}, u32[]{:S(2)}) copy-start(f32[4,18,16,256]{3,2,1,0:T(8,128)} %refs_3_.1) | copy-start | bytes 3538948
  13.3 7.1 %collective-permute-start = (f32[128,128]{1,0:T(8,128)S(1)}, f32[128,128]{1,0:T(8,128)S(1)}, u32[]{:S(2)}, u32[]{:S(2)}) collective-permute-start(f32[128,128]{1,0:T(8,128)S(1)} %get-tuple-element.35), channel_id=1, source_target_pairs={{0,4},{4,8},{8,12},{12,16},{16,20},{20,24},{24,28},{1,5},{5,9},{9,... | collective-permute-start | bytes 196616 | tf_op jit(solution)/shard_map/ppermute | solution.py:516
  16.8 6.2 %collective-permute-start.1 = (f32[128,128]{1,0:T(8,128)S(1)}, f32[128,128]{1,0:T(8,128)S(1)}, u32[]{:S(2)}, u32[]{:S(2)}) collective-permute-start(f32[128,128]{1,0:T(8,128)S(1)} %get-tuple-element.36), channel_id=1, source_target_pairs={{4,0},{8,4},{12,8},{16,12},{20,16},{24,20},{28,24},{5,1},{9,5},{13... | collective-permute-start | bytes 196616 | tf_op jit(solution)/shard_map/ppermute | solution.py:516
  22.9 4.3 %collective-permute-start.3 = (f32[144,128]{1,0:T(8,128)S(1)}, f32[144,128]{1,0:T(8,128)S(1)}, u32[]{:S(2)}, u32[]{:S(2)}) collective-permute-start(f32[144,128]{1,0:T(8,128)S(1)} %maximum_dynamic-update-slice_fusion.1), channel_id=1, source_target_pairs={{1,0},{2,1},{3,2},{5,4},{6,5},{7,6},{9,8},{10,9},{11,10},{13,12},{... | collective-permute-start | bytes 221192 | tf_op jit(solution)/shard_map/ppermute | solution.py:516
  24.9 5.7 %collective-permute-start.2 = (f32[144,128]{1,0:T(8,128)S(1)}, f32[144,128]{1,0:T(8,128)S(1)}, u32[]{:S(2)}, u32[]{:S(2)}) collective-permute-start(f32[144,128]{1,0:T(8,128)S(1)} %maximum_dynamic-update-slice_fusion), channel_id=1, source_target_pairs={{0,1},{1,2},{2,3},{4,5},{5,6},{6,7},{8,9},{9,10},{10,11},{12,13},{... | collective-permute-start | bytes 221192 | tf_op jit(solution)/shard_map/ppermute | solution.py:516
  37.0 6.9 %collective-permute-start.4 = (f32[96,128]{1,0:T(8,128)S(1)}, f32[96,128]{1,0:T(8,128)S(1)}, u32[]{:S(2)}, u32[]{:S(2)}) collective-permute-start(f32[96,128]{1,0:T(8,128)S(1)} %get-tuple-element.42), channel_id=1, source_target_pairs={{0,4},{4,8},{8,12},{12,16},{16,20},{20,24},{24,28},{1,5},{5,9},{9,... | collective-permute-start | bytes 147464 | tf_op jit(solution)/shard_map/ppermute | solution.py:516
  41.3 6.0 %collective-permute-start.5 = (f32[96,128]{1,0:T(8,128)S(1)}, f32[96,128]{1,0:T(8,128)S(1)}, u32[]{:S(2)}, u32[]{:S(2)}) collective-permute-start(f32[96,128]{1,0:T(8,128)S(1)} %get-tuple-element.43), channel_id=1, source_target_pairs={{4,0},{8,4},{12,8},{16,12},{20,16},{24,20},{28,24},{5,1},{9,5},{13... | collective-permute-start | bytes 147464 | tf_op jit(solution)/shard_map/ppermute | solution.py:516
  47.3 4.3 %collective-permute-start.7 = (f32[112,128]{1,0:T(8,128)S(1)}, f32[112,128]{1,0:T(8,128)S(1)}, u32[]{:S(2)}, u32[]{:S(2)}) collective-permute-start(f32[112,128]{1,0:T(8,128)S(1)} %maximum_dynamic-update-slice_fusion.3), channel_id=1, source_target_pairs={{1,0},{2,1},{3,2},{5,4},{6,5},{7,6},{9,8},{10,9},{11,10},{13,12},{... | collective-permute-start | bytes 172040 | tf_op jit(solution)/shard_map/ppermute | solution.py:516
  49.2 5.5 %collective-permute-start.6 = (f32[112,128]{1,0:T(8,128)S(1)}, f32[112,128]{1,0:T(8,128)S(1)}, u32[]{:S(2)}, u32[]{:S(2)}) collective-permute-start(f32[112,128]{1,0:T(8,128)S(1)} %maximum_dynamic-update-slice_fusion.2), channel_id=1, source_target_pairs={{0,1},{1,2},{2,3},{4,5},{5,6},{6,7},{8,9},{9,10},{10,11},{12,13},{... | collective-permute-start | bytes 172040 | tf_op jit(solution)/shard_map/ppermute | solution.py:516
  60.6 6.9 %collective-permute-start.8 = (f32[96,128]{1,0:T(8,128)S(1)}, f32[96,128]{1,0:T(8,128)S(1)}, u32[]{:S(2)}, u32[]{:S(2)}) collective-permute-start(f32[96,128]{1,0:T(8,128)S(1)} %get-tuple-element.50), channel_id=1, source_target_pairs={{0,4},{4,8},{8,12},{12,16},{16,20},{20,24},{24,28},{1,5},{5,9},{9,... | collective-permute-start | bytes 147464 | tf_op jit(solution)/shard_map/ppermute | solution.py:516
  64.1 6.0 %collective-permute-start.9 = (f32[96,128]{1,0:T(8,128)S(1)}, f32[96,128]{1,0:T(8,128)S(1)}, u32[]{:S(2)}, u32[]{:S(2)}) collective-permute-start(f32[96,128]{1,0:T(8,128)S(1)} %get-tuple-element.51), channel_id=1, source_target_pairs={{4,0},{8,4},{12,8},{16,12},{20,16},{24,20},{28,24},{5,1},{9,5},{13... | collective-permute-start | bytes 147464 | tf_op jit(solution)/shard_map/ppermute | solution.py:516
  70.1 4.3 %collective-permute-start.11 = (f32[112,128]{1,0:T(8,128)S(1)}, f32[112,128]{1,0:T(8,128)S(1)}, u32[]{:S(2)}, u32[]{:S(2)}) collective-permute-start(f32[112,128]{1,0:T(8,128)S(1)} %maximum_dynamic-update-slice_fusion.5), channel_id=1, source_target_pairs={{1,0},{2,1},{3,2},{5,4},{6,5},{7,6},{9,8},{10,9},{11,10},{13,12},{... | collective-permute-start | bytes 172040 | tf_op jit(solution)/shard_map/ppermute | solution.py:516
  72.0 5.5 %collective-permute-start.10 = (f32[112,128]{1,0:T(8,128)S(1)}, f32[112,128]{1,0:T(8,128)S(1)}, u32[]{:S(2)}, u32[]{:S(2)}) collective-permute-start(f32[112,128]{1,0:T(8,128)S(1)} %maximum_dynamic-update-slice_fusion.4), channel_id=1, source_target_pairs={{0,1},{1,2},{2,3},{4,5},{5,6},{6,7},{8,9},{9,10},{10,11},{12,13},{... | collective-permute-start | bytes 172040 | tf_op jit(solution)/shard_map/ppermute | solution.py:516

commit v2 on v1

--- a/solution.py
+++ b/solution.py
@@ -12,7 +12,7 @@
 SUB = 8
 PAD = 8
 VX, VY, VZ, XX, YY, ZZ, XY, XZ, YZ = range(9)
-HB, LAME, SHEAR, RETAIN, SPRING_LAME, SPRING_SHEAR = 0, 1, 2, 3, 6, 7
+HB, LAME, SHEAR, RETAIN, SPRING_LAME, SPRING_SHEAR, ALIVE = 0, 1, 2, 3, 6, 7, 8
 ALONG_X = (XX, XY, XZ)
 ALONG_Y = (XY, YY, YZ)
 ALONG_Z = (XZ, YZ, ZZ)
@@ -204,9 +204,9 @@
 
 
 def first_kernel(
-    g, live, table, water_hbm, material_hbm, motion_hbm, kinds_hbm,
+    g, live_hbm, table_hbm, water_hbm, material_hbm, motion_hbm, kinds_hbm,
     water_out, bricks_out, params, hb_water, hk_water, row_first, row_last, col_first, col_last,
-    press, stress, water, material, motion, kinds, sems,
+    press, stress, water, material, motion, kinds, live, table, sems,
 ):
     nx, ny, plane, across = g.nx, g.ny, g.plane, g.across
     copies = [
@@ -215,10 +215,15 @@
         pltpu.make_async_copy(water_hbm.at[0], press.at[pl.ds(1, nx), pl.ds(PAD, ny), :], sems.at[2]),
         pltpu.make_async_copy(material_hbm, material, sems.at[3]),
         pltpu.make_async_copy(water_hbm.at[pl.ds(1, 3)], water, sems.at[4]),
+        pltpu.make_async_copy(live_hbm, live, sems.at[5]),
+        pltpu.make_async_copy(table_hbm, table, sems.at[6]),
     ]
     for copy in copies:
         copy.start()
     lane = lane_ids()
+    set_zero_pads(g, press, stress)
+    copies[5].wait()
+    copies[6].wait()
     levels = table.shape[0]
     scales = (0.5, 0.5, 1.0, 1.0, 1.0, 1.0, 0.5, 1.0)
     columns = []
@@ -227,7 +232,6 @@
         for level in range(levels):
             column = jnp.where(lane == level, table[level, c], column)
         columns.append(column * factor)
-    set_zero_pads(g, press, stress)
 
     copies[0].wait()
     copies[1].wait()
@@ -243,6 +247,7 @@
             for c in range(8):
                 value = pick(columns[c], index)
                 params[c * across + tj, here, :] = value if 3 <= c < 6 else value * alive
+            params[ALIVE * across + tj, here, :] = jnp.zeros((SUB, LANES), jnp.float32) + alive
             for field in range(XX, YZ + 1):
                 value = motion[slot, field, rows, lanes] * alive
                 bricks_out[field * across + tj, here, :] = value
@@ -288,8 +293,6 @@
         del refs[:count]
         return taken
 
-    if first:
-        (live,) = take(1)
     water, bricks, memory, params, hb_water, hk_water = take(6)
     row_before, row_after, col_before, col_after = take(4)
     if not first:
@@ -428,7 +431,7 @@
             slot = g.slot(ti, tj)
             rows, lanes = g.place(ti, tj)
             if first:
-                alive = live[slot].astype(jnp.float32)
+                alive = param(ALIVE)
             stresses, memories = [], {}
             for comp in range(6):
                 if comp < 3:
@@ -544,7 +547,6 @@
     def f32(*shape):
         return jax.ShapeDtypeStruct(shape, jnp.float32)
 
-    smem = pl.BlockSpec(memory_space=pltpu.SMEM)
     vmem = pl.BlockSpec(memory_space=pltpu.VMEM)
     hbm = pl.BlockSpec(memory_space=pltpu.HBM)
     params = pltpu.CompilerParams(vmem_limit_bytes=24 * 1024 * 1024)
@@ -558,9 +560,9 @@
     results = pl.pallas_call(
         functools.partial(first_kernel, g),
         out_shape=[
-            f32(4 * plane, nz), f32(9 * across, nx, LANES), f32(8 * across, nx, LANES), f32(plane, nz), f32(plane, nz),
+            f32(4 * plane, nz), f32(9 * across, nx, LANES), f32(9 * across, nx, LANES), f32(plane, nz), f32(plane, nz),
         ] + messages(True),
-        in_specs=[smem] * 2 + [hbm] * 4,
+        in_specs=[hbm] * 6,
         out_specs=[vmem] * 9,
         scratch_shapes=[
             press,
@@ -569,11 +571,18 @@
             pltpu.VMEM(water_material.shape, jnp.int32),
             pltpu.VMEM(brick_velocity_stress.shape, jnp.float32),
             pltpu.VMEM(brick_cell_material.shape, jnp.int32),
-            pltpu.SemaphoreType.DMA((5,)),
+            pltpu.SMEM(brick_live.shape, jnp.int32),
+            pltpu.SMEM(material_table.shape, jnp.float32),
+            pltpu.SemaphoreType.DMA((7,)),
         ],
         compiler_params=params,
         name="first_velocity",
-    )(brick_live, material_table, water_state, water_material, brick_velocity_stress, brick_cell_material)
+    )(*[
+        pltpu.with_memory_space_constraint(value, pltpu.HBM)
+        for value in (
+            brick_live, material_table, water_state, water_material, brick_velocity_stress, brick_cell_material,
+        )
+    ])
     water, bricks, coefficients, hb_water, hk_water = results[:5]
     sends = results[5:]
     memory = brick_relaxation_memory
@@ -588,11 +597,10 @@
             out_shape = [f32(4 * plane, nz), f32(9 * across, nx, LANES), f32(18 * across, nx, LANES)] + messages(False)
         if first:
             out_shape += [f32(128, LANES)]
-        alive = (brick_live,) if first else ()
         results = pl.pallas_call(
             functools.partial(step_kernel, g, first, last),
             out_shape=out_shape,
-            in_specs=[smem] * len(alive) + [vmem] * (10 + len(constants)),
+            in_specs=[vmem] * (10 + len(constants)),
             out_specs=[vmem] * len(out_shape),
             scratch_shapes=[
                 press,
@@ -603,7 +611,7 @@
             ],
             compiler_params=params,
             name="time_step",
-        )(*alive, water, bricks, memory, coefficients, hb_water, hk_water, *received, *constants)
+        )(water, bricks, memory, coefficients, hb_water, hk_water, *received, *constants)
         water, bricks, memory = results[:3]
         if not last:
             sends = results[3:7]

time: 84.2 us -> 77.4 us (0.919)
  local copies, waits for them, and re-layouts: 5.88 us -> 0.01 us
    unnamed x14 -> x2, local copies, waits for them, and re-layouts: 5.87 us -> 0.01 us
where the time goes in v2:
time: 77.4 us; the launch traced here: 76.1 us
  starting transfers between devices  33.2 us (43%)
  Pallas kernels  23.6 us (30%)
  waiting for transfers between devices  18.5 us (24%)
  between operations  0.8 us (1%)
    ppermute x12, starting transfers between devices, shift(): lax.ppermute(value, axis, pairs if up else [(j, i) for i, j in pairs])  33.2 us
    ppermute x12, waiting for transfers between devices, shift(): lax.ppermute(value, axis, pairs if up else [(j, i) for i, j in pairs])  18.5 us
    pallas_call x3, Pallas kernels, body(): pl.pallas_call(functools.partial(step_kernel, g, first, last), out_shape=...  16.9 us
    pallas_call x1, Pallas kernels, body(): pl.pallas_call(functools.partial(first_kernel, g), out_shape=[f32(4 * pla...  6.75 us
  transfers between devices with their start and end apart: 12, of which 9 were waited for; matrix products, arithmetic and copies ran while one was open for 0% of the time, Pallas kernels for 0%

profile of v2, /device:TPU:10, one launch (start us, length us, event | category | flops | bytes accessed | tf_op | source)
XLA Modules:
  0.0 76.1 jit_solution(9901893775801388300)
XLA Ops:
  0.6 0.0 copy-start
  0.6 6.7 %first_velocity.1 = (f32[4096,128]{1,0:T(8,128)S(1)}, f32[36,32,128]{2,1,0:T(8,128)S(1)}, f32[36,32,128]{2,1,0:T(8,128)S(1)}, f32[1024,128]{1,0:T(8,128)S(1)}, f...) custom-call(s32[4]{0:T(128)} %live_hbm.1, ...), custom_call_target="tpu_custom_call" | custom-call | tf_op jit(solution)/shard_map/first_velocity/pallas_call | solution.py:560
  7.4 3.4 %collective-permute-start = (f32[128,128]{1,0:T(8,128)S(1)}, f32[128,128]{1,0:T(8,128)S(1)}, u32[]{:S(2)}, u32[]{:S(2)}) collective-permute-start(f32[128,128]{1,0:T(8,128)S(1)} %get-tuple-element.35), channel_id=1, source_target_pairs={{0,4},{4,8},{8,12},{12,16},{16,20},{20,24},{24,28},{1,5},{5,9},{9,... | collective-permute-start | bytes 196616 | tf_op jit(solution)/shard_map/ppermute | solution.py:519
  10.8 3.3 %collective-permute-start.1 = (f32[128,128]{1,0:T(8,128)S(1)}, f32[128,128]{1,0:T(8,128)S(1)}, u32[]{:S(2)}, u32[]{:S(2)}) collective-permute-start(f32[128,128]{1,0:T(8,128)S(1)} %get-tuple-element.36), channel_id=1, source_target_pairs={{4,0},{8,4},{12,8},{16,12},{20,16},{24,20},{28,24},{5,1},{9,5},{13... | collective-permute-start | bytes 196616 | tf_op jit(solution)/shard_map/ppermute | solution.py:519
  14.2 0.3 collective-permute-done.refs_6_
  14.5 2.5 %collective-permute-done.1.refs_7_ = f32[128,128]{1,0:T(8,128)S(1)} collective-permute-done((f32[128,128]{1,0:T(8,128)S(1)}, f32[128,128]{1,0:T(8,128)S(1)}, u32[]{:S(2)}, u32[]{:S(2)}) %collective-permute-start.1) | collective-permute-done | bytes 65568 | tf_op jit(solution)/shard_map/ppermute | solution.py:519
  17.0 1.9 %collective-permute-start.3 = (f32[144,128]{1,0:T(8,128)S(1)}, f32[144,128]{1,0:T(8,128)S(1)}, u32[]{:S(2)}, u32[]{:S(2)}) collective-permute-start(f32[144,128]{1,0:T(8,128)S(1)} %maximum_dynamic-update-slice_fusion.1), channel_id=1, source_target_pairs={{1,0},{2,1},{3,2},{5,4},{6,5},{7,6},{9,8},{10,9},{11,10},{13,12},{... | collective-permute-start | bytes 221192 | tf_op jit(solution)/shard_map/ppermute | solution.py:519
  18.9 2.4 %collective-permute-start.2 = (f32[144,128]{1,0:T(8,128)S(1)}, f32[144,128]{1,0:T(8,128)S(1)}, u32[]{:S(2)}, u32[]{:S(2)}) collective-permute-start(f32[144,128]{1,0:T(8,128)S(1)} %maximum_dynamic-update-slice_fusion), channel_id=1, source_target_pairs={{0,1},{1,2},{2,3},{4,5},{5,6},{6,7},{8,9},{9,10},{10,11},{12,13},{... | collective-permute-start | bytes 221192 | tf_op jit(solution)/shard_map/ppermute | solution.py:519
  21.3 0.0 collective-permute-done.3.refs_9_
  21.4 3.2 %collective-permute-done.2.refs_8_ = f32[144,128]{1,0:T(8,128)S(1)} collective-permute-done((f32[144,128]{1,0:T(8,128)S(1)}, f32[144,128]{1,0:T(8,128)S(1)}, u32[]{:S(2)}, u32[]{:S(2)}) %collective-permute-start.2) | collective-permute-done | bytes 73760 | tf_op jit(solution)/shard_map/ppermute | solution.py:519
  24.6 0.0 copy-done
  24.6 5.9 %time_step.3 = (f32[4096,128]{1,0:T(8,128)S(1)}, f32[36,32,128]{2,1,0:T(8,128)S(1)}, f32[72,32,128]{2,1,0:T(8,128)S(1)}, f32[96,128]{1,0:T(8,128)S(1)}, f32[96,1...) custom-call(f32[4096,128]{1,0:T(8,128)S(1)} %get-tuple-element.30.refs_0_, ...), custom_call_target="tpu_custom_call" | custom-call | tf_op jit(solution)/shard_map/time_step/pallas_call | solution.py:600
  30.5 4.3 %collective-permute-start.4 = (f32[96,128]{1,0:T(8,128)S(1)}, f32[96,128]{1,0:T(8,128)S(1)}, u32[]{:S(2)}, u32[]{:S(2)}) collective-permute-start(f32[96,128]{1,0:T(8,128)S(1)} %get-tuple-element.42), channel_id=1, source_target_pairs={{0,4},{4,8},{8,12},{12,16},{16,20},{20,24},{24,28},{1,5},{5,9},{9,... | collective-permute-start | bytes 147464 | tf_op jit(solution)/shard_map/ppermute | solution.py:519
  34.8 2.4 %collective-permute-start.5 = (f32[96,128]{1,0:T(8,128)S(1)}, f32[96,128]{1,0:T(8,128)S(1)}, u32[]{:S(2)}, u32[]{:S(2)}) collective-permute-start(f32[96,128]{1,0:T(8,128)S(1)} %get-tuple-element.43), channel_id=1, source_target_pairs={{4,0},{8,4},{12,8},{16,12},{20,16},{24,20},{28,24},{5,1},{9,5},{13... | collective-permute-start | bytes 147464 | tf_op jit(solution)/shard_map/ppermute | solution.py:519
  37.2 0.2 collective-permute-done.4.refs_6_
  37.4 3.4 %collective-permute-done.5.refs_7_ = f32[96,128]{1,0:T(8,128)S(1)} collective-permute-done((f32[96,128]{1,0:T(8,128)S(1)}, f32[96,128]{1,0:T(8,128)S(1)}, u32[]{:S(2)}, u32[]{:S(2)}) %collective-permute-start.5) | collective-permute-done | bytes 49184 | tf_op jit(solution)/shard_map/ppermute | solution.py:519
  40.8 1.9 %collective-permute-start.7 = (f32[112,128]{1,0:T(8,128)S(1)}, f32[112,128]{1,0:T(8,128)S(1)}, u32[]{:S(2)}, u32[]{:S(2)}) collective-permute-start(f32[112,128]{1,0:T(8,128)S(1)} %maximum_dynamic-update-slice_fusion.3), channel_id=1, source_target_pairs={{1,0},{2,1},{3,2},{5,4},{6,5},{7,6},{9,8},{10,9},{11,10},{13,12},{... | collective-permute-start | bytes 172040 | tf_op jit(solution)/shard_map/ppermute | solution.py:519
  42.7 2.4 %collective-permute-start.6 = (f32[112,128]{1,0:T(8,128)S(1)}, f32[112,128]{1,0:T(8,128)S(1)}, u32[]{:S(2)}, u32[]{:S(2)}) collective-permute-start(f32[112,128]{1,0:T(8,128)S(1)} %maximum_dynamic-update-slice_fusion.2), channel_id=1, source_target_pairs={{0,1},{1,2},{2,3},{4,5},{5,6},{6,7},{8,9},{9,10},{10,11},{12,13},{... | collective-permute-start | bytes 172040 | tf_op jit(solution)/shard_map/ppermute | solution.py:519
  45.1 0.0 collective-permute-done.7.refs_9_
  45.1 3.1 %collective-permute-done.6.refs_8_ = f32[112,128]{1,0:T(8,128)S(1)} collective-permute-done((f32[112,128]{1,0:T(8,128)S(1)}, f32[112,128]{1,0:T(8,128)S(1)}, u32[]{:S(2)}, u32[]{:S(2)}) %collective-permute-start.6) | collective-permute-done | bytes 57376 | tf_op jit(solution)/shard_map/ppermute | solution.py:519
  48.2 5.8 %time_step.4 = (f32[4096,128]{1,0:T(8,128)S(1)}, f32[36,32,128]{2,1,0:T(8,128)S(1)}, f32[72,32,128]{2,1,0:T(8,128)S(1)}, f32[96,128]{1,0:T(8,128)S(1)}, f32[96,1...) custom-call(f32[4096,128]{1,0:T(8,128)S(1)} %get-tuple-element.39.refs_0_, ...), custom_call_target="tpu_custom_call" | custom-call | tf_op jit(solution)/shard_map/time_step/pallas_call | solution.py:600
  54.1 3.4 %collective-permute-start.8 = (f32[96,128]{1,0:T(8,128)S(1)}, f32[96,128]{1,0:T(8,128)S(1)}, u32[]{:S(2)}, u32[]{:S(2)}) collective-permute-start(f32[96,128]{1,0:T(8,128)S(1)} %get-tuple-element.50), channel_id=1, source_target_pairs={{0,4},{4,8},{8,12},{12,16},{16,20},{20,24},{24,28},{1,5},{5,9},{9,... | collective-permute-start | bytes 147464 | tf_op jit(solution)/shard_map/ppermute | solution.py:519
  57.5 3.3 %collective-permute-start.9 = (f32[96,128]{1,0:T(8,128)S(1)}, f32[96,128]{1,0:T(8,128)S(1)}, u32[]{:S(2)}, u32[]{:S(2)}) collective-permute-start(f32[96,128]{1,0:T(8,128)S(1)} %get-tuple-element.51), channel_id=1, source_target_pairs={{4,0},{8,4},{12,8},{16,12},{20,16},{24,20},{28,24},{5,1},{9,5},{13... | collective-permute-start | bytes 147464 | tf_op jit(solution)/shard_map/ppermute | solution.py:519
  60.8 0.1 collective-permute-done.8.refs_6_
  61.0 2.5 %collective-permute-done.9.refs_7_ = f32[96,128]{1,0:T(8,128)S(1)} collective-permute-done((f32[96,128]{1,0:T(8,128)S(1)}, f32[96,128]{1,0:T(8,128)S(1)}, u32[]{:S(2)}, u32[]{:S(2)}) %collective-permute-start.9) | collective-permute-done | bytes 49184 | tf_op jit(solution)/shard_map/ppermute | solution.py:519
  63.5 1.9 %collective-permute-start.11 = (f32[112,128]{1,0:T(8,128)S(1)}, f32[112,128]{1,0:T(8,128)S(1)}, u32[]{:S(2)}, u32[]{:S(2)}) collective-permute-start(f32[112,128]{1,0:T(8,128)S(1)} %maximum_dynamic-update-slice_fusion.5), channel_id=1, source_target_pairs={{1,0},{2,1},{3,2},{5,4},{6,5},{7,6},{9,8},{10,9},{11,10},{13,12},{... | collective-permute-start | bytes 172040 | tf_op jit(solution)/shard_map/ppermute | solution.py:519
  65.4 2.4 %collective-permute-start.10 = (f32[112,128]{1,0:T(8,128)S(1)}, f32[112,128]{1,0:T(8,128)S(1)}, u32[]{:S(2)}, u32[]{:S(2)}) collective-permute-start(f32[112,128]{1,0:T(8,128)S(1)} %maximum_dynamic-update-slice_fusion.4), channel_id=1, source_target_pairs={{0,1},{1,2},{2,3},{4,5},{5,6},{6,7},{8,9},{9,10},{10,11},{12,13},{... | collective-permute-start | bytes 172040 | tf_op jit(solution)/shard_map/ppermute | solution.py:519
  67.8 0.0 collective-permute-done.11.refs_9_
  67.8 3.1 %collective-permute-done.10.refs_8_ = f32[112,128]{1,0:T(8,128)S(1)} collective-permute-done((f32[112,128]{1,0:T(8,128)S(1)}, f32[112,128]{1,0:T(8,128)S(1)}, u32[]{:S(2)}, u32[]{:S(2)}) %collective-permute-start.10) | collective-permute-done | bytes 57376 | tf_op jit(solution)/shard_map/ppermute | solution.py:519
  70.9 5.2 %time_step.5 = (f32[4096,128]{1,0:T(8,128)}, f32[4,9,16,256]{3,2,1,0:T(8,128)}, f32[4,18,16,256]{3,2,1,0:T(8,128)}) custom-call(f32[4096,128]{1,0:T(8,128)S(1)} %get-tuple-element.47.refs_0_, f32[36,32,128]{2,1,0:T(8,128)S(1)} %get-tuple-element.48.refs_1_, f32[72,32,128]{2,1,0:T(8,128)S(1)} %get-tuple-element.49.refs_2_, ...), custom_call_target="tpu_custom_call" | custom-call | tf_op jit(solution)/shard_map/time_step/pallas_call | solution.py:600
  (12 shorter events, 0.0 us)
Async XLA Ops:
  0.6 24.0 %copy-start = (f32[4,18,16,256]{3,2,1,0:T(8,128)S(1)}, f32[4,18,16,256]{3,2,1,0:T(8,128)}, u32[]{:S(2)}) copy-start(f32[4,18,16,256]{3,2,1,0:T(8,128)} %refs_2_.1) | copy-start | bytes 3538948
  7.4 7.1 %collective-permute-start = (f32[128,128]{1,0:T(8,128)S(1)}, f32[128,128]{1,0:T(8,128)S(1)}, u32[]{:S(2)}, u32[]{:S(2)}) collective-permute-start(f32[128,128]{1,0:T(8,128)S(1)} %get-tuple-element.35), channel_id=1, source_target_pairs={{0,4},{4,8},{8,12},{12,16},{16,20},{20,24},{24,28},{1,5},{5,9},{9,... | collective-permute-start | bytes 196616 | tf_op jit(solution)/shard_map/ppermute | solution.py:519
  10.8 6.2 %collective-permute-start.1 = (f32[128,128]{1,0:T(8,128)S(1)}, f32[128,128]{1,0:T(8,128)S(1)}, u32[]{:S(2)}, u32[]{:S(2)}) collective-permute-start(f32[128,128]{1,0:T(8,128)S(1)} %get-tuple-element.36), channel_id=1, source_target_pairs={{4,0},{8,4},{12,8},{16,12},{20,16},{24,20},{28,24},{5,1},{9,5},{13... | collective-permute-start | bytes 196616 | tf_op jit(solution)/shard_map/ppermute | solution.py:519
  17.0 4.3 %collective-permute-start.3 = (f32[144,128]{1,0:T(8,128)S(1)}, f32[144,128]{1,0:T(8,128)S(1)}, u32[]{:S(2)}, u32[]{:S(2)}) collective-permute-start(f32[144,128]{1,0:T(8,128)S(1)} %maximum_dynamic-update-slice_fusion.1), channel_id=1, source_target_pairs={{1,0},{2,1},{3,2},{5,4},{6,5},{7,6},{9,8},{10,9},{11,10},{13,12},{... | collective-permute-start | bytes 221192 | tf_op jit(solution)/shard_map/ppermute | solution.py:519
  18.9 5.7 %collective-permute-start.2 = (f32[144,128]{1,0:T(8,128)S(1)}, f32[144,128]{1,0:T(8,128)S(1)}, u32[]{:S(2)}, u32[]{:S(2)}) collective-permute-start(f32[144,128]{1,0:T(8,128)S(1)} %maximum_dynamic-update-slice_fusion), channel_id=1, source_target_pairs={{0,1},{1,2},{2,3},{4,5},{5,6},{6,7},{8,9},{9,10},{10,11},{12,13},{... | collective-permute-start | bytes 221192 | tf_op jit(solution)/shard_map/ppermute | solution.py:519
  30.5 6.9 %collective-permute-start.4 = (f32[96,128]{1,0:T(8,128)S(1)}, f32[96,128]{1,0:T(8,128)S(1)}, u32[]{:S(2)}, u32[]{:S(2)}) collective-permute-start(f32[96,128]{1,0:T(8,128)S(1)} %get-tuple-element.42), channel_id=1, source_target_pairs={{0,4},{4,8},{8,12},{12,16},{16,20},{20,24},{24,28},{1,5},{5,9},{9,... | collective-permute-start | bytes 147464 | tf_op jit(solution)/shard_map/ppermute | solution.py:519
  34.8 6.0 %collective-permute-start.5 = (f32[96,128]{1,0:T(8,128)S(1)}, f32[96,128]{1,0:T(8,128)S(1)}, u32[]{:S(2)}, u32[]{:S(2)}) collective-permute-start(f32[96,128]{1,0:T(8,128)S(1)} %get-tuple-element.43), channel_id=1, source_target_pairs={{4,0},{8,4},{12,8},{16,12},{20,16},{24,20},{28,24},{5,1},{9,5},{13... | collective-permute-start | bytes 147464 | tf_op jit(solution)/shard_map/ppermute | solution.py:519
  40.8 4.3 %collective-permute-start.7 = (f32[112,128]{1,0:T(8,128)S(1)}, f32[112,128]{1,0:T(8,128)S(1)}, u32[]{:S(2)}, u32[]{:S(2)}) collective-permute-start(f32[112,128]{1,0:T(8,128)S(1)} %maximum_dynamic-update-slice_fusion.3), channel_id=1, source_target_pairs={{1,0},{2,1},{3,2},{5,4},{6,5},{7,6},{9,8},{10,9},{11,10},{13,12},{... | collective-permute-start | bytes 172040 | tf_op jit(solution)/shard_map/ppermute | solution.py:519
  42.7 5.5 %collective-permute-start.6 = (f32[112,128]{1,0:T(8,128)S(1)}, f32[112,128]{1,0:T(8,128)S(1)}, u32[]{:S(2)}, u32[]{:S(2)}) collective-permute-start(f32[112,128]{1,0:T(8,128)S(1)} %maximum_dynamic-update-slice_fusion.2), channel_id=1, source_target_pairs={{0,1},{1,2},{2,3},{4,5},{5,6},{6,7},{8,9},{9,10},{10,11},{12,13},{... | collective-permute-start | bytes 172040 | tf_op jit(solution)/shard_map/ppermute | solution.py:519
  54.1 6.9 %collective-permute-start.8 = (f32[96,128]{1,0:T(8,128)S(1)}, f32[96,128]{1,0:T(8,128)S(1)}, u32[]{:S(2)}, u32[]{:S(2)}) collective-permute-start(f32[96,128]{1,0:T(8,128)S(1)} %get-tuple-element.50), channel_id=1, source_target_pairs={{0,4},{4,8},{8,12},{12,16},{16,20},{20,24},{24,28},{1,5},{5,9},{9,... | collective-permute-start | bytes 147464 | tf_op jit(solution)/shard_map/ppermute | solution.py:519
  57.5 6.0 %collective-permute-start.9 = (f32[96,128]{1,0:T(8,128)S(1)}, f32[96,128]{1,0:T(8,128)S(1)}, u32[]{:S(2)}, u32[]{:S(2)}) collective-permute-start(f32[96,128]{1,0:T(8,128)S(1)} %get-tuple-element.51), channel_id=1, source_target_pairs={{4,0},{8,4},{12,8},{16,12},{20,16},{24,20},{28,24},{5,1},{9,5},{13... | collective-permute-start | bytes 147464 | tf_op jit(solution)/shard_map/ppermute | solution.py:519
  63.5 4.3 %collective-permute-start.11 = (f32[112,128]{1,0:T(8,128)S(1)}, f32[112,128]{1,0:T(8,128)S(1)}, u32[]{:S(2)}, u32[]{:S(2)}) collective-permute-start(f32[112,128]{1,0:T(8,128)S(1)} %maximum_dynamic-update-slice_fusion.5), channel_id=1, source_target_pairs={{1,0},{2,1},{3,2},{5,4},{6,5},{7,6},{9,8},{10,9},{11,10},{13,12},{... | collective-permute-start | bytes 172040 | tf_op jit(solution)/shard_map/ppermute | solution.py:519
  65.4 5.5 %collective-permute-start.10 = (f32[112,128]{1,0:T(8,128)S(1)}, f32[112,128]{1,0:T(8,128)S(1)}, u32[]{:S(2)}, u32[]{:S(2)}) collective-permute-start(f32[112,128]{1,0:T(8,128)S(1)} %maximum_dynamic-update-slice_fusion.4), channel_id=1, source_target_pairs={{0,1},{1,2},{2,3},{4,5},{5,6},{6,7},{8,9},{9,10},{10,11},{12,13},{... | collective-permute-start | bytes 172040 | tf_op jit(solution)/shard_map/ppermute | solution.py:519

commit v3 on v2

v3 whole, which is shorter than its diff:
```python
import functools

import jax
import jax.numpy as jnp
from jax import lax
from jax.experimental import pallas as pl
from jax.experimental.pallas import tpu as pltpu
from jax.sharding import PartitionSpec as P

STEPS = 3
LANES = 128
SUB = 8
PAD = 8
VX, VY, VZ, XX, YY, ZZ, XY, XZ, YZ = range(9)
HB, LAME, SHEAR, RETAIN, SPRING_LAME, SPRING_SHEAR, ALIVE = 0, 1, 2, 3, 6, 7, 8
ALONG_X = (XX, XY, XZ)
ALONG_Y = (XY, YY, YZ)
ALONG_Z = (XZ, YZ, ZZ)
M_P, M_U, M_BRICK, M_CORNER = 0, 32, 64, 96
COL_CONST, ROW_CONST = 96, 112


def lane_ids():
    return lax.broadcasted_iota(jnp.int32, (SUB, LANES), 1)


def roll(value, shift):
    shift = shift % LANES
    return value if shift == 0 else pltpu.roll(value, shift, 1)


def roll_row(row, shift):
    shift = shift % LANES
    if shift == 0:
        return row
    return pltpu.roll(jnp.broadcast_to(row, (SUB, LANES)), shift, 1)[0:1, :]


def pick(values, indices):
    return jnp.take_along_axis(values, indices, axis=1, mode="promise_in_bounds")


def aligned(start, size=SUB):
    return pl.ds(start if isinstance(start, int) else pl.multiple_of(start, SUB), size)


class Grid:
    def __init__(self, nx, ny, edge):
        self.nx, self.ny, self.edge = nx, ny, edge
        self.plane = nx * ny
        self.across = ny * edge // LANES
        self.yper = LANES // edge
        self.half = self.across // 2
        self.xtiles, self.ytiles = nx // SUB, ny // SUB
        self.per = edge // SUB

    def slot(self, ti, tj):
        return 2 * (ti // self.per) + tj // self.half

    def place(self, ti, tj):
        return aligned((ti % self.per) * SUB), pl.ds((tj % self.half) * LANES, LANES)


def set_zero_pads(g, press, stress):
    zero = jnp.zeros((SUB, LANES), jnp.float32)
    for t in range(g.ytiles):
        press[0, pl.ds(PAD + SUB * t, SUB), :] = zero
        press[g.nx + 1, pl.ds(PAD + SUB * t, SUB), :] = zero

    @pl.loop(1, g.nx + 1)
    def _(x):
        press[x, pl.ds(0, SUB), :] = zero
        press[x, pl.ds(PAD + g.ny, SUB), :] = zero

    for field in ALONG_X:
        for tj in range(g.across):
            key = (field - XX) * g.across + tj
            stress[key, pl.ds(0, SUB), :] = zero
            stress[key, pl.ds(PAD + g.nx, SUB), :] = zero


def shifted_top(g, load, ys, lane):
    top = None
    for k, y in enumerate(ys):
        value = roll(load(y), g.edge * k + g.edge - 1)
        top = value if top is None else jnp.where(lane >= g.edge * k, value, top)
    return top


def along_y(g, rolled, tj, lane):
    zero = jnp.zeros((SUB, LANES), jnp.float32)
    after = rolled[tj + 1][1] if tj + 1 < len(rolled) else zero
    before = rolled[tj - 1][0] if tj > 0 else zero
    ahead = jnp.where(lane < LANES - g.edge, rolled[tj][1], after)
    behind = jnp.where(lane >= g.edge, rolled[tj][0], before)
    return ahead - behind


def along_z(g, value, beyond, depth):
    zero = jnp.zeros((SUB, LANES), jnp.float32)
    return jnp.where(depth == g.edge - 1, beyond, roll(value, -1)) - jnp.where(depth == 0, zero, roll(value, 1))


def water_z(g, value, below, lane):
    zero = jnp.zeros((SUB, LANES), jnp.float32)
    return jnp.where(lane == LANES - 1, zero, roll(value, -1)) - jnp.where(lane == 0, below, roll(value, 1))


def surface_pick():
    return lax.broadcasted_iota(jnp.int32, (SUB, LANES), 0)


def water_velocity(g, layers, water_out, press, stress, hb_water, load_u):
    lane = lane_ids()
    top_pick = surface_pick() * g.edge + (g.edge - 1)

    def water_layer(x):
        results = []
        for t in range(g.ytiles):
            rows = pl.ds(PAD + SUB * t, SUB)
            here = press[x + 1, rows, :]
            dx = press[x + 2, rows, :] - press[x, rows, :]
            dy = press[x + 1, pl.ds(PAD + SUB * t + 1, SUB), :] - press[x + 1, pl.ds(PAD + SUB * t - 1, SUB), :]
            surface = jnp.broadcast_to(stress[(ZZ - XX) * g.across + t, pl.ds(PAD + x, 1), :], (SUB, LANES))
            dz = water_z(g, here, -pick(surface, top_pick), lane)
            own = x * g.ny + SUB * t
            hb = hb_water[aligned(own), :]
            for k, change in ((1, dx), (2, dy), (3, dz)):
                results.append((k * g.plane + own, load_u(k, x, t) - hb * change))
        return results

    turns, layer = layers

    @pl.loop(0, turns)
    def _(turn):
        x = layer(turn)
        for row, value in water_layer(x) + water_layer(x + 1):
            water_out[aligned(row), :] = value


def brick_velocity(g, water_out, stress, load_v, bricks_out, load_hb):
    lane = lane_ids()
    depth = lane % g.edge
    zero = jnp.zeros((SUB, LANES), jnp.float32)
    across, ny = g.across, g.ny

    @pl.loop(0, g.xtiles)
    def _(ti):
        row = pl.multiple_of(SUB * ti, SUB)
        here = pl.ds(pl.multiple_of(row + PAD, SUB), SUB)

        def load(field, tj):
            return stress[(field - XX) * across + tj, here, :]

        def along_x(field, tj):
            key = (field - XX) * across + tj
            return stress[key, pl.ds(row + PAD + 1, SUB), :] - stress[key, pl.ds(row + PAD - 1, SUB), :]

        results = []
        for target, fx, fy, fz in zip((VX, VY, VZ), ALONG_X, ALONG_Y, ALONG_Z):
            rolled = [(roll(value, g.edge), roll(value, -g.edge)) for value in (load(fy, tj) for tj in range(across))]
            for tj in range(across):
                beyond = zero
                if fz == ZZ:
                    ys = [g.yper * tj + k for k in range(g.yper)]
                    beyond = -shifted_top(g, lambda y: water_out[pl.ds(row * ny + y, SUB, stride=ny), :], ys, lane)
                change = along_x(fx, tj) + along_y(g, rolled, tj, lane) + along_z(g, load(fz, tj), beyond, depth)
                results.append((target * across + tj, load_v(target, ti, tj) + load_hb(ti, tj) * change))
        for key, value in results:
            bricks_out[key, pl.ds(row, SUB), :] = value


def brick_stress(g, ti, first, bricks, memory, params, speed, tops, store):
    edge, across = g.edge, g.across
    wide = across + 2
    lane = lane_ids()
    depth = lane % edge
    row = SUB * ti if isinstance(ti, int) else pl.multiple_of(SUB * ti, SUB)
    here, inner = aligned(row), aligned(row + PAD)
    rolled = []
    for field in (VX, VY, VZ):
        values = [speed[field * wide + tj, inner, :] for tj in range(wide)]
        rolled.append([(roll(value, edge), roll(value, -edge)) for value in values])
    for tj in range(across):
        ys = [g.yper * tj + k for k in range(g.yper)]
        dx, dy, dz, speeds = [], [], [], []
        for field in (VX, VY, VZ):
            key = field * wide + 1 + tj
            value = speed[key, inner, :]
            speeds.append(value)
            dx.append(speed[key, pl.ds(row + PAD + 1, SUB), :] - speed[key, pl.ds(row + PAD - 1, SUB), :])
            dy.append(along_y(g, rolled[field], tj + 1, lane))
            dz.append(along_z(g, value, shifted_top(g, tops[field], ys, lane), depth))
        strain = [dx[0], dy[1], dz[2], dy[0] + dx[1], dz[0] + dx[2], dz[1] + dy[2]]
        dilation = strain[0] + strain[1] + strain[2]

        def param(c):
            return params[c * across + tj, here, :]

        lame, shear = param(LAME) * dilation, param(SHEAR)
        spring_lame, spring_shear = param(SPRING_LAME) * dilation, param(SPRING_SHEAR)
        retain = [param(RETAIN + l) for l in range(3)]
        half_shear, half_spring = 0.5 * shear, 0.5 * spring_shear
        slot = g.slot(ti, tj)
        rows, lanes = g.place(ti, tj)
        if first:
            alive = param(ALIVE)
        stresses, memories = [], {}
        for comp in range(6):
            if comp < 3:
                elastic = shear * strain[comp] + lame
                relaxed = spring_shear * strain[comp] + spring_lame
            else:
                elastic = half_shear * strain[comp]
                relaxed = half_spring * strain[comp]
            summed = None
            for l in range(3):
                place = 6 * l + comp
                if first:
                    old = memory[slot, place, rows, lanes] * alive
                else:
                    old = memory[place * across + tj, here, :]
                new = relaxed + retain[l] * (old - relaxed)
                memories[place] = new
                summed = new if summed is None else summed + new
            stresses.append(bricks[(XX + comp) * across + tj, here, :] + elastic - summed)
        store(ti, tj, here, inner, speeds, stresses, memories)


def store_planes(g, bricks_out, memory_out, stress):
    def store(ti, tj, here, inner, speeds, stresses, memories):
        for place, value in memories.items():
            memory_out[place * g.across + tj, here, :] = value
        for comp, value in enumerate(stresses):
            bricks_out[(XX + comp) * g.across + tj, here, :] = value
            stress[comp * g.across + tj, inner, :] = value

    return store


def store_slots(g, motion, memory):
    def store(ti, tj, here, inner, speeds, stresses, memories):
        slot = g.slot(ti, tj)
        rows, lanes = g.place(ti, tj)
        for place, value in memories.items():
            memory[slot, place, rows, lanes] = value
        for field, value in enumerate(speeds + stresses):
            motion[slot, field, rows, lanes] = value

    return store


def pack(g, water, bricks, params, hb_water, row_first, row_last, col_first, col_last, first):
    nx, ny, plane, across, edge = g.nx, g.ny, g.plane, g.across, g.edge
    lane = lane_ids()
    for out, x in ((row_first, 0), (row_last, nx - 1)):
        for t in range(g.ytiles):
            own = x * ny + SUB * t
            out[pl.ds(M_P + SUB * t, SUB), :] = water[pl.ds(own, SUB), :]
            out[pl.ds(M_U + SUB * t, SUB), :] = water[pl.ds(plane + own, SUB), :]
            if first:
                out[pl.ds(ROW_CONST + SUB * t, SUB), :] = hb_water[pl.ds(own, SUB), :]
        for tj in range(across):
            block = M_BRICK + SUB * tj
            for k, field in enumerate(ALONG_X + (VX, VY, VZ)):
                out[pl.ds(block + k, 1), :] = bricks[field * across + tj, pl.ds(x, 1), :]
            out[pl.ds(block + 6, 1), :] = params[HB * across + tj, pl.ds(x, 1), :]
            out[pl.ds(block + 7, 1), :] = jnp.zeros((1, LANES), jnp.float32)
        out[pl.ds(M_CORNER, 2 * SUB), :] = jnp.zeros((2 * SUB, LANES), jnp.float32)
    for out, y, tj in ((col_first, 0, 0), (col_last, ny - 1, across - 1)):
        for t in range(g.xtiles):
            own = SUB * t * ny + y
            out[pl.ds(M_P + SUB * t, SUB), :] = water[pl.ds(own, SUB, stride=ny), :]
            out[pl.ds(M_U + SUB * t, SUB), :] = water[pl.ds(2 * plane + own, SUB, stride=ny), :]
            if first:
                out[pl.ds(COL_CONST + SUB * t, SUB), :] = hb_water[pl.ds(own, SUB, stride=ny), :]
            rows = pl.ds(SUB * t, SUB)
            pieces = [bricks[field * across + tj, rows, :] for field in ALONG_Y + (VX, VY, VZ)]
            pieces.append(params[HB * across + tj, rows, :])
            beside = (1, 0) if t == 0 else (SUB - 2, SUB - 1)
            shear = bricks[XZ * across + tj, rows, :]
            if t == 0 or t == g.xtiles - 1:
                shear = pltpu.roll(shear, 1 if t == 0 else SUB - 1, 0)
            sub = lax.broadcasted_iota(jnp.int32, (SUB, LANES), 0)
            pieces.append(jnp.where(sub == beside[0], shear, bricks[XX * across + tj, rows, :]))
            packed = None
            for k, value in enumerate(pieces):
                moved = roll(value, edge * (k - y % g.yper))
                packed = moved if packed is None else jnp.where(lane >= edge * k, moved, packed)
            out[pl.ds(M_BRICK + SUB * t, SUB), :] = packed


def first_kernel(
    g, live_hbm, table_hbm, water_hbm, material_hbm, motion_hbm, kinds_hbm,
    water_out, bricks_out, params, hb_water, hk_water, row_first, row_last, col_first, col_last,
    press, stress, water, material, motion, kinds, live, table, sems,
):
    nx, ny, plane, across = g.nx, g.ny, g.plane, g.across
    copies = [
        pltpu.make_async_copy(motion_hbm, motion, sems.at[0]),
        pltpu.make_async_copy(kinds_hbm, kinds, sems.at[1]),
        pltpu.make_async_copy(water_hbm.at[0], press.at[pl.ds(1, nx), pl.ds(PAD, ny), :], sems.at[2]),
        pltpu.make_async_copy(material_hbm, material, sems.at[3]),
        pltpu.make_async_copy(water_hbm.at[pl.ds(1, 3)], water, sems.at[4]),
        pltpu.make_async_copy(live_hbm, live, sems.at[5]),
        pltpu.make_async_copy(table_hbm, table, sems.at[6]),
    ]
    for copy in copies:
        copy.start()
    lane = lane_ids()
    set_zero_pads(g, press, stress)
    copies[5].wait()
    copies[6].wait()
    levels = table.shape[0]
    scales = (0.5, 0.5, 1.0, 1.0, 1.0, 1.0, 0.5, 1.0)
    columns = []
    for c, factor in enumerate(scales):
        column = jnp.zeros((SUB, LANES), jnp.float32)
        for level in range(levels):
            column = jnp.where(lane == level, table[level, c], column)
        columns.append(column * factor)

    copies[0].wait()
    copies[1].wait()

    @pl.loop(0, g.xtiles)
    def _(ti):
        for tj in range(across):
            slot = g.slot(ti, tj)
            rows, lanes = g.place(ti, tj)
            alive = live[slot].astype(jnp.float32)
            here = aligned(SUB * ti)
            index = kinds[slot, rows, lanes]
            for c in range(8):
                value = pick(columns[c], index)
                params[c * across + tj, here, :] = value if 3 <= c < 6 else value * alive
            params[ALIVE * across + tj, here, :] = jnp.zeros((SUB, LANES), jnp.float32) + alive
            for field in range(XX, YZ + 1):
                value = motion[slot, field, rows, lanes] * alive
                bricks_out[field * across + tj, here, :] = value
                stress[(field - XX) * across + tj, aligned(PAD + SUB * ti), :] = value

    copies[2].wait()
    copies[3].wait()

    @pl.loop(0, nx)
    def _(x):
        results = []
        for t in range(g.ytiles):
            own = x * ny + SUB * t
            index = material[x, pl.ds(SUB * t, SUB), :]
            results.append((own, pick(columns[0], index), pick(columns[1], index), press[x + 1, pl.ds(PAD + SUB * t, SUB), :]))
        for own, hb, hk, p in results:
            hb_water[aligned(own), :] = hb
            hk_water[aligned(own), :] = hk
            water_out[aligned(own), :] = p

    copies[4].wait()

    def load_u(k, x, t):
        return water[k - 1, x, pl.ds(SUB * t, SUB), :]

    def load_v(field, ti, tj):
        slot = g.slot(ti, tj)
        rows, lanes = g.place(ti, tj)
        return motion[slot, field, rows, lanes] * live[slot].astype(jnp.float32)

    def load_hb(ti, tj):
        return params[HB * across + tj, aligned(SUB * ti), :]

    water_velocity(g, (nx // 2, lambda turn: 2 * turn), water_out, press, stress, hb_water, load_u)
    brick_velocity(g, water_out, stress, load_v, bricks_out, load_hb)
    pack(g, water_out, bricks_out, params, hb_water, row_first, row_last, col_first, col_last, True)


def slots_of(g, array, ti):
    slot = g.slot(ti, 0)
    return array.at[pl.ds(slot, 2), :, pl.ds((ti % g.per) * SUB, SUB), :]


class Refs:
    def __init__(self, refs):
        self.refs = list(refs)

    def take(self, count):
        taken, self.refs = self.refs[:count], self.refs[count:]
        return taken


def inner_kernel(g, first, last, *refs):
    refs = Refs(refs)
    water, bricks, memory, params, hb_water, hk_water, col_before, col_after = refs.take(8)
    if not first:
        (const_in,) = refs.take(1)
    uy, speed = refs.take(2)
    if last:
        water_hbm, motion_hbm, memory_hbm = refs.take(3)
    else:
        water_out, press, stress, bricks_out, memory_out = refs.take(5)
    if first:
        (const_out,) = refs.take(1)
    if last:
        press_buf, uy_buf, motion_buf, memory_buf, sems = refs.take(5)

    nx, ny, edge, across, plane = g.nx, g.ny, g.edge, g.across, g.plane
    wide = across + 2
    lane = lane_ids()
    top_pick = surface_pick() * edge + (edge - 1)
    py = ny + 2 * PAD
    low, high = SUB, nx - SUB
    copies = []

    def send(source, target):
        copies.append(pltpu.make_async_copy(source, target, sems.at[len(copies)]))
        copies[-1].start()

    def part(component, start, stop):
        return pl.ds(component * plane + start * ny, (stop - start) * ny)

    if last:
        send(water.at[part(3, 0, nx), :], water_hbm.at[part(3, 0, nx), :])
        send(water.at[part(1, 1, nx - 1), :], water_hbm.at[part(1, 1, nx - 1), :])
    else:
        set_zero_pads(g, press, stress)

    @pl.loop(0, nx)
    def _(x):
        for t in range(g.ytiles):
            own = x * ny + SUB * t
            uy[aligned(x * py + PAD + SUB * t), :] = water[aligned(2 * plane + own), :]
            if last:
                uy_buf[aligned(own), :] = water[aligned(2 * plane + own), :]

    for side, (ref, y, halo, sign) in enumerate(((col_before, 0, -1, 1.0), (col_after, ny - 1, ny, -1.0))):
        for t in range(g.xtiles):
            own = pl.ds(SUB * t * ny + y, SUB, stride=ny)
            here = pl.ds(SUB * t * py + PAD + y, SUB, stride=py)
            place = pl.ds(32 * side + SUB * t, SUB)
            if first:
                theirs = ref[pl.ds(COL_CONST + SUB * t, SUB), :]
                const_out[place, :] = theirs
            else:
                theirs = const_in[place, :]
            value = uy[here, :] + sign * hb_water[own, :] * ref[pl.ds(M_P + SUB * t, SUB), :]
            uy[here, :] = value
            if last:
                uy_buf[own, :] = value
            uy[pl.ds(SUB * t * py + PAD + halo, SUB, stride=py), :] = (
                ref[pl.ds(M_U + SUB * t, SUB), :] - sign * theirs * water[own, :]
            )
    if last:
        send(uy_buf, water_hbm.at[part(2, 0, nx), :])

    for field in (VX, VY, VZ):
        for tj in range(across):
            for ti in range(g.xtiles):
                speed[field * wide + 1 + tj, pl.ds(PAD + SUB * ti, SUB), :] = bricks[field * across + tj, pl.ds(SUB * ti, SUB), :]
    for ref, tj, halo, sign in ((col_before, 0, 0, 1.0), (col_after, across - 1, wide - 1, -1.0)):
        near = 0 if tj == 0 else LANES - edge
        far = LANES - edge - near
        inside = (lane >= near) & (lane < near + edge)
        for ti in range(g.xtiles):
            column = ref[pl.ds(M_BRICK + SUB * ti, SUB), :]
            own_hb = jnp.where(inside, sign * params[HB * across + tj, pl.ds(SUB * ti, SUB), :], 0.0)
            their_hb = sign * roll(column, far - 6 * edge)
            here = pl.ds(PAD + SUB * ti, SUB)
            for c in (VX, VY, VZ):
                key = c * wide + 1 + tj
                speed[key, here, :] = bricks[c * across + tj, pl.ds(SUB * ti, SUB), :] - own_hb * roll(column, near - c * edge)
                own = bricks[ALONG_Y[c] * across + tj, pl.ds(SUB * ti, SUB), :]
                speed[c * wide + halo, here, :] = roll(column, far - (3 + c) * edge) + their_hb * roll(own, far - near)

    store = store_slots(g, motion_buf, memory_buf) if last else store_planes(g, bricks_out, memory_out, stress)

    @pl.loop(1, g.xtiles - 1)
    def _(ti):
        row = pl.multiple_of(SUB * ti, SUB)
        tops = (
            lambda y: water[pl.ds(plane + row * ny + y, SUB, stride=ny), :],
            lambda y: uy[pl.ds(row * py + PAD + y, SUB, stride=py), :],
            lambda y: water[pl.ds(3 * plane + row * ny + y, SUB, stride=ny), :],
        )
        brick_stress(g, ti, first, bricks, memory, params, speed, tops, store)

    if last:
        for ti in range(1, g.xtiles - 1):
            send(slots_of(g, motion_buf, ti), slots_of(g, motion_hbm, ti))
            send(slots_of(g, memory_buf, ti), slots_of(g, memory_hbm, ti))

    def layer(x):
        results = []
        for t in range(g.ytiles):
            own = x * ny + SUB * t
            dx = water[aligned(plane + own + ny), :] - water[aligned(plane + own - ny), :]
            results.append(
                (x, t, own, water_stress(g, x, t, dx, water, uy, speed, hk_water, lane, top_pick))
            )
        return results

    @pl.loop(0, (nx - 4) // 2)
    def _(turn):
        for x, t, own, value in layer(2 + 2 * turn) + layer(3 + 2 * turn):
            if last:
                press_buf[aligned(own), :] = value
            else:
                water_out[aligned(own), :] = value
                press[x + 1, pl.ds(PAD + SUB * t, SUB), :] = value

    if last:
        send(press_buf.at[part(0, 2, nx - 2), :], water_hbm.at[part(0, 2, nx - 2), :])
        for copy in copies:
            copy.wait()
    else:
        def load_u(k, x, t):
            if k == 2:
                return uy[aligned(x * py + PAD + SUB * t), :]
            return water[aligned(k * plane + x * ny + SUB * t), :]

        layers = ((high - low) // 2, lambda turn: low + 2 * turn)
        water_velocity(g, layers, water_out, press, stress, hb_water, load_u)


def water_stress(g, x, t, dx, water, uy, speed, hk_water, lane, top_pick):
    row = x * (g.ny + 2 * PAD) + PAD + SUB * t
    own = x * g.ny + SUB * t
    dy = uy[pl.ds(row + 1, SUB), :] - uy[pl.ds(row - 1, SUB), :]
    surface = jnp.broadcast_to(speed[VZ * (g.across + 2) + 1 + t, pl.ds(PAD + x, 1), :], (SUB, LANES))
    dz = water_z(g, water[aligned(3 * g.plane + own), :], pick(surface, top_pick), lane)
    return water[aligned(own), :] - hk_water[aligned(own), :] * (dx + dy + dz)


def edge_kernel(g, first, last, *refs):
    refs = Refs(refs)
    water, bricks, memory, params, hb_water, hk_water, col_before, col_after, row_before, row_after = refs.take(10)
    if not first:
        (const_in,) = refs.take(1)
    (uy,) = refs.take(1)
    refs.take(4 if last else 6)
    (speed,) = refs.take(1)
    if last:
        water_hbm, motion_hbm, memory_hbm = refs.take(3)
    else:
        water_out, press, stress, bricks_out, memory_out = refs.take(5)
        sends = refs.take(4)
    if first:
        (const_out,) = refs.take(1)
    (ux,) = refs.take(1)
    if last:
        press_buf, motion_buf, memory_buf, sems = refs.take(4)

    nx, ny, edge, across, plane = g.nx, g.ny, g.edge, g.across, g.plane
    wide = across + 2
    lane = lane_ids()
    top_pick = surface_pick() * edge + (edge - 1)
    py = ny + 2 * PAD
    copies = []

    def send(source, target):
        copies.append(pltpu.make_async_copy(source, target, sems.at[len(copies)]))
        copies[-1].start()

    @pl.loop(0, SUB)
    def _(x):
        for t in range(g.ytiles):
            own = x * ny + SUB * t
            ux[aligned(ny + own), :] = water[aligned(plane + own), :]
            ux[aligned((1 + SUB) * ny + own), :] = water[aligned(plane + (nx - SUB) * ny + own), :]

    sides = ((row_before, 0, -1, 1.0, 1, 0), (row_after, nx - 1, nx, -1.0, 2 * SUB, 2 * SUB + 1))
    for side, (ref, x, halo, sign, own_layer, halo_layer) in enumerate(sides):
        for t in range(g.ytiles):
            own = pl.ds(x * ny + SUB * t, SUB)
            place = pl.ds(32 * side + SUB * t, SUB)
            if first:
                theirs = ref[pl.ds(ROW_CONST + SUB * t, SUB), :]
                const_out[place, :] = theirs
            else:
                theirs = const_in[place, :]
            here = pl.ds(own_layer * ny + SUB * t, SUB)
            ux[here, :] = ux[here, :] + sign * hb_water[own, :] * ref[pl.ds(M_P + SUB * t, SUB), :]
            ux[pl.ds(halo_layer * ny + SUB * t, SUB), :] = ref[pl.ds(M_U + SUB * t, SUB), :] - sign * theirs * water[own, :]
    if last:
        for layer, x in ((1, 0), (2 * SUB, nx - 1)):
            send(ux.at[pl.ds(layer * ny, ny), :], water_hbm.at[pl.ds(plane + x * ny, ny), :])

    for ref, x, halo, sign, _, _ in sides:
        for tj in range(across):
            block = M_BRICK + SUB * tj
            own_hb = sign * params[HB * across + tj, pl.ds(x, 1), :]
            their_hb = sign * ref[pl.ds(block + 6, 1), :]
            for c in (VX, VY, VZ):
                here = pl.ds(PAD + x, 1)
                key = c * wide + 1 + tj
                speed[key, here, :] = speed[key, here, :] - own_hb * ref[pl.ds(block + c, 1), :]
                speed[key, pl.ds(PAD + halo, 1), :] = (
                    ref[pl.ds(block + 3 + c, 1), :] + their_hb * bricks[ALONG_X[c] * across + tj, pl.ds(x, 1), :]
                )
        edge_row = SUB - 1 if x == 0 else 0
        beside_row = SUB - 2 if x == 0 else 1
        for k, (col_ref, tj, col_halo, col_sign) in enumerate(((col_before, 0, 0, 1.0), (col_after, across - 1, wide - 1, -1.0))):
            near = 0 if tj == 0 else LANES - edge
            far = LANES - edge - near
            inside = (lane[0:1, :] >= near) & (lane[0:1, :] < near + edge)
            corner = ref[pl.ds(M_CORNER + SUB * k + edge_row, 1), :]
            beside = ref[pl.ds(M_CORNER + SUB * k + beside_row, 1), :]
            across_y = [roll_row(corner, near - c * edge) for c in range(3)]
            across_x = (roll_row(corner, far - 7 * edge), roll_row(corner, far), roll_row(beside, far - 7 * edge))
            row_hb = jnp.where(inside, col_sign * ref[pl.ds(M_BRICK + SUB * tj + 6, 1), :], 0.0)
            col_hb = sign * roll_row(col_ref[pl.ds(M_BRICK + x, 1), :], far - 6 * edge)
            for c in (VX, VY, VZ):
                key, here = c * wide + 1 + tj, pl.ds(PAD + halo, 1)
                speed[key, here, :] = speed[key, here, :] - row_hb * across_y[c]
                key, here = c * wide + col_halo, pl.ds(PAD + x, 1)
                speed[key, here, :] = speed[key, here, :] - col_hb * across_x[c]

    store = store_slots(g, motion_buf, memory_buf) if last else store_planes(g, bricks_out, memory_out, stress)

    @pl.loop(0, 2)
    def _(turn):
        ti = turn * (g.xtiles - 1)
        row = pl.multiple_of(SUB * ti, SUB)
        above = pl.multiple_of((1 + SUB * turn) * ny, SUB)
        tops = (
            lambda y: ux[pl.ds(above + y, SUB, stride=ny), :],
            lambda y: uy[pl.ds(row * py + PAD + y, SUB, stride=py), :],
            lambda y: water[pl.ds(3 * plane + row * ny + y, SUB, stride=ny), :],
        )
        brick_stress(g, ti, first, bricks, memory, params, speed, tops, store)

    if last:
        for ti in (0, g.xtiles - 1):
            send(slots_of(g, motion_buf, ti), slots_of(g, motion_hbm, ti))
            send(slots_of(g, memory_buf, ti), slots_of(g, memory_hbm, ti))

    for pair, (x, layer) in enumerate(((0, 1), (nx - 2, 2 * SUB - 1))):
        for step in range(2):
            for t in range(g.ytiles):
                dx = (
                    ux[pl.ds((layer + step + 1) * ny + SUB * t, SUB), :] - ux[pl.ds((layer + step - 1) * ny + SUB * t, SUB), :]
                )
                value = water_stress(g, x + step, t, dx, water, uy, speed, hk_water, lane, top_pick)
                if last:
                    press_buf[pl.ds((2 * pair + step) * ny + SUB * t, SUB), :] = value
                else:
                    water_out[pl.ds((x + step) * ny + SUB * t, SUB), :] = value
                    press[x + step + 1, pl.ds(PAD + SUB * t, SUB), :] = value

    if last:
        for pair, x in enumerate((0, nx - 2)):
            send(press_buf.at[pl.ds(2 * pair * ny, 2 * ny), :], water_hbm.at[pl.ds(x * ny, 2 * ny), :])
        for copy in copies:
            copy.wait()
    else:
        def load_u(k, x, t):
            if k == 1:
                layer = x - (x // (nx - SUB)) * (nx - 2 * SUB) + 1
                return ux[aligned(layer * ny + SUB * t), :]
            if k == 2:
                return uy[aligned(x * py + PAD + SUB * t), :]
            return water[aligned(3 * plane + x * ny + SUB * t), :]

        def load_v(field, ti, tj):
            return speed[field * wide + 1 + tj, aligned(PAD + SUB * ti), :]

        def load_hb(ti, tj):
            return params[HB * across + tj, aligned(SUB * ti), :]

        layers = (SUB, lambda turn: 2 * turn + (turn // (SUB // 2)) * (nx - 2 * SUB))
        water_velocity(g, layers, water_out, press, stress, hb_water, load_u)
        brick_velocity(g, water_out, stress, load_v, bricks_out, load_hb)
        pack(g, water_out, bricks_out, params, hb_water, *sends, False)


def shift(value, axis, up):
    count = lax.axis_size(axis)
    pairs = [(i, i + 1) for i in range(count - 1)]
    return lax.ppermute(value, axis, pairs if up else [(j, i) for i, j in pairs])


def exchange(g, sends):
    row_first, row_last, col_first, col_last = sends
    col_before = shift(col_last, "col", True)
    col_after = shift(col_first, "col", False)

    def with_corners(message, start):
        start += M_BRICK
        corners = jnp.concatenate([col_before[start : start + SUB], col_after[start : start + SUB]])
        return lax.dynamic_update_slice(message, corners, (M_CORNER, 0))

    row_before = shift(with_corners(row_last, g.nx - SUB), "row", True)
    row_after = shift(with_corners(row_first, 0), "row", False)
    return col_before, col_after, row_before, row_after


def body(
    brick_velocity_stress,
    brick_relaxation_memory,
    brick_cell_material,
    brick_live,
    water_state,
    water_material,
    material_table,
):
    _, nx, ny, nz = water_state.shape
    g = Grid(nx, ny, brick_cell_material.shape[1])
    across, plane = g.across, g.plane

    def f32(*shape):
        return jax.ShapeDtypeStruct(shape, jnp.float32)

    vmem = pl.BlockSpec(memory_space=pltpu.VMEM)
    hbm = pl.BlockSpec(memory_space=pltpu.HBM)
    params = pltpu.CompilerParams(vmem_limit_bytes=24 * 1024 * 1024)
    press = pltpu.VMEM((nx + 2, ny + 2 * PAD, nz), jnp.float32)
    stress = pltpu.VMEM((6 * across, nx + 2 * PAD, LANES), jnp.float32)

    def messages(first):
        extra = 32 if first else 0
        return [f32(112 + extra, LANES)] * 2 + [f32(96 + extra, LANES)] * 2

    def buffer(*shape):
        return pltpu.VMEM(shape, jnp.float32)

    def held(*values):
        return [pltpu.with_memory_space_constraint(value, pltpu.VMEM) for value in values]

    results = pl.pallas_call(
        functools.partial(first_kernel, g),
        out_shape=[
            f32(4 * plane, nz), f32(9 * across, nx, LANES), f32(9 * across, nx, LANES), f32(plane, nz), f32(plane, nz),
        ] + messages(True),
        in_specs=[hbm] * 6,
        out_specs=[vmem] * 9,
        scratch_shapes=[
            press,
            stress,
            pltpu.VMEM((3, nx, ny, nz), jnp.float32),
            pltpu.VMEM(water_material.shape, jnp.int32),
            pltpu.VMEM(brick_velocity_stress.shape, jnp.float32),
            pltpu.VMEM(brick_cell_material.shape, jnp.int32),
            pltpu.SMEM(brick_live.shape, jnp.int32),
            pltpu.SMEM(material_table.shape, jnp.float32),
            pltpu.SemaphoreType.DMA((7,)),
        ],
        compiler_params=params,
        name="first_velocity",
    )(*[
        pltpu.with_memory_space_constraint(value, pltpu.HBM)
        for value in (
            brick_live, material_table, water_state, water_material, brick_velocity_stress, brick_cell_material,
        )
    ])
    water, bricks, coefficients, hb_water, hk_water = results[:5]
    sends = results[5:]
    memory = brick_relaxation_memory
    col_const, row_const = (), ()
    uy_shape = (nx * (ny + 2 * PAD), nz)
    speed_shape = (3 * (across + 2), nx + 2 * PAD, LANES)
    ux = buffer((2 * SUB + 2) * ny, nz)
    slot_buffers = [
        pltpu.VMEM(brick_velocity_stress.shape, jnp.float32),
        pltpu.VMEM(brick_relaxation_memory.shape, jnp.float32),
    ]
    finals = [f32(4 * plane, nz), f32(*brick_velocity_stress.shape), f32(*brick_relaxation_memory.shape)]
    planes = [
        buffer(4 * plane, nz),
        buffer(nx + 2, ny + 2 * PAD, nz),
        buffer(6 * across, nx + 2 * PAD, LANES),
        buffer(9 * across, nx, LANES),
        buffer(18 * across, nx, LANES),
    ]
    for step in range(STEPS):
        first, last = step == 0, step == STEPS - 1
        *columns, row_before, row_after = exchange(g, sends)
        state = (water, bricks, memory, coefficients, hb_water, hk_water)
        shapes = finals if last else planes
        spaces = [hbm if last else vmem] * len(shapes)
        inner = pl.pallas_call(
            functools.partial(inner_kernel, g, first, last),
            out_shape=[buffer(*uy_shape), buffer(*speed_shape)] + shapes + ([buffer(64, LANES)] if first else []),
            in_specs=[vmem] * (8 + len(col_const)),
            out_specs=[vmem] * 2 + spaces + ([vmem] if first else []),
            scratch_shapes=[buffer(plane, nz), buffer(plane, nz)] + slot_buffers + [pltpu.SemaphoreType.DMA((8,))] if last else [],
            compiler_params=params,
            cost_estimate=pl.CostEstimate(flops=20_000_000, bytes_accessed=8_000_000, transcendentals=0),
            name="inner",
        )(*held(*state), *columns, *col_const)
        if first:
            col_const = (inner[-1],)
            inner = inner[:-1]
        uy, *partial = inner
        count = 10 + len(row_const) + 1
        results = pl.pallas_call(
            functools.partial(edge_kernel, g, first, last),
            out_shape=[buffer(*speed_shape)] + shapes + ([] if last else messages(False)) + ([buffer(64, LANES)] if first else []),
            in_specs=[vmem] * (count + 1) + spaces,
            out_specs=[vmem] + spaces + [vmem] * (0 if last else 4) + ([vmem] if first else []),
            input_output_aliases={count + k: k for k in range(1 + len(shapes))},
            scratch_shapes=[ux] + ([buffer(4 * ny, nz)] + slot_buffers + [pltpu.SemaphoreType.DMA((8,))] if last else []),
            compiler_params=params,
            name="edges",
        )(*held(*state), *columns, row_before, row_after, *row_const, *held(uy), *(held(partial[0]) + (list(partial[1:]) if last else held(*partial[1:]))))
        if last:
            return results[2], results[3], results[1].reshape(water_state.shape)
        _, water, _, _, bricks, memory = results[:6]
        sends = results[6:10]
        if first:
            row_const = (results[10],)


def solution(mesh):
    return jax.shard_map(
        body,
        mesh=mesh,
        in_specs=(
            P(("row", "col"), None, None, None),
            P(("row", "col"), None, None, None),
            P(("row", "col"), None, None),
            P(("row", "col")),
            P(None, "row", "col", None),
            P("row", "col", None),
            P(),
        ),
        out_specs=(
            P(("row", "col"), None, None, None),
            P(("row", "col"), None, None, None),
            P(None, "row", "col", None),
        ),
        check_vma=False,
    )
```

time: 77.4 us -> 68.4 us (0.88)
  the two profiles are of different devices: /device:TPU:10 before, /device:TPU:5 now
where the time goes in v3:
time: 68.4 us; the launch traced here: 68 us
  starting transfers between devices  32.8 us (48%)
  Pallas kernels  23.6 us (35%)
  waiting for transfers between devices  10.6 us (15%)
  between operations  0.91 us (1%)
    ppermute x12, starting transfers between devices, shift(): lax.ppermute(value, axis, pairs if up else [(j, i) for i, j in pairs])  32.8 us
    ppermute x12, waiting for transfers between devices, shift(): lax.ppermute(value, axis, pairs if up else [(j, i) for i, j in pairs])  10.6 us
    pallas_call x3, Pallas kernels, body(): pl.pallas_call(functools.partial(inner_kernel, g, first, last), out_shape...  10.1 us
    pallas_call x3, Pallas kernels, body(): pl.pallas_call(functools.partial(edge_kernel, g, first, last), out_shape=...  6.78 us
    pallas_call x1, Pallas kernels, body(): pl.pallas_call(functools.partial(first_kernel, g), out_shape=[f32(4 * pla...  6.76 us
  transfers between devices with their start and end apart: 12, of which 3 were waited for; matrix products, arithmetic and copies ran while one was open for 0% of the time, Pallas kernels for 15%

profile of v3, /device:TPU:5, one launch (start us, length us, event | category | flops | bytes accessed | tf_op | source)
XLA Modules:
  0.0 68.0 jit_solution(12567540250205279078)
XLA Ops:
  0.6 0.0 copy-start
  0.6 6.8 %first_velocity.1 = (f32[4096,128]{1,0:T(8,128)S(1)}, f32[36,32,128]{2,1,0:T(8,128)S(1)}, f32[36,32,128]{2,1,0:T(8,128)S(1)}, f32[1024,128]{1,0:T(8,128)S(1)}, f...) custom-call(s32[4]{0:T(128)} %live_hbm.1, ...), custom_call_target="tpu_custom_call" | custom-call | tf_op jit(solution)/shard_map/first_velocity/pallas_call | solution.py:727
  7.4 3.7 %collective-permute-start = (f32[128,128]{1,0:T(8,128)S(1)}, f32[128,128]{1,0:T(8,128)S(1)}, u32[]{:S(2)}, u32[]{:S(2)}) collective-permute-start(f32[128,128]{1,0:T(8,128)S(1)} %get-tuple-element.55), channel_id=1, source_target_pairs={{0,1},{1,2},{2,3},{4,5},{5,6},{6,7},{8,9},{9,10},{10,11},{12,13},{... | collective-permute-start | bytes 196616 | tf_op jit(solution)/shard_map/ppermute | solution.py:677
  11.1 1.9 %collective-permute-start.1 = (f32[128,128]{1,0:T(8,128)S(1)}, f32[128,128]{1,0:T(8,128)S(1)}, u32[]{:S(2)}, u32[]{:S(2)}) collective-permute-start(f32[128,128]{1,0:T(8,128)S(1)} %get-tuple-element.56), channel_id=1, source_target_pairs={{1,0},{2,1},{3,2},{5,4},{6,5},{7,6},{9,8},{10,9},{11,10},{13,12},{... | collective-permute-start | bytes 196616 | tf_op jit(solution)/shard_map/ppermute | solution.py:677
  13.0 0.0 collective-permute-done.refs_6_
  13.0 3.6 %collective-permute-done.1.refs_7_ = f32[128,128]{1,0:T(8,128)S(1)} collective-permute-done((f32[128,128]{1,0:T(8,128)S(1)}, f32[128,128]{1,0:T(8,128)S(1)}, u32[]{:S(2)}, u32[]{:S(2)}) %collective-permute-start.1) | collective-permute-done | bytes 65568 | tf_op jit(solution)/shard_map/ppermute | solution.py:677
  16.7 2.1 %collective-permute-start.3 = (f32[144,128]{1,0:T(8,128)S(1)}, f32[144,128]{1,0:T(8,128)S(1)}, u32[]{:S(2)}, u32[]{:S(2)}) collective-permute-start(f32[144,128]{1,0:T(8,128)S(1)} %maximum_dynamic-update-slice_fusion.1), channel_id=1, source_target_pairs={{4,0},{8,4},{12,8},{16,12},{20,16},{24,20},{28,24},{5,1},{9,5},{13... | collective-permute-start | bytes 221192 | tf_op jit(solution)/shard_map/ppermute | solution.py:677
  18.8 4.0 %collective-permute-start.2 = (f32[144,128]{1,0:T(8,128)S(1)}, f32[144,128]{1,0:T(8,128)S(1)}, u32[]{:S(2)}, u32[]{:S(2)}) collective-permute-start(f32[144,128]{1,0:T(8,128)S(1)} %maximum_dynamic-update-slice_fusion), channel_id=1, source_target_pairs={{0,4},{4,8},{8,12},{12,16},{16,20},{20,24},{24,28},{1,5},{5,9},{9,... | collective-permute-start | bytes 221192 | tf_op jit(solution)/shard_map/ppermute | solution.py:677
  22.9 0.0 copy-done
  22.9 3.4 %inner.3 = (f32[1536,128]{1,0:T(8,128)S(1)}, f32[18,48,128]{2,1,0:T(8,128)S(1)}, f32[4096,128]{1,0:T(8,128)S(1)}, f32[34,48,128]{2,1,0:T(8,128)S(1)}, f32[24,48,...) custom-call(f32[4096,128]{1,0:T(8,128)S(1)} %get-tuple-element.50.refs_0_, ...), custom_call_target="tpu_custom_call" | custom-call | flops 20000000 | bytes 8000000 | tf_op jit(solution)/shard_map/inner/pallas_call | solution.py:778
  26.3 0.0 collective-permute-done.3.refs_9_
  26.3 0.0 collective-permute-done.2.refs_8_
  26.3 2.5 %edges.3 = (f32[18,48,128]{2,1,0:T(8,128)S(1)}, f32[4096,128]{1,0:T(8,128)S(1)}, f32[34,48,128]{2,1,0:T(8,128)S(1)}, f32[24,48,128]{2,1,0:T(8,128)S(1)}, f32[36,...) custom-call(f32[4096,128]{1,0:T(8,128)S(1)} %get-tuple-element.50.re, ...), custom_call_target="tpu_custom_call", output_to_operand_aliasing={{0}: (11, {}), {1}: (12, {}), {2}: (13, {}), {3}: (14, {}),... | custom-call | tf_op jit(solution)/shard_map/edges/pallas_call | solution.py:793
  28.8 2.4 %collective-permute-start.4 = (f32[96,128]{1,0:T(8,128)S(1)}, f32[96,128]{1,0:T(8,128)S(1)}, u32[]{:S(2)}, u32[]{:S(2)}) collective-permute-start(f32[96,128]{1,0:T(8,128)S(1)} %get-tuple-element.69), channel_id=1, source_target_pairs={{0,1},{1,2},{2,3},{4,5},{5,6},{6,7},{8,9},{9,10},{10,11},{12,13},{... | collective-permute-start | bytes 147464 | tf_op jit(solution)/shard_map/ppermute | solution.py:677
  31.3 1.9 %collective-permute-start.5 = (f32[96,128]{1,0:T(8,128)S(1)}, f32[96,128]{1,0:T(8,128)S(1)}, u32[]{:S(2)}, u32[]{:S(2)}) collective-permute-start(f32[96,128]{1,0:T(8,128)S(1)} %get-tuple-element.70), channel_id=1, source_target_pairs={{1,0},{2,1},{3,2},{5,4},{6,5},{7,6},{9,8},{10,9},{11,10},{13,12},{... | collective-permute-start | bytes 147464 | tf_op jit(solution)/shard_map/ppermute | solution.py:677
  33.2 0.0 collective-permute-done.4.refs_6_
  33.2 3.5 %collective-permute-done.5.refs_7_ = f32[96,128]{1,0:T(8,128)S(1)} collective-permute-done((f32[96,128]{1,0:T(8,128)S(1)}, f32[96,128]{1,0:T(8,128)S(1)}, u32[]{:S(2)}, u32[]{:S(2)}) %collective-permute-start.5) | collective-permute-done | bytes 49184 | tf_op jit(solution)/shard_map/ppermute | solution.py:677
  36.7 1.9 %collective-permute-start.7 = (f32[112,128]{1,0:T(8,128)S(1)}, f32[112,128]{1,0:T(8,128)S(1)}, u32[]{:S(2)}, u32[]{:S(2)}) collective-permute-start(f32[112,128]{1,0:T(8,128)S(1)} %maximum_dynamic-update-slice_fusion.3), channel_id=1, source_target_pairs={{4,0},{8,4},{12,8},{16,12},{20,16},{24,20},{28,24},{5,1},{9,5},{13... | collective-permute-start | bytes 172040 | tf_op jit(solution)/shard_map/ppermute | solution.py:677
  38.6 4.3 %collective-permute-start.6 = (f32[112,128]{1,0:T(8,128)S(1)}, f32[112,128]{1,0:T(8,128)S(1)}, u32[]{:S(2)}, u32[]{:S(2)}) collective-permute-start(f32[112,128]{1,0:T(8,128)S(1)} %maximum_dynamic-update-slice_fusion.2), channel_id=1, source_target_pairs={{0,4},{4,8},{8,12},{12,16},{16,20},{20,24},{24,28},{1,5},{5,9},{9,... | collective-permute-start | bytes 172040 | tf_op jit(solution)/shard_map/ppermute | solution.py:677
  42.9 3.4 %inner.4 = (f32[1536,128]{1,0:T(8,128)S(1)}, f32[18,48,128]{2,1,0:T(8,128)S(1)}, f32[4096,128]{1,0:T(8,128)S(1)}, f32[34,48,128]{2,1,0:T(8,128)S(1)}, f32[24,48,...) custom-call(f32[4096,128]{1,0:T(8,128)S(1)} %get-tuple-element.66.refs_0_, ...), custom_call_target="tpu_custom_call" | custom-call | flops 20000000 | bytes 8000000 | tf_op jit(solution)/shard_map/inner/pallas_call | solution.py:778
  46.2 0.0 collective-permute-done.7.refs_9_
  46.3 0.0 collective-permute-done.6.refs_8_
  46.3 2.5 %edges.4 = (f32[18,48,128]{2,1,0:T(8,128)S(1)}, f32[4096,128]{1,0:T(8,128)S(1)}, f32[34,48,128]{2,1,0:T(8,128)S(1)}, f32[24,48,128]{2,1,0:T(8,128)S(1)}, f32[36,...) custom-call(f32[4096,128]{1,0:T(8,128)S(1)} %get-tuple-element.66.re, ...), custom_call_target="tpu_custom_call", output_to_operand_aliasing={{0}: (12, {}), {1}: (13, {}), {2}: (14, {}), {3}: (15, {}),... | custom-call | tf_op jit(solution)/shard_map/edges/pallas_call | solution.py:793
  48.8 2.5 %collective-permute-start.8 = (f32[96,128]{1,0:T(8,128)S(1)}, f32[96,128]{1,0:T(8,128)S(1)}, u32[]{:S(2)}, u32[]{:S(2)}) collective-permute-start(f32[96,128]{1,0:T(8,128)S(1)} %get-tuple-element.85), channel_id=1, source_target_pairs={{0,1},{1,2},{2,3},{4,5},{5,6},{6,7},{8,9},{9,10},{10,11},{12,13},{... | collective-permute-start | bytes 147464 | tf_op jit(solution)/shard_map/ppermute | solution.py:677
  51.2 1.9 %collective-permute-start.9 = (f32[96,128]{1,0:T(8,128)S(1)}, f32[96,128]{1,0:T(8,128)S(1)}, u32[]{:S(2)}, u32[]{:S(2)}) collective-permute-start(f32[96,128]{1,0:T(8,128)S(1)} %get-tuple-element.86), channel_id=1, source_target_pairs={{1,0},{2,1},{3,2},{5,4},{6,5},{7,6},{9,8},{10,9},{11,10},{13,12},{... | collective-permute-start | bytes 147464 | tf_op jit(solution)/shard_map/ppermute | solution.py:677
  53.2 0.0 collective-permute-done.8.refs_6_
  53.2 3.5 %collective-permute-done.9.refs_7_ = f32[96,128]{1,0:T(8,128)S(1)} collective-permute-done((f32[96,128]{1,0:T(8,128)S(1)}, f32[96,128]{1,0:T(8,128)S(1)}, u32[]{:S(2)}, u32[]{:S(2)}) %collective-permute-start.9) | collective-permute-done | bytes 49184 | tf_op jit(solution)/shard_map/ppermute | solution.py:677
  56.6 1.9 %collective-permute-start.11 = (f32[112,128]{1,0:T(8,128)S(1)}, f32[112,128]{1,0:T(8,128)S(1)}, u32[]{:S(2)}, u32[]{:S(2)}) collective-permute-start(f32[112,128]{1,0:T(8,128)S(1)} %maximum_dynamic-update-slice_fusion.5), channel_id=1, source_target_pairs={{4,0},{8,4},{12,8},{16,12},{20,16},{24,20},{28,24},{5,1},{9,5},{13... | collective-permute-start | bytes 172040 | tf_op jit(solution)/shard_map/ppermute | solution.py:677
  58.6 4.3 %collective-permute-start.10 = (f32[112,128]{1,0:T(8,128)S(1)}, f32[112,128]{1,0:T(8,128)S(1)}, u32[]{:S(2)}, u32[]{:S(2)}) collective-permute-start(f32[112,128]{1,0:T(8,128)S(1)} %maximum_dynamic-update-slice_fusion.4), channel_id=1, source_target_pairs={{0,4},{4,8},{8,12},{12,16},{16,20},{20,24},{24,28},{1,5},{5,9},{9,... | collective-permute-start | bytes 172040 | tf_op jit(solution)/shard_map/ppermute | solution.py:677
  62.8 3.3 %inner.5 = (f32[1536,128]{1,0:T(8,128)S(1)}, f32[18,48,128]{2,1,0:T(8,128)S(1)}, f32[4096,128]{1,0:T(8,128)}, f32[4,9,16,256]{3,2,1,0:T(8,128)}, f32[4,18,16,256]{3,2,1,0:T(8,128)}) custom-call(f32[4096,128]{1,0:T(8,128)S(1)} %get-tuple-element.82.refs_0_, f32[36,32,128]{2,1,0:T(8,128)S(1)} %get-tuple-element.83.refs_1_, ...), custom_call_target="tpu_custom_call" | custom-call | flops 20000000 | bytes 8000000 | tf_op jit(solution)/shard_map/inner/pallas_call | solution.py:778
  66.1 0.0 collective-permute-done.11.refs_9_
  66.2 0.0 collective-permute-done.10.refs_8_
  66.2 1.8 %edges.5 = (f32[18,48,128]{2,1,0:T(8,128)S(1)}, f32[4096,128]{1,0:T(8,128)}, f32[4,9,16,256]{3,2,1,0:T(8,128)}, f32[4,18,16,256]{3,2,1,0:T(8,128)}) custom-call(f32[4096,128]{1,0:T(8,128)S(1)} %get-tuple-element.82.refs_0_, ...), custom_call_target="tpu_custom_call", output_to_operand_aliasing={{0}: (12, {}), {1}: (13, {}), {2}: (14, {}), {3}: (15, {})} | custom-call | tf_op jit(solution)/shard_map/edges/pallas_call | solution.py:793
  (12 shorter events, 0.0 us)
Async XLA Ops:
  0.6 22.3 %copy-start = (f32[4,18,16,256]{3,2,1,0:T(8,128)S(1)}, f32[4,18,16,256]{3,2,1,0:T(8,128)}, u32[]{:S(2)}) copy-start(f32[4,18,16,256]{3,2,1,0:T(8,128)} %refs_2_.3) | copy-start | bytes 3538948
  7.4 5.6 %collective-permute-start = (f32[128,128]{1,0:T(8,128)S(1)}, f32[128,128]{1,0:T(8,128)S(1)}, u32[]{:S(2)}, u32[]{:S(2)}) collective-permute-start(f32[128,128]{1,0:T(8,128)S(1)} %get-tuple-element.55), channel_id=1, source_target_pairs={{0,1},{1,2},{2,3},{4,5},{5,6},{6,7},{8,9},{9,10},{10,11},{12,13},{... | collective-permute-start | bytes 196616 | tf_op jit(solution)/shard_map/ppermute | solution.py:677
  11.1 5.6 %collective-permute-start.1 = (f32[128,128]{1,0:T(8,128)S(1)}, f32[128,128]{1,0:T(8,128)S(1)}, u32[]{:S(2)}, u32[]{:S(2)}) collective-permute-start(f32[128,128]{1,0:T(8,128)S(1)} %get-tuple-element.56), channel_id=1, source_target_pairs={{1,0},{2,1},{3,2},{5,4},{6,5},{7,6},{9,8},{10,9},{11,10},{13,12},{... | collective-permute-start | bytes 196616 | tf_op jit(solution)/shard_map/ppermute | solution.py:677
  16.7 9.6 %collective-permute-start.3 = (f32[144,128]{1,0:T(8,128)S(1)}, f32[144,128]{1,0:T(8,128)S(1)}, u32[]{:S(2)}, u32[]{:S(2)}) collective-permute-start(f32[144,128]{1,0:T(8,128)S(1)} %maximum_dynamic-update-slice_fusion.1), channel_id=1, source_target_pairs={{4,0},{8,4},{12,8},{16,12},{20,16},{24,20},{28,24},{5,1},{9,5},{13... | collective-permute-start | bytes 221192 | tf_op jit(solution)/shard_map/ppermute | solution.py:677
  18.8 7.5 %collective-permute-start.2 = (f32[144,128]{1,0:T(8,128)S(1)}, f32[144,128]{1,0:T(8,128)S(1)}, u32[]{:S(2)}, u32[]{:S(2)}) collective-permute-start(f32[144,128]{1,0:T(8,128)S(1)} %maximum_dynamic-update-slice_fusion), channel_id=1, source_target_pairs={{0,4},{4,8},{8,12},{12,16},{16,20},{20,24},{24,28},{1,5},{5,9},{9,... | collective-permute-start | bytes 221192 | tf_op jit(solution)/shard_map/ppermute | solution.py:677
  28.8 4.4 %collective-permute-start.4 = (f32[96,128]{1,0:T(8,128)S(1)}, f32[96,128]{1,0:T(8,128)S(1)}, u32[]{:S(2)}, u32[]{:S(2)}) collective-permute-start(f32[96,128]{1,0:T(8,128)S(1)} %get-tuple-element.69), channel_id=1, source_target_pairs={{0,1},{1,2},{2,3},{4,5},{5,6},{6,7},{8,9},{9,10},{10,11},{12,13},{... | collective-permute-start | bytes 147464 | tf_op jit(solution)/shard_map/ppermute | solution.py:677
  31.3 5.4 %collective-permute-start.5 = (f32[96,128]{1,0:T(8,128)S(1)}, f32[96,128]{1,0:T(8,128)S(1)}, u32[]{:S(2)}, u32[]{:S(2)}) collective-permute-start(f32[96,128]{1,0:T(8,128)S(1)} %get-tuple-element.70), channel_id=1, source_target_pairs={{1,0},{2,1},{3,2},{5,4},{6,5},{7,6},{9,8},{10,9},{11,10},{13,12},{... | collective-permute-start | bytes 147464 | tf_op jit(solution)/shard_map/ppermute | solution.py:677
  36.7 9.6 %collective-permute-start.7 = (f32[112,128]{1,0:T(8,128)S(1)}, f32[112,128]{1,0:T(8,128)S(1)}, u32[]{:S(2)}, u32[]{:S(2)}) collective-permute-start(f32[112,128]{1,0:T(8,128)S(1)} %maximum_dynamic-update-slice_fusion.3), channel_id=1, source_target_pairs={{4,0},{8,4},{12,8},{16,12},{20,16},{24,20},{28,24},{5,1},{9,5},{13... | collective-permute-start | bytes 172040 | tf_op jit(solution)/shard_map/ppermute | solution.py:677
  38.6 7.7 %collective-permute-start.6 = (f32[112,128]{1,0:T(8,128)S(1)}, f32[112,128]{1,0:T(8,128)S(1)}, u32[]{:S(2)}, u32[]{:S(2)}) collective-permute-start(f32[112,128]{1,0:T(8,128)S(1)} %maximum_dynamic-update-slice_fusion.2), channel_id=1, source_target_pairs={{0,4},{4,8},{8,12},{12,16},{16,20},{20,24},{24,28},{1,5},{5,9},{9,... | collective-permute-start | bytes 172040 | tf_op jit(solution)/shard_map/ppermute | solution.py:677
  48.8 4.4 %collective-permute-start.8 = (f32[96,128]{1,0:T(8,128)S(1)}, f32[96,128]{1,0:T(8,128)S(1)}, u32[]{:S(2)}, u32[]{:S(2)}) collective-permute-start(f32[96,128]{1,0:T(8,128)S(1)} %get-tuple-element.85), channel_id=1, source_target_pairs={{0,1},{1,2},{2,3},{4,5},{5,6},{6,7},{8,9},{9,10},{10,11},{12,13},{... | collective-permute-start | bytes 147464 | tf_op jit(solution)/shard_map/ppermute | solution.py:677
  51.2 5.4 %collective-permute-start.9 = (f32[96,128]{1,0:T(8,128)S(1)}, f32[96,128]{1,0:T(8,128)S(1)}, u32[]{:S(2)}, u32[]{:S(2)}) collective-permute-start(f32[96,128]{1,0:T(8,128)S(1)} %get-tuple-element.86), channel_id=1, source_target_pairs={{1,0},{2,1},{3,2},{5,4},{6,5},{7,6},{9,8},{10,9},{11,10},{13,12},{... | collective-permute-start | bytes 147464 | tf_op jit(solution)/shard_map/ppermute | solution.py:677
  56.6 9.5 %collective-permute-start.11 = (f32[112,128]{1,0:T(8,128)S(1)}, f32[112,128]{1,0:T(8,128)S(1)}, u32[]{:S(2)}, u32[]{:S(2)}) collective-permute-start(f32[112,128]{1,0:T(8,128)S(1)} %maximum_dynamic-update-slice_fusion.5), channel_id=1, source_target_pairs={{4,0},{8,4},{12,8},{16,12},{20,16},{24,20},{28,24},{5,1},{9,5},{13... | collective-permute-start | bytes 172040 | tf_op jit(solution)/shard_map/ppermute | solution.py:677
  58.6 7.6 %collective-permute-start.10 = (f32[112,128]{1,0:T(8,128)S(1)}, f32[112,128]{1,0:T(8,128)S(1)}, u32[]{:S(2)}, u32[]{:S(2)}) collective-permute-start(f32[112,128]{1,0:T(8,128)S(1)} %maximum_dynamic-update-slice_fusion.4), channel_id=1, source_target_pairs={{0,4},{4,8},{8,12},{12,16},{16,20},{20,24},{24,28},{1,5},{5,9},{9,... | collective-permute-start | bytes 172040 | tf_op jit(solution)/shard_map/ppermute | solution.py:677

commit v4 on v3

--- a/solution.py
+++ b/solution.py
@@ -61,7 +61,7 @@
         return aligned((ti % self.per) * SUB), pl.ds((tj % self.half) * LANES, LANES)
 
 
-def set_zero_pads(g, press, stress):
+def zero_press_pads(g, press):
     zero = jnp.zeros((SUB, LANES), jnp.float32)
     for t in range(g.ytiles):
         press[0, pl.ds(PAD + SUB * t, SUB), :] = zero
@@ -72,6 +72,9 @@
         press[x, pl.ds(0, SUB), :] = zero
         press[x, pl.ds(PAD + g.ny, SUB), :] = zero
 
+
+def zero_stress_pads(g, stress):
+    zero = jnp.zeros((SUB, LANES), jnp.float32)
     for field in ALONG_X:
         for tj in range(g.across):
             key = (field - XX) * g.across + tj
@@ -110,7 +113,7 @@
     return lax.broadcasted_iota(jnp.int32, (SUB, LANES), 0)
 
 
-def water_velocity(g, layers, water_out, press, stress, hb_water, load_u):
+def water_velocity(g, layers, water_out, press, surface_row, load_hb, load_u):
     lane = lane_ids()
     top_pick = surface_pick() * g.edge + (g.edge - 1)
 
@@ -121,10 +124,10 @@
             here = press[x + 1, rows, :]
             dx = press[x + 2, rows, :] - press[x, rows, :]
             dy = press[x + 1, pl.ds(PAD + SUB * t + 1, SUB), :] - press[x + 1, pl.ds(PAD + SUB * t - 1, SUB), :]
-            surface = jnp.broadcast_to(stress[(ZZ - XX) * g.across + t, pl.ds(PAD + x, 1), :], (SUB, LANES))
+            surface = jnp.broadcast_to(surface_row(t, x), (SUB, LANES))
             dz = water_z(g, here, -pick(surface, top_pick), lane)
             own = x * g.ny + SUB * t
-            hb = hb_water[aligned(own), :]
+            hb = load_hb(x, t)
             for k, change in ((1, dx), (2, dy), (3, dz)):
                 results.append((k * g.plane + own, load_u(k, x, t) - hb * change))
         return results
@@ -250,16 +253,18 @@
     return store
 
 
-def pack(g, water, bricks, params, hb_water, row_first, row_last, col_first, col_last, first):
-    nx, ny, plane, across, edge = g.nx, g.ny, g.plane, g.across, g.edge
+def pack(g, water, bricks, params, edges, row_first, row_last, col_first, col_last, first):
+    row_u, row_hb, col_u, col_hb = edges
+    nx, ny, across, edge = g.nx, g.ny, g.across, g.edge
     lane = lane_ids()
-    for out, x in ((row_first, 0), (row_last, nx - 1)):
+    for side, (out, x, inward, sign) in enumerate(((row_first, 0, 1, 1.0), (row_last, nx - 1, nx - 2, -1.0))):
         for t in range(g.ytiles):
             own = x * ny + SUB * t
+            hb = row_hb(side, t)
             out[pl.ds(M_P + SUB * t, SUB), :] = water[pl.ds(own, SUB), :]
-            out[pl.ds(M_U + SUB * t, SUB), :] = water[pl.ds(plane + own, SUB), :]
+            out[pl.ds(M_U + SUB * t, SUB), :] = row_u(side, t) - sign * hb * water[pl.ds(inward * ny + SUB * t, SUB), :]
             if first:
-                out[pl.ds(ROW_CONST + SUB * t, SUB), :] = hb_water[pl.ds(own, SUB), :]
+                out[pl.ds(ROW_CONST + SUB * t, SUB), :] = hb
         for tj in range(across):
             block = M_BRICK + SUB * tj
             for k, field in enumerate(ALONG_X + (VX, VY, VZ)):
@@ -267,13 +272,17 @@
             out[pl.ds(block + 6, 1), :] = params[HB * across + tj, pl.ds(x, 1), :]
             out[pl.ds(block + 7, 1), :] = jnp.zeros((1, LANES), jnp.float32)
         out[pl.ds(M_CORNER, 2 * SUB), :] = jnp.zeros((2 * SUB, LANES), jnp.float32)
-    for out, y, tj in ((col_first, 0, 0), (col_last, ny - 1, across - 1)):
+    sides = ((col_first, 0, 1, 0, 1.0), (col_last, ny - 1, ny - 2, across - 1, -1.0))
+    for side, (out, y, inward, tj, sign) in enumerate(sides):
         for t in range(g.xtiles):
             own = SUB * t * ny + y
+            hb = col_hb(side, t)
             out[pl.ds(M_P + SUB * t, SUB), :] = water[pl.ds(own, SUB, stride=ny), :]
-            out[pl.ds(M_U + SUB * t, SUB), :] = water[pl.ds(2 * plane + own, SUB, stride=ny), :]
+            out[pl.ds(M_U + SUB * t, SUB), :] = (
+                col_u(side, t) - sign * hb * water[pl.ds(SUB * t * ny + inward, SUB, stride=ny), :]
+            )
             if first:
-                out[pl.ds(COL_CONST + SUB * t, SUB), :] = hb_water[pl.ds(own, SUB, stride=ny), :]
+                out[pl.ds(COL_CONST + SUB * t, SUB), :] = hb
             rows = pl.ds(SUB * t, SUB)
             pieces = [bricks[field * across + tj, rows, :] for field in ALONG_Y + (VX, VY, VZ)]
             pieces.append(params[HB * across + tj, rows, :])
@@ -292,36 +301,38 @@
 
 def first_kernel(
     g, live_hbm, table_hbm, water_hbm, material_hbm, motion_hbm, kinds_hbm,
-    water_out, bricks_out, params, hb_water, hk_water, row_first, row_last, col_first, col_last,
-    press, stress, water, material, motion, kinds, live, table, sems,
+    water_out, bricks_out, params, columns, row_first, row_last, col_first, col_last,
+    stress, pressure, ux_edge, uy_edge, material_x, material_y, motion, kinds, live, table, sems,
 ):
-    nx, ny, plane, across = g.nx, g.ny, g.plane, g.across
-    copies = [
-        pltpu.make_async_copy(motion_hbm, motion, sems.at[0]),
-        pltpu.make_async_copy(kinds_hbm, kinds, sems.at[1]),
-        pltpu.make_async_copy(water_hbm.at[0], press.at[pl.ds(1, nx), pl.ds(PAD, ny), :], sems.at[2]),
-        pltpu.make_async_copy(material_hbm, material, sems.at[3]),
-        pltpu.make_async_copy(water_hbm.at[pl.ds(1, 3)], water, sems.at[4]),
-        pltpu.make_async_copy(live_hbm, live, sems.at[5]),
-        pltpu.make_async_copy(table_hbm, table, sems.at[6]),
-    ]
-    for copy in copies:
-        copy.start()
+    nx, ny, across = g.nx, g.ny, g.across
+    copies = []
+
+    def fetch(source, target):
+        copies.append(pltpu.make_async_copy(source, target, sems.at[len(copies)]))
+        copies[-1].start()
+
+    fetch(live_hbm, live)
+    fetch(table_hbm, table)
+    fetch(kinds_hbm, kinds)
+    fetch(motion_hbm, motion)
+    fetch(water_hbm.at[0], pressure)
+    for side, (x, y) in enumerate(((0, 0), (nx - 1, ny - SUB))):
+        fetch(water_hbm.at[1, x], ux_edge.at[side])
+        fetch(material_hbm.at[x], material_x.at[side])
+        fetch(water_hbm.at[2, :, pl.ds(y, SUB), :], uy_edge.at[side])
+        fetch(material_hbm.at[:, pl.ds(y, SUB), :], material_y.at[side])
     lane = lane_ids()
-    set_zero_pads(g, press, stress)
-    copies[5].wait()
-    copies[6].wait()
-    levels = table.shape[0]
+    zero_stress_pads(g, stress)
+    copies[0].wait()
+    copies[1].wait()
     scales = (0.5, 0.5, 1.0, 1.0, 1.0, 1.0, 0.5, 1.0)
-    columns = []
     for c, factor in enumerate(scales):
         column = jnp.zeros((SUB, LANES), jnp.float32)
-        for level in range(levels):
+        for level in range(table.shape[0]):
             column = jnp.where(lane == level, table[level, c], column)
-        columns.append(column * factor)
-
-    copies[0].wait()
-    copies[1].wait()
+        columns[c] = column * factor
+    copies[2].wait()
+    copies[3].wait()
 
     @pl.loop(0, g.xtiles)
     def _(ti):
@@ -340,25 +351,16 @@
                 bricks_out[field * across + tj, here, :] = value
                 stress[(field - XX) * across + tj, aligned(PAD + SUB * ti), :] = value
 
-    copies[2].wait()
-    copies[3].wait()
-
-    @pl.loop(0, nx)
-    def _(x):
+    copies[4].wait()
+
+    @pl.loop(0, nx // 2)
+    def _(turn):
         results = []
-        for t in range(g.ytiles):
-            own = x * ny + SUB * t
-            index = material[x, pl.ds(SUB * t, SUB), :]
-            results.append((own, pick(columns[0], index), pick(columns[1], index), press[x + 1, pl.ds(PAD + SUB * t, SUB), :]))
-        for own, hb, hk, p in results:
-            hb_water[aligned(own), :] = hb
-            hk_water[aligned(own), :] = hk
-            water_out[aligned(own), :] = p
-
-    copies[4].wait()
-
-    def load_u(k, x, t):
-        return water[k - 1, x, pl.ds(SUB * t, SUB), :]
+        for x in (2 * turn, 2 * turn + 1):
+            for t in range(g.ytiles):
+                results.append((x * ny + SUB * t, pressure[x, pl.ds(SUB * t, SUB), :]))
+        for own, value in results:
+            water_out[aligned(own), :] = value
 
     def load_v(field, ti, tj):
         slot = g.slot(ti, tj)
@@ -368,9 +370,74 @@
     def load_hb(ti, tj):
         return params[HB * across + tj, aligned(SUB * ti), :]
 
-    water_velocity(g, (nx // 2, lambda turn: 2 * turn), water_out, press, stress, hb_water, load_u)
     brick_velocity(g, water_out, stress, load_v, bricks_out, load_hb)
-    pack(g, water_out, bricks_out, params, hb_water, row_first, row_last, col_first, col_last, True)
+    for copy in copies[5:]:
+        copy.wait()
+
+    def rows_of(side, t):
+        return side, pl.ds(SUB * t, SUB), side * (SUB - 1)
+
+    edges = (
+        lambda side, t: ux_edge[side, pl.ds(SUB * t, SUB), :],
+        lambda side, t: pick(columns[0], material_x[side, pl.ds(SUB * t, SUB), :]),
+        lambda side, t: uy_edge[(*rows_of(side, t), slice(None))],
+        lambda side, t: pick(columns[0], material_y[(*rows_of(side, t), slice(None))]),
+    )
+    pack(g, water_out, bricks_out, params, edges, row_first, row_last, col_first, col_last, True)
+
+
+def first_water_kernel(
+    g, pressure, row_first, row_last, bricks, columns, state, material, water_out, first_same, last_same, hb_water, hk_water, press
+):
+    nx, ny = g.nx, g.ny
+    zero_press_pads(g, press)
+
+    @pl.loop(0, nx // 2)
+    def _(turn):
+        results = []
+        for x in (2 * turn, 2 * turn + 1):
+            for t in range(g.ytiles):
+                own = x * ny + SUB * t
+                index = material[x, pl.ds(SUB * t, SUB), :]
+                results.append((x, t, own, pick(columns[0], index), pick(columns[1], index), pressure[aligned(own), :]))
+        for x, t, own, hb, hk, value in results:
+            hb_water[aligned(own), :] = hb
+            hk_water[aligned(own), :] = hk
+            press[x + 1, pl.ds(PAD + SUB * t, SUB), :] = value
+
+    water_velocity(
+        g,
+        (nx // 2, lambda turn: 2 * turn),
+        water_out,
+        press,
+        lambda t, x: bricks[ZZ * g.across + t, pl.ds(x, 1), :],
+        lambda x, t: hb_water[aligned(x * ny + SUB * t), :],
+        lambda k, x, t: state[k, x, pl.ds(SUB * t, SUB), :],
+    )
+
+
+def edge_water_kernel(
+    g, same, row_first, row_last, water, press, stress, hb_water, ux, uy, water_out, first_same, last_same
+):
+    nx, ny, plane = g.nx, g.ny, g.plane
+
+    def load_u(k, x, t):
+        if k == 1:
+            layer = x - (x // (nx - SUB)) * (nx - 2 * SUB) + 1
+            return ux[aligned(layer * ny + SUB * t), :]
+        if k == 2:
+            return uy[aligned(x * (ny + 2 * PAD) + PAD + SUB * t), :]
+        return water[aligned(3 * plane + x * ny + SUB * t), :]
+
+    water_velocity(
+        g,
+        (SUB, lambda turn: 2 * turn + (turn // (SUB // 2)) * (nx - 2 * SUB)),
+        water_out,
+        press,
+        lambda t, x: stress[(ZZ - XX) * g.across + t, pl.ds(PAD + x, 1), :],
+        lambda x, t: hb_water[aligned(x * ny + SUB * t), :],
+        load_u,
+    )
 
 
 def slots_of(g, array, ti):
@@ -421,7 +488,8 @@
         send(water.at[part(3, 0, nx), :], water_hbm.at[part(3, 0, nx), :])
         send(water.at[part(1, 1, nx - 1), :], water_hbm.at[part(1, 1, nx - 1), :])
     else:
-        set_zero_pads(g, press, stress)
+        zero_press_pads(g, press)
+        zero_stress_pads(g, stress)
 
     @pl.loop(0, nx)
     def _(x):
@@ -517,7 +585,15 @@
             return water[aligned(k * plane + x * ny + SUB * t), :]
 
         layers = ((high - low) // 2, lambda turn: low + 2 * turn)
-        water_velocity(g, layers, water_out, press, stress, hb_water, load_u)
+        water_velocity(
+            g,
+            layers,
+            water_out,
+            press,
+            lambda t, x: stress[(ZZ - XX) * across + t, pl.ds(PAD + x, 1), :],
+            lambda x, t: hb_water[aligned(x * ny + SUB * t), :],
+            load_u,
+        )
 
 
 def water_stress(g, x, t, dx, water, uy, speed, hk_water, lane, top_pick):
@@ -542,9 +618,9 @@
     else:
         water_out, press, stress, bricks_out, memory_out = refs.take(5)
         sends = refs.take(4)
+    (ux,) = refs.take(1)
     if first:
         (const_out,) = refs.take(1)
-    (ux,) = refs.take(1)
     if last:
         press_buf, motion_buf, memory_buf, sems = refs.take(4)
 
@@ -651,24 +727,23 @@
         for copy in copies:
             copy.wait()
     else:
-        def load_u(k, x, t):
-            if k == 1:
-                layer = x - (x // (nx - SUB)) * (nx - 2 * SUB) + 1
-                return ux[aligned(layer * ny + SUB * t), :]
-            if k == 2:
-                return uy[aligned(x * py + PAD + SUB * t), :]
-            return water[aligned(3 * plane + x * ny + SUB * t), :]
-
         def load_v(field, ti, tj):
             return speed[field * wide + 1 + tj, aligned(PAD + SUB * ti), :]
 
         def load_hb(ti, tj):
             return params[HB * across + tj, aligned(SUB * ti), :]
 
-        layers = (SUB, lambda turn: 2 * turn + (turn // (SUB // 2)) * (nx - 2 * SUB))
-        water_velocity(g, layers, water_out, press, stress, hb_water, load_u)
+        def column(side, t):
+            return pl.ds(SUB * t * ny + side * (ny - 1), SUB, stride=ny)
+
+        faces = (
+            lambda side, t: ux[pl.ds((1 + side * (2 * SUB - 1)) * ny + SUB * t, SUB), :],
+            lambda side, t: hb_water[pl.ds(side * (nx - 1) * ny + SUB * t, SUB), :],
+            lambda side, t: uy[pl.ds(SUB * t * py + PAD + side * (ny - 1), SUB, stride=py), :],
+            lambda side, t: hb_water[column(side, t), :],
+        )
         brick_velocity(g, water_out, stress, load_v, bricks_out, load_hb)
-        pack(g, water_out, bricks_out, params, hb_water, *sends, False)
+        pack(g, water_out, bricks_out, params, faces, *sends, False)
 
 
 def shift(value, axis, up):
@@ -711,9 +786,6 @@
     vmem = pl.BlockSpec(memory_space=pltpu.VMEM)
     hbm = pl.BlockSpec(memory_space=pltpu.HBM)
     params = pltpu.CompilerParams(vmem_limit_bytes=24 * 1024 * 1024)
-    press = pltpu.VMEM((nx + 2, ny + 2 * PAD, nz), jnp.float32)
-    stress = pltpu.VMEM((6 * across, nx + 2 * PAD, LANES), jnp.float32)
-
     def messages(first):
         extra = 32 if first else 0
         return [f32(112 + extra, LANES)] * 2 + [f32(96 + extra, LANES)] * 2
@@ -724,39 +796,55 @@
     def held(*values):
         return [pltpu.with_memory_space_constraint(value, pltpu.VMEM) for value in values]
 
-    results = pl.pallas_call(
+    def pinned(*values):
+        return [pltpu.with_memory_space_constraint(value, pltpu.HBM) for value in values]
+
+    press = buffer(nx + 2, ny + 2 * PAD, nz)
+    stress = buffer(6 * across, nx + 2 * PAD, LANES)
+    work = pl.CostEstimate(flops=20_000_000, bytes_accessed=8_000_000, transcendentals=0)
+    water, bricks, coefficients, columns, *sends = pl.pallas_call(
         functools.partial(first_kernel, g),
         out_shape=[
-            f32(4 * plane, nz), f32(9 * across, nx, LANES), f32(9 * across, nx, LANES), f32(plane, nz), f32(plane, nz),
+            buffer(4 * plane, nz), f32(9 * across, nx, LANES), f32(9 * across, nx, LANES), f32(8, SUB, LANES),
         ] + messages(True),
         in_specs=[hbm] * 6,
-        out_specs=[vmem] * 9,
+        out_specs=[vmem] * 8,
         scratch_shapes=[
-            press,
             stress,
-            pltpu.VMEM((3, nx, ny, nz), jnp.float32),
-            pltpu.VMEM(water_material.shape, jnp.int32),
+            buffer(nx, ny, nz),
+            buffer(2, ny, nz),
+            buffer(2, nx, SUB, nz),
+            pltpu.VMEM((2, ny, nz), jnp.int32),
+            pltpu.VMEM((2, nx, SUB, nz), jnp.int32),
             pltpu.VMEM(brick_velocity_stress.shape, jnp.float32),
             pltpu.VMEM(brick_cell_material.shape, jnp.int32),
             pltpu.SMEM(brick_live.shape, jnp.int32),
             pltpu.SMEM(material_table.shape, jnp.float32),
-            pltpu.SemaphoreType.DMA((7,)),
+            pltpu.SemaphoreType.DMA((13,)),
         ],
         compiler_params=params,
-        name="first_velocity",
-    )(*[
-        pltpu.with_memory_space_constraint(value, pltpu.HBM)
-        for value in (
-            brick_live, material_table, water_state, water_material, brick_velocity_stress, brick_cell_material,
-        )
-    ])
-    water, bricks, coefficients, hb_water, hk_water = results[:5]
-    sends = results[5:]
+        name="first_bricks",
+    )(*pinned(brick_live, material_table, water_state, water_material, brick_velocity_stress, brick_cell_material))
+
+    def passed(*messages):
+        return [buffer(*message.shape) for message in messages]
+
+    water, sends[0], sends[1], hb_water, hk_water = pl.pallas_call(
+        functools.partial(first_water_kernel, g),
+        out_shape=[buffer(4 * plane, nz)] + passed(*sends[:2]) + [f32(plane, nz), f32(plane, nz)],
+        in_specs=[vmem] * 7,
+        out_specs=[vmem] * 5,
+        input_output_aliases={0: 0, 1: 1, 2: 2},
+        scratch_shapes=[press],
+        compiler_params=params,
+        cost_estimate=work,
+        name="first_water",
+    )(*held(water, *sends[:2], bricks, columns, water_state, water_material))
     memory = brick_relaxation_memory
     col_const, row_const = (), ()
     uy_shape = (nx * (ny + 2 * PAD), nz)
     speed_shape = (3 * (across + 2), nx + 2 * PAD, LANES)
-    ux = buffer((2 * SUB + 2) * ny, nz)
+    ux_buffer = buffer((2 * SUB + 2) * ny, nz)
     slot_buffers = [
         pltpu.VMEM(brick_velocity_stress.shape, jnp.float32),
         pltpu.VMEM(brick_relaxation_memory.shape, jnp.float32),
@@ -782,7 +870,7 @@
             out_specs=[vmem] * 2 + spaces + ([vmem] if first else []),
             scratch_shapes=[buffer(plane, nz), buffer(plane, nz)] + slot_buffers + [pltpu.SemaphoreType.DMA((8,))] if last else [],
             compiler_params=params,
-            cost_estimate=pl.CostEstimate(flops=20_000_000, bytes_accessed=8_000_000, transcendentals=0),
+            cost_estimate=work,
             name="inner",
         )(*held(*state), *columns, *col_const)
         if first:
@@ -792,20 +880,34 @@
         count = 10 + len(row_const) + 1
         results = pl.pallas_call(
             functools.partial(edge_kernel, g, first, last),
-            out_shape=[buffer(*speed_shape)] + shapes + ([] if last else messages(False)) + ([buffer(64, LANES)] if first else []),
+            out_shape=[buffer(*speed_shape)]
+            + shapes
+            + ([] if last else messages(False) + [ux_buffer])
+            + ([buffer(64, LANES)] if first else []),
             in_specs=[vmem] * (count + 1) + spaces,
-            out_specs=[vmem] + spaces + [vmem] * (0 if last else 4) + ([vmem] if first else []),
+            out_specs=[vmem] + spaces + [vmem] * (0 if last else 5) + ([vmem] if first else []),
             input_output_aliases={count + k: k for k in range(1 + len(shapes))},
-            scratch_shapes=[ux] + ([buffer(4 * ny, nz)] + slot_buffers + [pltpu.SemaphoreType.DMA((8,))] if last else []),
+            scratch_shapes=[ux_buffer, buffer(4 * ny, nz)] + slot_buffers + [pltpu.SemaphoreType.DMA((8,))] if last else [],
             compiler_params=params,
             name="edges",
         )(*held(*state), *columns, row_before, row_after, *row_const, *held(uy), *(held(partial[0]) + (list(partial[1:]) if last else held(*partial[1:]))))
         if last:
             return results[2], results[3], results[1].reshape(water_state.shape)
-        _, water, _, _, bricks, memory = results[:6]
-        sends = results[6:10]
+        old_water = water
+        _, water, pressed, stressed, bricks, memory = results[:6]
+        sends = list(results[6:10])
         if first:
-            row_const = (results[10],)
+            row_const = (results[11],)
+        water, sends[0], sends[1] = pl.pallas_call(
+            functools.partial(edge_water_kernel, g),
+            out_shape=[buffer(4 * plane, nz)] + passed(*sends[:2]),
+            in_specs=[vmem] * 9,
+            out_specs=[vmem] * 3,
+            input_output_aliases={0: 0, 1: 1, 2: 2},
+            compiler_params=params,
+            cost_estimate=work,
+            name="edge_water",
+        )(*held(water, *sends[:2], old_water, pressed, stressed, hb_water, results[10], uy))
 
 
 def solution(mesh):

time: 68.4 us -> 64.5 us (0.943)
  waiting for transfers between devices: 10.6 us -> 5.48 us
  starting transfers between devices: 32.8 us -> 34.5 us
    ppermute x12, waiting for transfers between devices: 10.6 us -> 5.48 us  [shift(): lax.ppermute(value, axis, pairs if up else [(j, i) for i, j in pairs])]
    ppermute x12, starting transfers between devices: 32.8 us -> 34.5 us  [shift(): lax.ppermute(value, axis, pairs if up else [(j, i) for i, j in pairs])]
    pallas_call x3, Pallas kernels: 6.78 us -> 5.18 us  [body(): pl.pallas_call(functools.partial(edge_kernel, g, first, last), out_shape=...]
    pallas_call x1 -> x4, Pallas kernels: 6.76 us -> 7.88 us  [the longest x1 3.43 us: body(): pl.pallas_call(functools.partial(first_water_kernel, g), out_shape=[buffe...]
  transfers between devices with their start and end apart: 12 -> 12, of which waited for: 3 -> 3; matrix products, arithmetic and copies ran while one was open for 0% -> 0% of each run, Pallas kernels for 15% -> 24%
where the time goes in v4:
time: 64.5 us; the launch traced here: 64.1 us
  starting transfers between devices  34.5 us (53%)
  Pallas kernels  23.1 us (36%)
  waiting for transfers between devices  5.48 us (8%)
  between operations  0.96 us (1%)
    ppermute x12, starting transfers between devices, shift(): lax.ppermute(value, axis, pairs if up else [(j, i) for i, j in pairs])  34.5 us
    pallas_call x3, Pallas kernels, body(): pl.pallas_call(functools.partial(inner_kernel, g, first, last), out_shape...  10.1 us
    ppermute x12, waiting for transfers between devices, shift(): lax.ppermute(value, axis, pairs if up else [(j, i) for i, j in pairs])  5.48 us
    pallas_call x3, Pallas kernels, body(): pl.pallas_call(functools.partial(edge_kernel, g, first, last), out_shape=...  5.18 us
    pallas_call x1, Pallas kernels, body(): pl.pallas_call(functools.partial(first_water_kernel, g), out_shape=[buffe...  3.43 us
    pallas_call x1, Pallas kernels, body(): pl.pallas_call(functools.partial(first_kernel, g), out_shape=[buffer(4 *...  2.84 us
    pallas_call x2, Pallas kernels, body(): pl.pallas_call(functools.partial(edge_water_kernel, g), out_shape=[buffer...  1.61 us
  transfers between devices with their start and end apart: 12, of which 3 were waited for; matrix products, arithmetic and copies ran while one was open for 0% of the time, Pallas kernels for 24%

profile of v4, /device:TPU:5, one launch (start us, length us, event | category | flops | bytes accessed | tf_op | source)
XLA Modules:
  0.0 64.1 jit_solution(3786408944752174240)
XLA Ops:
  0.6 0.0 copy-start.2
  0.6 0.0 copy-start
  0.7 2.8 %first_bricks.1 = (f32[4096,128]{1,0:T(8,128)S(1)}, f32[36,32,128]{2,1,0:T(8,128)S(1)}, f32[36,32,128]{2,1,0:T(8,128)S(1)}, f32[8,8,128]{2,1,0:T(8,128)S(1)}, f3...) custom-call(s32[4]{0:T(128)} %live_hbm.1, f32[8,8]{1,0:T(8,128)} %table_hbm.1, ...), custom_call_target="tpu_custom_call" | custom-call | tf_op jit(solution)/shard_map/first_bricks/pallas_call | solution.py:805
  3.5 3.7 %collective-permute-start = (f32[128,128]{1,0:T(8,128)S(1)}, f32[128,128]{1,0:T(8,128)S(1)}, u32[]{:S(2)}, u32[]{:S(2)}) collective-permute-start(f32[128,128]{1,0:T(8,128)S(1)} %get-tuple-element.75), channel_id=1, source_target_pairs={{0,1},{1,2},{2,3},{4,5},{5,6},{6,7},{8,9},{9,10},{10,11},{12,13},{... | collective-permute-start | bytes 196616 | tf_op jit(solution)/shard_map/ppermute | solution.py:752
  7.2 1.9 %collective-permute-start.1 = (f32[128,128]{1,0:T(8,128)S(1)}, f32[128,128]{1,0:T(8,128)S(1)}, u32[]{:S(2)}, u32[]{:S(2)}) collective-permute-start(f32[128,128]{1,0:T(8,128)S(1)} %get-tuple-element.76), channel_id=1, source_target_pairs={{1,0},{2,1},{3,2},{5,4},{6,5},{7,6},{9,8},{10,9},{11,10},{13,12},{... | collective-permute-start | bytes 196616 | tf_op jit(solution)/shard_map/ppermute | solution.py:752
  9.1 0.0 copy-done.2
  9.1 0.0 copy-done
  9.1 0.0 copy-start.1
  9.1 3.4 %first_water.1 = (f32[4096,128]{1,0:T(8,128)S(1)}, f32[144,128]{1,0:T(8,128)S(1)}, f32[144,128]{1,0:T(8,128)S(1)}, f32[1024,128]{1,0:T(8,128)S(1)}, f32[1024,128]{1,0:T(8,128)S(1)}) custom-call(f32[4096,128]{1,0:T(8,128)S(1)} %get-tuple-element.66.pressure, ...), custom_call_target="tpu_custom_call", output_to_operand_aliasing={{0}: (0, {}), {1}: (1, {}), {2}: (2, {})} | custom-call | flops 20000000 | bytes 8000000 | tf_op jit(solution)/shard_map/first_water/pallas_call | solution.py:832
  12.6 0.0 collective-permute-done.refs_6_
  12.6 0.2 collective-permute-done.1.refs_7_
  12.8 2.1 %collective-permute-start.3 = (f32[144,128]{1,0:T(8,128)S(1)}, f32[144,128]{1,0:T(8,128)S(1)}, u32[]{:S(2)}, u32[]{:S(2)}) collective-permute-start(f32[144,128]{1,0:T(8,128)S(1)} %maximum_dynamic-update-slice_fusion.1), channel_id=1, source_target_pairs={{4,0},{8,4},{12,8},{16,12},{20,16},{24,20},{28,24},{5,1},{9,5},{13... | collective-permute-start | bytes 221192 | tf_op jit(solution)/shard_map/ppermute | solution.py:752
  14.9 4.0 %collective-permute-start.2 = (f32[144,128]{1,0:T(8,128)S(1)}, f32[144,128]{1,0:T(8,128)S(1)}, u32[]{:S(2)}, u32[]{:S(2)}) collective-permute-start(f32[144,128]{1,0:T(8,128)S(1)} %maximum_dynamic-update-slice_fusion), channel_id=1, source_target_pairs={{0,4},{4,8},{8,12},{12,16},{16,20},{20,24},{24,28},{1,5},{5,9},{9,... | collective-permute-start | bytes 221192 | tf_op jit(solution)/shard_map/ppermute | solution.py:752
  19.0 0.0 copy-done.1
  19.0 3.4 %inner.3 = (f32[1536,128]{1,0:T(8,128)S(1)}, f32[18,48,128]{2,1,0:T(8,128)S(1)}, f32[4096,128]{1,0:T(8,128)S(1)}, f32[34,48,128]{2,1,0:T(8,128)S(1)}, f32[24,48,...) custom-call(f32[4096,128]{1,0:T(8,128)S(1)} %get-tuple-element.71.refs_0_.wat, ...), custom_call_target="tpu_custom_call" | custom-call | flops 20000000 | bytes 8000000 | tf_op jit(solution)/shard_map/inner/pallas_call | solution.py:866
  22.4 0.0 collective-permute-done.3.refs_9_
  22.4 0.0 collective-permute-done.2.refs_8_
  22.4 1.7 %edges.3 = (f32[18,48,128]{2,1,0:T(8,128)S(1)}, f32[4096,128]{1,0:T(8,128)S(1)}, f32[34,48,128]{2,1,0:T(8,128)S(1)}, f32[24,48,128]{2,1,0:T(8,128)S(1)}, f32[36,...) custom-call(f32[4096,128]{1,0:T(8,128)S(1)} %get-tuple-element.71.re, ...), custom_call_target="tpu_custom_call", output_to_operand_aliasing={{0}: (11, {}), {1}: (12, {}), {2}: (13, {}), {3}: (14, {}),... | custom-call | tf_op jit(solution)/shard_map/edges/pallas_call | solution.py:881
  24.1 4.1 %collective-permute-start.4 = (f32[96,128]{1,0:T(8,128)S(1)}, f32[96,128]{1,0:T(8,128)S(1)}, u32[]{:S(2)}, u32[]{:S(2)}) collective-permute-start(f32[96,128]{1,0:T(8,128)S(1)} %get-tuple-element.95), channel_id=1, source_target_pairs={{0,1},{1,2},{2,3},{4,5},{5,6},{6,7},{8,9},{9,10},{10,11},{12,13},{... | collective-permute-start | bytes 147464 | tf_op jit(solution)/shard_map/ppermute | solution.py:752
  28.2 1.9 %collective-permute-start.5 = (f32[96,128]{1,0:T(8,128)S(1)}, f32[96,128]{1,0:T(8,128)S(1)}, u32[]{:S(2)}, u32[]{:S(2)}) collective-permute-start(f32[96,128]{1,0:T(8,128)S(1)} %get-tuple-element.96), channel_id=1, source_target_pairs={{1,0},{2,1},{3,2},{5,4},{6,5},{7,6},{9,8},{10,9},{11,10},{13,12},{... | collective-permute-start | bytes 147464 | tf_op jit(solution)/shard_map/ppermute | solution.py:752
  30.1 0.8 %edge_water.2 = (f32[4096,128]{1,0:T(8,128)S(1)}, f32[112,128]{1,0:T(8,128)S(1)}, f32[112,128]{1,0:T(8,128)S(1)}) custom-call(f32[4096,128]{1,0:T(8,128)S(1)} %get-tuple-element.86.same, f32[112,128]{1,0:T(8,128)S(1)} %get-tuple-element.87.row_first, ...), custom_call_target="tpu_custom_call", output_to_operand_aliasing={{0}: (0, {}), {1}: (1, {}), {2}: (2, {})} | custom-call | flops 20000000 | bytes 8000000 | tf_op jit(solution)/shard_map/edge_water/pallas_call | solution.py:901
  30.9 0.0 collective-permute-done.4.refs_6_
  30.9 2.6 %collective-permute-done.5.refs_7_ = f32[96,128]{1,0:T(8,128)S(1)} collective-permute-done((f32[96,128]{1,0:T(8,128)S(1)}, f32[96,128]{1,0:T(8,128)S(1)}, u32[]{:S(2)}, u32[]{:S(2)}) %collective-permute-start.5) | collective-permute-done | bytes 49184 | tf_op jit(solution)/shard_map/ppermute | solution.py:752
  33.6 1.9 %collective-permute-start.7 = (f32[112,128]{1,0:T(8,128)S(1)}, f32[112,128]{1,0:T(8,128)S(1)}, u32[]{:S(2)}, u32[]{:S(2)}) collective-permute-start(f32[112,128]{1,0:T(8,128)S(1)} %maximum_dynamic-update-slice_fusion.3), channel_id=1, source_target_pairs={{4,0},{8,4},{12,8},{16,12},{20,16},{24,20},{28,24},{5,1},{9,5},{13... | collective-permute-start | bytes 172040 | tf_op jit(solution)/shard_map/ppermute | solution.py:752
  35.5 4.3 %collective-permute-start.6 = (f32[112,128]{1,0:T(8,128)S(1)}, f32[112,128]{1,0:T(8,128)S(1)}, u32[]{:S(2)}, u32[]{:S(2)}) collective-permute-start(f32[112,128]{1,0:T(8,128)S(1)} %maximum_dynamic-update-slice_fusion.2), channel_id=1, source_target_pairs={{0,4},{4,8},{8,12},{12,16},{16,20},{20,24},{24,28},{1,5},{5,9},{9,... | collective-permute-start | bytes 172040 | tf_op jit(solution)/shard_map/ppermute | solution.py:752
  39.8 3.4 %inner.4 = (f32[1536,128]{1,0:T(8,128)S(1)}, f32[18,48,128]{2,1,0:T(8,128)S(1)}, f32[4096,128]{1,0:T(8,128)S(1)}, f32[34,48,128]{2,1,0:T(8,128)S(1)}, f32[24,48,...) custom-call(f32[4096,128]{1,0:T(8,128)S(1)} %get-tuple-element.92.refs_0_.water, ...), custom_call_target="tpu_custom_call" | custom-call | flops 20000000 | bytes 8000000 | tf_op jit(solution)/shard_map/inner/pallas_call | solution.py:866
  43.2 0.0 collective-permute-done.7.refs_9_
  43.2 0.0 collective-permute-done.6.refs_8_
  43.2 1.7 %edges.4 = (f32[18,48,128]{2,1,0:T(8,128)S(1)}, f32[4096,128]{1,0:T(8,128)S(1)}, f32[34,48,128]{2,1,0:T(8,128)S(1)}, f32[24,48,128]{2,1,0:T(8,128)S(1)}, f32[36,...) custom-call(f32[4096,128]{1,0:T(8,128)S(1)} %get-tuple-element.92.re, ...), custom_call_target="tpu_custom_call", output_to_operand_aliasing={{0}: (12, {}), {1}: (13, {}), {2}: (14, {}), {3}: (15, {}),... | custom-call | tf_op jit(solution)/shard_map/edges/pallas_call | solution.py:881
  44.9 2.5 %collective-permute-start.8 = (f32[96,128]{1,0:T(8,128)S(1)}, f32[96,128]{1,0:T(8,128)S(1)}, u32[]{:S(2)}, u32[]{:S(2)}) collective-permute-start(f32[96,128]{1,0:T(8,128)S(1)} %get-tuple-element.117), channel_id=1, source_target_pairs={{0,1},{1,2},{2,3},{4,5},{5,6},{6,7},{8,9},{9,10},{10,11},{12,13},{... | collective-permute-start | bytes 147464 | tf_op jit(solution)/shard_map/ppermute | solution.py:752
  47.4 1.9 %collective-permute-start.9 = (f32[96,128]{1,0:T(8,128)S(1)}, f32[96,128]{1,0:T(8,128)S(1)}, u32[]{:S(2)}, u32[]{:S(2)}) collective-permute-start(f32[96,128]{1,0:T(8,128)S(1)} %get-tuple-element.118), channel_id=1, source_target_pairs={{1,0},{2,1},{3,2},{5,4},{6,5},{7,6},{9,8},{10,9},{11,10},{13,12},{... | collective-permute-start | bytes 147464 | tf_op jit(solution)/shard_map/ppermute | solution.py:752
  49.3 0.8 %edge_water.3 = (f32[4096,128]{1,0:T(8,128)S(1)}, f32[112,128]{1,0:T(8,128)S(1)}, f32[112,128]{1,0:T(8,128)S(1)}) custom-call(f32[4096,128]{1,0:T(8,128)S(1)} %get-tuple-element.108.same, f32[112,128]{1,0:T(8,128)S(1)} %get-tuple-element.109.row_first, ...), custom_call_target="tpu_custom_call", output_to_operand_aliasing={{0}: (0, {}), {1}: (1, {}), {2}: (2, {})} | custom-call | flops 20000000 | bytes 8000000 | tf_op jit(solution)/shard_map/edge_water/pallas_call | solution.py:901
  50.1 0.0 collective-permute-done.8.refs_6_
  50.1 2.6 %collective-permute-done.9.refs_7_ = f32[96,128]{1,0:T(8,128)S(1)} collective-permute-done((f32[96,128]{1,0:T(8,128)S(1)}, f32[96,128]{1,0:T(8,128)S(1)}, u32[]{:S(2)}, u32[]{:S(2)}) %collective-permute-start.9) | collective-permute-done | bytes 49184 | tf_op jit(solution)/shard_map/ppermute | solution.py:752
  52.8 1.9 %collective-permute-start.11 = (f32[112,128]{1,0:T(8,128)S(1)}, f32[112,128]{1,0:T(8,128)S(1)}, u32[]{:S(2)}, u32[]{:S(2)}) collective-permute-start(f32[112,128]{1,0:T(8,128)S(1)} %maximum_dynamic-update-slice_fusion.5), channel_id=1, source_target_pairs={{4,0},{8,4},{12,8},{16,12},{20,16},{24,20},{28,24},{5,1},{9,5},{13... | collective-permute-start | bytes 172040 | tf_op jit(solution)/shard_map/ppermute | solution.py:752
  54.7 4.3 %collective-permute-start.10 = (f32[112,128]{1,0:T(8,128)S(1)}, f32[112,128]{1,0:T(8,128)S(1)}, u32[]{:S(2)}, u32[]{:S(2)}) collective-permute-start(f32[112,128]{1,0:T(8,128)S(1)} %maximum_dynamic-update-slice_fusion.4), channel_id=1, source_target_pairs={{0,4},{4,8},{8,12},{12,16},{16,20},{20,24},{24,28},{1,5},{5,9},{9,... | collective-permute-start | bytes 172040 | tf_op jit(solution)/shard_map/ppermute | solution.py:752
  59.0 3.3 %inner.5 = (f32[1536,128]{1,0:T(8,128)S(1)}, f32[18,48,128]{2,1,0:T(8,128)S(1)}, f32[4096,128]{1,0:T(8,128)}, f32[4,9,16,256]{3,2,1,0:T(8,128)}, f32[4,18,16,256]{3,2,1,0:T(8,128)}) custom-call(f32[4096,128]{1,0:T(8,128)S(1)} %get-tuple-element.114.refs_0_, f32[36,32,128]{2,1,0:T(8,128)S(1)} %get-tuple-element.115.refs_1_, ...), custom_call_target="tpu_custom_call" | custom-call | flops 20000000 | bytes 8000000 | tf_op jit(solution)/shard_map/inner/pallas_call | solution.py:866
  62.3 0.0 collective-permute-done.11.refs_9_
  62.3 0.0 collective-permute-done.10.refs_8_
  62.3 1.8 %edges.5 = (f32[18,48,128]{2,1,0:T(8,128)S(1)}, f32[4096,128]{1,0:T(8,128)}, f32[4,9,16,256]{3,2,1,0:T(8,128)}, f32[4,18,16,256]{3,2,1,0:T(8,128)}) custom-call(f32[4096,128]{1,0:T(8,128)S(1)} %get-tuple-element.114.refs_0_, ...), custom_call_target="tpu_custom_call", output_to_operand_aliasing={{0}: (12, {}), {1}: (13, {}), {2}: (14, {}), {3}: (15, {})} | custom-call | tf_op jit(solution)/shard_map/edges/pallas_call | solution.py:881
  (12 shorter events, 0.0 us)
Async XLA Ops:
  0.6 8.5 %copy-start.2 = (s32[32,32,128]{2,1,0:T(8,128)S(1)}, s32[32,32,128]{2,1,0:T(8,128)}, u32[]{:S(2)}) copy-start(s32[32,32,128]{2,1,0:T(8,128)} %material.1) | copy-start | bytes 1572868
  0.6 8.5 %copy-start = (f32[4,32,32,128]{3,2,1,0:T(8,128)S(1)}, f32[4,32,32,128]{3,2,1,0:T(8,128)}, u32[]{:S(2)}) copy-start(f32[4,32,32,128]{3,2,1,0:T(8,128)} %state.1) | copy-start | bytes 6291460
  3.5 9.1 %collective-permute-start = (f32[128,128]{1,0:T(8,128)S(1)}, f32[128,128]{1,0:T(8,128)S(1)}, u32[]{:S(2)}, u32[]{:S(2)}) collective-permute-start(f32[128,128]{1,0:T(8,128)S(1)} %get-tuple-element.75), channel_id=1, source_target_pairs={{0,1},{1,2},{2,3},{4,5},{5,6},{6,7},{8,9},{9,10},{10,11},{12,13},{... | collective-permute-start | bytes 196616 | tf_op jit(solution)/shard_map/ppermute | solution.py:752
  7.2 5.6 %collective-permute-start.1 = (f32[128,128]{1,0:T(8,128)S(1)}, f32[128,128]{1,0:T(8,128)S(1)}, u32[]{:S(2)}, u32[]{:S(2)}) collective-permute-start(f32[128,128]{1,0:T(8,128)S(1)} %get-tuple-element.76), channel_id=1, source_target_pairs={{1,0},{2,1},{3,2},{5,4},{6,5},{7,6},{9,8},{10,9},{11,10},{13,12},{... | collective-permute-start | bytes 196616 | tf_op jit(solution)/shard_map/ppermute | solution.py:752
  9.1 9.8 %copy-start.1 = (f32[4,18,16,256]{3,2,1,0:T(8,128)S(1)}, f32[4,18,16,256]{3,2,1,0:T(8,128)}, u32[]{:S(2)}) copy-start(f32[4,18,16,256]{3,2,1,0:T(8,128)} %refs_2_.3) | copy-start | bytes 3538948
  12.8 9.6 %collective-permute-start.3 = (f32[144,128]{1,0:T(8,128)S(1)}, f32[144,128]{1,0:T(8,128)S(1)}, u32[]{:S(2)}, u32[]{:S(2)}) collective-permute-start(f32[144,128]{1,0:T(8,128)S(1)} %maximum_dynamic-update-slice_fusion.1), channel_id=1, source_target_pairs={{4,0},{8,4},{12,8},{16,12},{20,16},{24,20},{28,24},{5,1},{9,5},{13... | collective-permute-start | bytes 221192 | tf_op jit(solution)/shard_map/ppermute | solution.py:752
  14.9 7.5 %collective-permute-start.2 = (f32[144,128]{1,0:T(8,128)S(1)}, f32[144,128]{1,0:T(8,128)S(1)}, u32[]{:S(2)}, u32[]{:S(2)}) collective-permute-start(f32[144,128]{1,0:T(8,128)S(1)} %maximum_dynamic-update-slice_fusion), channel_id=1, source_target_pairs={{0,4},{4,8},{8,12},{12,16},{16,20},{20,24},{24,28},{1,5},{5,9},{9,... | collective-permute-start | bytes 221192 | tf_op jit(solution)/shard_map/ppermute | solution.py:752
  24.1 6.8 %collective-permute-start.4 = (f32[96,128]{1,0:T(8,128)S(1)}, f32[96,128]{1,0:T(8,128)S(1)}, u32[]{:S(2)}, u32[]{:S(2)}) collective-permute-start(f32[96,128]{1,0:T(8,128)S(1)} %get-tuple-element.95), channel_id=1, source_target_pairs={{0,1},{1,2},{2,3},{4,5},{5,6},{6,7},{8,9},{9,10},{10,11},{12,13},{... | collective-permute-start | bytes 147464 | tf_op jit(solution)/shard_map/ppermute | solution.py:752
  28.2 5.4 %collective-permute-start.5 = (f32[96,128]{1,0:T(8,128)S(1)}, f32[96,128]{1,0:T(8,128)S(1)}, u32[]{:S(2)}, u32[]{:S(2)}) collective-permute-start(f32[96,128]{1,0:T(8,128)S(1)} %get-tuple-element.96), channel_id=1, source_target_pairs={{1,0},{2,1},{3,2},{5,4},{6,5},{7,6},{9,8},{10,9},{11,10},{13,12},{... | collective-permute-start | bytes 147464 | tf_op jit(solution)/shard_map/ppermute | solution.py:752
  33.6 9.6 %collective-permute-start.7 = (f32[112,128]{1,0:T(8,128)S(1)}, f32[112,128]{1,0:T(8,128)S(1)}, u32[]{:S(2)}, u32[]{:S(2)}) collective-permute-start(f32[112,128]{1,0:T(8,128)S(1)} %maximum_dynamic-update-slice_fusion.3), channel_id=1, source_target_pairs={{4,0},{8,4},{12,8},{16,12},{20,16},{24,20},{28,24},{5,1},{9,5},{13... | collective-permute-start | bytes 172040 | tf_op jit(solution)/shard_map/ppermute | solution.py:752
  35.5 7.7 %collective-permute-start.6 = (f32[112,128]{1,0:T(8,128)S(1)}, f32[112,128]{1,0:T(8,128)S(1)}, u32[]{:S(2)}, u32[]{:S(2)}) collective-permute-start(f32[112,128]{1,0:T(8,128)S(1)} %maximum_dynamic-update-slice_fusion.2), channel_id=1, source_target_pairs={{0,4},{4,8},{8,12},{12,16},{16,20},{20,24},{24,28},{1,5},{5,9},{9,... | collective-permute-start | bytes 172040 | tf_op jit(solution)/shard_map/ppermute | solution.py:752
  44.9 5.2 %collective-permute-start.8 = (f32[96,128]{1,0:T(8,128)S(1)}, f32[96,128]{1,0:T(8,128)S(1)}, u32[]{:S(2)}, u32[]{:S(2)}) collective-permute-start(f32[96,128]{1,0:T(8,128)S(1)} %get-tuple-element.117), channel_id=1, source_target_pairs={{0,1},{1,2},{2,3},{4,5},{5,6},{6,7},{8,9},{9,10},{10,11},{12,13},{... | collective-permute-start | bytes 147464 | tf_op jit(solution)/shard_map/ppermute | solution.py:752
  47.4 5.4 %collective-permute-start.9 = (f32[96,128]{1,0:T(8,128)S(1)}, f32[96,128]{1,0:T(8,128)S(1)}, u32[]{:S(2)}, u32[]{:S(2)}) collective-permute-start(f32[96,128]{1,0:T(8,128)S(1)} %get-tuple-element.118), channel_id=1, source_target_pairs={{1,0},{2,1},{3,2},{5,4},{6,5},{7,6},{9,8},{10,9},{11,10},{13,12},{... | collective-permute-start | bytes 147464 | tf_op jit(solution)/shard_map/ppermute | solution.py:752
  52.8 9.5 %collective-permute-start.11 = (f32[112,128]{1,0:T(8,128)S(1)}, f32[112,128]{1,0:T(8,128)S(1)}, u32[]{:S(2)}, u32[]{:S(2)}) collective-permute-start(f32[112,128]{1,0:T(8,128)S(1)} %maximum_dynamic-update-slice_fusion.5), channel_id=1, source_target_pairs={{4,0},{8,4},{12,8},{16,12},{20,16},{24,20},{28,24},{5,1},{9,5},{13... | collective-permute-start | bytes 172040 | tf_op jit(solution)/shard_map/ppermute | solution.py:752
  54.7 7.6 %collective-permute-start.10 = (f32[112,128]{1,0:T(8,128)S(1)}, f32[112,128]{1,0:T(8,128)S(1)}, u32[]{:S(2)}, u32[]{:S(2)}) collective-permute-start(f32[112,128]{1,0:T(8,128)S(1)} %maximum_dynamic-update-slice_fusion.4), channel_id=1, source_target_pairs={{0,4},{4,8},{8,12},{12,16},{16,20},{20,24},{24,28},{1,5},{5,9},{9,... | collective-permute-start | bytes 172040 | tf_op jit(solution)/shard_map/ppermute | solution.py:752

commit v5 on v4

--- a/solution.py
+++ b/solution.py
@@ -16,8 +16,7 @@
 ALONG_X = (XX, XY, XZ)
 ALONG_Y = (XY, YY, YZ)
 ALONG_Z = (XZ, YZ, ZZ)
-M_P, M_U, M_BRICK, M_CORNER = 0, 32, 64, 96
-COL_CONST, ROW_CONST = 96, 112
+M_P, M_U, M_BRICK, M_CORNER, M_CONST = 0, 32, 64, 96, 112
 
 
 def lane_ids():
@@ -253,8 +252,26 @@
     return store
 
 
-def pack(g, water, bricks, params, edges, row_first, row_last, col_first, col_last, first):
+def route(odd, first, last, out_far, out_near):
+    for start in range(0, out_far.shape[0], SUB):
+        rows = pl.ds(start, SUB)
+        one, other = first[rows, :], last[rows, :]
+        out_far[rows, :] = jnp.where(odd, other, one)
+        out_near[rows, :] = jnp.where(odd, one, other)
+
+
+def unroute(odd, from_far, from_near, before, after):
+    for start in range(0, from_far.shape[0], SUB):
+        rows = pl.ds(start, SUB)
+        far, near = from_far[rows, :], from_near[rows, :]
+        before[rows, :] = jnp.where(odd, near, far)
+        after[rows, :] = jnp.where(odd, far, near)
+
+
+def pack(g, water, bricks, params, edges, odd, buffers, sends, first):
     row_u, row_hb, col_u, col_hb = edges
+    row_first, row_last, col_first, col_last = buffers
+    row_odd, col_odd = odd[0] > 0.0, odd[1] > 0.0
     nx, ny, across, edge = g.nx, g.ny, g.across, g.edge
     lane = lane_ids()
     for side, (out, x, inward, sign) in enumerate(((row_first, 0, 1, 1.0), (row_last, nx - 1, nx - 2, -1.0))):
@@ -264,7 +281,7 @@
             out[pl.ds(M_P + SUB * t, SUB), :] = water[pl.ds(own, SUB), :]
             out[pl.ds(M_U + SUB * t, SUB), :] = row_u(side, t) - sign * hb * water[pl.ds(inward * ny + SUB * t, SUB), :]
             if first:
-                out[pl.ds(ROW_CONST + SUB * t, SUB), :] = hb
+                out[pl.ds(M_CONST + SUB * t, SUB), :] = hb
         for tj in range(across):
             block = M_BRICK + SUB * tj
             for k, field in enumerate(ALONG_X + (VX, VY, VZ)):
@@ -282,7 +299,7 @@
                 col_u(side, t) - sign * hb * water[pl.ds(SUB * t * ny + inward, SUB, stride=ny), :]
             )
             if first:
-                out[pl.ds(COL_CONST + SUB * t, SUB), :] = hb
+                out[pl.ds(M_CONST + SUB * t, SUB), :] = hb
             rows = pl.ds(SUB * t, SUB)
             pieces = [bricks[field * across + tj, rows, :] for field in ALONG_Y + (VX, VY, VZ)]
             pieces.append(params[HB * across + tj, rows, :])
@@ -297,12 +314,18 @@
                 moved = roll(value, edge * (k - y % g.yper))
                 packed = moved if packed is None else jnp.where(lane >= edge * k, moved, packed)
             out[pl.ds(M_BRICK + SUB * t, SUB), :] = packed
+            if t == 0:
+                corner = packed
+        out[pl.ds(M_CORNER, SUB), :] = jnp.where(row_odd, packed, corner)
+        out[pl.ds(M_CORNER + SUB, SUB), :] = jnp.where(row_odd, corner, packed)
+    route(row_odd, row_first, row_last, *sends[:2])
+    route(col_odd, col_first, col_last, *sends[2:])
 
 
 def first_kernel(
-    g, live_hbm, table_hbm, water_hbm, material_hbm, motion_hbm, kinds_hbm,
-    water_out, bricks_out, params, columns, row_first, row_last, col_first, col_last,
-    stress, pressure, ux_edge, uy_edge, material_x, material_y, motion, kinds, live, table, sems,
+    g, live_hbm, table_hbm, water_hbm, material_hbm, motion_hbm, kinds_hbm, odd,
+    water_out, bricks_out, params, columns, row_far, row_near, col_far, col_near,
+    stress, pressure, ux_edge, uy_edge, material_x, material_y, motion, kinds, live, table, sems, *buffers,
 ):
     nx, ny, across = g.nx, g.ny, g.across
     copies = []
@@ -383,7 +406,7 @@
         lambda side, t: uy_edge[(*rows_of(side, t), slice(None))],
         lambda side, t: pick(columns[0], material_y[(*rows_of(side, t), slice(None))]),
     )
-    pack(g, water_out, bricks_out, params, edges, row_first, row_last, col_first, col_last, True)
+    pack(g, water_out, bricks_out, params, edges, odd, buffers, (row_far, row_near, col_far, col_near), True)
 
 
 def first_water_kernel(
@@ -456,7 +479,7 @@
 
 def inner_kernel(g, first, last, *refs):
     refs = Refs(refs)
-    water, bricks, memory, params, hb_water, hk_water, col_before, col_after = refs.take(8)
+    water, bricks, memory, params, hb_water, hk_water, odd, col_far, col_near = refs.take(9)
     if not first:
         (const_in,) = refs.take(1)
     uy, speed = refs.take(2)
@@ -466,8 +489,10 @@
         water_out, press, stress, bricks_out, memory_out = refs.take(5)
     if first:
         (const_out,) = refs.take(1)
+    col_before, col_after = refs.take(2)
     if last:
         press_buf, uy_buf, motion_buf, memory_buf, sems = refs.take(5)
+    unroute(odd[1] > 0.0, col_far, col_near, col_before, col_after)
 
     nx, ny, edge, across, plane = g.nx, g.ny, g.edge, g.across, g.plane
     wide = across + 2
@@ -505,7 +530,7 @@
             here = pl.ds(SUB * t * py + PAD + y, SUB, stride=py)
             place = pl.ds(32 * side + SUB * t, SUB)
             if first:
-                theirs = ref[pl.ds(COL_CONST + SUB * t, SUB), :]
+                theirs = ref[pl.ds(M_CONST + SUB * t, SUB), :]
                 const_out[place, :] = theirs
             else:
                 theirs = const_in[place, :]
@@ -607,7 +632,7 @@
 
 def edge_kernel(g, first, last, *refs):
     refs = Refs(refs)
-    water, bricks, memory, params, hb_water, hk_water, col_before, col_after, row_before, row_after = refs.take(10)
+    water, bricks, memory, params, hb_water, hk_water, odd, col_far, col_near, row_far, row_near = refs.take(11)
     if not first:
         (const_in,) = refs.take(1)
     (uy,) = refs.take(1)
@@ -621,8 +646,17 @@
     (ux,) = refs.take(1)
     if first:
         (const_out,) = refs.take(1)
+    col_before, col_after, row_before, row_after = refs.take(4)
     if last:
         press_buf, motion_buf, memory_buf, sems = refs.take(4)
+    else:
+        buffers = refs.take(4)
+    unroute(odd[1] > 0.0, col_far, col_near, col_before, col_after)
+    unroute(odd[0] > 0.0, row_far, row_near, row_before, row_after)
+    for ref in (row_before, row_after):
+        far, near = ref[pl.ds(M_CORNER, SUB), :], ref[pl.ds(M_CORNER + SUB, SUB), :]
+        ref[pl.ds(M_CORNER, SUB), :] = jnp.where(odd[1] > 0.0, near, far)
+        ref[pl.ds(M_CORNER + SUB, SUB), :] = jnp.where(odd[1] > 0.0, far, near)
 
     nx, ny, edge, across, plane = g.nx, g.ny, g.edge, g.across, g.plane
     wide = across + 2
@@ -648,7 +682,7 @@
             own = pl.ds(x * ny + SUB * t, SUB)
             place = pl.ds(32 * side + SUB * t, SUB)
             if first:
-                theirs = ref[pl.ds(ROW_CONST + SUB * t, SUB), :]
+                theirs = ref[pl.ds(M_CONST + SUB * t, SUB), :]
                 const_out[place, :] = theirs
             else:
                 theirs = const_in[place, :]
@@ -743,28 +777,26 @@
             lambda side, t: hb_water[column(side, t), :],
         )
         brick_velocity(g, water_out, stress, load_v, bricks_out, load_hb)
-        pack(g, water_out, bricks_out, params, faces, *sends, False)
-
-
-def shift(value, axis, up):
-    count = lax.axis_size(axis)
-    pairs = [(i, i + 1) for i in range(count - 1)]
-    return lax.ppermute(value, axis, pairs if up else [(j, i) for i, j in pairs])
-
-
-def exchange(g, sends):
-    row_first, row_last, col_first, col_last = sends
-    col_before = shift(col_last, "col", True)
-    col_after = shift(col_first, "col", False)
+        pack(g, water_out, bricks_out, params, faces, odd, buffers, sends, False)
+
+
+def swap(value, axis, start):
+    pairs = [(i, i + 1) for i in range(start, lax.axis_size(axis) - 1, 2)]
+    return lax.ppermute(value, axis, pairs + [(j, i) for i, j in pairs])
+
+
+def exchange(sends):
+    row_far, row_near, col_far, col_near = sends
+    col_far = swap(col_far, "col", 1)
+    col_near = swap(col_near, "col", 0)
 
     def with_corners(message, start):
-        start += M_BRICK
-        corners = jnp.concatenate([col_before[start : start + SUB], col_after[start : start + SUB]])
+        corners = jnp.concatenate([col_far[start : start + SUB], col_near[start : start + SUB]])
         return lax.dynamic_update_slice(message, corners, (M_CORNER, 0))
 
-    row_before = shift(with_corners(row_last, g.nx - SUB), "row", True)
-    row_after = shift(with_corners(row_first, 0), "row", False)
-    return col_before, col_after, row_before, row_after
+    row_far = swap(with_corners(row_far, M_CORNER), "row", 1)
+    row_near = swap(with_corners(row_near, M_CORNER + SUB), "row", 0)
+    return col_far, col_near, row_far, row_near
 
 
 def body(
@@ -787,8 +819,7 @@
     hbm = pl.BlockSpec(memory_space=pltpu.HBM)
     params = pltpu.CompilerParams(vmem_limit_bytes=24 * 1024 * 1024)
     def messages(first):
-        extra = 32 if first else 0
-        return [f32(112 + extra, LANES)] * 2 + [f32(96 + extra, LANES)] * 2
+        return [f32(M_CONST + (32 if first else 0), LANES)] * 4
 
     def buffer(*shape):
         return pltpu.VMEM(shape, jnp.float32)
@@ -799,6 +830,11 @@
     def pinned(*values):
         return [pltpu.with_memory_space_constraint(value, pltpu.HBM) for value in values]
 
+    def message_buffers(count, first):
+        return [buffer(M_CONST + (32 if first else 0), LANES)] * count
+
+    odd = jnp.stack([lax.axis_index(axis) & 1 for axis in ("row", "col")]).astype(jnp.float32)
+    odd = jnp.broadcast_to(odd[:, None, None], (2, SUB, LANES))
     press = buffer(nx + 2, ny + 2 * PAD, nz)
     stress = buffer(6 * across, nx + 2 * PAD, LANES)
     work = pl.CostEstimate(flops=20_000_000, bytes_accessed=8_000_000, transcendentals=0)
@@ -807,7 +843,7 @@
         out_shape=[
             buffer(4 * plane, nz), f32(9 * across, nx, LANES), f32(9 * across, nx, LANES), f32(8, SUB, LANES),
         ] + messages(True),
-        in_specs=[hbm] * 6,
+        in_specs=[hbm] * 6 + [vmem],
         out_specs=[vmem] * 8,
         scratch_shapes=[
             stress,
@@ -821,10 +857,11 @@
             pltpu.SMEM(brick_live.shape, jnp.int32),
             pltpu.SMEM(material_table.shape, jnp.float32),
             pltpu.SemaphoreType.DMA((13,)),
-        ],
+        ]
+        + message_buffers(4, True),
         compiler_params=params,
         name="first_bricks",
-    )(*pinned(brick_live, material_table, water_state, water_material, brick_velocity_stress, brick_cell_material))
+    )(*pinned(brick_live, material_table, water_state, water_material, brick_velocity_stress, brick_cell_material), odd)
 
     def passed(*messages):
         return [buffer(*message.shape) for message in messages]
@@ -859,16 +896,17 @@
     ]
     for step in range(STEPS):
         first, last = step == 0, step == STEPS - 1
-        *columns, row_before, row_after = exchange(g, sends)
-        state = (water, bricks, memory, coefficients, hb_water, hk_water)
+        *columns, row_far, row_near = exchange(sends)
+        state = (water, bricks, memory, coefficients, hb_water, hk_water, odd)
         shapes = finals if last else planes
         spaces = [hbm if last else vmem] * len(shapes)
         inner = pl.pallas_call(
             functools.partial(inner_kernel, g, first, last),
             out_shape=[buffer(*uy_shape), buffer(*speed_shape)] + shapes + ([buffer(64, LANES)] if first else []),
-            in_specs=[vmem] * (8 + len(col_const)),
+            in_specs=[vmem] * (9 + len(col_const)),
             out_specs=[vmem] * 2 + spaces + ([vmem] if first else []),
-            scratch_shapes=[buffer(plane, nz), buffer(plane, nz)] + slot_buffers + [pltpu.SemaphoreType.DMA((8,))] if last else [],
+            scratch_shapes=message_buffers(2, first)
+            + ([buffer(plane, nz), buffer(plane, nz)] + slot_buffers + [pltpu.SemaphoreType.DMA((8,))] if last else []),
             compiler_params=params,
             cost_estimate=work,
             name="inner",
@@ -877,7 +915,7 @@
             col_const = (inner[-1],)
             inner = inner[:-1]
         uy, *partial = inner
-        count = 10 + len(row_const) + 1
+        count = 11 + len(row_const) + 1
         results = pl.pallas_call(
             functools.partial(edge_kernel, g, first, last),
             out_shape=[buffer(*speed_shape)]
@@ -887,10 +925,16 @@
             in_specs=[vmem] * (count + 1) + spaces,
             out_specs=[vmem] + spaces + [vmem] * (0 if last else 5) + ([vmem] if first else []),
             input_output_aliases={count + k: k for k in range(1 + len(shapes))},
-            scratch_shapes=[ux_buffer, buffer(4 * ny, nz)] + slot_buffers + [pltpu.SemaphoreType.DMA((8,))] if last else [],
+            scratch_shapes=([ux_buffer] if last else [])
+            + message_buffers(4, first)
+            + (
+                [buffer(4 * ny, nz)] + slot_buffers + [pltpu.SemaphoreType.DMA((8,))]
+                if last
+                else message_buffers(4, False)
+            ),
             compiler_params=params,
             name="edges",
-        )(*held(*state), *columns, row_before, row_after, *row_const, *held(uy), *(held(partial[0]) + (list(partial[1:]) if last else held(*partial[1:]))))
+        )(*held(*state), *columns, row_far, row_near, *row_const, *held(uy), *(held(partial[0]) + (list(partial[1:]) if last else held(*partial[1:]))))
         if last:
             return results[2], results[3], results[1].reshape(water_state.shape)
         old_water = water

time: 64.5 us -> 51.4 us (0.80)
  the two profiles are of different devices: /device:TPU:5 before, /device:TPU:10 now
where the time goes in v5:
time: 51.4 us; the launch traced here: 51.2 us
  Pallas kernels  23.4 us (46%)
  starting transfers between devices  16.8 us (33%)
  waiting for transfers between devices  9.95 us (19%)
  between operations  0.86 us (2%)
    ppermute x12, starting transfers between devices, swap(): return lax.ppermute(value, axis, pairs + [(j, i) for i, j in pairs])  16.8 us
    pallas_call x3, Pallas kernels, body(): pl.pallas_call(functools.partial(inner_kernel, g, first, last), out_shape...  10.2 us
    ppermute x12, waiting for transfers between devices, swap(): return lax.ppermute(value, axis, pairs + [(j, i) for i, j in pairs])  9.95 us
    pallas_call x3, Pallas kernels, body(): pl.pallas_call(functools.partial(edge_kernel, g, first, last), out_shape=...  5.27 us
    pallas_call x1, Pallas kernels, body(): pl.pallas_call(functools.partial(first_water_kernel, g), out_shape=[buffe...  3.43 us
    pallas_call x1, Pallas kernels, body(): pl.pallas_call(functools.partial(first_kernel, g), out_shape=[buffer(4 *...  2.8 us
    pallas_call x2, Pallas kernels, body(): pl.pallas_call(functools.partial(edge_water_kernel, g), out_shape=[buffer...  1.7 us
  transfers between devices with their start and end apart: 12, of which 6 were waited for; matrix products, arithmetic and copies ran while one was open for 0% of the time, Pallas kernels for 30%

profile of v5, /device:TPU:10, one launch (start us, length us, event | category | flops | bytes accessed | tf_op | source)
XLA Modules:
  0.0 51.2 jit_solution(8081690672503856375)
XLA Ops:
  0.6 0.0 copy-start.2
  0.6 0.0 copy-start
  0.7 0.1 add_convert_fusion
  0.7 0.1 broadcast_in_dim.2.odd.refs_6_
  0.8 2.8 %first_bricks.1 = (f32[4096,128]{1,0:T(8,128)S(1)}, f32[36,32,128]{2,1,0:T(8,128)S(1)}, f32[36,32,128]{2,1,0:T(8,128)S(1)}, f32[8,8,128]{2,1,0:T(8,128)S(1)}, f3...) custom-call(s32[4]{0:T(128)} %live_hbm.1, f32[8,8]{1,0:T(8,128)} %table_hbm.1, ...), custom_call_target="tpu_custom_call" | custom-call | tf_op jit(solution)/shard_map/first_bricks/pallas_call | solution.py:841
  3.6 1.9 %collective-permute-start = (f32[144,128]{1,0:T(8,128)S(1)}, f32[144,128]{1,0:T(8,128)S(1)}, u32[]{:S(2)}, u32[]{:S(2)}) collective-permute-start(f32[144,128]{1,0:T(8,128)S(1)} %get-tuple-element.75), channel_id=1, source_target_pairs={{1,2},{2,1},{5,6},{6,5},{9,10},{10,9},{13,14},{14,13},{17,18},{18,... | collective-permute-start | bytes 221192 | tf_op jit(solution)/shard_map/ppermute | solution.py:785
  5.5 0.1 collective-permute-start.1
  5.6 0.0 copy-done.2
  5.6 0.0 copy-done
  5.6 0.0 copy-start.1
  5.7 3.4 %first_water.1 = (f32[4096,128]{1,0:T(8,128)S(1)}, f32[144,128]{1,0:T(8,128)S(1)}, f32[144,128]{1,0:T(8,128)S(1)}, f32[1024,128]{1,0:T(8,128)S(1)}, f32[1024,128]{1,0:T(8,128)S(1)}) custom-call(f32[4096,128]{1,0:T(8,128)S(1)} %get-tuple-element.66.pressure, ...), custom_call_target="tpu_custom_call", output_to_operand_aliasing={{0}: (0, {}), {1}: (1, {}), {2}: (2, {})} | custom-call | flops 20000000 | bytes 8000000 | tf_op jit(solution)/shard_map/first_water/pallas_call | solution.py:869
  9.1 0.2 collective-permute-done.refs_7_
  9.3 0.0 collective-permute-done.1.refs_8_
  9.3 1.6 %collective-permute-start.3 = (f32[144,128]{1,0:T(8,128)S(1)}, f32[144,128]{1,0:T(8,128)S(1)}, u32[]{:S(2)}, u32[]{:S(2)}) collective-permute-start(f32[144,128]{1,0:T(8,128)S(1)} %maximum_dynamic-update-slice_fusion.1), channel_id=1, source_target_pairs={{0,4},{8,12},{16,20},{24,28},{4,0},{12,8},{20,16},{28,24},{1,5},{9... | collective-permute-start | bytes 221192 | tf_op jit(solution)/shard_map/ppermute | solution.py:785
  10.9 2.3 %collective-permute-start.2 = (f32[144,128]{1,0:T(8,128)S(1)}, f32[144,128]{1,0:T(8,128)S(1)}, u32[]{:S(2)}, u32[]{:S(2)}) collective-permute-start(f32[144,128]{1,0:T(8,128)S(1)} %maximum_dynamic-update-slice_fusion), channel_id=1, source_target_pairs={{4,8},{12,16},{20,24},{8,4},{16,12},{24,20},{5,9},{13,17},{21,25},... | collective-permute-start | bytes 221192 | tf_op jit(solution)/shard_map/ppermute | solution.py:785
  13.2 0.0 copy-done.1
  13.2 3.5 %inner.3 = (f32[1536,128]{1,0:T(8,128)S(1)}, f32[18,48,128]{2,1,0:T(8,128)S(1)}, f32[4096,128]{1,0:T(8,128)S(1)}, f32[34,48,128]{2,1,0:T(8,128)S(1)}, f32[24,48,...) custom-call(f32[4096,128]{1,0:T(8,128)S(1)} %get-tuple-element.71.refs_0_.wat, ...), custom_call_target="tpu_custom_call" | custom-call | flops 20000000 | bytes 8000000 | tf_op jit(solution)/shard_map/inner/pallas_call | solution.py:903
  16.7 0.0 collective-permute-done.3.refs_10_
  16.7 1.3 %collective-permute-done.2.refs_9_ = f32[144,128]{1,0:T(8,128)S(1)} collective-permute-done((f32[144,128]{1,0:T(8,128)S(1)}, f32[144,128]{1,0:T(8,128)S(1)}, u32[]{:S(2)}, u32[]{:S(2)}) %collective-permute-start.2) | collective-permute-done | bytes 73760 | tf_op jit(solution)/shard_map/ppermute | solution.py:785
  18.0 1.7 %edges.3 = (f32[18,48,128]{2,1,0:T(8,128)S(1)}, f32[4096,128]{1,0:T(8,128)S(1)}, f32[34,48,128]{2,1,0:T(8,128)S(1)}, f32[24,48,128]{2,1,0:T(8,128)S(1)}, f32[36,...) custom-call(f32[4096,128]{1,0:T(8,128)S(1)} %get-tuple-element.71.re, ...), custom_call_target="tpu_custom_call", output_to_operand_aliasing={{0}: (12, {}), {1}: (13, {}), {2}: (14, {}), {3}: (15, {}),... | custom-call | tf_op jit(solution)/shard_map/edges/pallas_call | solution.py:919
  19.8 2.1 %collective-permute-start.4 = (f32[112,128]{1,0:T(8,128)S(1)}, f32[112,128]{1,0:T(8,128)S(1)}, u32[]{:S(2)}, u32[]{:S(2)}) collective-permute-start(f32[112,128]{1,0:T(8,128)S(1)} %get-tuple-element.95), channel_id=1, source_target_pairs={{1,2},{2,1},{5,6},{6,5},{9,10},{10,9},{13,14},{14,13},{17,18},{18,... | collective-permute-start | bytes 172040 | tf_op jit(solution)/shard_map/ppermute | solution.py:785
  21.8 0.1 collective-permute-start.5
  21.9 0.9 %edge_water.2 = (f32[4096,128]{1,0:T(8,128)S(1)}, f32[112,128]{1,0:T(8,128)S(1)}, f32[112,128]{1,0:T(8,128)S(1)}) custom-call(f32[4096,128]{1,0:T(8,128)S(1)} %get-tuple-element.86.same, f32[112,128]{1,0:T(8,128)S(1)} %get-tuple-element.87.row_first, ...), custom_call_target="tpu_custom_call", output_to_operand_aliasing={{0}: (0, {}), {1}: (1, {}), {2}: (2, {})} | custom-call | flops 20000000 | bytes 8000000 | tf_op jit(solution)/shard_map/edge_water/pallas_call | solution.py:945
  22.8 2.5 %collective-permute-done.4.refs_7_ = f32[112,128]{1,0:T(8,128)S(1)} collective-permute-done((f32[112,128]{1,0:T(8,128)S(1)}, f32[112,128]{1,0:T(8,128)S(1)}, u32[]{:S(2)}, u32[]{:S(2)}) %collective-permute-start.4) | collective-permute-done | bytes 57376 | tf_op jit(solution)/shard_map/ppermute | solution.py:785
  25.3 0.0 collective-permute-done.5.refs_8_
  25.3 1.4 %collective-permute-start.7 = (f32[112,128]{1,0:T(8,128)S(1)}, f32[112,128]{1,0:T(8,128)S(1)}, u32[]{:S(2)}, u32[]{:S(2)}) collective-permute-start(f32[112,128]{1,0:T(8,128)S(1)} %maximum_dynamic-update-slice_fusion.3), channel_id=1, source_target_pairs={{0,4},{8,12},{16,20},{24,28},{4,0},{12,8},{20,16},{28,24},{1,5},{9... | collective-permute-start | bytes 172040 | tf_op jit(solution)/shard_map/ppermute | solution.py:785
  26.7 1.9 %collective-permute-start.6 = (f32[112,128]{1,0:T(8,128)S(1)}, f32[112,128]{1,0:T(8,128)S(1)}, u32[]{:S(2)}, u32[]{:S(2)}) collective-permute-start(f32[112,128]{1,0:T(8,128)S(1)} %maximum_dynamic-update-slice_fusion.2), channel_id=1, source_target_pairs={{4,8},{12,16},{20,24},{8,4},{16,12},{24,20},{5,9},{13,17},{21,25},... | collective-permute-start | bytes 172040 | tf_op jit(solution)/shard_map/ppermute | solution.py:785
  28.6 3.5 %inner.4 = (f32[1536,128]{1,0:T(8,128)S(1)}, f32[18,48,128]{2,1,0:T(8,128)S(1)}, f32[4096,128]{1,0:T(8,128)S(1)}, f32[34,48,128]{2,1,0:T(8,128)S(1)}, f32[24,48,...) custom-call(f32[4096,128]{1,0:T(8,128)S(1)} %get-tuple-element.92.refs_0_.water, ...), custom_call_target="tpu_custom_call" | custom-call | flops 20000000 | bytes 8000000 | tf_op jit(solution)/shard_map/inner/pallas_call | solution.py:903
  32.1 0.0 collective-permute-done.7.refs_10_
  32.1 1.6 %collective-permute-done.6.refs_9_ = f32[112,128]{1,0:T(8,128)S(1)} collective-permute-done((f32[112,128]{1,0:T(8,128)S(1)}, f32[112,128]{1,0:T(8,128)S(1)}, u32[]{:S(2)}, u32[]{:S(2)}) %collective-permute-start.6) | collective-permute-done | bytes 57376 | tf_op jit(solution)/shard_map/ppermute | solution.py:785
  33.6 1.7 %edges.4 = (f32[18,48,128]{2,1,0:T(8,128)S(1)}, f32[4096,128]{1,0:T(8,128)S(1)}, f32[34,48,128]{2,1,0:T(8,128)S(1)}, f32[24,48,128]{2,1,0:T(8,128)S(1)}, f32[36,...) custom-call(f32[4096,128]{1,0:T(8,128)S(1)} %get-tuple-element.92.re, ...), custom_call_target="tpu_custom_call", output_to_operand_aliasing={{0}: (13, {}), {1}: (14, {}), {2}: (15, {}), {3}: (16, {}),... | custom-call | tf_op jit(solution)/shard_map/edges/pallas_call | solution.py:919
  35.4 1.9 %collective-permute-start.8 = (f32[112,128]{1,0:T(8,128)S(1)}, f32[112,128]{1,0:T(8,128)S(1)}, u32[]{:S(2)}, u32[]{:S(2)}) collective-permute-start(f32[112,128]{1,0:T(8,128)S(1)} %get-tuple-element.117), channel_id=1, source_target_pairs={{1,2},{2,1},{5,6},{6,5},{9,10},{10,9},{13,14},{14,13},{17,18},{18,... | collective-permute-start | bytes 172040 | tf_op jit(solution)/shard_map/ppermute | solution.py:785
  37.3 0.1 collective-permute-start.9
  37.4 0.9 %edge_water.3 = (f32[4096,128]{1,0:T(8,128)S(1)}, f32[112,128]{1,0:T(8,128)S(1)}, f32[112,128]{1,0:T(8,128)S(1)}) custom-call(f32[4096,128]{1,0:T(8,128)S(1)} %get-tuple-element.108.same, f32[112,128]{1,0:T(8,128)S(1)} %get-tuple-element.109.row_first, ...), custom_call_target="tpu_custom_call", output_to_operand_aliasing={{0}: (0, {}), {1}: (1, {}), {2}: (2, {})} | custom-call | flops 20000000 | bytes 8000000 | tf_op jit(solution)/shard_map/edge_water/pallas_call | solution.py:945
  38.3 2.6 %collective-permute-done.8.refs_7_ = f32[112,128]{1,0:T(8,128)S(1)} collective-permute-done((f32[112,128]{1,0:T(8,128)S(1)}, f32[112,128]{1,0:T(8,128)S(1)}, u32[]{:S(2)}, u32[]{:S(2)}) %collective-permute-start.8) | collective-permute-done | bytes 57376 | tf_op jit(solution)/shard_map/ppermute | solution.py:785
  40.9 0.0 collective-permute-done.9.refs_8_
  40.9 1.6 %collective-permute-start.11 = (f32[112,128]{1,0:T(8,128)S(1)}, f32[112,128]{1,0:T(8,128)S(1)}, u32[]{:S(2)}, u32[]{:S(2)}) collective-permute-start(f32[112,128]{1,0:T(8,128)S(1)} %maximum_dynamic-update-slice_fusion.5), channel_id=1, source_target_pairs={{0,4},{8,12},{16,20},{24,28},{4,0},{12,8},{20,16},{28,24},{1,5},{9... | collective-permute-start | bytes 172040 | tf_op jit(solution)/shard_map/ppermute | solution.py:785
  42.5 1.9 %collective-permute-start.10 = (f32[112,128]{1,0:T(8,128)S(1)}, f32[112,128]{1,0:T(8,128)S(1)}, u32[]{:S(2)}, u32[]{:S(2)}) collective-permute-start(f32[112,128]{1,0:T(8,128)S(1)} %maximum_dynamic-update-slice_fusion.4), channel_id=1, source_target_pairs={{4,8},{12,16},{20,24},{8,4},{16,12},{24,20},{5,9},{13,17},{21,25},... | collective-permute-start | bytes 172040 | tf_op jit(solution)/shard_map/ppermute | solution.py:785
  44.4 3.3 %inner.5 = (f32[1536,128]{1,0:T(8,128)S(1)}, f32[18,48,128]{2,1,0:T(8,128)S(1)}, f32[4096,128]{1,0:T(8,128)}, f32[4,9,16,256]{3,2,1,0:T(8,128)}, f32[4,18,16,256]{3,2,1,0:T(8,128)}) custom-call(f32[4096,128]{1,0:T(8,128)S(1)} %get-tuple-element.114.refs_0_, f32[36,32,128]{2,1,0:T(8,128)S(1)} %get-tuple-element.115.refs_1_, ...), custom_call_target="tpu_custom_call" | custom-call | flops 20000000 | bytes 8000000 | tf_op jit(solution)/shard_map/inner/pallas_call | solution.py:903
  47.7 0.0 collective-permute-done.11.refs_10_
  47.7 1.7 %collective-permute-done.10.refs_9_ = f32[112,128]{1,0:T(8,128)S(1)} collective-permute-done((f32[112,128]{1,0:T(8,128)S(1)}, f32[112,128]{1,0:T(8,128)S(1)}, u32[]{:S(2)}, u32[]{:S(2)}) %collective-permute-start.10) | collective-permute-done | bytes 57376 | tf_op jit(solution)/shard_map/ppermute | solution.py:785
  49.4 1.8 %edges.5 = (f32[18,48,128]{2,1,0:T(8,128)S(1)}, f32[4096,128]{1,0:T(8,128)}, f32[4,9,16,256]{3,2,1,0:T(8,128)}, f32[4,18,16,256]{3,2,1,0:T(8,128)}) custom-call(f32[4096,128]{1,0:T(8,128)S(1)} %get-tuple-element.114.refs_0_, ...), custom_call_target="tpu_custom_call", output_to_operand_aliasing={{0}: (13, {}), {1}: (14, {}), {2}: (15, {}), {3}: (16, {})} | custom-call | tf_op jit(solution)/shard_map/edges/pallas_call | solution.py:919
  (12 shorter events, 0.0 us)
Async XLA Ops:
  0.6 5.0 %copy-start.2 = (s32[32,32,128]{2,1,0:T(8,128)S(1)}, s32[32,32,128]{2,1,0:T(8,128)}, u32[]{:S(2)}) copy-start(s32[32,32,128]{2,1,0:T(8,128)} %material.1) | copy-start | bytes 1572868
  0.6 5.0 %copy-start = (f32[4,32,32,128]{3,2,1,0:T(8,128)S(1)}, f32[4,32,32,128]{3,2,1,0:T(8,128)}, u32[]{:S(2)}) copy-start(f32[4,32,32,128]{3,2,1,0:T(8,128)} %state.1) | copy-start | bytes 6291460
  3.6 5.7 %collective-permute-start = (f32[144,128]{1,0:T(8,128)S(1)}, f32[144,128]{1,0:T(8,128)S(1)}, u32[]{:S(2)}, u32[]{:S(2)}) collective-permute-start(f32[144,128]{1,0:T(8,128)S(1)} %get-tuple-element.75), channel_id=1, source_target_pairs={{1,2},{2,1},{5,6},{6,5},{9,10},{10,9},{13,14},{14,13},{17,18},{18,... | collective-permute-start | bytes 221192 | tf_op jit(solution)/shard_map/ppermute | solution.py:785
  5.5 3.7 %collective-permute-start.1 = (f32[144,128]{1,0:T(8,128)S(1)}, f32[144,128]{1,0:T(8,128)S(1)}, u32[]{:S(2)}, u32[]{:S(2)}) collective-permute-start(f32[144,128]{1,0:T(8,128)S(1)} %get-tuple-element.76), channel_id=1, source_target_pairs={{0,1},{2,3},{1,0},{3,2},{4,5},{6,7},{5,4},{7,6},{8,9},{10,11},{9,8... | collective-permute-start | bytes 221192 | tf_op jit(solution)/shard_map/ppermute | solution.py:785
  5.6 7.5 %copy-start.1 = (f32[4,18,16,256]{3,2,1,0:T(8,128)S(1)}, f32[4,18,16,256]{3,2,1,0:T(8,128)}, u32[]{:S(2)}) copy-start(f32[4,18,16,256]{3,2,1,0:T(8,128)} %refs_2_.3) | copy-start | bytes 3538948
  9.3 7.4 %collective-permute-start.3 = (f32[144,128]{1,0:T(8,128)S(1)}, f32[144,128]{1,0:T(8,128)S(1)}, u32[]{:S(2)}, u32[]{:S(2)}) collective-permute-start(f32[144,128]{1,0:T(8,128)S(1)} %maximum_dynamic-update-slice_fusion.1), channel_id=1, source_target_pairs={{0,4},{8,12},{16,20},{24,28},{4,0},{12,8},{20,16},{28,24},{1,5},{9... | collective-permute-start | bytes 221192 | tf_op jit(solution)/shard_map/ppermute | solution.py:785
  10.9 7.1 %collective-permute-start.2 = (f32[144,128]{1,0:T(8,128)S(1)}, f32[144,128]{1,0:T(8,128)S(1)}, u32[]{:S(2)}, u32[]{:S(2)}) collective-permute-start(f32[144,128]{1,0:T(8,128)S(1)} %maximum_dynamic-update-slice_fusion), channel_id=1, source_target_pairs={{4,8},{12,16},{20,24},{8,4},{16,12},{24,20},{5,9},{13,17},{21,25},... | collective-permute-start | bytes 221192 | tf_op jit(solution)/shard_map/ppermute | solution.py:785
  19.8 5.5 %collective-permute-start.4 = (f32[112,128]{1,0:T(8,128)S(1)}, f32[112,128]{1,0:T(8,128)S(1)}, u32[]{:S(2)}, u32[]{:S(2)}) collective-permute-start(f32[112,128]{1,0:T(8,128)S(1)} %get-tuple-element.95), channel_id=1, source_target_pairs={{1,2},{2,1},{5,6},{6,5},{9,10},{10,9},{13,14},{14,13},{17,18},{18,... | collective-permute-start | bytes 172040 | tf_op jit(solution)/shard_map/ppermute | solution.py:785
  21.8 3.4 %collective-permute-start.5 = (f32[112,128]{1,0:T(8,128)S(1)}, f32[112,128]{1,0:T(8,128)S(1)}, u32[]{:S(2)}, u32[]{:S(2)}) collective-permute-start(f32[112,128]{1,0:T(8,128)S(1)} %get-tuple-element.96), channel_id=1, source_target_pairs={{0,1},{2,3},{1,0},{3,2},{4,5},{6,7},{5,4},{7,6},{8,9},{10,11},{9,8... | collective-permute-start | bytes 172040 | tf_op jit(solution)/shard_map/ppermute | solution.py:785
  25.3 6.8 %collective-permute-start.7 = (f32[112,128]{1,0:T(8,128)S(1)}, f32[112,128]{1,0:T(8,128)S(1)}, u32[]{:S(2)}, u32[]{:S(2)}) collective-permute-start(f32[112,128]{1,0:T(8,128)S(1)} %maximum_dynamic-update-slice_fusion.3), channel_id=1, source_target_pairs={{0,4},{8,12},{16,20},{24,28},{4,0},{12,8},{20,16},{28,24},{1,5},{9... | collective-permute-start | bytes 172040 | tf_op jit(solution)/shard_map/ppermute | solution.py:785
  26.7 7.0 %collective-permute-start.6 = (f32[112,128]{1,0:T(8,128)S(1)}, f32[112,128]{1,0:T(8,128)S(1)}, u32[]{:S(2)}, u32[]{:S(2)}) collective-permute-start(f32[112,128]{1,0:T(8,128)S(1)} %maximum_dynamic-update-slice_fusion.2), channel_id=1, source_target_pairs={{4,8},{12,16},{20,24},{8,4},{16,12},{24,20},{5,9},{13,17},{21,25},... | collective-permute-start | bytes 172040 | tf_op jit(solution)/shard_map/ppermute | solution.py:785
  35.4 5.5 %collective-permute-start.8 = (f32[112,128]{1,0:T(8,128)S(1)}, f32[112,128]{1,0:T(8,128)S(1)}, u32[]{:S(2)}, u32[]{:S(2)}) collective-permute-start(f32[112,128]{1,0:T(8,128)S(1)} %get-tuple-element.117), channel_id=1, source_target_pairs={{1,2},{2,1},{5,6},{6,5},{9,10},{10,9},{13,14},{14,13},{17,18},{18,... | collective-permute-start | bytes 172040 | tf_op jit(solution)/shard_map/ppermute | solution.py:785
  37.3 3.6 %collective-permute-start.9 = (f32[112,128]{1,0:T(8,128)S(1)}, f32[112,128]{1,0:T(8,128)S(1)}, u32[]{:S(2)}, u32[]{:S(2)}) collective-permute-start(f32[112,128]{1,0:T(8,128)S(1)} %get-tuple-element.118), channel_id=1, source_target_pairs={{0,1},{2,3},{1,0},{3,2},{4,5},{6,7},{5,4},{7,6},{8,9},{10,11},{9,8... | collective-permute-start | bytes 172040 | tf_op jit(solution)/shard_map/ppermute | solution.py:785
  40.9 6.8 %collective-permute-start.11 = (f32[112,128]{1,0:T(8,128)S(1)}, f32[112,128]{1,0:T(8,128)S(1)}, u32[]{:S(2)}, u32[]{:S(2)}) collective-permute-start(f32[112,128]{1,0:T(8,128)S(1)} %maximum_dynamic-update-slice_fusion.5), channel_id=1, source_target_pairs={{0,4},{8,12},{16,20},{24,28},{4,0},{12,8},{20,16},{28,24},{1,5},{9... | collective-permute-start | bytes 172040 | tf_op jit(solution)/shard_map/ppermute | solution.py:785
  42.5 7.0 %collective-permute-start.10 = (f32[112,128]{1,0:T(8,128)S(1)}, f32[112,128]{1,0:T(8,128)S(1)}, u32[]{:S(2)}, u32[]{:S(2)}) collective-permute-start(f32[112,128]{1,0:T(8,128)S(1)} %maximum_dynamic-update-slice_fusion.4), channel_id=1, source_target_pairs={{4,8},{12,16},{20,24},{8,4},{16,12},{24,20},{5,9},{13,17},{21,25},... | collective-permute-start | bytes 172040 | tf_op jit(solution)/shard_map/ppermute | solution.py:785

commit v6 on v5

--- a/solution.py
+++ b/solution.py
@@ -794,8 +794,11 @@
         corners = jnp.concatenate([col_far[start : start + SUB], col_near[start : start + SUB]])
         return lax.dynamic_update_slice(message, corners, (M_CORNER, 0))
 
-    row_far = swap(with_corners(row_far, M_CORNER), "row", 1)
-    row_near = swap(with_corners(row_near, M_CORNER + SUB), "row", 0)
+    row_far, row_near = lax.optimization_barrier(
+        (with_corners(row_far, M_CORNER), with_corners(row_near, M_CORNER + SUB))
+    )
+    row_far = swap(row_far, "row", 1)
+    row_near = swap(row_near, "row", 0)
     return col_far, col_near, row_far, row_near
 
 

time: 51.4 us -> 52.6 us (1.023)
  the two profiles are of different devices: /device:TPU:10 before, /device:TPU:1 now
where the time goes in v6:
time: 52.6 us; the launch traced here: 52.3 us
  starting transfers between devices  24.2 us (46%)
  Pallas kernels  23.5 us (45%)
  waiting for transfers between devices  3.48 us (7%)
  between operations  0.92 us (2%)
    ppermute x12, starting transfers between devices, swap(): return lax.ppermute(value, axis, pairs + [(j, i) for i, j in pairs])  24.2 us
    pallas_call x3, Pallas kernels, body(): pl.pallas_call(functools.partial(inner_kernel, g, first, last), out_shape...  10.2 us
    pallas_call x3, Pallas kernels, body(): pl.pallas_call(functools.partial(edge_kernel, g, first, last), out_shape=...  5.33 us
    ppermute x12, waiting for transfers between devices, swap(): return lax.ppermute(value, axis, pairs + [(j, i) for i, j in pairs])  3.48 us
    pallas_call x1, Pallas kernels, body(): pl.pallas_call(functools.partial(first_water_kernel, g), out_shape=[buffe...  3.43 us
    pallas_call x1, Pallas kernels, body(): pl.pallas_call(functools.partial(first_kernel, g), out_shape=[buffer(4 *...  2.8 us
    pallas_call x2, Pallas kernels, body(): pl.pallas_call(functools.partial(edge_water_kernel, g), out_shape=[buffer...  1.7 us
  transfers between devices with their start and end apart: 12, of which 2 were waited for; matrix products, arithmetic and copies ran while one was open for 0% of the time, Pallas kernels for 29%

profile of v6, /device:TPU:1, one launch (start us, length us, event | category | flops | bytes accessed | tf_op | source)
XLA Modules:
  0.0 52.3 jit_solution(471356653566099360)
XLA Ops:
  0.6 0.0 copy-start.2
  0.6 0.0 copy-start
  0.7 0.1 add_convert_fusion
  0.7 0.1 broadcast_in_dim.2.odd.refs_6_
  0.8 2.8 %first_bricks.1 = (f32[4096,128]{1,0:T(8,128)S(1)}, f32[36,32,128]{2,1,0:T(8,128)S(1)}, f32[36,32,128]{2,1,0:T(8,128)S(1)}, f32[8,8,128]{2,1,0:T(8,128)S(1)}, f3...) custom-call(s32[4]{0:T(128)} %live_hbm.1, f32[8,8]{1,0:T(8,128)} %table_hbm.1, ...), custom_call_target="tpu_custom_call" | custom-call | tf_op jit(solution)/shard_map/first_bricks/pallas_call | solution.py:844
  3.6 4.5 %collective-permute-start = (f32[144,128]{1,0:T(8,128)S(1)}, f32[144,128]{1,0:T(8,128)S(1)}, u32[]{:S(2)}, u32[]{:S(2)}) collective-permute-start(f32[144,128]{1,0:T(8,128)S(1)} %get-tuple-element.81), channel_id=1, source_target_pairs={{1,2},{2,1},{5,6},{6,5},{9,10},{10,9},{13,14},{14,13},{17,18},{18,... | collective-permute-start | bytes 221192 | tf_op jit(solution)/shard_map/ppermute | solution.py:785
  8.1 0.1 collective-permute-start.1
  8.2 0.0 copy-done.2
  8.2 0.0 copy-done
  8.2 0.0 copy-start.1
  8.2 3.4 %first_water.1 = (f32[4096,128]{1,0:T(8,128)S(1)}, f32[144,128]{1,0:T(8,128)S(1)}, f32[144,128]{1,0:T(8,128)S(1)}, f32[1024,128]{1,0:T(8,128)S(1)}, f32[1024,128]{1,0:T(8,128)S(1)}) custom-call(f32[4096,128]{1,0:T(8,128)S(1)} %get-tuple-element.72.pressure, ...), custom_call_target="tpu_custom_call", output_to_operand_aliasing={{0}: (0, {}), {1}: (1, {}), {2}: (2, {})} | custom-call | flops 20000000 | bytes 8000000 | tf_op jit(solution)/shard_map/first_water/pallas_call | solution.py:872
  11.7 0.0 collective-permute-done.refs_7_
  11.7 0.0 collective-permute-done.1.refs_8_
  11.7 0.7 %collective-permute-start.2 = (f32[144,128]{1,0:T(8,128)S(1)}, f32[144,128]{1,0:T(8,128)S(1)}, u32[]{:S(2)}, u32[]{:S(2)}) collective-permute-start(f32[144,128]{1,0:T(8,128)S(1)} %get-tuple-element.85), channel_id=1, source_target_pairs={{4,8},{12,16},{20,24},{8,4},{16,12},{24,20},{5,9},{13,17},{21,25},... | collective-permute-start | bytes 221192 | tf_op jit(solution)/shard_map/ppermute | solution.py:785
  12.4 3.8 %collective-permute-start.3 = (f32[144,128]{1,0:T(8,128)S(1)}, f32[144,128]{1,0:T(8,128)S(1)}, u32[]{:S(2)}, u32[]{:S(2)}) collective-permute-start(f32[144,128]{1,0:T(8,128)S(1)} %get-tuple-element.86), channel_id=1, source_target_pairs={{0,4},{8,12},{16,20},{24,28},{4,0},{12,8},{20,16},{28,24},{1,5},{9... | collective-permute-start | bytes 221192 | tf_op jit(solution)/shard_map/ppermute | solution.py:785
  16.2 0.0 copy-done.1
  16.2 3.5 %inner.3 = (f32[1536,128]{1,0:T(8,128)S(1)}, f32[18,48,128]{2,1,0:T(8,128)S(1)}, f32[4096,128]{1,0:T(8,128)S(1)}, f32[34,48,128]{2,1,0:T(8,128)S(1)}, f32[24,48,...) custom-call(f32[4096,128]{1,0:T(8,128)S(1)} %get-tuple-element.77.refs_0_.wat, ...), custom_call_target="tpu_custom_call" | custom-call | flops 20000000 | bytes 8000000 | tf_op jit(solution)/shard_map/inner/pallas_call | solution.py:906
  19.7 0.0 collective-permute-done.2.refs_9_
  19.7 0.0 collective-permute-done.3.refs_10_
  19.7 1.8 %edges.3 = (f32[18,48,128]{2,1,0:T(8,128)S(1)}, f32[4096,128]{1,0:T(8,128)S(1)}, f32[34,48,128]{2,1,0:T(8,128)S(1)}, f32[24,48,128]{2,1,0:T(8,128)S(1)}, f32[36,...) custom-call(f32[4096,128]{1,0:T(8,128)S(1)} %get-tuple-element.77.re, ...), custom_call_target="tpu_custom_call", output_to_operand_aliasing={{0}: (12, {}), {1}: (13, {}), {2}: (14, {}), {3}: (15, {}),... | custom-call | tf_op jit(solution)/shard_map/edges/pallas_call | solution.py:922
  21.5 2.6 %collective-permute-start.4 = (f32[112,128]{1,0:T(8,128)S(1)}, f32[112,128]{1,0:T(8,128)S(1)}, u32[]{:S(2)}, u32[]{:S(2)}) collective-permute-start(f32[112,128]{1,0:T(8,128)S(1)} %get-tuple-element.103), channel_id=1, source_target_pairs={{1,2},{2,1},{5,6},{6,5},{9,10},{10,9},{13,14},{14,13},{17,18},{18,... | collective-permute-start | bytes 172040 | tf_op jit(solution)/shard_map/ppermute | solution.py:785
  24.1 0.1 collective-permute-start.5
  24.2 0.9 %edge_water.2 = (f32[4096,128]{1,0:T(8,128)S(1)}, f32[112,128]{1,0:T(8,128)S(1)}, f32[112,128]{1,0:T(8,128)S(1)}) custom-call(f32[4096,128]{1,0:T(8,128)S(1)} %get-tuple-element.94.same, f32[112,128]{1,0:T(8,128)S(1)} %get-tuple-element.95.row_first, ...), custom_call_target="tpu_custom_call", output_to_operand_aliasing={{0}: (0, {}), {1}: (1, {}), {2}: (2, {})} | custom-call | flops 20000000 | bytes 8000000 | tf_op jit(solution)/shard_map/edge_water/pallas_call | solution.py:948
  25.0 1.9 %collective-permute-done.4.refs_7_ = f32[112,128]{1,0:T(8,128)S(1)} collective-permute-done((f32[112,128]{1,0:T(8,128)S(1)}, f32[112,128]{1,0:T(8,128)S(1)}, u32[]{:S(2)}, u32[]{:S(2)}) %collective-permute-start.4) | collective-permute-done | bytes 57376 | tf_op jit(solution)/shard_map/ppermute | solution.py:785
  27.0 0.0 collective-permute-done.5.refs_8_
  27.0 0.7 %collective-permute-start.6 = (f32[112,128]{1,0:T(8,128)S(1)}, f32[112,128]{1,0:T(8,128)S(1)}, u32[]{:S(2)}, u32[]{:S(2)}) collective-permute-start(f32[112,128]{1,0:T(8,128)S(1)} %maximum_dynamic-update-slice_fusion.2), channel_id=1, source_target_pairs={{4,8},{12,16},{20,24},{8,4},{16,12},{24,20},{5,9},{13,17},{21,25},... | collective-permute-start | bytes 172040 | tf_op jit(solution)/shard_map/ppermute | solution.py:785
  27.7 4.3 %collective-permute-start.7 = (f32[112,128]{1,0:T(8,128)S(1)}, f32[112,128]{1,0:T(8,128)S(1)}, u32[]{:S(2)}, u32[]{:S(2)}) collective-permute-start(f32[112,128]{1,0:T(8,128)S(1)} %maximum_dynamic-update-slice_fusion.3), channel_id=1, source_target_pairs={{0,4},{8,12},{16,20},{24,28},{4,0},{12,8},{20,16},{28,24},{1,5},{9... | collective-permute-start | bytes 172040 | tf_op jit(solution)/shard_map/ppermute | solution.py:785
  32.0 3.4 %inner.4 = (f32[1536,128]{1,0:T(8,128)S(1)}, f32[18,48,128]{2,1,0:T(8,128)S(1)}, f32[4096,128]{1,0:T(8,128)S(1)}, f32[34,48,128]{2,1,0:T(8,128)S(1)}, f32[24,48,...) custom-call(f32[4096,128]{1,0:T(8,128)S(1)} %get-tuple-element.100.refs_0_.water, ...), custom_call_target="tpu_custom_call" | custom-call | flops 20000000 | bytes 8000000 | tf_op jit(solution)/shard_map/inner/pallas_call | solution.py:906
  35.4 0.0 collective-permute-done.6.refs_9_
  35.4 0.0 collective-permute-done.7.refs_10_
  35.4 1.8 %edges.4 = (f32[18,48,128]{2,1,0:T(8,128)S(1)}, f32[4096,128]{1,0:T(8,128)S(1)}, f32[34,48,128]{2,1,0:T(8,128)S(1)}, f32[24,48,128]{2,1,0:T(8,128)S(1)}, f32[36,...) custom-call(f32[4096,128]{1,0:T(8,128)S(1)} %get-tuple-element.100.r, ...), custom_call_target="tpu_custom_call", output_to_operand_aliasing={{0}: (13, {}), {1}: (14, {}), {2}: (15, {}), {3}: (16, {}),... | custom-call | tf_op jit(solution)/shard_map/edges/pallas_call | solution.py:922
  37.2 3.0 %collective-permute-start.8 = (f32[112,128]{1,0:T(8,128)S(1)}, f32[112,128]{1,0:T(8,128)S(1)}, u32[]{:S(2)}, u32[]{:S(2)}) collective-permute-start(f32[112,128]{1,0:T(8,128)S(1)} %get-tuple-element.127), channel_id=1, source_target_pairs={{1,2},{2,1},{5,6},{6,5},{9,10},{10,9},{13,14},{14,13},{17,18},{18,... | collective-permute-start | bytes 172040 | tf_op jit(solution)/shard_map/ppermute | solution.py:785
  40.2 0.1 collective-permute-start.9
  40.3 0.9 %edge_water.3 = (f32[4096,128]{1,0:T(8,128)S(1)}, f32[112,128]{1,0:T(8,128)S(1)}, f32[112,128]{1,0:T(8,128)S(1)}) custom-call(f32[4096,128]{1,0:T(8,128)S(1)} %get-tuple-element.118.same, f32[112,128]{1,0:T(8,128)S(1)} %get-tuple-element.119.row_first, ...), custom_call_target="tpu_custom_call", output_to_operand_aliasing={{0}: (0, {}), {1}: (1, {}), {2}: (2, {})} | custom-call | flops 20000000 | bytes 8000000 | tf_op jit(solution)/shard_map/edge_water/pallas_call | solution.py:948
  41.2 1.5 %collective-permute-done.8.refs_7_ = f32[112,128]{1,0:T(8,128)S(1)} collective-permute-done((f32[112,128]{1,0:T(8,128)S(1)}, f32[112,128]{1,0:T(8,128)S(1)}, u32[]{:S(2)}, u32[]{:S(2)}) %collective-permute-start.8) | collective-permute-done | bytes 57376 | tf_op jit(solution)/shard_map/ppermute | solution.py:785
  42.7 0.0 collective-permute-done.9.refs_8_
  42.7 0.7 %collective-permute-start.10 = (f32[112,128]{1,0:T(8,128)S(1)}, f32[112,128]{1,0:T(8,128)S(1)}, u32[]{:S(2)}, u32[]{:S(2)}) collective-permute-start(f32[112,128]{1,0:T(8,128)S(1)} %maximum_dynamic-update-slice_fusion.4), channel_id=1, source_target_pairs={{4,8},{12,16},{20,24},{8,4},{16,12},{24,20},{5,9},{13,17},{21,25},... | collective-permute-start | bytes 172040 | tf_op jit(solution)/shard_map/ppermute | solution.py:785
  43.4 3.8 %collective-permute-start.11 = (f32[112,128]{1,0:T(8,128)S(1)}, f32[112,128]{1,0:T(8,128)S(1)}, u32[]{:S(2)}, u32[]{:S(2)}) collective-permute-start(f32[112,128]{1,0:T(8,128)S(1)} %maximum_dynamic-update-slice_fusion.5), channel_id=1, source_target_pairs={{0,4},{8,12},{16,20},{24,28},{4,0},{12,8},{20,16},{28,24},{1,5},{9... | collective-permute-start | bytes 172040 | tf_op jit(solution)/shard_map/ppermute | solution.py:785
  47.2 3.3 %inner.5 = (f32[1536,128]{1,0:T(8,128)S(1)}, f32[18,48,128]{2,1,0:T(8,128)S(1)}, f32[4096,128]{1,0:T(8,128)}, f32[4,9,16,256]{3,2,1,0:T(8,128)}, f32[4,18,16,256]{3,2,1,0:T(8,128)}) custom-call(f32[4096,128]{1,0:T(8,128)S(1)} %get-tuple-element.124.refs_0_, f32[36,32,128]{2,1,0:T(8,128)S(1)} %get-tuple-element.125.refs_1_, ...), custom_call_target="tpu_custom_call" | custom-call | flops 20000000 | bytes 8000000 | tf_op jit(solution)/shard_map/inner/pallas_call | solution.py:906
  50.5 0.0 collective-permute-done.10.refs_9_
  50.5 0.0 collective-permute-done.11.refs_10_
  50.5 1.8 %edges.5 = (f32[18,48,128]{2,1,0:T(8,128)S(1)}, f32[4096,128]{1,0:T(8,128)}, f32[4,9,16,256]{3,2,1,0:T(8,128)}, f32[4,18,16,256]{3,2,1,0:T(8,128)}) custom-call(f32[4096,128]{1,0:T(8,128)S(1)} %get-tuple-element.124.refs_0_, ...), custom_call_target="tpu_custom_call", output_to_operand_aliasing={{0}: (13, {}), {1}: (14, {}), {2}: (15, {}), {3}: (16, {})} | custom-call | tf_op jit(solution)/shard_map/edges/pallas_call | solution.py:922
  (11 shorter events, 0.0 us)
Async XLA Ops:
  0.6 7.6 %copy-start.2 = (s32[32,32,128]{2,1,0:T(8,128)S(1)}, s32[32,32,128]{2,1,0:T(8,128)}, u32[]{:S(2)}) copy-start(s32[32,32,128]{2,1,0:T(8,128)} %material.1) | copy-start | bytes 1572868
  0.6 7.6 %copy-start = (f32[4,32,32,128]{3,2,1,0:T(8,128)S(1)}, f32[4,32,32,128]{3,2,1,0:T(8,128)}, u32[]{:S(2)}) copy-start(f32[4,32,32,128]{3,2,1,0:T(8,128)} %state.1) | copy-start | bytes 6291460
  3.6 8.1 %collective-permute-start = (f32[144,128]{1,0:T(8,128)S(1)}, f32[144,128]{1,0:T(8,128)S(1)}, u32[]{:S(2)}, u32[]{:S(2)}) collective-permute-start(f32[144,128]{1,0:T(8,128)S(1)} %get-tuple-element.81), channel_id=1, source_target_pairs={{1,2},{2,1},{5,6},{6,5},{9,10},{10,9},{13,14},{14,13},{17,18},{18,... | collective-permute-start | bytes 221192 | tf_op jit(solution)/shard_map/ppermute | solution.py:785
  8.1 3.6 %collective-permute-start.1 = (f32[144,128]{1,0:T(8,128)S(1)}, f32[144,128]{1,0:T(8,128)S(1)}, u32[]{:S(2)}, u32[]{:S(2)}) collective-permute-start(f32[144,128]{1,0:T(8,128)S(1)} %get-tuple-element.82), channel_id=1, source_target_pairs={{0,1},{2,3},{1,0},{3,2},{4,5},{6,7},{5,4},{7,6},{8,9},{10,11},{9,8... | collective-permute-start | bytes 221192 | tf_op jit(solution)/shard_map/ppermute | solution.py:785
  8.2 8.0 %copy-start.1 = (f32[4,18,16,256]{3,2,1,0:T(8,128)S(1)}, f32[4,18,16,256]{3,2,1,0:T(8,128)}, u32[]{:S(2)}) copy-start(f32[4,18,16,256]{3,2,1,0:T(8,128)} %refs_2_.3) | copy-start | bytes 3538948
  11.7 7.9 %collective-permute-start.2 = (f32[144,128]{1,0:T(8,128)S(1)}, f32[144,128]{1,0:T(8,128)S(1)}, u32[]{:S(2)}, u32[]{:S(2)}) collective-permute-start(f32[144,128]{1,0:T(8,128)S(1)} %get-tuple-element.85), channel_id=1, source_target_pairs={{4,8},{12,16},{20,24},{8,4},{16,12},{24,20},{5,9},{13,17},{21,25},... | collective-permute-start | bytes 221192 | tf_op jit(solution)/shard_map/ppermute | solution.py:785
  12.4 7.3 %collective-permute-start.3 = (f32[144,128]{1,0:T(8,128)S(1)}, f32[144,128]{1,0:T(8,128)S(1)}, u32[]{:S(2)}, u32[]{:S(2)}) collective-permute-start(f32[144,128]{1,0:T(8,128)S(1)} %get-tuple-element.86), channel_id=1, source_target_pairs={{0,4},{8,12},{16,20},{24,28},{4,0},{12,8},{20,16},{28,24},{1,5},{9... | collective-permute-start | bytes 221192 | tf_op jit(solution)/shard_map/ppermute | solution.py:785
  21.5 5.5 %collective-permute-start.4 = (f32[112,128]{1,0:T(8,128)S(1)}, f32[112,128]{1,0:T(8,128)S(1)}, u32[]{:S(2)}, u32[]{:S(2)}) collective-permute-start(f32[112,128]{1,0:T(8,128)S(1)} %get-tuple-element.103), channel_id=1, source_target_pairs={{1,2},{2,1},{5,6},{6,5},{9,10},{10,9},{13,14},{14,13},{17,18},{18,... | collective-permute-start | bytes 172040 | tf_op jit(solution)/shard_map/ppermute | solution.py:785
  24.1 2.9 %collective-permute-start.5 = (f32[112,128]{1,0:T(8,128)S(1)}, f32[112,128]{1,0:T(8,128)S(1)}, u32[]{:S(2)}, u32[]{:S(2)}) collective-permute-start(f32[112,128]{1,0:T(8,128)S(1)} %get-tuple-element.104), channel_id=1, source_target_pairs={{0,1},{2,3},{1,0},{3,2},{4,5},{6,7},{5,4},{7,6},{8,9},{10,11},{9,8... | collective-permute-start | bytes 172040 | tf_op jit(solution)/shard_map/ppermute | solution.py:785
  27.0 8.4 %collective-permute-start.6 = (f32[112,128]{1,0:T(8,128)S(1)}, f32[112,128]{1,0:T(8,128)S(1)}, u32[]{:S(2)}, u32[]{:S(2)}) collective-permute-start(f32[112,128]{1,0:T(8,128)S(1)} %maximum_dynamic-update-slice_fusion.2), channel_id=1, source_target_pairs={{4,8},{12,16},{20,24},{8,4},{16,12},{24,20},{5,9},{13,17},{21,25},... | collective-permute-start | bytes 172040 | tf_op jit(solution)/shard_map/ppermute | solution.py:785
  27.7 7.8 %collective-permute-start.7 = (f32[112,128]{1,0:T(8,128)S(1)}, f32[112,128]{1,0:T(8,128)S(1)}, u32[]{:S(2)}, u32[]{:S(2)}) collective-permute-start(f32[112,128]{1,0:T(8,128)S(1)} %maximum_dynamic-update-slice_fusion.3), channel_id=1, source_target_pairs={{0,4},{8,12},{16,20},{24,28},{4,0},{12,8},{20,16},{28,24},{1,5},{9... | collective-permute-start | bytes 172040 | tf_op jit(solution)/shard_map/ppermute | solution.py:785
  37.2 5.5 %collective-permute-start.8 = (f32[112,128]{1,0:T(8,128)S(1)}, f32[112,128]{1,0:T(8,128)S(1)}, u32[]{:S(2)}, u32[]{:S(2)}) collective-permute-start(f32[112,128]{1,0:T(8,128)S(1)} %get-tuple-element.127), channel_id=1, source_target_pairs={{1,2},{2,1},{5,6},{6,5},{9,10},{10,9},{13,14},{14,13},{17,18},{18,... | collective-permute-start | bytes 172040 | tf_op jit(solution)/shard_map/ppermute | solution.py:785
  40.2 2.5 %collective-permute-start.9 = (f32[112,128]{1,0:T(8,128)S(1)}, f32[112,128]{1,0:T(8,128)S(1)}, u32[]{:S(2)}, u32[]{:S(2)}) collective-permute-start(f32[112,128]{1,0:T(8,128)S(1)} %get-tuple-element.128), channel_id=1, source_target_pairs={{0,1},{2,3},{1,0},{3,2},{4,5},{6,7},{5,4},{7,6},{8,9},{10,11},{9,8... | collective-permute-start | bytes 172040 | tf_op jit(solution)/shard_map/ppermute | solution.py:785
  42.7 7.8 %collective-permute-start.10 = (f32[112,128]{1,0:T(8,128)S(1)}, f32[112,128]{1,0:T(8,128)S(1)}, u32[]{:S(2)}, u32[]{:S(2)}) collective-permute-start(f32[112,128]{1,0:T(8,128)S(1)} %maximum_dynamic-update-slice_fusion.4), channel_id=1, source_target_pairs={{4,8},{12,16},{20,24},{8,4},{16,12},{24,20},{5,9},{13,17},{21,25},... | collective-permute-start | bytes 172040 | tf_op jit(solution)/shard_map/ppermute | solution.py:785
  43.4 7.1 %collective-permute-start.11 = (f32[112,128]{1,0:T(8,128)S(1)}, f32[112,128]{1,0:T(8,128)S(1)}, u32[]{:S(2)}, u32[]{:S(2)}) collective-permute-start(f32[112,128]{1,0:T(8,128)S(1)} %maximum_dynamic-update-slice_fusion.5), channel_id=1, source_target_pairs={{0,4},{8,12},{16,20},{24,28},{4,0},{12,8},{20,16},{28,24},{1,5},{9... | collective-permute-start | bytes 172040 | tf_op jit(solution)/shard_map/ppermute | solution.py:785

commit v7 on v5

--- a/solution.py
+++ b/solution.py
@@ -66,10 +66,12 @@
         press[0, pl.ds(PAD + SUB * t, SUB), :] = zero
         press[g.nx + 1, pl.ds(PAD + SUB * t, SUB), :] = zero
 
-    @pl.loop(1, g.nx + 1)
-    def _(x):
-        press[x, pl.ds(0, SUB), :] = zero
-        press[x, pl.ds(PAD + g.ny, SUB), :] = zero
+    @pl.loop(0, g.nx // SUB)
+    def _(turn):
+        for step in range(SUB):
+            x = SUB * turn + step + 1
+            press[x, pl.ds(0, SUB), :] = zero
+            press[x, pl.ds(PAD + g.ny, SUB), :] = zero
 
 
 def zero_stress_pads(g, stress):
@@ -260,8 +262,8 @@
         out_near[rows, :] = jnp.where(odd, one, other)
 
 
-def unroute(odd, from_far, from_near, before, after):
-    for start in range(0, from_far.shape[0], SUB):
+def unroute(odd, from_far, from_near, before, after, starts=None):
+    for start in starts or range(0, from_far.shape[0], SUB):
         rows = pl.ds(start, SUB)
         far, near = from_far[rows, :], from_near[rows, :]
         before[rows, :] = jnp.where(odd, near, far)
@@ -444,22 +446,32 @@
 ):
     nx, ny, plane = g.nx, g.ny, g.plane
 
-    def load_u(k, x, t):
-        if k == 1:
-            layer = x - (x // (nx - SUB)) * (nx - 2 * SUB) + 1
-            return ux[aligned(layer * ny + SUB * t), :]
-        if k == 2:
-            return uy[aligned(x * (ny + 2 * PAD) + PAD + SUB * t), :]
-        return water[aligned(3 * plane + x * ny + SUB * t), :]
-
-    water_velocity(
-        g,
-        (SUB, lambda turn: 2 * turn + (turn // (SUB // 2)) * (nx - 2 * SUB)),
-        water_out,
-        press,
-        lambda t, x: stress[(ZZ - XX) * g.across + t, pl.ds(PAD + x, 1), :],
-        lambda x, t: hb_water[aligned(x * ny + SUB * t), :],
-        load_u,
+    def water_layers(layers, ux_row):
+        def load_u(k, x, t):
+            if k == 1:
+                return ux_row(x, t)
+            if k == 2:
+                return uy[aligned(x * (ny + 2 * PAD) + PAD + SUB * t), :]
+            return water[aligned(3 * plane + x * ny + SUB * t), :]
+
+        water_velocity(
+            g,
+            layers,
+            water_out,
+            press,
+            lambda t, x: stress[(ZZ - XX) * g.across + t, pl.ds(PAD + x, 1), :],
+            lambda x, t: hb_water[aligned(x * ny + SUB * t), :],
+            load_u,
+        )
+
+    def near_face(x, t):
+        layer = x - (x // (nx - SUB)) * (nx - 2 * SUB) + 1
+        return ux[aligned(layer * ny + SUB * t), :]
+
+    water_layers((SUB, lambda turn: 2 * turn + (turn // (SUB // 2)) * (nx - 2 * SUB)), near_face)
+    water_layers(
+        ((nx - 2 * SUB) // 2, lambda turn: SUB + 2 * turn),
+        lambda x, t: water[aligned(plane + x * ny + SUB * t), :],
     )
 
 
@@ -499,7 +511,6 @@
     lane = lane_ids()
     top_pick = surface_pick() * edge + (edge - 1)
     py = ny + 2 * PAD
-    low, high = SUB, nx - SUB
     copies = []
 
     def send(source, target):
@@ -516,13 +527,17 @@
         zero_press_pads(g, press)
         zero_stress_pads(g, stress)
 
-    @pl.loop(0, nx)
-    def _(x):
-        for t in range(g.ytiles):
-            own = x * ny + SUB * t
-            uy[aligned(x * py + PAD + SUB * t), :] = water[aligned(2 * plane + own), :]
+    @pl.loop(0, nx // 4)
+    def _(turn):
+        results = []
+        for x in (4 * turn + step for step in range(4)):
+            for t in range(g.ytiles):
+                own = x * ny + SUB * t
+                results.append((own, x * py + PAD + SUB * t, water[aligned(2 * plane + own), :]))
+        for own, row, value in results:
+            uy[aligned(row), :] = value
             if last:
-                uy_buf[aligned(own), :] = water[aligned(2 * plane + own), :]
+                uy_buf[aligned(own), :] = value
 
     for side, (ref, y, halo, sign) in enumerate(((col_before, 0, -1, 1.0), (col_after, ny - 1, ny, -1.0))):
         for t in range(g.xtiles):
@@ -603,22 +618,6 @@
         send(press_buf.at[part(0, 2, nx - 2), :], water_hbm.at[part(0, 2, nx - 2), :])
         for copy in copies:
             copy.wait()
-    else:
-        def load_u(k, x, t):
-            if k == 2:
-                return uy[aligned(x * py + PAD + SUB * t), :]
-            return water[aligned(k * plane + x * ny + SUB * t), :]
-
-        layers = ((high - low) // 2, lambda turn: low + 2 * turn)
-        water_velocity(
-            g,
-            layers,
-            water_out,
-            press,
-            lambda t, x: stress[(ZZ - XX) * across + t, pl.ds(PAD + x, 1), :],
-            lambda x, t: hb_water[aligned(x * ny + SUB * t), :],
-            load_u,
-        )
 
 
 def water_stress(g, x, t, dx, water, uy, speed, hk_water, lane, top_pick):
@@ -651,7 +650,7 @@
         press_buf, motion_buf, memory_buf, sems = refs.take(4)
     else:
         buffers = refs.take(4)
-    unroute(odd[1] > 0.0, col_far, col_near, col_before, col_after)
+    unroute(odd[1] > 0.0, col_far, col_near, col_before, col_after, (M_BRICK, M_BRICK + g.nx - SUB))
     unroute(odd[0] > 0.0, row_far, row_near, row_before, row_after)
     for ref in (row_before, row_after):
         far, near = ref[pl.ds(M_CORNER, SUB), :], ref[pl.ds(M_CORNER + SUB, SUB), :]
@@ -693,16 +692,22 @@
         for layer, x in ((1, 0), (2 * SUB, nx - 1)):
             send(ux.at[pl.ds(layer * ny, ny), :], water_hbm.at[pl.ds(plane + x * ny, ny), :])
 
+    speed_rows = {}
+
+    def speed_row(key, x):
+        if (key, x) not in speed_rows:
+            speed_rows[key, x] = speed[key, pl.ds(PAD + x, 1), :]
+        return speed_rows[key, x]
+
     for ref, x, halo, sign, _, _ in sides:
         for tj in range(across):
             block = M_BRICK + SUB * tj
             own_hb = sign * params[HB * across + tj, pl.ds(x, 1), :]
             their_hb = sign * ref[pl.ds(block + 6, 1), :]
             for c in (VX, VY, VZ):
-                here = pl.ds(PAD + x, 1)
                 key = c * wide + 1 + tj
-                speed[key, here, :] = speed[key, here, :] - own_hb * ref[pl.ds(block + c, 1), :]
-                speed[key, pl.ds(PAD + halo, 1), :] = (
+                speed_rows[key, x] = speed_row(key, x) - own_hb * ref[pl.ds(block + c, 1), :]
+                speed_rows[key, halo] = (
                     ref[pl.ds(block + 3 + c, 1), :] + their_hb * bricks[ALONG_X[c] * across + tj, pl.ds(x, 1), :]
                 )
         edge_row = SUB - 1 if x == 0 else 0
@@ -718,10 +723,12 @@
             row_hb = jnp.where(inside, col_sign * ref[pl.ds(M_BRICK + SUB * tj + 6, 1), :], 0.0)
             col_hb = sign * roll_row(col_ref[pl.ds(M_BRICK + x, 1), :], far - 6 * edge)
             for c in (VX, VY, VZ):
-                key, here = c * wide + 1 + tj, pl.ds(PAD + halo, 1)
-                speed[key, here, :] = speed[key, here, :] - row_hb * across_y[c]
-                key, here = c * wide + col_halo, pl.ds(PAD + x, 1)
-                speed[key, here, :] = speed[key, here, :] - col_hb * across_x[c]
+                key = c * wide + 1 + tj
+                speed_rows[key, halo] = speed_row(key, halo) - row_hb * across_y[c]
+                key = c * wide + col_halo
+                speed_rows[key, x] = speed_row(key, x) - col_hb * across_x[c]
+    for (key, x), value in speed_rows.items():
+        speed[key, pl.ds(PAD + x, 1), :] = value
 
     store = store_slots(g, motion_buf, memory_buf) if last else store_planes(g, bricks_out, memory_out, stress)
 

time: 51.4 us -> 50.7 us (0.986)
  starting transfers between devices: 16.8 us -> 15.8 us
  waiting for transfers between devices: 9.95 us -> 10.9 us
  Pallas kernels: 23.4 us -> 22.6 us
    pallas_call x3, Pallas kernels: 10.2 us -> 7.95 us  [body(): pl.pallas_call(functools.partial(inner_kernel, g, first, last), out_shape...]
    pallas_call x2, Pallas kernels: 1.7 us -> 3.33 us  [body(): pl.pallas_call(functools.partial(edge_water_kernel, g), out_shape=[buffer...]
    ppermute x12, waiting for transfers between devices: 9.95 us -> 10.9 us  [swap(): return lax.ppermute(value, axis, pairs + [(j, i) for i, j in pairs])]
    ppermute x12, starting transfers between devices: 16.8 us -> 15.8 us  [swap(): return lax.ppermute(value, axis, pairs + [(j, i) for i, j in pairs])]
  transfers between devices with their start and end apart: 12 -> 12, of which waited for: 6 -> 6; matrix products, arithmetic and copies ran while one was open for 0% -> 0% of each run, Pallas kernels for 30% -> 29%
where the time goes in v7:
time: 50.7 us; the launch traced here: 50.4 us
  Pallas kernels  22.6 us (45%)
  starting transfers between devices  15.8 us (31%)
  waiting for transfers between devices  10.9 us (21%)
  between operations  0.86 us (2%)
    ppermute x12, starting transfers between devices, swap(): return lax.ppermute(value, axis, pairs + [(j, i) for i, j in pairs])  15.8 us
    ppermute x12, waiting for transfers between devices, swap(): return lax.ppermute(value, axis, pairs + [(j, i) for i, j in pairs])  10.9 us
    pallas_call x3, Pallas kernels, body(): pl.pallas_call(functools.partial(inner_kernel, g, first, last), out_shape...  7.95 us
    pallas_call x3, Pallas kernels, body(): pl.pallas_call(functools.partial(edge_kernel, g, first, last), out_shape=...  5.27 us
    pallas_call x2, Pallas kernels, body(): pl.pallas_call(functools.partial(edge_water_kernel, g), out_shape=[buffer...  3.33 us
    pallas_call x1, Pallas kernels, body(): pl.pallas_call(functools.partial(first_water_kernel, g), out_shape=[buffe...  3.27 us
    pallas_call x1, Pallas kernels, body(): pl.pallas_call(functools.partial(first_kernel, g), out_shape=[buffer(4 *...  2.8 us
  transfers between devices with their start and end apart: 12, of which 6 were waited for; matrix products, arithmetic and copies ran while one was open for 0% of the time, Pallas kernels for 29%

profile of v7, /device:TPU:10, one launch (start us, length us, event | category | flops | bytes accessed | tf_op | source)
XLA Modules:
  0.0 50.4 jit_solution(2809102163768544060)
XLA Ops:
  0.6 0.0 copy-start.2
  0.6 0.0 copy-start
  0.7 0.1 add_convert_fusion
  0.7 0.1 broadcast_in_dim.2.odd.refs_6_
  0.8 2.8 %first_bricks.1 = (f32[4096,128]{1,0:T(8,128)S(1)}, f32[36,32,128]{2,1,0:T(8,128)S(1)}, f32[36,32,128]{2,1,0:T(8,128)S(1)}, f32[8,8,128]{2,1,0:T(8,128)S(1)}, f3...) custom-call(s32[4]{0:T(128)} %live_hbm.1, f32[8,8]{1,0:T(8,128)} %table_hbm.1, ...), custom_call_target="tpu_custom_call" | custom-call | tf_op jit(solution)/shard_map/first_bricks/pallas_call | solution.py:848
  3.6 1.9 %collective-permute-start = (f32[144,128]{1,0:T(8,128)S(1)}, f32[144,128]{1,0:T(8,128)S(1)}, u32[]{:S(2)}, u32[]{:S(2)}) collective-permute-start(f32[144,128]{1,0:T(8,128)S(1)} %get-tuple-element.75), channel_id=1, source_target_pairs={{1,2},{2,1},{5,6},{6,5},{9,10},{10,9},{13,14},{14,13},{17,18},{18,... | collective-permute-start | bytes 221192 | tf_op jit(solution)/shard_map/ppermute | solution.py:792
  5.5 0.1 collective-permute-start.1
  5.6 0.0 copy-done.2
  5.6 0.0 copy-done
  5.6 0.0 copy-start.1
  5.7 3.3 %first_water.1 = (f32[4096,128]{1,0:T(8,128)S(1)}, f32[144,128]{1,0:T(8,128)S(1)}, f32[144,128]{1,0:T(8,128)S(1)}, f32[1024,128]{1,0:T(8,128)S(1)}, f32[1024,128]{1,0:T(8,128)S(1)}) custom-call(f32[4096,128]{1,0:T(8,128)S(1)} %get-tuple-element.66.pressure, ...), custom_call_target="tpu_custom_call", output_to_operand_aliasing={{0}: (0, {}), {1}: (1, {}), {2}: (2, {})} | custom-call | flops 20000000 | bytes 8000000 | tf_op jit(solution)/shard_map/first_water/pallas_call | solution.py:876
  8.9 0.4 collective-permute-done.refs_7_
  9.3 0.0 collective-permute-done.1.refs_8_
  9.3 1.6 %collective-permute-start.3 = (f32[144,128]{1,0:T(8,128)S(1)}, f32[144,128]{1,0:T(8,128)S(1)}, u32[]{:S(2)}, u32[]{:S(2)}) collective-permute-start(f32[144,128]{1,0:T(8,128)S(1)} %maximum_dynamic-update-slice_fusion.1), channel_id=1, source_target_pairs={{0,4},{8,12},{16,20},{24,28},{4,0},{12,8},{20,16},{28,24},{1,5},{9... | collective-permute-start | bytes 221192 | tf_op jit(solution)/shard_map/ppermute | solution.py:792
  10.9 2.3 %collective-permute-start.2 = (f32[144,128]{1,0:T(8,128)S(1)}, f32[144,128]{1,0:T(8,128)S(1)}, u32[]{:S(2)}, u32[]{:S(2)}) collective-permute-start(f32[144,128]{1,0:T(8,128)S(1)} %maximum_dynamic-update-slice_fusion), channel_id=1, source_target_pairs={{4,8},{12,16},{20,24},{8,4},{16,12},{24,20},{5,9},{13,17},{21,25},... | collective-permute-start | bytes 221192 | tf_op jit(solution)/shard_map/ppermute | solution.py:792
  13.2 0.0 copy-done.1
  13.2 2.4 %inner.3 = (f32[1536,128]{1,0:T(8,128)S(1)}, f32[18,48,128]{2,1,0:T(8,128)S(1)}, f32[4096,128]{1,0:T(8,128)S(1)}, f32[34,48,128]{2,1,0:T(8,128)S(1)}, f32[24,48,...) custom-call(f32[4096,128]{1,0:T(8,128)S(1)} %get-tuple-element.71.refs_0_.wat, ...), custom_call_target="tpu_custom_call" | custom-call | flops 20000000 | bytes 8000000 | tf_op jit(solution)/shard_map/inner/pallas_call | solution.py:910
  15.6 0.0 collective-permute-done.3.refs_10_
  15.6 2.4 %collective-permute-done.2.refs_9_ = f32[144,128]{1,0:T(8,128)S(1)} collective-permute-done((f32[144,128]{1,0:T(8,128)S(1)}, f32[144,128]{1,0:T(8,128)S(1)}, u32[]{:S(2)}, u32[]{:S(2)}) %collective-permute-start.2) | collective-permute-done | bytes 73760 | tf_op jit(solution)/shard_map/ppermute | solution.py:792
  18.0 1.7 %edges.3 = (f32[18,48,128]{2,1,0:T(8,128)S(1)}, f32[4096,128]{1,0:T(8,128)S(1)}, f32[34,48,128]{2,1,0:T(8,128)S(1)}, f32[24,48,128]{2,1,0:T(8,128)S(1)}, f32[36,...) custom-call(f32[4096,128]{1,0:T(8,128)S(1)} %get-tuple-element.71.re, ...), custom_call_target="tpu_custom_call", output_to_operand_aliasing={{0}: (12, {}), {1}: (13, {}), {2}: (14, {}), {3}: (15, {}),... | custom-call | tf_op jit(solution)/shard_map/edges/pallas_call | solution.py:926
  19.8 1.9 %collective-permute-start.4 = (f32[112,128]{1,0:T(8,128)S(1)}, f32[112,128]{1,0:T(8,128)S(1)}, u32[]{:S(2)}, u32[]{:S(2)}) collective-permute-start(f32[112,128]{1,0:T(8,128)S(1)} %get-tuple-element.95), channel_id=1, source_target_pairs={{1,2},{2,1},{5,6},{6,5},{9,10},{10,9},{13,14},{14,13},{17,18},{18,... | collective-permute-start | bytes 172040 | tf_op jit(solution)/shard_map/ppermute | solution.py:792
  21.7 0.1 collective-permute-start.5
  21.8 1.7 %edge_water.2 = (f32[4096,128]{1,0:T(8,128)S(1)}, f32[112,128]{1,0:T(8,128)S(1)}, f32[112,128]{1,0:T(8,128)S(1)}) custom-call(f32[4096,128]{1,0:T(8,128)S(1)} %get-tuple-element.86.same, f32[112,128]{1,0:T(8,128)S(1)} %get-tuple-element.87.row_first, ...), custom_call_target="tpu_custom_call", output_to_operand_aliasing={{0}: (0, {}), {1}: (1, {}), {2}: (2, {})} | custom-call | flops 20000000 | bytes 8000000 | tf_op jit(solution)/shard_map/edge_water/pallas_call | solution.py:952
  23.5 1.8 %collective-permute-done.4.refs_7_ = f32[112,128]{1,0:T(8,128)S(1)} collective-permute-done((f32[112,128]{1,0:T(8,128)S(1)}, f32[112,128]{1,0:T(8,128)S(1)}, u32[]{:S(2)}, u32[]{:S(2)}) %collective-permute-start.4) | collective-permute-done | bytes 57376 | tf_op jit(solution)/shard_map/ppermute | solution.py:792
  25.3 0.0 collective-permute-done.5.refs_8_
  25.3 0.6 %collective-permute-start.7 = (f32[112,128]{1,0:T(8,128)S(1)}, f32[112,128]{1,0:T(8,128)S(1)}, u32[]{:S(2)}, u32[]{:S(2)}) collective-permute-start(f32[112,128]{1,0:T(8,128)S(1)} %maximum_dynamic-update-slice_fusion.3), channel_id=1, source_target_pairs={{0,4},{8,12},{16,20},{24,28},{4,0},{12,8},{20,16},{28,24},{1,5},{9... | collective-permute-start | bytes 172040 | tf_op jit(solution)/shard_map/ppermute | solution.py:792
  25.9 1.9 %collective-permute-start.6 = (f32[112,128]{1,0:T(8,128)S(1)}, f32[112,128]{1,0:T(8,128)S(1)}, u32[]{:S(2)}, u32[]{:S(2)}) collective-permute-start(f32[112,128]{1,0:T(8,128)S(1)} %maximum_dynamic-update-slice_fusion.2), channel_id=1, source_target_pairs={{4,8},{12,16},{20,24},{8,4},{16,12},{24,20},{5,9},{13,17},{21,25},... | collective-permute-start | bytes 172040 | tf_op jit(solution)/shard_map/ppermute | solution.py:792
  27.8 2.4 %inner.4 = (f32[1536,128]{1,0:T(8,128)S(1)}, f32[18,48,128]{2,1,0:T(8,128)S(1)}, f32[4096,128]{1,0:T(8,128)S(1)}, f32[34,48,128]{2,1,0:T(8,128)S(1)}, f32[24,48,...) custom-call(f32[4096,128]{1,0:T(8,128)S(1)} %get-tuple-element.92.refs_0_.water, ...), custom_call_target="tpu_custom_call" | custom-call | flops 20000000 | bytes 8000000 | tf_op jit(solution)/shard_map/inner/pallas_call | solution.py:910
  30.2 0.0 collective-permute-done.7.refs_10_
  30.2 2.6 %collective-permute-done.6.refs_9_ = f32[112,128]{1,0:T(8,128)S(1)} collective-permute-done((f32[112,128]{1,0:T(8,128)S(1)}, f32[112,128]{1,0:T(8,128)S(1)}, u32[]{:S(2)}, u32[]{:S(2)}) %collective-permute-start.6) | collective-permute-done | bytes 57376 | tf_op jit(solution)/shard_map/ppermute | solution.py:792
  32.8 1.7 %edges.4 = (f32[18,48,128]{2,1,0:T(8,128)S(1)}, f32[4096,128]{1,0:T(8,128)S(1)}, f32[34,48,128]{2,1,0:T(8,128)S(1)}, f32[24,48,128]{2,1,0:T(8,128)S(1)}, f32[36,...) custom-call(f32[4096,128]{1,0:T(8,128)S(1)} %get-tuple-element.92.re, ...), custom_call_target="tpu_custom_call", output_to_operand_aliasing={{0}: (13, {}), {1}: (14, {}), {2}: (15, {}), {3}: (16, {}),... | custom-call | tf_op jit(solution)/shard_map/edges/pallas_call | solution.py:926
  34.6 1.9 %collective-permute-start.8 = (f32[112,128]{1,0:T(8,128)S(1)}, f32[112,128]{1,0:T(8,128)S(1)}, u32[]{:S(2)}, u32[]{:S(2)}) collective-permute-start(f32[112,128]{1,0:T(8,128)S(1)} %get-tuple-element.117), channel_id=1, source_target_pairs={{1,2},{2,1},{5,6},{6,5},{9,10},{10,9},{13,14},{14,13},{17,18},{18,... | collective-permute-start | bytes 172040 | tf_op jit(solution)/shard_map/ppermute | solution.py:792
  36.5 0.1 collective-permute-start.9
  36.6 1.7 %edge_water.3 = (f32[4096,128]{1,0:T(8,128)S(1)}, f32[112,128]{1,0:T(8,128)S(1)}, f32[112,128]{1,0:T(8,128)S(1)}) custom-call(f32[4096,128]{1,0:T(8,128)S(1)} %get-tuple-element.108.same, f32[112,128]{1,0:T(8,128)S(1)} %get-tuple-element.109.row_first, ...), custom_call_target="tpu_custom_call", output_to_operand_aliasing={{0}: (0, {}), {1}: (1, {}), {2}: (2, {})} | custom-call | flops 20000000 | bytes 8000000 | tf_op jit(solution)/shard_map/edge_water/pallas_call | solution.py:952
  38.2 1.8 %collective-permute-done.8.refs_7_ = f32[112,128]{1,0:T(8,128)S(1)} collective-permute-done((f32[112,128]{1,0:T(8,128)S(1)}, f32[112,128]{1,0:T(8,128)S(1)}, u32[]{:S(2)}, u32[]{:S(2)}) %collective-permute-start.8) | collective-permute-done | bytes 57376 | tf_op jit(solution)/shard_map/ppermute | solution.py:792
  40.1 0.0 collective-permute-done.9.refs_8_
  40.1 1.6 %collective-permute-start.11 = (f32[112,128]{1,0:T(8,128)S(1)}, f32[112,128]{1,0:T(8,128)S(1)}, u32[]{:S(2)}, u32[]{:S(2)}) collective-permute-start(f32[112,128]{1,0:T(8,128)S(1)} %maximum_dynamic-update-slice_fusion.5), channel_id=1, source_target_pairs={{0,4},{8,12},{16,20},{24,28},{4,0},{12,8},{20,16},{28,24},{1,5},{9... | collective-permute-start | bytes 172040 | tf_op jit(solution)/shard_map/ppermute | solution.py:792
  41.7 1.9 %collective-permute-start.10 = (f32[112,128]{1,0:T(8,128)S(1)}, f32[112,128]{1,0:T(8,128)S(1)}, u32[]{:S(2)}, u32[]{:S(2)}) collective-permute-start(f32[112,128]{1,0:T(8,128)S(1)} %maximum_dynamic-update-slice_fusion.4), channel_id=1, source_target_pairs={{4,8},{12,16},{20,24},{8,4},{16,12},{24,20},{5,9},{13,17},{21,25},... | collective-permute-start | bytes 172040 | tf_op jit(solution)/shard_map/ppermute | solution.py:792
  43.6 3.2 %inner.5 = (f32[1536,128]{1,0:T(8,128)S(1)}, f32[18,48,128]{2,1,0:T(8,128)S(1)}, f32[4096,128]{1,0:T(8,128)}, f32[4,9,16,256]{3,2,1,0:T(8,128)}, f32[4,18,16,256]{3,2,1,0:T(8,128)}) custom-call(f32[4096,128]{1,0:T(8,128)S(1)} %get-tuple-element.114.refs_0_, f32[36,32,128]{2,1,0:T(8,128)S(1)} %get-tuple-element.115.refs_1_, ...), custom_call_target="tpu_custom_call" | custom-call | flops 20000000 | bytes 8000000 | tf_op jit(solution)/shard_map/inner/pallas_call | solution.py:910
  46.8 0.0 collective-permute-done.11.refs_10_
  46.8 1.8 %collective-permute-done.10.refs_9_ = f32[112,128]{1,0:T(8,128)S(1)} collective-permute-done((f32[112,128]{1,0:T(8,128)S(1)}, f32[112,128]{1,0:T(8,128)S(1)}, u32[]{:S(2)}, u32[]{:S(2)}) %collective-permute-start.10) | collective-permute-done | bytes 57376 | tf_op jit(solution)/shard_map/ppermute | solution.py:792
  48.6 1.8 %edges.5 = (f32[18,48,128]{2,1,0:T(8,128)S(1)}, f32[4096,128]{1,0:T(8,128)}, f32[4,9,16,256]{3,2,1,0:T(8,128)}, f32[4,18,16,256]{3,2,1,0:T(8,128)}) custom-call(f32[4096,128]{1,0:T(8,128)S(1)} %get-tuple-element.114.refs_0_, ...), custom_call_target="tpu_custom_call", output_to_operand_aliasing={{0}: (13, {}), {1}: (14, {}), {2}: (15, {}), {3}: (16, {})} | custom-call | tf_op jit(solution)/shard_map/edges/pallas_call | solution.py:926
  (12 shorter events, 0.0 us)
Async XLA Ops:
  0.6 5.0 %copy-start.2 = (s32[32,32,128]{2,1,0:T(8,128)S(1)}, s32[32,32,128]{2,1,0:T(8,128)}, u32[]{:S(2)}) copy-start(s32[32,32,128]{2,1,0:T(8,128)} %material.1) | copy-start | bytes 1572868
  0.6 5.0 %copy-start = (f32[4,32,32,128]{3,2,1,0:T(8,128)S(1)}, f32[4,32,32,128]{3,2,1,0:T(8,128)}, u32[]{:S(2)}) copy-start(f32[4,32,32,128]{3,2,1,0:T(8,128)} %state.1) | copy-start | bytes 6291460
  3.6 5.7 %collective-permute-start = (f32[144,128]{1,0:T(8,128)S(1)}, f32[144,128]{1,0:T(8,128)S(1)}, u32[]{:S(2)}, u32[]{:S(2)}) collective-permute-start(f32[144,128]{1,0:T(8,128)S(1)} %get-tuple-element.75), channel_id=1, source_target_pairs={{1,2},{2,1},{5,6},{6,5},{9,10},{10,9},{13,14},{14,13},{17,18},{18,... | collective-permute-start | bytes 221192 | tf_op jit(solution)/shard_map/ppermute | solution.py:792
  5.5 3.7 %collective-permute-start.1 = (f32[144,128]{1,0:T(8,128)S(1)}, f32[144,128]{1,0:T(8,128)S(1)}, u32[]{:S(2)}, u32[]{:S(2)}) collective-permute-start(f32[144,128]{1,0:T(8,128)S(1)} %get-tuple-element.76), channel_id=1, source_target_pairs={{0,1},{2,3},{1,0},{3,2},{4,5},{6,7},{5,4},{7,6},{8,9},{10,11},{9,8... | collective-permute-start | bytes 221192 | tf_op jit(solution)/shard_map/ppermute | solution.py:792
  5.6 7.5 %copy-start.1 = (f32[4,18,16,256]{3,2,1,0:T(8,128)S(1)}, f32[4,18,16,256]{3,2,1,0:T(8,128)}, u32[]{:S(2)}) copy-start(f32[4,18,16,256]{3,2,1,0:T(8,128)} %refs_2_.3) | copy-start | bytes 3538948
  9.3 6.3 %collective-permute-start.3 = (f32[144,128]{1,0:T(8,128)S(1)}, f32[144,128]{1,0:T(8,128)S(1)}, u32[]{:S(2)}, u32[]{:S(2)}) collective-permute-start(f32[144,128]{1,0:T(8,128)S(1)} %maximum_dynamic-update-slice_fusion.1), channel_id=1, source_target_pairs={{0,4},{8,12},{16,20},{24,28},{4,0},{12,8},{20,16},{28,24},{1,5},{9... | collective-permute-start | bytes 221192 | tf_op jit(solution)/shard_map/ppermute | solution.py:792
  10.9 7.1 %collective-permute-start.2 = (f32[144,128]{1,0:T(8,128)S(1)}, f32[144,128]{1,0:T(8,128)S(1)}, u32[]{:S(2)}, u32[]{:S(2)}) collective-permute-start(f32[144,128]{1,0:T(8,128)S(1)} %maximum_dynamic-update-slice_fusion), channel_id=1, source_target_pairs={{4,8},{12,16},{20,24},{8,4},{16,12},{24,20},{5,9},{13,17},{21,25},... | collective-permute-start | bytes 221192 | tf_op jit(solution)/shard_map/ppermute | solution.py:792
  19.8 5.5 %collective-permute-start.4 = (f32[112,128]{1,0:T(8,128)S(1)}, f32[112,128]{1,0:T(8,128)S(1)}, u32[]{:S(2)}, u32[]{:S(2)}) collective-permute-start(f32[112,128]{1,0:T(8,128)S(1)} %get-tuple-element.95), channel_id=1, source_target_pairs={{1,2},{2,1},{5,6},{6,5},{9,10},{10,9},{13,14},{14,13},{17,18},{18,... | collective-permute-start | bytes 172040 | tf_op jit(solution)/shard_map/ppermute | solution.py:792
  21.7 3.6 %collective-permute-start.5 = (f32[112,128]{1,0:T(8,128)S(1)}, f32[112,128]{1,0:T(8,128)S(1)}, u32[]{:S(2)}, u32[]{:S(2)}) collective-permute-start(f32[112,128]{1,0:T(8,128)S(1)} %get-tuple-element.96), channel_id=1, source_target_pairs={{0,1},{2,3},{1,0},{3,2},{4,5},{6,7},{5,4},{7,6},{8,9},{10,11},{9,8... | collective-permute-start | bytes 172040 | tf_op jit(solution)/shard_map/ppermute | solution.py:792
  25.3 4.9 %collective-permute-start.7 = (f32[112,128]{1,0:T(8,128)S(1)}, f32[112,128]{1,0:T(8,128)S(1)}, u32[]{:S(2)}, u32[]{:S(2)}) collective-permute-start(f32[112,128]{1,0:T(8,128)S(1)} %maximum_dynamic-update-slice_fusion.3), channel_id=1, source_target_pairs={{0,4},{8,12},{16,20},{24,28},{4,0},{12,8},{20,16},{28,24},{1,5},{9... | collective-permute-start | bytes 172040 | tf_op jit(solution)/shard_map/ppermute | solution.py:792
  25.9 7.0 %collective-permute-start.6 = (f32[112,128]{1,0:T(8,128)S(1)}, f32[112,128]{1,0:T(8,128)S(1)}, u32[]{:S(2)}, u32[]{:S(2)}) collective-permute-start(f32[112,128]{1,0:T(8,128)S(1)} %maximum_dynamic-update-slice_fusion.2), channel_id=1, source_target_pairs={{4,8},{12,16},{20,24},{8,4},{16,12},{24,20},{5,9},{13,17},{21,25},... | collective-permute-start | bytes 172040 | tf_op jit(solution)/shard_map/ppermute | solution.py:792
  34.6 5.5 %collective-permute-start.8 = (f32[112,128]{1,0:T(8,128)S(1)}, f32[112,128]{1,0:T(8,128)S(1)}, u32[]{:S(2)}, u32[]{:S(2)}) collective-permute-start(f32[112,128]{1,0:T(8,128)S(1)} %get-tuple-element.117), channel_id=1, source_target_pairs={{1,2},{2,1},{5,6},{6,5},{9,10},{10,9},{13,14},{14,13},{17,18},{18,... | collective-permute-start | bytes 172040 | tf_op jit(solution)/shard_map/ppermute | solution.py:792
  36.5 3.6 %collective-permute-start.9 = (f32[112,128]{1,0:T(8,128)S(1)}, f32[112,128]{1,0:T(8,128)S(1)}, u32[]{:S(2)}, u32[]{:S(2)}) collective-permute-start(f32[112,128]{1,0:T(8,128)S(1)} %get-tuple-element.118), channel_id=1, source_target_pairs={{0,1},{2,3},{1,0},{3,2},{4,5},{6,7},{5,4},{7,6},{8,9},{10,11},{9,8... | collective-permute-start | bytes 172040 | tf_op jit(solution)/shard_map/ppermute | solution.py:792
  40.1 6.7 %collective-permute-start.11 = (f32[112,128]{1,0:T(8,128)S(1)}, f32[112,128]{1,0:T(8,128)S(1)}, u32[]{:S(2)}, u32[]{:S(2)}) collective-permute-start(f32[112,128]{1,0:T(8,128)S(1)} %maximum_dynamic-update-slice_fusion.5), channel_id=1, source_target_pairs={{0,4},{8,12},{16,20},{24,28},{4,0},{12,8},{20,16},{28,24},{1,5},{9... | collective-permute-start | bytes 172040 | tf_op jit(solution)/shard_map/ppermute | solution.py:792
  41.7 7.0 %collective-permute-start.10 = (f32[112,128]{1,0:T(8,128)S(1)}, f32[112,128]{1,0:T(8,128)S(1)}, u32[]{:S(2)}, u32[]{:S(2)}) collective-permute-start(f32[112,128]{1,0:T(8,128)S(1)} %maximum_dynamic-update-slice_fusion.4), channel_id=1, source_target_pairs={{4,8},{12,16},{20,24},{8,4},{16,12},{24,20},{5,9},{13,17},{21,25},... | collective-permute-start | bytes 172040 | tf_op jit(solution)/shard_map/ppermute | solution.py:792

commit v8 on v7

--- a/solution.py
+++ b/solution.py
@@ -16,7 +16,8 @@
 ALONG_X = (XX, XY, XZ)
 ALONG_Y = (XY, YY, YZ)
 ALONG_Z = (XZ, YZ, ZZ)
-M_P, M_U, M_BRICK, M_CORNER, M_CONST = 0, 32, 64, 96, 112
+M_P, M_U, M_BRICK, M_CORNER, M_RELAY = 0, 32, 64, 92, 96
+ROW_CONST, COL_CONST = 96, 104
 
 
 def lane_ids():
@@ -283,14 +284,12 @@
             out[pl.ds(M_P + SUB * t, SUB), :] = water[pl.ds(own, SUB), :]
             out[pl.ds(M_U + SUB * t, SUB), :] = row_u(side, t) - sign * hb * water[pl.ds(inward * ny + SUB * t, SUB), :]
             if first:
-                out[pl.ds(M_CONST + SUB * t, SUB), :] = hb
+                out[pl.ds(ROW_CONST + SUB * t, SUB), :] = hb
         for tj in range(across):
-            block = M_BRICK + SUB * tj
             for k, field in enumerate(ALONG_X + (VX, VY, VZ)):
-                out[pl.ds(block + k, 1), :] = bricks[field * across + tj, pl.ds(x, 1), :]
-            out[pl.ds(block + 6, 1), :] = params[HB * across + tj, pl.ds(x, 1), :]
-            out[pl.ds(block + 7, 1), :] = jnp.zeros((1, LANES), jnp.float32)
-        out[pl.ds(M_CORNER, 2 * SUB), :] = jnp.zeros((2 * SUB, LANES), jnp.float32)
+                out[pl.ds(M_BRICK + k * across + tj, 1), :] = bricks[field * across + tj, pl.ds(x, 1), :]
+            out[pl.ds(M_BRICK + 6 * across + tj, 1), :] = params[HB * across + tj, pl.ds(x, 1), :]
+        out[pl.ds(M_CORNER, 4), :] = jnp.zeros((4, LANES), jnp.float32)
     sides = ((col_first, 0, 1, 0, 1.0), (col_last, ny - 1, ny - 2, across - 1, -1.0))
     for side, (out, y, inward, tj, sign) in enumerate(sides):
         for t in range(g.xtiles):
@@ -301,7 +300,7 @@
                 col_u(side, t) - sign * hb * water[pl.ds(SUB * t * ny + inward, SUB, stride=ny), :]
             )
             if first:
-                out[pl.ds(M_CONST + SUB * t, SUB), :] = hb
+                out[pl.ds(COL_CONST + SUB * t, SUB), :] = hb
             rows = pl.ds(SUB * t, SUB)
             pieces = [bricks[field * across + tj, rows, :] for field in ALONG_Y + (VX, VY, VZ)]
             pieces.append(params[HB * across + tj, rows, :])
@@ -318,8 +317,12 @@
             out[pl.ds(M_BRICK + SUB * t, SUB), :] = packed
             if t == 0:
                 corner = packed
-        out[pl.ds(M_CORNER, SUB), :] = jnp.where(row_odd, packed, corner)
-        out[pl.ds(M_CORNER + SUB, SUB), :] = jnp.where(row_odd, corner, packed)
+        one = (corner[0:1, :], corner[1:2, :])
+        other = (packed[SUB - 1 : SUB, :], packed[SUB - 2 : SUB - 1, :])
+        out[pl.ds(M_RELAY, SUB), :] = jnp.zeros((SUB, LANES), jnp.float32)
+        for k in range(2):
+            out[pl.ds(M_RELAY + k, 1), :] = jnp.where(row_odd[0:1, :], other[k], one[k])
+            out[pl.ds(M_RELAY + 2 + k, 1), :] = jnp.where(row_odd[0:1, :], one[k], other[k])
     route(row_odd, row_first, row_last, *sends[:2])
     route(col_odd, col_first, col_last, *sends[2:])
 
@@ -496,14 +499,14 @@
         (const_in,) = refs.take(1)
     uy, speed = refs.take(2)
     if last:
-        water_hbm, motion_hbm, memory_hbm = refs.take(3)
+        water_hbm, press_buf, motion_buf, memory_buf = refs.take(4)
     else:
         water_out, press, stress, bricks_out, memory_out = refs.take(5)
     if first:
         (const_out,) = refs.take(1)
     col_before, col_after = refs.take(2)
     if last:
-        press_buf, uy_buf, motion_buf, memory_buf, sems = refs.take(5)
+        uy_buf, sems = refs.take(2)
     unroute(odd[1] > 0.0, col_far, col_near, col_before, col_after)
 
     nx, ny, edge, across, plane = g.nx, g.ny, g.edge, g.across, g.plane
@@ -545,7 +548,7 @@
             here = pl.ds(SUB * t * py + PAD + y, SUB, stride=py)
             place = pl.ds(32 * side + SUB * t, SUB)
             if first:
-                theirs = ref[pl.ds(M_CONST + SUB * t, SUB), :]
+                theirs = ref[pl.ds(COL_CONST + SUB * t, SUB), :]
                 const_out[place, :] = theirs
             else:
                 theirs = const_in[place, :]
@@ -590,11 +593,6 @@
         )
         brick_stress(g, ti, first, bricks, memory, params, speed, tops, store)
 
-    if last:
-        for ti in range(1, g.xtiles - 1):
-            send(slots_of(g, motion_buf, ti), slots_of(g, motion_hbm, ti))
-            send(slots_of(g, memory_buf, ti), slots_of(g, memory_hbm, ti))
-
     def layer(x):
         results = []
         for t in range(g.ytiles):
@@ -615,7 +613,6 @@
                 press[x + 1, pl.ds(PAD + SUB * t, SUB), :] = value
 
     if last:
-        send(press_buf.at[part(0, 2, nx - 2), :], water_hbm.at[part(0, 2, nx - 2), :])
         for copy in copies:
             copy.wait()
 
@@ -635,7 +632,9 @@
     if not first:
         (const_in,) = refs.take(1)
     (uy,) = refs.take(1)
-    refs.take(4 if last else 6)
+    if last:
+        inner_press, inner_motion, inner_memory = refs.take(3)
+    refs.take(2 if last else 6)
     (speed,) = refs.take(1)
     if last:
         water_hbm, motion_hbm, memory_hbm = refs.take(3)
@@ -652,10 +651,7 @@
         buffers = refs.take(4)
     unroute(odd[1] > 0.0, col_far, col_near, col_before, col_after, (M_BRICK, M_BRICK + g.nx - SUB))
     unroute(odd[0] > 0.0, row_far, row_near, row_before, row_after)
-    for ref in (row_before, row_after):
-        far, near = ref[pl.ds(M_CORNER, SUB), :], ref[pl.ds(M_CORNER + SUB, SUB), :]
-        ref[pl.ds(M_CORNER, SUB), :] = jnp.where(odd[1] > 0.0, near, far)
-        ref[pl.ds(M_CORNER + SUB, SUB), :] = jnp.where(odd[1] > 0.0, far, near)
+    col_odd = odd[1, pl.ds(0, 1), :] > 0.0
 
     nx, ny, edge, across, plane = g.nx, g.ny, g.edge, g.across, g.plane
     wide = across + 2
@@ -668,6 +664,13 @@
         copies.append(pltpu.make_async_copy(source, target, sems.at[len(copies)]))
         copies[-1].start()
 
+    if last:
+        middle = pl.ds(2 * ny, (nx - 4) * ny)
+        send(inner_press.at[middle, :], water_hbm.at[middle, :])
+        for ti in range(1, g.xtiles - 1):
+            send(slots_of(g, inner_memory, ti), slots_of(g, memory_hbm, ti))
+            send(slots_of(g, inner_motion, ti), slots_of(g, motion_hbm, ti))
+
     @pl.loop(0, SUB)
     def _(x):
         for t in range(g.ytiles):
@@ -681,7 +684,7 @@
             own = pl.ds(x * ny + SUB * t, SUB)
             place = pl.ds(32 * side + SUB * t, SUB)
             if first:
-                theirs = ref[pl.ds(M_CONST + SUB * t, SUB), :]
+                theirs = ref[pl.ds(ROW_CONST + SUB * t, SUB), :]
                 const_out[place, :] = theirs
             else:
                 theirs = const_in[place, :]
@@ -701,26 +704,24 @@
 
     for ref, x, halo, sign, _, _ in sides:
         for tj in range(across):
-            block = M_BRICK + SUB * tj
             own_hb = sign * params[HB * across + tj, pl.ds(x, 1), :]
-            their_hb = sign * ref[pl.ds(block + 6, 1), :]
+            their_hb = sign * ref[pl.ds(M_BRICK + 6 * across + tj, 1), :]
             for c in (VX, VY, VZ):
                 key = c * wide + 1 + tj
-                speed_rows[key, x] = speed_row(key, x) - own_hb * ref[pl.ds(block + c, 1), :]
+                speed_rows[key, x] = speed_row(key, x) - own_hb * ref[pl.ds(M_BRICK + c * across + tj, 1), :]
                 speed_rows[key, halo] = (
-                    ref[pl.ds(block + 3 + c, 1), :] + their_hb * bricks[ALONG_X[c] * across + tj, pl.ds(x, 1), :]
+                    ref[pl.ds(M_BRICK + (3 + c) * across + tj, 1), :] + their_hb * bricks[ALONG_X[c] * across + tj, pl.ds(x, 1), :]
                 )
-        edge_row = SUB - 1 if x == 0 else 0
-        beside_row = SUB - 2 if x == 0 else 1
+        relayed = [ref[pl.ds(M_CORNER + k, 1), :] for k in range(4)]
         for k, (col_ref, tj, col_halo, col_sign) in enumerate(((col_before, 0, 0, 1.0), (col_after, across - 1, wide - 1, -1.0))):
             near = 0 if tj == 0 else LANES - edge
             far = LANES - edge - near
             inside = (lane[0:1, :] >= near) & (lane[0:1, :] < near + edge)
-            corner = ref[pl.ds(M_CORNER + SUB * k + edge_row, 1), :]
-            beside = ref[pl.ds(M_CORNER + SUB * k + beside_row, 1), :]
+            corner = jnp.where(col_odd, relayed[2 - 2 * k], relayed[2 * k])
+            beside = jnp.where(col_odd, relayed[3 - 2 * k], relayed[2 * k + 1])
             across_y = [roll_row(corner, near - c * edge) for c in range(3)]
             across_x = (roll_row(corner, far - 7 * edge), roll_row(corner, far), roll_row(beside, far - 7 * edge))
-            row_hb = jnp.where(inside, col_sign * ref[pl.ds(M_BRICK + SUB * tj + 6, 1), :], 0.0)
+            row_hb = jnp.where(inside, col_sign * ref[pl.ds(M_BRICK + 6 * across + tj, 1), :], 0.0)
             col_hb = sign * roll_row(col_ref[pl.ds(M_BRICK + x, 1), :], far - 6 * edge)
             for c in (VX, VY, VZ):
                 key = c * wide + 1 + tj
@@ -798,11 +799,11 @@
     col_near = swap(col_near, "col", 0)
 
     def with_corners(message, start):
-        corners = jnp.concatenate([col_far[start : start + SUB], col_near[start : start + SUB]])
+        corners = jnp.concatenate([col_far[start : start + 2], col_near[start : start + 2]])
         return lax.dynamic_update_slice(message, corners, (M_CORNER, 0))
 
-    row_far = swap(with_corners(row_far, M_CORNER), "row", 1)
-    row_near = swap(with_corners(row_near, M_CORNER + SUB), "row", 0)
+    row_far = swap(with_corners(row_far, M_RELAY), "row", 1)
+    row_near = swap(with_corners(row_near, M_RELAY + 2), "row", 0)
     return col_far, col_near, row_far, row_near
 
 
@@ -826,7 +827,7 @@
     hbm = pl.BlockSpec(memory_space=pltpu.HBM)
     params = pltpu.CompilerParams(vmem_limit_bytes=24 * 1024 * 1024)
     def messages(first):
-        return [f32(M_CONST + (32 if first else 0), LANES)] * 4
+        return [f32(start + (32 if first else 0), LANES) for start in (ROW_CONST, ROW_CONST, COL_CONST, COL_CONST)]
 
     def buffer(*shape):
         return pltpu.VMEM(shape, jnp.float32)
@@ -837,8 +838,9 @@
     def pinned(*values):
         return [pltpu.with_memory_space_constraint(value, pltpu.HBM) for value in values]
 
-    def message_buffers(count, first):
-        return [buffer(M_CONST + (32 if first else 0), LANES)] * count
+    def message_buffers(kinds, first):
+        starts = {"row": ROW_CONST, "col": COL_CONST}
+        return [buffer(starts[kind] + (32 if first else 0), LANES) for kind in kinds for _ in range(2)]
 
     odd = jnp.stack([lax.axis_index(axis) & 1 for axis in ("row", "col")]).astype(jnp.float32)
     odd = jnp.broadcast_to(odd[:, None, None], (2, SUB, LANES))
@@ -865,7 +867,7 @@
             pltpu.SMEM(material_table.shape, jnp.float32),
             pltpu.SemaphoreType.DMA((13,)),
         ]
-        + message_buffers(4, True),
+        + message_buffers(("row", "col"), True),
         compiler_params=params,
         name="first_bricks",
     )(*pinned(brick_live, material_table, water_state, water_material, brick_velocity_stress, brick_cell_material), odd)
@@ -905,15 +907,17 @@
         first, last = step == 0, step == STEPS - 1
         *columns, row_far, row_near = exchange(sends)
         state = (water, bricks, memory, coefficients, hb_water, hk_water, odd)
-        shapes = finals if last else planes
-        spaces = [hbm if last else vmem] * len(shapes)
+        held_out = [buffer(plane, nz)] + slot_buffers if last else planes
         inner = pl.pallas_call(
             functools.partial(inner_kernel, g, first, last),
-            out_shape=[buffer(*uy_shape), buffer(*speed_shape)] + shapes + ([buffer(64, LANES)] if first else []),
+            out_shape=[buffer(*uy_shape), buffer(*speed_shape)]
+            + finals[: 1 if last else 0]
+            + held_out
+            + ([buffer(64, LANES)] if first else []),
             in_specs=[vmem] * (9 + len(col_const)),
-            out_specs=[vmem] * 2 + spaces + ([vmem] if first else []),
-            scratch_shapes=message_buffers(2, first)
-            + ([buffer(plane, nz), buffer(plane, nz)] + slot_buffers + [pltpu.SemaphoreType.DMA((8,))] if last else []),
+            out_specs=[vmem] * 2 + [hbm] * (1 if last else 0) + [vmem] * (len(held_out) + (1 if first else 0)),
+            scratch_shapes=message_buffers(("col",), first)
+            + ([buffer(plane, nz), pltpu.SemaphoreType.DMA((3,))] if last else []),
             compiler_params=params,
             cost_estimate=work,
             name="inner",
@@ -921,27 +925,32 @@
         if first:
             col_const = (inner[-1],)
             inner = inner[:-1]
-        uy, *partial = inner
-        count = 11 + len(row_const) + 1
+        inputs = held(*state) + list(columns) + [row_far, row_near] + list(row_const)
+        if last:
+            uy, speed, partial, *rest = inner
+            inputs += held(uy, *rest)
+            same, spaces, out_shape = [*held(speed), partial], [vmem, hbm], [buffer(*speed_shape)] + finals
+        else:
+            uy, *partial = inner
+            inputs += held(uy)
+            same, spaces, out_shape = held(*partial), [vmem] * len(partial), [buffer(*speed_shape)] + planes
+        rest_shape = ([] if last else messages(False) + [ux_buffer]) + ([buffer(64, LANES)] if first else [])
         results = pl.pallas_call(
             functools.partial(edge_kernel, g, first, last),
-            out_shape=[buffer(*speed_shape)]
-            + shapes
-            + ([] if last else messages(False) + [ux_buffer])
-            + ([buffer(64, LANES)] if first else []),
-            in_specs=[vmem] * (count + 1) + spaces,
-            out_specs=[vmem] + spaces + [vmem] * (0 if last else 5) + ([vmem] if first else []),
-            input_output_aliases={count + k: k for k in range(1 + len(shapes))},
+            out_shape=out_shape + rest_shape,
+            in_specs=[vmem] * len(inputs) + spaces,
+            out_specs=[vmem] + [hbm if last else vmem] * (len(out_shape) - 1) + [vmem] * len(rest_shape),
+            input_output_aliases={len(inputs) + k: k for k in range(len(same))},
             scratch_shapes=([ux_buffer] if last else [])
-            + message_buffers(4, first)
+            + message_buffers(("col", "row"), first)
             + (
-                [buffer(4 * ny, nz)] + slot_buffers + [pltpu.SemaphoreType.DMA((8,))]
+                [buffer(4 * ny, nz)] + slot_buffers + [pltpu.SemaphoreType.DMA((13,))]
                 if last
-                else message_buffers(4, False)
+                else message_buffers(("row", "col"), False)
             ),
             compiler_params=params,
             name="edges",
-        )(*held(*state), *columns, row_far, row_near, *row_const, *held(uy), *(held(partial[0]) + (list(partial[1:]) if last else held(*partial[1:]))))
+        )(*inputs, *same)
         if last:
             return results[2], results[3], results[1].reshape(water_state.shape)
         old_water = water

time: 50.7 us -> 50.3 us (level)
  Pallas kernels: 22.6 us -> 21.8 us
    pallas_call x3, Pallas kernels: 7.95 us -> 7.11 us  [body(): pl.pallas_call(functools.partial(inner_kernel, g, first, last), out_shape...]
  transfers between devices with their start and end apart: 12 -> 12, of which waited for: 6 -> 6; matrix products, arithmetic and copies ran while one was open for 0% -> 0% of each run, Pallas kernels for 29% -> 27%
where the time goes in v8:
time: 50.3 us; the launch traced here: 50.1 us
  Pallas kernels  21.8 us (43%)
  starting transfers between devices  15.9 us (32%)
  waiting for transfers between devices  11.3 us (22%)
  between operations  0.87 us (2%)
    ppermute x12, starting transfers between devices, swap(): return lax.ppermute(value, axis, pairs + [(j, i) for i, j in pairs])  15.9 us
    ppermute x12, waiting for transfers between devices, swap(): return lax.ppermute(value, axis, pairs + [(j, i) for i, j in pairs])  11.3 us
    pallas_call x3, Pallas kernels, body(): pl.pallas_call(functools.partial(inner_kernel, g, first, last), out_shape...  7.11 us
    pallas_call x3, Pallas kernels, body(): pl.pallas_call(functools.partial(edge_kernel, g, first, last), out_shape=...  5.26 us
    pallas_call x1, Pallas kernels, body(): pl.pallas_call(functools.partial(first_water_kernel, g), out_shape=[buffe...  3.32 us
    pallas_call x2, Pallas kernels, body(): pl.pallas_call(functools.partial(edge_water_kernel, g), out_shape=[buffer...  3.3 us
    pallas_call x1, Pallas kernels, body(): pl.pallas_call(functools.partial(first_kernel, g), out_shape=[buffer(4 *...  2.81 us
  transfers between devices with their start and end apart: 12, of which 6 were waited for; matrix products, arithmetic and copies ran while one was open for 0% of the time, Pallas kernels for 27%

profile of v8, /device:TPU:10, one launch (start us, length us, event | category | flops | bytes accessed | tf_op | source)
XLA Modules:
  0.0 50.1 jit_solution(8396906491278014764)
XLA Ops:
  0.6 0.0 copy-start.2
  0.6 0.0 copy-start
  0.7 0.1 add_convert_fusion
  0.7 0.1 broadcast_in_dim.2.odd.refs_6_
  0.8 2.8 %first_bricks.1 = (f32[4096,128]{1,0:T(8,128)S(1)}, f32[36,32,128]{2,1,0:T(8,128)S(1)}, f32[36,32,128]{2,1,0:T(8,128)S(1)}, f32[8,8,128]{2,1,0:T(8,128)S(1)}, f3...) custom-call(s32[4]{0:T(128)} %live_hbm.1, f32[8,8]{1,0:T(8,128)} %table_hbm.1, ...), custom_call_target="tpu_custom_call" | custom-call | tf_op jit(solution)/shard_map/first_bricks/pallas_call | solution.py:850
  3.6 1.9 %collective-permute-start = (f32[136,128]{1,0:T(8,128)S(1)}, f32[136,128]{1,0:T(8,128)S(1)}, u32[]{:S(2)}, u32[]{:S(2)}) collective-permute-start(f32[136,128]{1,0:T(8,128)S(1)} %get-tuple-element.76), channel_id=1, source_target_pairs={{1,2},{2,1},{5,6},{6,5},{9,10},{10,9},{13,14},{14,13},{17,18},{18,... | collective-permute-start | bytes 208904 | tf_op jit(solution)/shard_map/ppermute | solution.py:793
  5.6 0.1 collective-permute-start.1
  5.6 0.0 copy-done.2
  5.6 0.0 copy-done
  5.7 0.0 copy-start.1
  5.7 3.3 %first_water.1 = (f32[4096,128]{1,0:T(8,128)S(1)}, f32[128,128]{1,0:T(8,128)S(1)}, f32[128,128]{1,0:T(8,128)S(1)}, f32[1024,128]{1,0:T(8,128)S(1)}, f32[1024,128]{1,0:T(8,128)S(1)}) custom-call(f32[4096,128]{1,0:T(8,128)S(1)} %get-tuple-element.67.pressure, ...), custom_call_target="tpu_custom_call", output_to_operand_aliasing={{0}: (0, {}), {1}: (1, {}), {2}: (2, {})} | custom-call | flops 20000000 | bytes 8000000 | tf_op jit(solution)/shard_map/first_water/pallas_call | solution.py:878
  9.0 0.3 collective-permute-done.refs_7_
  9.3 0.0 collective-permute-done.1.refs_8_
  9.3 1.6 %collective-permute-start.3 = (f32[128,128]{1,0:T(8,128)S(1)}, f32[128,128]{1,0:T(8,128)S(1)}, u32[]{:S(2)}, u32[]{:S(2)}) collective-permute-start(f32[128,128]{1,0:T(8,128)S(1)} %maximum_dynamic-update-slice_fusion.1), channel_id=1, source_target_pairs={{0,4},{8,12},{16,20},{24,28},{4,0},{12,8},{20,16},{28,24},{1,5},{9... | collective-permute-start | bytes 196616 | tf_op jit(solution)/shard_map/ppermute | solution.py:793
  10.9 2.3 %collective-permute-start.2 = (f32[128,128]{1,0:T(8,128)S(1)}, f32[128,128]{1,0:T(8,128)S(1)}, u32[]{:S(2)}, u32[]{:S(2)}) collective-permute-start(f32[128,128]{1,0:T(8,128)S(1)} %maximum_dynamic-update-slice_fusion), channel_id=1, source_target_pairs={{4,8},{12,16},{20,24},{8,4},{16,12},{24,20},{5,9},{13,17},{21,25},... | collective-permute-start | bytes 196616 | tf_op jit(solution)/shard_map/ppermute | solution.py:793
  13.2 0.0 copy-done.1
  13.2 2.4 %inner.3 = (f32[1536,128]{1,0:T(8,128)S(1)}, f32[18,48,128]{2,1,0:T(8,128)S(1)}, f32[4096,128]{1,0:T(8,128)S(1)}, f32[34,48,128]{2,1,0:T(8,128)S(1)}, f32[24,48,...) custom-call(f32[4096,128]{1,0:T(8,128)S(1)} %get-tuple-element.72.refs_0_.wat, ...), custom_call_target="tpu_custom_call" | custom-call | flops 20000000 | bytes 8000000 | tf_op jit(solution)/shard_map/inner/pallas_call | solution.py:911
  15.6 0.0 collective-permute-done.3.refs_10_
  15.6 2.3 %collective-permute-done.2.refs_9_ = f32[128,128]{1,0:T(8,128)S(1)} collective-permute-done((f32[128,128]{1,0:T(8,128)S(1)}, f32[128,128]{1,0:T(8,128)S(1)}, u32[]{:S(2)}, u32[]{:S(2)}) %collective-permute-start.2) | collective-permute-done | bytes 65568 | tf_op jit(solution)/shard_map/ppermute | solution.py:793
  17.9 1.7 %edges.3 = (f32[18,48,128]{2,1,0:T(8,128)S(1)}, f32[4096,128]{1,0:T(8,128)S(1)}, f32[34,48,128]{2,1,0:T(8,128)S(1)}, f32[24,48,128]{2,1,0:T(8,128)S(1)}, f32[36,...) custom-call(f32[4096,128]{1,0:T(8,128)S(1)} %get-tuple-element.72.re, ...), custom_call_target="tpu_custom_call", output_to_operand_aliasing={{0}: (12, {}), {1}: (13, {}), {2}: (14, {}), {3}: (15, {}),... | custom-call | tf_op jit(solution)/shard_map/edges/pallas_call | solution.py:938
  19.6 2.0 %collective-permute-start.4 = (f32[104,128]{1,0:T(8,128)S(1)}, f32[104,128]{1,0:T(8,128)S(1)}, u32[]{:S(2)}, u32[]{:S(2)}) collective-permute-start(f32[104,128]{1,0:T(8,128)S(1)} %get-tuple-element.96), channel_id=1, source_target_pairs={{1,2},{2,1},{5,6},{6,5},{9,10},{10,9},{13,14},{14,13},{17,18},{18,... | collective-permute-start | bytes 159752 | tf_op jit(solution)/shard_map/ppermute | solution.py:793
  21.6 0.1 collective-permute-start.5
  21.7 1.6 %edge_water.2 = (f32[4096,128]{1,0:T(8,128)S(1)}, f32[96,128]{1,0:T(8,128)S(1)}, f32[96,128]{1,0:T(8,128)S(1)}) custom-call(f32[4096,128]{1,0:T(8,128)S(1)} %get-tuple-element.87.same, f32[96,128]{1,0:T(8,128)S(1)} %get-tuple-element.88.row_first, ...), custom_call_target="tpu_custom_call", output_to_operand_aliasing={{0}: (0, {}), {1}: (1, {}), {2}: (2, {})} | custom-call | flops 20000000 | bytes 8000000 | tf_op jit(solution)/shard_map/edge_water/pallas_call | solution.py:961
  23.4 1.8 %collective-permute-done.4.refs_7_ = f32[104,128]{1,0:T(8,128)S(1)} collective-permute-done((f32[104,128]{1,0:T(8,128)S(1)}, f32[104,128]{1,0:T(8,128)S(1)}, u32[]{:S(2)}, u32[]{:S(2)}) %collective-permute-start.4) | collective-permute-done | bytes 53280 | tf_op jit(solution)/shard_map/ppermute | solution.py:793
  25.1 0.0 collective-permute-done.5.refs_8_
  25.1 0.6 %collective-permute-start.7 = (f32[96,128]{1,0:T(8,128)S(1)}, f32[96,128]{1,0:T(8,128)S(1)}, u32[]{:S(2)}, u32[]{:S(2)}) collective-permute-start(f32[96,128]{1,0:T(8,128)S(1)} %maximum_dynamic-update-slice_fusion.3), channel_id=1, source_target_pairs={{0,4},{8,12},{16,20},{24,28},{4,0},{12,8},{20,16},{28,24},{1,5},{9... | collective-permute-start | bytes 147464 | tf_op jit(solution)/shard_map/ppermute | solution.py:793
  25.7 1.9 %collective-permute-start.6 = (f32[96,128]{1,0:T(8,128)S(1)}, f32[96,128]{1,0:T(8,128)S(1)}, u32[]{:S(2)}, u32[]{:S(2)}) collective-permute-start(f32[96,128]{1,0:T(8,128)S(1)} %maximum_dynamic-update-slice_fusion.2), channel_id=1, source_target_pairs={{4,8},{12,16},{20,24},{8,4},{16,12},{24,20},{5,9},{13,17},{21,25},... | collective-permute-start | bytes 147464 | tf_op jit(solution)/shard_map/ppermute | solution.py:793
  27.6 2.3 %inner.4 = (f32[1536,128]{1,0:T(8,128)S(1)}, f32[18,48,128]{2,1,0:T(8,128)S(1)}, f32[4096,128]{1,0:T(8,128)S(1)}, f32[34,48,128]{2,1,0:T(8,128)S(1)}, f32[24,48,...) custom-call(f32[4096,128]{1,0:T(8,128)S(1)} %get-tuple-element.93.refs_0_.water, ...), custom_call_target="tpu_custom_call" | custom-call | flops 20000000 | bytes 8000000 | tf_op jit(solution)/shard_map/inner/pallas_call | solution.py:911
  30.0 0.0 collective-permute-done.7.refs_10_
  30.0 2.6 %collective-permute-done.6.refs_9_ = f32[96,128]{1,0:T(8,128)S(1)} collective-permute-done((f32[96,128]{1,0:T(8,128)S(1)}, f32[96,128]{1,0:T(8,128)S(1)}, u32[]{:S(2)}, u32[]{:S(2)}) %collective-permute-start.6) | collective-permute-done | bytes 49184 | tf_op jit(solution)/shard_map/ppermute | solution.py:793
  32.6 1.7 %edges.4 = (f32[18,48,128]{2,1,0:T(8,128)S(1)}, f32[4096,128]{1,0:T(8,128)S(1)}, f32[34,48,128]{2,1,0:T(8,128)S(1)}, f32[24,48,128]{2,1,0:T(8,128)S(1)}, f32[36,...) custom-call(f32[4096,128]{1,0:T(8,128)S(1)} %get-tuple-element.93.re, ...), custom_call_target="tpu_custom_call", output_to_operand_aliasing={{0}: (13, {}), {1}: (14, {}), {2}: (15, {}), {3}: (16, {}),... | custom-call | tf_op jit(solution)/shard_map/edges/pallas_call | solution.py:938
  34.3 1.9 %collective-permute-start.8 = (f32[104,128]{1,0:T(8,128)S(1)}, f32[104,128]{1,0:T(8,128)S(1)}, u32[]{:S(2)}, u32[]{:S(2)}) collective-permute-start(f32[104,128]{1,0:T(8,128)S(1)} %get-tuple-element.118), channel_id=1, source_target_pairs={{1,2},{2,1},{5,6},{6,5},{9,10},{10,9},{13,14},{14,13},{17,18},{18,... | collective-permute-start | bytes 159752 | tf_op jit(solution)/shard_map/ppermute | solution.py:793
  36.2 0.1 collective-permute-start.9
  36.3 1.7 %edge_water.3 = (f32[4096,128]{1,0:T(8,128)S(1)}, f32[96,128]{1,0:T(8,128)S(1)}, f32[96,128]{1,0:T(8,128)S(1)}) custom-call(f32[4096,128]{1,0:T(8,128)S(1)} %get-tuple-element.109.same, f32[96,128]{1,0:T(8,128)S(1)} %get-tuple-element.110.row_first, ...), custom_call_target="tpu_custom_call", output_to_operand_aliasing={{0}: (0, {}), {1}: (1, {}), {2}: (2, {})} | custom-call | flops 20000000 | bytes 8000000 | tf_op jit(solution)/shard_map/edge_water/pallas_call | solution.py:961
  38.0 1.8 %collective-permute-done.8.refs_7_ = f32[104,128]{1,0:T(8,128)S(1)} collective-permute-done((f32[104,128]{1,0:T(8,128)S(1)}, f32[104,128]{1,0:T(8,128)S(1)}, u32[]{:S(2)}, u32[]{:S(2)}) %collective-permute-start.8) | collective-permute-done | bytes 53280 | tf_op jit(solution)/shard_map/ppermute | solution.py:793
  39.8 0.0 collective-permute-done.9.refs_8_
  39.8 1.6 %collective-permute-start.11 = (f32[96,128]{1,0:T(8,128)S(1)}, f32[96,128]{1,0:T(8,128)S(1)}, u32[]{:S(2)}, u32[]{:S(2)}) collective-permute-start(f32[96,128]{1,0:T(8,128)S(1)} %maximum_dynamic-update-slice_fusion.5), channel_id=1, source_target_pairs={{0,4},{8,12},{16,20},{24,28},{4,0},{12,8},{20,16},{28,24},{1,5},{9... | collective-permute-start | bytes 147464 | tf_op jit(solution)/shard_map/ppermute | solution.py:793
  41.4 1.9 %collective-permute-start.10 = (f32[96,128]{1,0:T(8,128)S(1)}, f32[96,128]{1,0:T(8,128)S(1)}, u32[]{:S(2)}, u32[]{:S(2)}) collective-permute-start(f32[96,128]{1,0:T(8,128)S(1)} %maximum_dynamic-update-slice_fusion.4), channel_id=1, source_target_pairs={{4,8},{12,16},{20,24},{8,4},{16,12},{24,20},{5,9},{13,17},{21,25},... | collective-permute-start | bytes 147464 | tf_op jit(solution)/shard_map/ppermute | solution.py:793
  43.3 2.4 %inner.5 = (f32[1536,128]{1,0:T(8,128)S(1)}, f32[18,48,128]{2,1,0:T(8,128)S(1)}, f32[4096,128]{1,0:T(8,128)}, f32[1024,128]{1,0:T(8,128)S(1)}, f32[4,9,16,256]{3...) custom-call(f32[4096,128]{1,0:T(8,128)S(1)} %get-tuple-element.115.refs_0_, f32[36,32,128]{2,1,0:T(8,128)S(1)} %get-tuple-element.116.refs_1_, ...), custom_call_target="tpu_custom_call" | custom-call | flops 20000000 | bytes 8000000 | tf_op jit(solution)/shard_map/inner/pallas_call | solution.py:911
  45.7 0.0 collective-permute-done.11.refs_10_
  45.8 2.5 %collective-permute-done.10.refs_9_ = f32[96,128]{1,0:T(8,128)S(1)} collective-permute-done((f32[96,128]{1,0:T(8,128)S(1)}, f32[96,128]{1,0:T(8,128)S(1)}, u32[]{:S(2)}, u32[]{:S(2)}) %collective-permute-start.10) | collective-permute-done | bytes 49184 | tf_op jit(solution)/shard_map/ppermute | solution.py:793
  48.3 1.8 %edges.5 = (f32[18,48,128]{2,1,0:T(8,128)S(1)}, f32[4096,128]{1,0:T(8,128)}, f32[4,9,16,256]{3,2,1,0:T(8,128)}, f32[4,18,16,256]{3,2,1,0:T(8,128)}) custom-call(f32[4096,128]{1,0:T(8,128)S(1)} %get-tuple-element.115.refs_0_, f32[36,32,128]{2,1,0:T(8,128)S(1)} %get-tuple-element.116.refs_1_, ...), custom_call_target="tpu_custom_call", output_to_operand_aliasing={{0}: (16, {}), {1}: (17, {})} | custom-call | tf_op jit(solution)/shard_map/edges/pallas_call | solution.py:938
  (12 shorter events, 0.1 us)
Async XLA Ops:
  0.6 5.0 %copy-start.2 = (s32[32,32,128]{2,1,0:T(8,128)S(1)}, s32[32,32,128]{2,1,0:T(8,128)}, u32[]{:S(2)}) copy-start(s32[32,32,128]{2,1,0:T(8,128)} %material.1) | copy-start | bytes 1572868
  0.6 5.0 %copy-start = (f32[4,32,32,128]{3,2,1,0:T(8,128)S(1)}, f32[4,32,32,128]{3,2,1,0:T(8,128)}, u32[]{:S(2)}) copy-start(f32[4,32,32,128]{3,2,1,0:T(8,128)} %state.1) | copy-start | bytes 6291460
  3.6 5.6 %collective-permute-start = (f32[136,128]{1,0:T(8,128)S(1)}, f32[136,128]{1,0:T(8,128)S(1)}, u32[]{:S(2)}, u32[]{:S(2)}) collective-permute-start(f32[136,128]{1,0:T(8,128)S(1)} %get-tuple-element.76), channel_id=1, source_target_pairs={{1,2},{2,1},{5,6},{6,5},{9,10},{10,9},{13,14},{14,13},{17,18},{18,... | collective-permute-start | bytes 208904 | tf_op jit(solution)/shard_map/ppermute | solution.py:793
  5.6 3.7 %collective-permute-start.1 = (f32[136,128]{1,0:T(8,128)S(1)}, f32[136,128]{1,0:T(8,128)S(1)}, u32[]{:S(2)}, u32[]{:S(2)}) collective-permute-start(f32[136,128]{1,0:T(8,128)S(1)} %get-tuple-element.77), channel_id=1, source_target_pairs={{0,1},{2,3},{1,0},{3,2},{4,5},{6,7},{5,4},{7,6},{8,9},{10,11},{9,8... | collective-permute-start | bytes 208904 | tf_op jit(solution)/shard_map/ppermute | solution.py:793
  5.7 7.5 %copy-start.1 = (f32[4,18,16,256]{3,2,1,0:T(8,128)S(1)}, f32[4,18,16,256]{3,2,1,0:T(8,128)}, u32[]{:S(2)}) copy-start(f32[4,18,16,256]{3,2,1,0:T(8,128)} %refs_2_.3) | copy-start | bytes 3538948
  9.3 6.3 %collective-permute-start.3 = (f32[128,128]{1,0:T(8,128)S(1)}, f32[128,128]{1,0:T(8,128)S(1)}, u32[]{:S(2)}, u32[]{:S(2)}) collective-permute-start(f32[128,128]{1,0:T(8,128)S(1)} %maximum_dynamic-update-slice_fusion.1), channel_id=1, source_target_pairs={{0,4},{8,12},{16,20},{24,28},{4,0},{12,8},{20,16},{28,24},{1,5},{9... | collective-permute-start | bytes 196616 | tf_op jit(solution)/shard_map/ppermute | solution.py:793
  10.9 7.0 %collective-permute-start.2 = (f32[128,128]{1,0:T(8,128)S(1)}, f32[128,128]{1,0:T(8,128)S(1)}, u32[]{:S(2)}, u32[]{:S(2)}) collective-permute-start(f32[128,128]{1,0:T(8,128)S(1)} %maximum_dynamic-update-slice_fusion), channel_id=1, source_target_pairs={{4,8},{12,16},{20,24},{8,4},{16,12},{24,20},{5,9},{13,17},{21,25},... | collective-permute-start | bytes 196616 | tf_op jit(solution)/shard_map/ppermute | solution.py:793
  19.6 5.5 %collective-permute-start.4 = (f32[104,128]{1,0:T(8,128)S(1)}, f32[104,128]{1,0:T(8,128)S(1)}, u32[]{:S(2)}, u32[]{:S(2)}) collective-permute-start(f32[104,128]{1,0:T(8,128)S(1)} %get-tuple-element.96), channel_id=1, source_target_pairs={{1,2},{2,1},{5,6},{6,5},{9,10},{10,9},{13,14},{14,13},{17,18},{18,... | collective-permute-start | bytes 159752 | tf_op jit(solution)/shard_map/ppermute | solution.py:793
  21.6 3.5 %collective-permute-start.5 = (f32[104,128]{1,0:T(8,128)S(1)}, f32[104,128]{1,0:T(8,128)S(1)}, u32[]{:S(2)}, u32[]{:S(2)}) collective-permute-start(f32[104,128]{1,0:T(8,128)S(1)} %get-tuple-element.97), channel_id=1, source_target_pairs={{0,1},{2,3},{1,0},{3,2},{4,5},{6,7},{5,4},{7,6},{8,9},{10,11},{9,8... | collective-permute-start | bytes 159752 | tf_op jit(solution)/shard_map/ppermute | solution.py:793
  25.1 4.8 %collective-permute-start.7 = (f32[96,128]{1,0:T(8,128)S(1)}, f32[96,128]{1,0:T(8,128)S(1)}, u32[]{:S(2)}, u32[]{:S(2)}) collective-permute-start(f32[96,128]{1,0:T(8,128)S(1)} %maximum_dynamic-update-slice_fusion.3), channel_id=1, source_target_pairs={{0,4},{8,12},{16,20},{24,28},{4,0},{12,8},{20,16},{28,24},{1,5},{9... | collective-permute-start | bytes 147464 | tf_op jit(solution)/shard_map/ppermute | solution.py:793
  25.7 6.9 %collective-permute-start.6 = (f32[96,128]{1,0:T(8,128)S(1)}, f32[96,128]{1,0:T(8,128)S(1)}, u32[]{:S(2)}, u32[]{:S(2)}) collective-permute-start(f32[96,128]{1,0:T(8,128)S(1)} %maximum_dynamic-update-slice_fusion.2), channel_id=1, source_target_pairs={{4,8},{12,16},{20,24},{8,4},{16,12},{24,20},{5,9},{13,17},{21,25},... | collective-permute-start | bytes 147464 | tf_op jit(solution)/shard_map/ppermute | solution.py:793
  34.3 5.5 %collective-permute-start.8 = (f32[104,128]{1,0:T(8,128)S(1)}, f32[104,128]{1,0:T(8,128)S(1)}, u32[]{:S(2)}, u32[]{:S(2)}) collective-permute-start(f32[104,128]{1,0:T(8,128)S(1)} %get-tuple-element.118), channel_id=1, source_target_pairs={{1,2},{2,1},{5,6},{6,5},{9,10},{10,9},{13,14},{14,13},{17,18},{18,... | collective-permute-start | bytes 159752 | tf_op jit(solution)/shard_map/ppermute | solution.py:793
  36.2 3.5 %collective-permute-start.9 = (f32[104,128]{1,0:T(8,128)S(1)}, f32[104,128]{1,0:T(8,128)S(1)}, u32[]{:S(2)}, u32[]{:S(2)}) collective-permute-start(f32[104,128]{1,0:T(8,128)S(1)} %get-tuple-element.119), channel_id=1, source_target_pairs={{0,1},{2,3},{1,0},{3,2},{4,5},{6,7},{5,4},{7,6},{8,9},{10,11},{9,8... | collective-permute-start | bytes 159752 | tf_op jit(solution)/shard_map/ppermute | solution.py:793
  39.8 5.9 %collective-permute-start.11 = (f32[96,128]{1,0:T(8,128)S(1)}, f32[96,128]{1,0:T(8,128)S(1)}, u32[]{:S(2)}, u32[]{:S(2)}) collective-permute-start(f32[96,128]{1,0:T(8,128)S(1)} %maximum_dynamic-update-slice_fusion.5), channel_id=1, source_target_pairs={{0,4},{8,12},{16,20},{24,28},{4,0},{12,8},{20,16},{28,24},{1,5},{9... | collective-permute-start | bytes 147464 | tf_op jit(solution)/shard_map/ppermute | solution.py:793
  41.4 6.9 %collective-permute-start.10 = (f32[96,128]{1,0:T(8,128)S(1)}, f32[96,128]{1,0:T(8,128)S(1)}, u32[]{:S(2)}, u32[]{:S(2)}) collective-permute-start(f32[96,128]{1,0:T(8,128)S(1)} %maximum_dynamic-update-slice_fusion.4), channel_id=1, source_target_pairs={{4,8},{12,16},{20,24},{8,4},{16,12},{24,20},{5,9},{13,17},{21,25},... | collective-permute-start | bytes 147464 | tf_op jit(solution)/shard_map/ppermute | solution.py:793

commit v9 on v8

--- a/solution.py
+++ b/solution.py
@@ -143,14 +143,17 @@
             water_out[aligned(row), :] = value
 
 
-def brick_velocity(g, water_out, stress, load_v, bricks_out, load_hb):
+def brick_velocity(g, tiles, water_out, stress, load_v, bricks_out, load_hb):
     lane = lane_ids()
     depth = lane % g.edge
     zero = jnp.zeros((SUB, LANES), jnp.float32)
     across, ny = g.across, g.ny
 
-    @pl.loop(0, g.xtiles)
-    def _(ti):
+    turns, tile = tiles
+
+    @pl.loop(0, turns)
+    def _(turn):
+        ti = tile(turn)
         row = pl.multiple_of(SUB * ti, SUB)
         here = pl.ds(pl.multiple_of(row + PAD, SUB), SUB)
 
@@ -175,41 +178,51 @@
             bricks_out[key, pl.ds(row, SUB), :] = value
 
 
-def brick_stress(g, ti, first, bricks, memory, params, speed, tops, store):
+def window(row):
+    def read(ref, key, offset=0):
+        return ref[key, pl.ds(row + offset, SUB), :]
+
+    return read
+
+
+def both_faces(g):
+    lower = lax.broadcasted_iota(jnp.int32, (SUB, LANES), 0) < SUB // 2
+
+    def read(ref, key, offset=0):
+        return jnp.where(lower, ref[key, pl.ds(offset, SUB), :], ref[key, pl.ds(g.nx - SUB + offset, SUB), :])
+
+    return read
+
+
+def brick_stress(g, read, bricks, memory, params, speed, tops, store):
     edge, across = g.edge, g.across
     wide = across + 2
     lane = lane_ids()
     depth = lane % edge
-    row = SUB * ti if isinstance(ti, int) else pl.multiple_of(SUB * ti, SUB)
-    here, inner = aligned(row), aligned(row + PAD)
     rolled = []
     for field in (VX, VY, VZ):
-        values = [speed[field * wide + tj, inner, :] for tj in range(wide)]
+        values = [read(speed, field * wide + tj, PAD) for tj in range(wide)]
         rolled.append([(roll(value, edge), roll(value, -edge)) for value in values])
     for tj in range(across):
         ys = [g.yper * tj + k for k in range(g.yper)]
         dx, dy, dz, speeds = [], [], [], []
         for field in (VX, VY, VZ):
             key = field * wide + 1 + tj
-            value = speed[key, inner, :]
+            value = read(speed, key, PAD)
             speeds.append(value)
-            dx.append(speed[key, pl.ds(row + PAD + 1, SUB), :] - speed[key, pl.ds(row + PAD - 1, SUB), :])
+            dx.append(read(speed, key, PAD + 1) - read(speed, key, PAD - 1))
             dy.append(along_y(g, rolled[field], tj + 1, lane))
             dz.append(along_z(g, value, shifted_top(g, tops[field], ys, lane), depth))
         strain = [dx[0], dy[1], dz[2], dy[0] + dx[1], dz[0] + dx[2], dz[1] + dy[2]]
         dilation = strain[0] + strain[1] + strain[2]
 
         def param(c):
-            return params[c * across + tj, here, :]
+            return read(params, c * across + tj)
 
         lame, shear = param(LAME) * dilation, param(SHEAR)
         spring_lame, spring_shear = param(SPRING_LAME) * dilation, param(SPRING_SHEAR)
         retain = [param(RETAIN + l) for l in range(3)]
         half_shear, half_spring = 0.5 * shear, 0.5 * spring_shear
-        slot = g.slot(ti, tj)
-        rows, lanes = g.place(ti, tj)
-        if first:
-            alive = param(ALIVE)
         stresses, memories = [], {}
         for comp in range(6):
             if comp < 3:
@@ -221,30 +234,29 @@
             summed = None
             for l in range(3):
                 place = 6 * l + comp
-                if first:
-                    old = memory[slot, place, rows, lanes] * alive
-                else:
-                    old = memory[place * across + tj, here, :]
+                old = read(memory, place * across + tj)
                 new = relaxed + retain[l] * (old - relaxed)
                 memories[place] = new
                 summed = new if summed is None else summed + new
-            stresses.append(bricks[(XX + comp) * across + tj, here, :] + elastic - summed)
-        store(ti, tj, here, inner, speeds, stresses, memories)
-
-
-def store_planes(g, bricks_out, memory_out, stress):
-    def store(ti, tj, here, inner, speeds, stresses, memories):
-        for place, value in memories.items():
-            memory_out[place * g.across + tj, here, :] = value
-        for comp, value in enumerate(stresses):
-            bricks_out[(XX + comp) * g.across + tj, here, :] = value
-            stress[comp * g.across + tj, inner, :] = value
+            stresses.append(read(bricks, (XX + comp) * across + tj) + elastic - summed)
+        store(tj, speeds, stresses, memories)
+
+
+def store_planes(g, bricks_out, memory_out, stress, pieces):
+    def store(tj, speeds, stresses, memories):
+        for first, count, row in pieces:
+            for place, value in memories.items():
+                memory_out[place * g.across + tj, pl.ds(row, count), :] = value[first : first + count, :]
+            for comp, value in enumerate(stresses):
+                value = value[first : first + count, :]
+                bricks_out[(XX + comp) * g.across + tj, pl.ds(row, count), :] = value
+                stress[comp * g.across + tj, pl.ds(row + PAD, count), :] = value
 
     return store
 
 
-def store_slots(g, motion, memory):
-    def store(ti, tj, here, inner, speeds, stresses, memories):
+def store_slots(g, motion, memory, ti):
+    def store(tj, speeds, stresses, memories):
         slot = g.slot(ti, tj)
         rows, lanes = g.place(ti, tj)
         for place, value in memories.items():
@@ -328,8 +340,8 @@
 
 
 def first_kernel(
-    g, live_hbm, table_hbm, water_hbm, material_hbm, motion_hbm, kinds_hbm, odd,
-    water_out, bricks_out, params, columns, row_far, row_near, col_far, col_near,
+    g, live_hbm, table_hbm, water_hbm, material_hbm, motion_hbm, kinds_hbm, memory_hbm, odd,
+    water_out, bricks_out, params, columns, memory, row_far, row_near, col_far, col_near,
     stress, pressure, ux_edge, uy_edge, material_x, material_y, motion, kinds, live, table, sems, *buffers,
 ):
     nx, ny, across = g.nx, g.ny, g.across
@@ -349,6 +361,7 @@
         fetch(material_hbm.at[x], material_x.at[side])
         fetch(water_hbm.at[2, :, pl.ds(y, SUB), :], uy_edge.at[side])
         fetch(material_hbm.at[:, pl.ds(y, SUB), :], material_y.at[side])
+    fetch(memory_hbm, memory)
     lane = lane_ids()
     zero_stress_pads(g, stress)
     copies[0].wait()
@@ -398,8 +411,8 @@
     def load_hb(ti, tj):
         return params[HB * across + tj, aligned(SUB * ti), :]
 
-    brick_velocity(g, water_out, stress, load_v, bricks_out, load_hb)
-    for copy in copies[5:]:
+    brick_velocity(g, (g.xtiles, lambda turn: turn), water_out, stress, load_v, bricks_out, load_hb)
+    for copy in copies[5:-1]:
         copy.wait()
 
     def rows_of(side, t):
@@ -412,12 +425,26 @@
         lambda side, t: pick(columns[0], material_y[(*rows_of(side, t), slice(None))]),
     )
     pack(g, water_out, bricks_out, params, edges, odd, buffers, (row_far, row_near, col_far, col_near), True)
+    copies[-1].wait()
 
 
 def first_water_kernel(
-    g, pressure, row_first, row_last, bricks, columns, state, material, water_out, first_same, last_same, hb_water, hk_water, press
+    g, pressure, row_first, row_last, bricks, columns, state, material, params, memory,
+    water_out, first_same, last_same, hb_water, hk_water, memory_out, press,
 ):
     nx, ny = g.nx, g.ny
+
+    @pl.loop(0, 18)
+    def _(place):
+        results = []
+        for ti in range(g.xtiles):
+            for tj in range(g.across):
+                rows, lanes = g.place(ti, tj)
+                value = memory[g.slot(ti, tj), place, rows, lanes]
+                results.append((tj, ti, value * params[ALIVE * g.across + tj, pl.ds(SUB * ti, SUB), :]))
+        for tj, ti, value in results:
+            memory_out[place * g.across + tj, pl.ds(SUB * ti, SUB), :] = value
+
     zero_press_pads(g, press)
 
     @pl.loop(0, nx // 2)
@@ -581,17 +608,22 @@
                 own = bricks[ALONG_Y[c] * across + tj, pl.ds(SUB * ti, SUB), :]
                 speed[c * wide + halo, here, :] = roll(column, far - (3 + c) * edge) + their_hb * roll(own, far - near)
 
-    store = store_slots(g, motion_buf, memory_buf) if last else store_planes(g, bricks_out, memory_out, stress)
-
-    @pl.loop(1, g.xtiles - 1)
-    def _(ti):
-        row = pl.multiple_of(SUB * ti, SUB)
+    windows = g.xtiles - 2 if last else g.xtiles
+
+    @pl.loop(0, windows)
+    def _(turn):
+        if last:
+            row = pl.multiple_of(SUB * (turn + 1), SUB)
+            store = store_slots(g, motion_buf, memory_buf, turn + 1)
+        else:
+            row = 2 + SUB * turn - 4 * (turn // (g.xtiles - 1))
+            store = store_planes(g, bricks_out, memory_out, stress, [(0, SUB, row)])
         tops = (
             lambda y: water[pl.ds(plane + row * ny + y, SUB, stride=ny), :],
             lambda y: uy[pl.ds(row * py + PAD + y, SUB, stride=py), :],
             lambda y: water[pl.ds(3 * plane + row * ny + y, SUB, stride=ny), :],
         )
-        brick_stress(g, ti, first, bricks, memory, params, speed, tops, store)
+        brick_stress(g, window(row), bricks, memory, params, speed, tops, store)
 
     def layer(x):
         results = []
@@ -615,6 +647,14 @@
     if last:
         for copy in copies:
             copy.wait()
+    else:
+        def load_v(field, ti, tj):
+            return speed[field * wide + 1 + tj, aligned(PAD + SUB * ti), :]
+
+        def load_hb(ti, tj):
+            return params[HB * across + tj, aligned(SUB * ti), :]
+
+        brick_velocity(g, (g.xtiles - 2, lambda turn: turn + 1), water_out, stress, load_v, bricks_out, load_hb)
 
 
 def water_stress(g, x, t, dx, water, uy, speed, hk_water, lane, top_pick):
@@ -731,19 +771,29 @@
     for (key, x), value in speed_rows.items():
         speed[key, pl.ds(PAD + x, 1), :] = value
 
-    store = store_slots(g, motion_buf, memory_buf) if last else store_planes(g, bricks_out, memory_out, stress)
-
-    @pl.loop(0, 2)
-    def _(turn):
-        ti = turn * (g.xtiles - 1)
-        row = pl.multiple_of(SUB * ti, SUB)
-        above = pl.multiple_of((1 + SUB * turn) * ny, SUB)
-        tops = (
+    def tops_at(row, above):
+        return (
             lambda y: ux[pl.ds(above + y, SUB, stride=ny), :],
             lambda y: uy[pl.ds(row * py + PAD + y, SUB, stride=py), :],
             lambda y: water[pl.ds(3 * plane + row * ny + y, SUB, stride=ny), :],
         )
-        brick_stress(g, ti, first, bricks, memory, params, speed, tops, store)
+
+    if last:
+        @pl.loop(0, 2)
+        def _(turn):
+            ti = turn * (g.xtiles - 1)
+            row = pl.multiple_of(SUB * ti, SUB)
+            tops = tops_at(row, pl.multiple_of((1 + SUB * turn) * ny, SUB))
+            brick_stress(g, window(row), bricks, memory, params, speed, tops, store_slots(g, motion_buf, memory_buf, ti))
+    else:
+        lower = lax.broadcasted_iota(jnp.int32, (SUB, LANES), 0) < SUB // 2
+
+        def joined(one, other):
+            return lambda y: jnp.where(lower, one(y), other(y))
+
+        tops = [joined(*pair) for pair in zip(tops_at(0, ny), tops_at(nx - SUB, (1 + SUB) * ny))]
+        store = store_planes(g, bricks_out, memory_out, stress, [(0, SUB // 2, 0), (SUB // 2, SUB // 2, nx - SUB // 2)])
+        brick_stress(g, both_faces(g), bricks, memory, params, speed, tops, store)
 
     if last:
         for ti in (0, g.xtiles - 1):
@@ -784,7 +834,7 @@
             lambda side, t: uy[pl.ds(SUB * t * py + PAD + side * (ny - 1), SUB, stride=py), :],
             lambda side, t: hb_water[column(side, t), :],
         )
-        brick_velocity(g, water_out, stress, load_v, bricks_out, load_hb)
+        brick_velocity(g, (2, lambda turn: turn * (g.xtiles - 1)), water_out, stress, load_v, bricks_out, load_hb)
         pack(g, water_out, bricks_out, params, faces, odd, buffers, sends, False)
 
 
@@ -847,13 +897,14 @@
     press = buffer(nx + 2, ny + 2 * PAD, nz)
     stress = buffer(6 * across, nx + 2 * PAD, LANES)
     work = pl.CostEstimate(flops=20_000_000, bytes_accessed=8_000_000, transcendentals=0)
-    water, bricks, coefficients, columns, *sends = pl.pallas_call(
+    water, bricks, coefficients, columns, memory, *sends = pl.pallas_call(
         functools.partial(first_kernel, g),
         out_shape=[
             buffer(4 * plane, nz), f32(9 * across, nx, LANES), f32(9 * across, nx, LANES), f32(8, SUB, LANES),
+            buffer(*brick_relaxation_memory.shape),
         ] + messages(True),
-        in_specs=[hbm] * 6 + [vmem],
-        out_specs=[vmem] * 8,
+        in_specs=[hbm] * 7 + [vmem],
+        out_specs=[vmem] * 9,
         scratch_shapes=[
             stress,
             buffer(nx, ny, nz),
@@ -865,28 +916,33 @@
             pltpu.VMEM(brick_cell_material.shape, jnp.int32),
             pltpu.SMEM(brick_live.shape, jnp.int32),
             pltpu.SMEM(material_table.shape, jnp.float32),
-            pltpu.SemaphoreType.DMA((13,)),
+            pltpu.SemaphoreType.DMA((14,)),
         ]
         + message_buffers(("row", "col"), True),
         compiler_params=params,
         name="first_bricks",
-    )(*pinned(brick_live, material_table, water_state, water_material, brick_velocity_stress, brick_cell_material), odd)
+    )(
+        *pinned(
+            brick_live, material_table, water_state, water_material,
+            brick_velocity_stress, brick_cell_material, brick_relaxation_memory,
+        ),
+        odd,
+    )
 
     def passed(*messages):
         return [buffer(*message.shape) for message in messages]
 
-    water, sends[0], sends[1], hb_water, hk_water = pl.pallas_call(
+    water, sends[0], sends[1], hb_water, hk_water, memory = pl.pallas_call(
         functools.partial(first_water_kernel, g),
-        out_shape=[buffer(4 * plane, nz)] + passed(*sends[:2]) + [f32(plane, nz), f32(plane, nz)],
-        in_specs=[vmem] * 7,
-        out_specs=[vmem] * 5,
+        out_shape=[buffer(4 * plane, nz)] + passed(*sends[:2]) + [f32(plane, nz), f32(plane, nz), f32(18 * across, nx, LANES)],
+        in_specs=[vmem] * 9,
+        out_specs=[vmem] * 6,
         input_output_aliases={0: 0, 1: 1, 2: 2},
         scratch_shapes=[press],
         compiler_params=params,
         cost_estimate=work,
         name="first_water",
-    )(*held(water, *sends[:2], bricks, columns, water_state, water_material))
-    memory = brick_relaxation_memory
+    )(*held(water, *sends[:2], bricks, columns, water_state, water_material, coefficients, memory))
     col_const, row_const = (), ()
     uy_shape = (nx * (ny + 2 * PAD), nz)
     speed_shape = (3 * (across + 2), nx + 2 * PAD, LANES)

time: 50.3 us -> 50 us (level)
  waiting for transfers between devices: 11.3 us -> 8.53 us
  starting transfers between devices: 15.9 us -> 17.2 us
  Pallas kernels: 21.8 us -> 22.9 us
    ppermute x12, waiting for transfers between devices: 11.3 us -> 8.53 us  [swap(): return lax.ppermute(value, axis, pairs + [(j, i) for i, j in pairs])]
    pallas_call x3, Pallas kernels: 7.11 us -> 9.1 us  [body(): pl.pallas_call(functools.partial(inner_kernel, g, first, last), out_shape...]
    ppermute x12, starting transfers between devices: 15.9 us -> 17.2 us  [swap(): return lax.ppermute(value, axis, pairs + [(j, i) for i, j in pairs])]
    pallas_call x3, Pallas kernels: 5.26 us -> 4.15 us  [body(): pl.pallas_call(functools.partial(edge_kernel, g, first, last), out_shape=...]
  transfers between devices with their start and end apart: 12 -> 12, of which waited for: 6 -> 6; matrix products, arithmetic and copies ran while one was open for 0% -> 0% of each run, Pallas kernels for 27% -> 32%
where the time goes in v9:
time: 50 us; the launch traced here: 49.7 us
  Pallas kernels  22.9 us (46%)
  starting transfers between devices  17.2 us (34%)
  waiting for transfers between devices  8.53 us (17%)
  between operations  0.84 us (2%)
    ppermute x12, starting transfers between devices, swap(): return lax.ppermute(value, axis, pairs + [(j, i) for i, j in pairs])  17.2 us
    pallas_call x3, Pallas kernels, body(): pl.pallas_call(functools.partial(inner_kernel, g, first, last), out_shape...  9.1 us
    ppermute x12, waiting for transfers between devices, swap(): return lax.ppermute(value, axis, pairs + [(j, i) for i, j in pairs])  8.53 us
    pallas_call x3, Pallas kernels, body(): pl.pallas_call(functools.partial(edge_kernel, g, first, last), out_shape=...  4.15 us
    pallas_call x1, Pallas kernels, body(): pl.pallas_call(functools.partial(first_water_kernel, g), out_shape=[buffe...  3.5 us
    pallas_call x2, Pallas kernels, body(): pl.pallas_call(functools.partial(edge_water_kernel, g), out_shape=[buffer...  3.3 us
    pallas_call x1, Pallas kernels, body(): pl.pallas_call(functools.partial(first_kernel, g), out_shape=[buffer(4 *...  2.83 us
  transfers between devices with their start and end apart: 12, of which 6 were waited for; matrix products, arithmetic and copies ran while one was open for 0% of the time, Pallas kernels for 32%

profile of v9, /device:TPU:10, one launch (start us, length us, event | category | flops | bytes accessed | tf_op | source)
XLA Modules:
  0.0 49.7 jit_solution(13298116346821135544)
XLA Ops:
  0.6 0.1 add_convert_fusion
  0.7 0.1 broadcast_in_dim.2.odd.refs_6_
  0.8 0.0 copy-start
  0.8 0.0 copy-start.1
  0.8 2.8 %first_bricks.1 = (f32[4096,128]{1,0:T(8,128)S(1)}, f32[36,32,128]{2,1,0:T(8,128)S(1)}, f32[36,32,128]{2,1,0:T(8,128)S(1)}, f32[8,8,128]{2,1,0:T(8,128)S(1)}, f3...) custom-call(s32[4]{0:T(128)} %live_hbm.1, ...), custom_call_target="tpu_custom_call" | custom-call | tf_op jit(solution)/shard_map/first_bricks/pallas_call | solution.py:900
  3.6 1.9 %collective-permute-start = (f32[136,128]{1,0:T(8,128)S(1)}, f32[136,128]{1,0:T(8,128)S(1)}, u32[]{:S(2)}, u32[]{:S(2)}) collective-permute-start(f32[136,128]{1,0:T(8,128)S(1)} %get-tuple-element.80), channel_id=1, source_target_pairs={{1,2},{2,1},{5,6},{6,5},{9,10},{10,9},{13,14},{14,13},{17,18},{18,... | collective-permute-start | bytes 208904 | tf_op jit(solution)/shard_map/ppermute | solution.py:843
  5.6 0.1 collective-permute-start.1
  5.6 0.0 copy-done
  5.6 0.0 copy-done.1
  5.7 3.5 %first_water.1 = (f32[4096,128]{1,0:T(8,128)S(1)}, f32[128,128]{1,0:T(8,128)S(1)}, f32[128,128]{1,0:T(8,128)S(1)}, f32[1024,128]{1,0:T(8,128)S(1)}, f32[1024,128]{1,0:T(8,128)S(1)}, /*index=5*/f32[72,32,128]{2,1,0:T(8,128)S(1)}) custom-call(f32[4096,128]{1,0:T(8,128)S(1)} %get-tuple-element.69.pressure, ...), custom_call_target="tpu_custom_call", output_to_operand_aliasing={{0}: (0, {}), {1}: (1, {}), {2}: (2, {})} | custom-call | flops 20000000 | bytes 8000000 | tf_op jit(solution)/shard_map/first_water/pallas_call | solution.py:935
  9.2 0.1 collective-permute-done.refs_7_
  9.3 0.0 collective-permute-done.1.refs_8_
  9.3 1.6 %collective-permute-start.3 = (f32[128,128]{1,0:T(8,128)S(1)}, f32[128,128]{1,0:T(8,128)S(1)}, u32[]{:S(2)}, u32[]{:S(2)}) collective-permute-start(f32[128,128]{1,0:T(8,128)S(1)} %maximum_dynamic-update-slice_fusion.1), channel_id=1, source_target_pairs={{0,4},{8,12},{16,20},{24,28},{4,0},{12,8},{20,16},{28,24},{1,5},{9... | collective-permute-start | bytes 196616 | tf_op jit(solution)/shard_map/ppermute | solution.py:843
  10.9 2.3 %collective-permute-start.2 = (f32[128,128]{1,0:T(8,128)S(1)}, f32[128,128]{1,0:T(8,128)S(1)}, u32[]{:S(2)}, u32[]{:S(2)}) collective-permute-start(f32[128,128]{1,0:T(8,128)S(1)} %maximum_dynamic-update-slice_fusion), channel_id=1, source_target_pairs={{4,8},{12,16},{20,24},{8,4},{16,12},{24,20},{5,9},{13,17},{21,25},... | collective-permute-start | bytes 196616 | tf_op jit(solution)/shard_map/ppermute | solution.py:843
  13.2 3.4 %inner.3 = (f32[1536,128]{1,0:T(8,128)S(1)}, f32[18,48,128]{2,1,0:T(8,128)S(1)}, f32[4096,128]{1,0:T(8,128)S(1)}, f32[34,48,128]{2,1,0:T(8,128)S(1)}, f32[24,48,...) custom-call(f32[4096,128]{1,0:T(8,128)S(1)} %get-tuple-element.76.refs_0_.wat, ...), custom_call_target="tpu_custom_call" | custom-call | flops 20000000 | bytes 8000000 | tf_op jit(solution)/shard_map/inner/pallas_call | solution.py:967
  16.5 0.0 collective-permute-done.3.refs_10_
  16.6 1.4 %collective-permute-done.2.refs_9_ = f32[128,128]{1,0:T(8,128)S(1)} collective-permute-done((f32[128,128]{1,0:T(8,128)S(1)}, f32[128,128]{1,0:T(8,128)S(1)}, u32[]{:S(2)}, u32[]{:S(2)}) %collective-permute-start.2) | collective-permute-done | bytes 65568 | tf_op jit(solution)/shard_map/ppermute | solution.py:843
  17.9 1.2 %edges.3 = (f32[18,48,128]{2,1,0:T(8,128)S(1)}, f32[4096,128]{1,0:T(8,128)S(1)}, f32[34,48,128]{2,1,0:T(8,128)S(1)}, f32[24,48,128]{2,1,0:T(8,128)S(1)}, f32[36,...) custom-call(f32[4096,128]{1,0:T(8,128)S(1)} %get-tuple-element.76.re, ...), custom_call_target="tpu_custom_call", output_to_operand_aliasing={{0}: (12, {}), {1}: (13, {}), {2}: (14, {}), {3}: (15, {}),... | custom-call | tf_op jit(solution)/shard_map/edges/pallas_call | solution.py:994
  19.1 2.2 %collective-permute-start.4 = (f32[104,128]{1,0:T(8,128)S(1)}, f32[104,128]{1,0:T(8,128)S(1)}, u32[]{:S(2)}, u32[]{:S(2)}) collective-permute-start(f32[104,128]{1,0:T(8,128)S(1)} %get-tuple-element.100), channel_id=1, source_target_pairs={{1,2},{2,1},{5,6},{6,5},{9,10},{10,9},{13,14},{14,13},{17,18},{18,... | collective-permute-start | bytes 159752 | tf_op jit(solution)/shard_map/ppermute | solution.py:843
  21.3 0.1 collective-permute-start.5
  21.3 1.6 %edge_water.2 = (f32[4096,128]{1,0:T(8,128)S(1)}, f32[96,128]{1,0:T(8,128)S(1)}, f32[96,128]{1,0:T(8,128)S(1)}) custom-call(f32[4096,128]{1,0:T(8,128)S(1)} %get-tuple-element.91.same, f32[96,128]{1,0:T(8,128)S(1)} %get-tuple-element.92.row_first, ...), custom_call_target="tpu_custom_call", output_to_operand_aliasing={{0}: (0, {}), {1}: (1, {}), {2}: (2, {})} | custom-call | flops 20000000 | bytes 8000000 | tf_op jit(solution)/shard_map/edge_water/pallas_call | solution.py:1017
  23.0 1.6 %collective-permute-done.4.refs_7_ = f32[104,128]{1,0:T(8,128)S(1)} collective-permute-done((f32[104,128]{1,0:T(8,128)S(1)}, f32[104,128]{1,0:T(8,128)S(1)}, u32[]{:S(2)}, u32[]{:S(2)}) %collective-permute-start.4) | collective-permute-done | bytes 53280 | tf_op jit(solution)/shard_map/ppermute | solution.py:843
  24.6 0.0 collective-permute-done.5.refs_8_
  24.6 1.4 %collective-permute-start.7 = (f32[96,128]{1,0:T(8,128)S(1)}, f32[96,128]{1,0:T(8,128)S(1)}, u32[]{:S(2)}, u32[]{:S(2)}) collective-permute-start(f32[96,128]{1,0:T(8,128)S(1)} %maximum_dynamic-update-slice_fusion.3), channel_id=1, source_target_pairs={{0,4},{8,12},{16,20},{24,28},{4,0},{12,8},{20,16},{28,24},{1,5},{9... | collective-permute-start | bytes 147464 | tf_op jit(solution)/shard_map/ppermute | solution.py:843
  26.0 1.9 %collective-permute-start.6 = (f32[96,128]{1,0:T(8,128)S(1)}, f32[96,128]{1,0:T(8,128)S(1)}, u32[]{:S(2)}, u32[]{:S(2)}) collective-permute-start(f32[96,128]{1,0:T(8,128)S(1)} %maximum_dynamic-update-slice_fusion.2), channel_id=1, source_target_pairs={{4,8},{12,16},{20,24},{8,4},{16,12},{24,20},{5,9},{13,17},{21,25},... | collective-permute-start | bytes 147464 | tf_op jit(solution)/shard_map/ppermute | solution.py:843
  27.9 3.3 %inner.4 = (f32[1536,128]{1,0:T(8,128)S(1)}, f32[18,48,128]{2,1,0:T(8,128)S(1)}, f32[4096,128]{1,0:T(8,128)S(1)}, f32[34,48,128]{2,1,0:T(8,128)S(1)}, f32[24,48,...) custom-call(f32[4096,128]{1,0:T(8,128)S(1)} %get-tuple-element.97.refs_0_.water, ...), custom_call_target="tpu_custom_call" | custom-call | flops 20000000 | bytes 8000000 | tf_op jit(solution)/shard_map/inner/pallas_call | solution.py:967
  31.2 0.0 collective-permute-done.7.refs_10_
  31.2 1.6 %collective-permute-done.6.refs_9_ = f32[96,128]{1,0:T(8,128)S(1)} collective-permute-done((f32[96,128]{1,0:T(8,128)S(1)}, f32[96,128]{1,0:T(8,128)S(1)}, u32[]{:S(2)}, u32[]{:S(2)}) %collective-permute-start.6) | collective-permute-done | bytes 49184 | tf_op jit(solution)/shard_map/ppermute | solution.py:843
  32.8 1.2 %edges.4 = (f32[18,48,128]{2,1,0:T(8,128)S(1)}, f32[4096,128]{1,0:T(8,128)S(1)}, f32[34,48,128]{2,1,0:T(8,128)S(1)}, f32[24,48,128]{2,1,0:T(8,128)S(1)}, f32[36,...) custom-call(f32[4096,128]{1,0:T(8,128)S(1)} %get-tuple-element.97.re, ...), custom_call_target="tpu_custom_call", output_to_operand_aliasing={{0}: (13, {}), {1}: (14, {}), {2}: (15, {}), {3}: (16, {}),... | custom-call | tf_op jit(solution)/shard_map/edges/pallas_call | solution.py:994
  34.0 2.4 %collective-permute-start.8 = (f32[104,128]{1,0:T(8,128)S(1)}, f32[104,128]{1,0:T(8,128)S(1)}, u32[]{:S(2)}, u32[]{:S(2)}) collective-permute-start(f32[104,128]{1,0:T(8,128)S(1)} %get-tuple-element.122), channel_id=1, source_target_pairs={{1,2},{2,1},{5,6},{6,5},{9,10},{10,9},{13,14},{14,13},{17,18},{18,... | collective-permute-start | bytes 159752 | tf_op jit(solution)/shard_map/ppermute | solution.py:843
  36.4 0.1 collective-permute-start.9
  36.4 1.7 %edge_water.3 = (f32[4096,128]{1,0:T(8,128)S(1)}, f32[96,128]{1,0:T(8,128)S(1)}, f32[96,128]{1,0:T(8,128)S(1)}) custom-call(f32[4096,128]{1,0:T(8,128)S(1)} %get-tuple-element.113.same, f32[96,128]{1,0:T(8,128)S(1)} %get-tuple-element.114.row_first, ...), custom_call_target="tpu_custom_call", output_to_operand_aliasing={{0}: (0, {}), {1}: (1, {}), {2}: (2, {})} | custom-call | flops 20000000 | bytes 8000000 | tf_op jit(solution)/shard_map/edge_water/pallas_call | solution.py:1017
  38.1 1.3 %collective-permute-done.8.refs_7_ = f32[104,128]{1,0:T(8,128)S(1)} collective-permute-done((f32[104,128]{1,0:T(8,128)S(1)}, f32[104,128]{1,0:T(8,128)S(1)}, u32[]{:S(2)}, u32[]{:S(2)}) %collective-permute-start.8) | collective-permute-done | bytes 53280 | tf_op jit(solution)/shard_map/ppermute | solution.py:843
  39.5 0.0 collective-permute-done.9.refs_8_
  39.5 1.5 %collective-permute-start.11 = (f32[96,128]{1,0:T(8,128)S(1)}, f32[96,128]{1,0:T(8,128)S(1)}, u32[]{:S(2)}, u32[]{:S(2)}) collective-permute-start(f32[96,128]{1,0:T(8,128)S(1)} %maximum_dynamic-update-slice_fusion.5), channel_id=1, source_target_pairs={{0,4},{8,12},{16,20},{24,28},{4,0},{12,8},{20,16},{28,24},{1,5},{9... | collective-permute-start | bytes 147464 | tf_op jit(solution)/shard_map/ppermute | solution.py:843
  41.0 1.9 %collective-permute-start.10 = (f32[96,128]{1,0:T(8,128)S(1)}, f32[96,128]{1,0:T(8,128)S(1)}, u32[]{:S(2)}, u32[]{:S(2)}) collective-permute-start(f32[96,128]{1,0:T(8,128)S(1)} %maximum_dynamic-update-slice_fusion.4), channel_id=1, source_target_pairs={{4,8},{12,16},{20,24},{8,4},{16,12},{24,20},{5,9},{13,17},{21,25},... | collective-permute-start | bytes 147464 | tf_op jit(solution)/shard_map/ppermute | solution.py:843
  42.9 2.4 %inner.5 = (f32[1536,128]{1,0:T(8,128)S(1)}, f32[18,48,128]{2,1,0:T(8,128)S(1)}, f32[4096,128]{1,0:T(8,128)}, f32[1024,128]{1,0:T(8,128)S(1)}, f32[4,9,16,256]{3...) custom-call(f32[4096,128]{1,0:T(8,128)S(1)} %get-tuple-element.119.refs_0_, f32[36,32,128]{2,1,0:T(8,128)S(1)} %get-tuple-element.120.refs_1_, ...), custom_call_target="tpu_custom_call" | custom-call | flops 20000000 | bytes 8000000 | tf_op jit(solution)/shard_map/inner/pallas_call | solution.py:967
  45.4 0.0 collective-permute-done.11.refs_10_
  45.4 2.5 %collective-permute-done.10.refs_9_ = f32[96,128]{1,0:T(8,128)S(1)} collective-permute-done((f32[96,128]{1,0:T(8,128)S(1)}, f32[96,128]{1,0:T(8,128)S(1)}, u32[]{:S(2)}, u32[]{:S(2)}) %collective-permute-start.10) | collective-permute-done | bytes 49184 | tf_op jit(solution)/shard_map/ppermute | solution.py:843
  47.9 1.8 %edges.5 = (f32[18,48,128]{2,1,0:T(8,128)S(1)}, f32[4096,128]{1,0:T(8,128)}, f32[4,9,16,256]{3,2,1,0:T(8,128)}, f32[4,18,16,256]{3,2,1,0:T(8,128)}) custom-call(f32[4096,128]{1,0:T(8,128)S(1)} %get-tuple-element.119.refs_0_, f32[36,32,128]{2,1,0:T(8,128)S(1)} %get-tuple-element.120.refs_1_, ...), custom_call_target="tpu_custom_call", output_to_operand_aliasing={{0}: (16, {}), {1}: (17, {})} | custom-call | tf_op jit(solution)/shard_map/edges/pallas_call | solution.py:994
  (12 shorter events, 0.1 us)
Async XLA Ops:
  0.8 4.8 %copy-start = (f32[4,32,32,128]{3,2,1,0:T(8,128)S(1)}, f32[4,32,32,128]{3,2,1,0:T(8,128)}, u32[]{:S(2)}) copy-start(f32[4,32,32,128]{3,2,1,0:T(8,128)} %state.1) | copy-start | bytes 6291460
  0.8 4.9 %copy-start.1 = (s32[32,32,128]{2,1,0:T(8,128)S(1)}, s32[32,32,128]{2,1,0:T(8,128)}, u32[]{:S(2)}) copy-start(s32[32,32,128]{2,1,0:T(8,128)} %material.1) | copy-start | bytes 1572868
  3.6 5.6 %collective-permute-start = (f32[136,128]{1,0:T(8,128)S(1)}, f32[136,128]{1,0:T(8,128)S(1)}, u32[]{:S(2)}, u32[]{:S(2)}) collective-permute-start(f32[136,128]{1,0:T(8,128)S(1)} %get-tuple-element.80), channel_id=1, source_target_pairs={{1,2},{2,1},{5,6},{6,5},{9,10},{10,9},{13,14},{14,13},{17,18},{18,... | collective-permute-start | bytes 208904 | tf_op jit(solution)/shard_map/ppermute | solution.py:843
  5.6 3.7 %collective-permute-start.1 = (f32[136,128]{1,0:T(8,128)S(1)}, f32[136,128]{1,0:T(8,128)S(1)}, u32[]{:S(2)}, u32[]{:S(2)}) collective-permute-start(f32[136,128]{1,0:T(8,128)S(1)} %get-tuple-element.81), channel_id=1, source_target_pairs={{0,1},{2,3},{1,0},{3,2},{4,5},{6,7},{5,4},{7,6},{8,9},{10,11},{9,8... | collective-permute-start | bytes 208904 | tf_op jit(solution)/shard_map/ppermute | solution.py:843
  9.3 7.3 %collective-permute-start.3 = (f32[128,128]{1,0:T(8,128)S(1)}, f32[128,128]{1,0:T(8,128)S(1)}, u32[]{:S(2)}, u32[]{:S(2)}) collective-permute-start(f32[128,128]{1,0:T(8,128)S(1)} %maximum_dynamic-update-slice_fusion.1), channel_id=1, source_target_pairs={{0,4},{8,12},{16,20},{24,28},{4,0},{12,8},{20,16},{28,24},{1,5},{9... | collective-permute-start | bytes 196616 | tf_op jit(solution)/shard_map/ppermute | solution.py:843
  10.9 7.0 %collective-permute-start.2 = (f32[128,128]{1,0:T(8,128)S(1)}, f32[128,128]{1,0:T(8,128)S(1)}, u32[]{:S(2)}, u32[]{:S(2)}) collective-permute-start(f32[128,128]{1,0:T(8,128)S(1)} %maximum_dynamic-update-slice_fusion), channel_id=1, source_target_pairs={{4,8},{12,16},{20,24},{8,4},{16,12},{24,20},{5,9},{13,17},{21,25},... | collective-permute-start | bytes 196616 | tf_op jit(solution)/shard_map/ppermute | solution.py:843
  19.1 5.5 %collective-permute-start.4 = (f32[104,128]{1,0:T(8,128)S(1)}, f32[104,128]{1,0:T(8,128)S(1)}, u32[]{:S(2)}, u32[]{:S(2)}) collective-permute-start(f32[104,128]{1,0:T(8,128)S(1)} %get-tuple-element.100), channel_id=1, source_target_pairs={{1,2},{2,1},{5,6},{6,5},{9,10},{10,9},{13,14},{14,13},{17,18},{18,... | collective-permute-start | bytes 159752 | tf_op jit(solution)/shard_map/ppermute | solution.py:843
  21.3 3.3 %collective-permute-start.5 = (f32[104,128]{1,0:T(8,128)S(1)}, f32[104,128]{1,0:T(8,128)S(1)}, u32[]{:S(2)}, u32[]{:S(2)}) collective-permute-start(f32[104,128]{1,0:T(8,128)S(1)} %get-tuple-element.101), channel_id=1, source_target_pairs={{0,1},{2,3},{1,0},{3,2},{4,5},{6,7},{5,4},{7,6},{8,9},{10,11},{9,8... | collective-permute-start | bytes 159752 | tf_op jit(solution)/shard_map/ppermute | solution.py:843
  24.6 6.6 %collective-permute-start.7 = (f32[96,128]{1,0:T(8,128)S(1)}, f32[96,128]{1,0:T(8,128)S(1)}, u32[]{:S(2)}, u32[]{:S(2)}) collective-permute-start(f32[96,128]{1,0:T(8,128)S(1)} %maximum_dynamic-update-slice_fusion.3), channel_id=1, source_target_pairs={{0,4},{8,12},{16,20},{24,28},{4,0},{12,8},{20,16},{28,24},{1,5},{9... | collective-permute-start | bytes 147464 | tf_op jit(solution)/shard_map/ppermute | solution.py:843
  26.0 6.9 %collective-permute-start.6 = (f32[96,128]{1,0:T(8,128)S(1)}, f32[96,128]{1,0:T(8,128)S(1)}, u32[]{:S(2)}, u32[]{:S(2)}) collective-permute-start(f32[96,128]{1,0:T(8,128)S(1)} %maximum_dynamic-update-slice_fusion.2), channel_id=1, source_target_pairs={{4,8},{12,16},{20,24},{8,4},{16,12},{24,20},{5,9},{13,17},{21,25},... | collective-permute-start | bytes 147464 | tf_op jit(solution)/shard_map/ppermute | solution.py:843
  34.0 5.5 %collective-permute-start.8 = (f32[104,128]{1,0:T(8,128)S(1)}, f32[104,128]{1,0:T(8,128)S(1)}, u32[]{:S(2)}, u32[]{:S(2)}) collective-permute-start(f32[104,128]{1,0:T(8,128)S(1)} %get-tuple-element.122), channel_id=1, source_target_pairs={{1,2},{2,1},{5,6},{6,5},{9,10},{10,9},{13,14},{14,13},{17,18},{18,... | collective-permute-start | bytes 159752 | tf_op jit(solution)/shard_map/ppermute | solution.py:843
  36.4 3.1 %collective-permute-start.9 = (f32[104,128]{1,0:T(8,128)S(1)}, f32[104,128]{1,0:T(8,128)S(1)}, u32[]{:S(2)}, u32[]{:S(2)}) collective-permute-start(f32[104,128]{1,0:T(8,128)S(1)} %get-tuple-element.123), channel_id=1, source_target_pairs={{0,1},{2,3},{1,0},{3,2},{4,5},{6,7},{5,4},{7,6},{8,9},{10,11},{9,8... | collective-permute-start | bytes 159752 | tf_op jit(solution)/shard_map/ppermute | solution.py:843
  39.5 5.9 %collective-permute-start.11 = (f32[96,128]{1,0:T(8,128)S(1)}, f32[96,128]{1,0:T(8,128)S(1)}, u32[]{:S(2)}, u32[]{:S(2)}) collective-permute-start(f32[96,128]{1,0:T(8,128)S(1)} %maximum_dynamic-update-slice_fusion.5), channel_id=1, source_target_pairs={{0,4},{8,12},{16,20},{24,28},{4,0},{12,8},{20,16},{28,24},{1,5},{9... | collective-permute-start | bytes 147464 | tf_op jit(solution)/shard_map/ppermute | solution.py:843
  41.0 6.9 %collective-permute-start.10 = (f32[96,128]{1,0:T(8,128)S(1)}, f32[96,128]{1,0:T(8,128)S(1)}, u32[]{:S(2)}, u32[]{:S(2)}) collective-permute-start(f32[96,128]{1,0:T(8,128)S(1)} %maximum_dynamic-update-slice_fusion.4), channel_id=1, source_target_pairs={{4,8},{12,16},{20,24},{8,4},{16,12},{24,20},{5,9},{13,17},{21,25},... | collective-permute-start | bytes 147464 | tf_op jit(solution)/shard_map/ppermute | solution.py:843

commit v10 on v9

--- a/solution.py
+++ b/solution.py
@@ -771,35 +771,6 @@
     for (key, x), value in speed_rows.items():
         speed[key, pl.ds(PAD + x, 1), :] = value
 
-    def tops_at(row, above):
-        return (
-            lambda y: ux[pl.ds(above + y, SUB, stride=ny), :],
-            lambda y: uy[pl.ds(row * py + PAD + y, SUB, stride=py), :],
-            lambda y: water[pl.ds(3 * plane + row * ny + y, SUB, stride=ny), :],
-        )
-
-    if last:
-        @pl.loop(0, 2)
-        def _(turn):
-            ti = turn * (g.xtiles - 1)
-            row = pl.multiple_of(SUB * ti, SUB)
-            tops = tops_at(row, pl.multiple_of((1 + SUB * turn) * ny, SUB))
-            brick_stress(g, window(row), bricks, memory, params, speed, tops, store_slots(g, motion_buf, memory_buf, ti))
-    else:
-        lower = lax.broadcasted_iota(jnp.int32, (SUB, LANES), 0) < SUB // 2
-
-        def joined(one, other):
-            return lambda y: jnp.where(lower, one(y), other(y))
-
-        tops = [joined(*pair) for pair in zip(tops_at(0, ny), tops_at(nx - SUB, (1 + SUB) * ny))]
-        store = store_planes(g, bricks_out, memory_out, stress, [(0, SUB // 2, 0), (SUB // 2, SUB // 2, nx - SUB // 2)])
-        brick_stress(g, both_faces(g), bricks, memory, params, speed, tops, store)
-
-    if last:
-        for ti in (0, g.xtiles - 1):
-            send(slots_of(g, motion_buf, ti), slots_of(g, motion_hbm, ti))
-            send(slots_of(g, memory_buf, ti), slots_of(g, memory_hbm, ti))
-
     for pair, (x, layer) in enumerate(((0, 1), (nx - 2, 2 * SUB - 1))):
         for step in range(2):
             for t in range(g.ytiles):
@@ -816,6 +787,32 @@
     if last:
         for pair, x in enumerate((0, nx - 2)):
             send(press_buf.at[pl.ds(2 * pair * ny, 2 * ny), :], water_hbm.at[pl.ds(x * ny, 2 * ny), :])
+
+    def tops_at(row, above):
+        return (
+            lambda y: ux[pl.ds(above + y, SUB, stride=ny), :],
+            lambda y: uy[pl.ds(row * py + PAD + y, SUB, stride=py), :],
+            lambda y: water[pl.ds(3 * plane + row * ny + y, SUB, stride=ny), :],
+        )
+
+    if last:
+        for turn, ti in enumerate((0, g.xtiles - 1)):
+            tops = tops_at(SUB * ti, (1 + SUB * turn) * ny)
+            store = store_slots(g, motion_buf, memory_buf, ti)
+            brick_stress(g, window(SUB * ti), bricks, memory, params, speed, tops, store)
+            send(slots_of(g, memory_buf, ti), slots_of(g, memory_hbm, ti))
+            send(slots_of(g, motion_buf, ti), slots_of(g, motion_hbm, ti))
+    else:
+        lower = lax.broadcasted_iota(jnp.int32, (SUB, LANES), 0) < SUB // 2
+
+        def joined(one, other):
+            return lambda y: jnp.where(lower, one(y), other(y))
+
+        tops = [joined(*pair) for pair in zip(tops_at(0, ny), tops_at(nx - SUB, (1 + SUB) * ny))]
+        store = store_planes(g, bricks_out, memory_out, stress, [(0, SUB // 2, 0), (SUB // 2, SUB // 2, nx - SUB // 2)])
+        brick_stress(g, both_faces(g), bricks, memory, params, speed, tops, store)
+
+    if last:
         for copy in copies:
             copy.wait()
     else:

time: 50 us -> 49.8 us (level)
  no operation moved by 1% of the time
where the time goes in v10:
time: 49.8 us; the launch traced here: 49.5 us
  Pallas kernels  22.7 us (46%)
  starting transfers between devices  17.2 us (35%)
  waiting for transfers between devices  8.53 us (17%)
  between operations  0.84 us (2%)
    ppermute x12, starting transfers between devices, swap(): return lax.ppermute(value, axis, pairs + [(j, i) for i, j in pairs])  17.2 us
    pallas_call x3, Pallas kernels, body(): pl.pallas_call(functools.partial(inner_kernel, g, first, last), out_shape...  9.1 us
    ppermute x12, waiting for transfers between devices, swap(): return lax.ppermute(value, axis, pairs + [(j, i) for i, j in pairs])  8.53 us
    pallas_call x3, Pallas kernels, body(): pl.pallas_call(functools.partial(edge_kernel, g, first, last), out_shape=...  3.97 us
    pallas_call x1, Pallas kernels, body(): pl.pallas_call(functools.partial(first_water_kernel, g), out_shape=[buffe...  3.5 us
    pallas_call x2, Pallas kernels, body(): pl.pallas_call(functools.partial(edge_water_kernel, g), out_shape=[buffer...  3.3 us
    pallas_call x1, Pallas kernels, body(): pl.pallas_call(functools.partial(first_kernel, g), out_shape=[buffer(4 *...  2.83 us
  transfers between devices with their start and end apart: 12, of which 6 were waited for; matrix products, arithmetic and copies ran while one was open for 0% of the time, Pallas kernels for 32%

profile of v10, /device:TPU:10, one launch (start us, length us, event | category | flops | bytes accessed | tf_op | source)
XLA Modules:
  0.0 49.5 jit_solution(11537237438361640260)
XLA Ops:
  0.6 0.1 add_convert_fusion
  0.7 0.1 broadcast_in_dim.2.odd.refs_6_
  0.8 0.0 copy-start
  0.8 0.0 copy-start.1
  0.8 2.8 %first_bricks.1 = (f32[4096,128]{1,0:T(8,128)S(1)}, f32[36,32,128]{2,1,0:T(8,128)S(1)}, f32[36,32,128]{2,1,0:T(8,128)S(1)}, f32[8,8,128]{2,1,0:T(8,128)S(1)}, f3...) custom-call(s32[4]{0:T(128)} %live_hbm.1, ...), custom_call_target="tpu_custom_call" | custom-call | tf_op jit(solution)/shard_map/first_bricks/pallas_call | solution.py:897
  3.6 1.9 %collective-permute-start = (f32[136,128]{1,0:T(8,128)S(1)}, f32[136,128]{1,0:T(8,128)S(1)}, u32[]{:S(2)}, u32[]{:S(2)}) collective-permute-start(f32[136,128]{1,0:T(8,128)S(1)} %get-tuple-element.80), channel_id=1, source_target_pairs={{1,2},{2,1},{5,6},{6,5},{9,10},{10,9},{13,14},{14,13},{17,18},{18,... | collective-permute-start | bytes 208904 | tf_op jit(solution)/shard_map/ppermute | solution.py:840
  5.6 0.1 collective-permute-start.1
  5.6 0.0 copy-done
  5.6 0.0 copy-done.1
  5.7 3.5 %first_water.1 = (f32[4096,128]{1,0:T(8,128)S(1)}, f32[128,128]{1,0:T(8,128)S(1)}, f32[128,128]{1,0:T(8,128)S(1)}, f32[1024,128]{1,0:T(8,128)S(1)}, f32[1024,128]{1,0:T(8,128)S(1)}, /*index=5*/f32[72,32,128]{2,1,0:T(8,128)S(1)}) custom-call(f32[4096,128]{1,0:T(8,128)S(1)} %get-tuple-element.69.pressure, ...), custom_call_target="tpu_custom_call", output_to_operand_aliasing={{0}: (0, {}), {1}: (1, {}), {2}: (2, {})} | custom-call | flops 20000000 | bytes 8000000 | tf_op jit(solution)/shard_map/first_water/pallas_call | solution.py:932
  9.2 0.1 collective-permute-done.refs_7_
  9.3 0.0 collective-permute-done.1.refs_8_
  9.3 1.6 %collective-permute-start.3 = (f32[128,128]{1,0:T(8,128)S(1)}, f32[128,128]{1,0:T(8,128)S(1)}, u32[]{:S(2)}, u32[]{:S(2)}) collective-permute-start(f32[128,128]{1,0:T(8,128)S(1)} %maximum_dynamic-update-slice_fusion.1), channel_id=1, source_target_pairs={{0,4},{8,12},{16,20},{24,28},{4,0},{12,8},{20,16},{28,24},{1,5},{9... | collective-permute-start | bytes 196616 | tf_op jit(solution)/shard_map/ppermute | solution.py:840
  10.9 2.3 %collective-permute-start.2 = (f32[128,128]{1,0:T(8,128)S(1)}, f32[128,128]{1,0:T(8,128)S(1)}, u32[]{:S(2)}, u32[]{:S(2)}) collective-permute-start(f32[128,128]{1,0:T(8,128)S(1)} %maximum_dynamic-update-slice_fusion), channel_id=1, source_target_pairs={{4,8},{12,16},{20,24},{8,4},{16,12},{24,20},{5,9},{13,17},{21,25},... | collective-permute-start | bytes 196616 | tf_op jit(solution)/shard_map/ppermute | solution.py:840
  13.2 3.4 %inner.3 = (f32[1536,128]{1,0:T(8,128)S(1)}, f32[18,48,128]{2,1,0:T(8,128)S(1)}, f32[4096,128]{1,0:T(8,128)S(1)}, f32[34,48,128]{2,1,0:T(8,128)S(1)}, f32[24,48,...) custom-call(f32[4096,128]{1,0:T(8,128)S(1)} %get-tuple-element.76.refs_0_.wat, ...), custom_call_target="tpu_custom_call" | custom-call | flops 20000000 | bytes 8000000 | tf_op jit(solution)/shard_map/inner/pallas_call | solution.py:964
  16.5 0.0 collective-permute-done.3.refs_10_
  16.6 1.4 %collective-permute-done.2.refs_9_ = f32[128,128]{1,0:T(8,128)S(1)} collective-permute-done((f32[128,128]{1,0:T(8,128)S(1)}, f32[128,128]{1,0:T(8,128)S(1)}, u32[]{:S(2)}, u32[]{:S(2)}) %collective-permute-start.2) | collective-permute-done | bytes 65568 | tf_op jit(solution)/shard_map/ppermute | solution.py:840
  17.9 1.2 %edges.3 = (f32[18,48,128]{2,1,0:T(8,128)S(1)}, f32[4096,128]{1,0:T(8,128)S(1)}, f32[34,48,128]{2,1,0:T(8,128)S(1)}, f32[24,48,128]{2,1,0:T(8,128)S(1)}, f32[36,...) custom-call(f32[4096,128]{1,0:T(8,128)S(1)} %get-tuple-element.76.re, ...), custom_call_target="tpu_custom_call", output_to_operand_aliasing={{0}: (12, {}), {1}: (13, {}), {2}: (14, {}), {3}: (15, {}),... | custom-call | tf_op jit(solution)/shard_map/edges/pallas_call | solution.py:991
  19.1 2.2 %collective-permute-start.4 = (f32[104,128]{1,0:T(8,128)S(1)}, f32[104,128]{1,0:T(8,128)S(1)}, u32[]{:S(2)}, u32[]{:S(2)}) collective-permute-start(f32[104,128]{1,0:T(8,128)S(1)} %get-tuple-element.100), channel_id=1, source_target_pairs={{1,2},{2,1},{5,6},{6,5},{9,10},{10,9},{13,14},{14,13},{17,18},{18,... | collective-permute-start | bytes 159752 | tf_op jit(solution)/shard_map/ppermute | solution.py:840
  21.3 0.1 collective-permute-start.5
  21.4 1.6 %edge_water.2 = (f32[4096,128]{1,0:T(8,128)S(1)}, f32[96,128]{1,0:T(8,128)S(1)}, f32[96,128]{1,0:T(8,128)S(1)}) custom-call(f32[4096,128]{1,0:T(8,128)S(1)} %get-tuple-element.91.same, f32[96,128]{1,0:T(8,128)S(1)} %get-tuple-element.92.row_first, ...), custom_call_target="tpu_custom_call", output_to_operand_aliasing={{0}: (0, {}), {1}: (1, {}), {2}: (2, {})} | custom-call | flops 20000000 | bytes 8000000 | tf_op jit(solution)/shard_map/edge_water/pallas_call | solution.py:1014
  23.0 1.6 %collective-permute-done.4.refs_7_ = f32[104,128]{1,0:T(8,128)S(1)} collective-permute-done((f32[104,128]{1,0:T(8,128)S(1)}, f32[104,128]{1,0:T(8,128)S(1)}, u32[]{:S(2)}, u32[]{:S(2)}) %collective-permute-start.4) | collective-permute-done | bytes 53280 | tf_op jit(solution)/shard_map/ppermute | solution.py:840
  24.6 0.0 collective-permute-done.5.refs_8_
  24.6 1.4 %collective-permute-start.7 = (f32[96,128]{1,0:T(8,128)S(1)}, f32[96,128]{1,0:T(8,128)S(1)}, u32[]{:S(2)}, u32[]{:S(2)}) collective-permute-start(f32[96,128]{1,0:T(8,128)S(1)} %maximum_dynamic-update-slice_fusion.3), channel_id=1, source_target_pairs={{0,4},{8,12},{16,20},{24,28},{4,0},{12,8},{20,16},{28,24},{1,5},{9... | collective-permute-start | bytes 147464 | tf_op jit(solution)/shard_map/ppermute | solution.py:840
  26.0 1.9 %collective-permute-start.6 = (f32[96,128]{1,0:T(8,128)S(1)}, f32[96,128]{1,0:T(8,128)S(1)}, u32[]{:S(2)}, u32[]{:S(2)}) collective-permute-start(f32[96,128]{1,0:T(8,128)S(1)} %maximum_dynamic-update-slice_fusion.2), channel_id=1, source_target_pairs={{4,8},{12,16},{20,24},{8,4},{16,12},{24,20},{5,9},{13,17},{21,25},... | collective-permute-start | bytes 147464 | tf_op jit(solution)/shard_map/ppermute | solution.py:840
  27.9 3.3 %inner.4 = (f32[1536,128]{1,0:T(8,128)S(1)}, f32[18,48,128]{2,1,0:T(8,128)S(1)}, f32[4096,128]{1,0:T(8,128)S(1)}, f32[34,48,128]{2,1,0:T(8,128)S(1)}, f32[24,48,...) custom-call(f32[4096,128]{1,0:T(8,128)S(1)} %get-tuple-element.97.refs_0_.water, ...), custom_call_target="tpu_custom_call" | custom-call | flops 20000000 | bytes 8000000 | tf_op jit(solution)/shard_map/inner/pallas_call | solution.py:964
  31.2 0.0 collective-permute-done.7.refs_10_
  31.2 1.6 %collective-permute-done.6.refs_9_ = f32[96,128]{1,0:T(8,128)S(1)} collective-permute-done((f32[96,128]{1,0:T(8,128)S(1)}, f32[96,128]{1,0:T(8,128)S(1)}, u32[]{:S(2)}, u32[]{:S(2)}) %collective-permute-start.6) | collective-permute-done | bytes 49184 | tf_op jit(solution)/shard_map/ppermute | solution.py:840
  32.9 1.2 %edges.4 = (f32[18,48,128]{2,1,0:T(8,128)S(1)}, f32[4096,128]{1,0:T(8,128)S(1)}, f32[34,48,128]{2,1,0:T(8,128)S(1)}, f32[24,48,128]{2,1,0:T(8,128)S(1)}, f32[36,...) custom-call(f32[4096,128]{1,0:T(8,128)S(1)} %get-tuple-element.97.re, ...), custom_call_target="tpu_custom_call", output_to_operand_aliasing={{0}: (13, {}), {1}: (14, {}), {2}: (15, {}), {3}: (16, {}),... | custom-call | tf_op jit(solution)/shard_map/edges/pallas_call | solution.py:991
  34.0 2.4 %collective-permute-start.8 = (f32[104,128]{1,0:T(8,128)S(1)}, f32[104,128]{1,0:T(8,128)S(1)}, u32[]{:S(2)}, u32[]{:S(2)}) collective-permute-start(f32[104,128]{1,0:T(8,128)S(1)} %get-tuple-element.122), channel_id=1, source_target_pairs={{1,2},{2,1},{5,6},{6,5},{9,10},{10,9},{13,14},{14,13},{17,18},{18,... | collective-permute-start | bytes 159752 | tf_op jit(solution)/shard_map/ppermute | solution.py:840
  36.4 0.1 collective-permute-start.9
  36.5 1.7 %edge_water.3 = (f32[4096,128]{1,0:T(8,128)S(1)}, f32[96,128]{1,0:T(8,128)S(1)}, f32[96,128]{1,0:T(8,128)S(1)}) custom-call(f32[4096,128]{1,0:T(8,128)S(1)} %get-tuple-element.113.same, f32[96,128]{1,0:T(8,128)S(1)} %get-tuple-element.114.row_first, ...), custom_call_target="tpu_custom_call", output_to_operand_aliasing={{0}: (0, {}), {1}: (1, {}), {2}: (2, {})} | custom-call | flops 20000000 | bytes 8000000 | tf_op jit(solution)/shard_map/edge_water/pallas_call | solution.py:1014
  38.2 1.3 %collective-permute-done.8.refs_7_ = f32[104,128]{1,0:T(8,128)S(1)} collective-permute-done((f32[104,128]{1,0:T(8,128)S(1)}, f32[104,128]{1,0:T(8,128)S(1)}, u32[]{:S(2)}, u32[]{:S(2)}) %collective-permute-start.8) | collective-permute-done | bytes 53280 | tf_op jit(solution)/shard_map/ppermute | solution.py:840
  39.5 0.0 collective-permute-done.9.refs_8_
  39.5 1.5 %collective-permute-start.11 = (f32[96,128]{1,0:T(8,128)S(1)}, f32[96,128]{1,0:T(8,128)S(1)}, u32[]{:S(2)}, u32[]{:S(2)}) collective-permute-start(f32[96,128]{1,0:T(8,128)S(1)} %maximum_dynamic-update-slice_fusion.5), channel_id=1, source_target_pairs={{0,4},{8,12},{16,20},{24,28},{4,0},{12,8},{20,16},{28,24},{1,5},{9... | collective-permute-start | bytes 147464 | tf_op jit(solution)/shard_map/ppermute | solution.py:840
  41.0 1.9 %collective-permute-start.10 = (f32[96,128]{1,0:T(8,128)S(1)}, f32[96,128]{1,0:T(8,128)S(1)}, u32[]{:S(2)}, u32[]{:S(2)}) collective-permute-start(f32[96,128]{1,0:T(8,128)S(1)} %maximum_dynamic-update-slice_fusion.4), channel_id=1, source_target_pairs={{4,8},{12,16},{20,24},{8,4},{16,12},{24,20},{5,9},{13,17},{21,25},... | collective-permute-start | bytes 147464 | tf_op jit(solution)/shard_map/ppermute | solution.py:840
  43.0 2.4 %inner.5 = (f32[1536,128]{1,0:T(8,128)S(1)}, f32[18,48,128]{2,1,0:T(8,128)S(1)}, f32[4096,128]{1,0:T(8,128)}, f32[1024,128]{1,0:T(8,128)S(1)}, f32[4,9,16,256]{3...) custom-call(f32[4096,128]{1,0:T(8,128)S(1)} %get-tuple-element.119.refs_0_, f32[36,32,128]{2,1,0:T(8,128)S(1)} %get-tuple-element.120.refs_1_, ...), custom_call_target="tpu_custom_call" | custom-call | flops 20000000 | bytes 8000000 | tf_op jit(solution)/shard_map/inner/pallas_call | solution.py:964
  45.4 0.0 collective-permute-done.11.refs_10_
  45.4 2.5 %collective-permute-done.10.refs_9_ = f32[96,128]{1,0:T(8,128)S(1)} collective-permute-done((f32[96,128]{1,0:T(8,128)S(1)}, f32[96,128]{1,0:T(8,128)S(1)}, u32[]{:S(2)}, u32[]{:S(2)}) %collective-permute-start.10) | collective-permute-done | bytes 49184 | tf_op jit(solution)/shard_map/ppermute | solution.py:840
  47.9 1.6 %edges.5 = (f32[18,48,128]{2,1,0:T(8,128)S(1)}, f32[4096,128]{1,0:T(8,128)}, f32[4,9,16,256]{3,2,1,0:T(8,128)}, f32[4,18,16,256]{3,2,1,0:T(8,128)}) custom-call(f32[4096,128]{1,0:T(8,128)S(1)} %get-tuple-element.119.refs_0_, f32[36,32,128]{2,1,0:T(8,128)S(1)} %get-tuple-element.120.refs_1_, ...), custom_call_target="tpu_custom_call", output_to_operand_aliasing={{0}: (16, {}), {1}: (17, {})} | custom-call | tf_op jit(solution)/shard_map/edges/pallas_call | solution.py:991
  (12 shorter events, 0.1 us)
Async XLA Ops:
  0.8 4.8 %copy-start = (f32[4,32,32,128]{3,2,1,0:T(8,128)S(1)}, f32[4,32,32,128]{3,2,1,0:T(8,128)}, u32[]{:S(2)}) copy-start(f32[4,32,32,128]{3,2,1,0:T(8,128)} %state.1) | copy-start | bytes 6291460
  0.8 4.9 %copy-start.1 = (s32[32,32,128]{2,1,0:T(8,128)S(1)}, s32[32,32,128]{2,1,0:T(8,128)}, u32[]{:S(2)}) copy-start(s32[32,32,128]{2,1,0:T(8,128)} %material.1) | copy-start | bytes 1572868
  3.6 5.6 %collective-permute-start = (f32[136,128]{1,0:T(8,128)S(1)}, f32[136,128]{1,0:T(8,128)S(1)}, u32[]{:S(2)}, u32[]{:S(2)}) collective-permute-start(f32[136,128]{1,0:T(8,128)S(1)} %get-tuple-element.80), channel_id=1, source_target_pairs={{1,2},{2,1},{5,6},{6,5},{9,10},{10,9},{13,14},{14,13},{17,18},{18,... | collective-permute-start | bytes 208904 | tf_op jit(solution)/shard_map/ppermute | solution.py:840
  5.6 3.7 %collective-permute-start.1 = (f32[136,128]{1,0:T(8,128)S(1)}, f32[136,128]{1,0:T(8,128)S(1)}, u32[]{:S(2)}, u32[]{:S(2)}) collective-permute-start(f32[136,128]{1,0:T(8,128)S(1)} %get-tuple-element.81), channel_id=1, source_target_pairs={{0,1},{2,3},{1,0},{3,2},{4,5},{6,7},{5,4},{7,6},{8,9},{10,11},{9,8... | collective-permute-start | bytes 208904 | tf_op jit(solution)/shard_map/ppermute | solution.py:840
  9.3 7.3 %collective-permute-start.3 = (f32[128,128]{1,0:T(8,128)S(1)}, f32[128,128]{1,0:T(8,128)S(1)}, u32[]{:S(2)}, u32[]{:S(2)}) collective-permute-start(f32[128,128]{1,0:T(8,128)S(1)} %maximum_dynamic-update-slice_fusion.1), channel_id=1, source_target_pairs={{0,4},{8,12},{16,20},{24,28},{4,0},{12,8},{20,16},{28,24},{1,5},{9... | collective-permute-start | bytes 196616 | tf_op jit(solution)/shard_map/ppermute | solution.py:840
  10.9 7.0 %collective-permute-start.2 = (f32[128,128]{1,0:T(8,128)S(1)}, f32[128,128]{1,0:T(8,128)S(1)}, u32[]{:S(2)}, u32[]{:S(2)}) collective-permute-start(f32[128,128]{1,0:T(8,128)S(1)} %maximum_dynamic-update-slice_fusion), channel_id=1, source_target_pairs={{4,8},{12,16},{20,24},{8,4},{16,12},{24,20},{5,9},{13,17},{21,25},... | collective-permute-start | bytes 196616 | tf_op jit(solution)/shard_map/ppermute | solution.py:840
  19.1 5.5 %collective-permute-start.4 = (f32[104,128]{1,0:T(8,128)S(1)}, f32[104,128]{1,0:T(8,128)S(1)}, u32[]{:S(2)}, u32[]{:S(2)}) collective-permute-start(f32[104,128]{1,0:T(8,128)S(1)} %get-tuple-element.100), channel_id=1, source_target_pairs={{1,2},{2,1},{5,6},{6,5},{9,10},{10,9},{13,14},{14,13},{17,18},{18,... | collective-permute-start | bytes 159752 | tf_op jit(solution)/shard_map/ppermute | solution.py:840
  21.3 3.3 %collective-permute-start.5 = (f32[104,128]{1,0:T(8,128)S(1)}, f32[104,128]{1,0:T(8,128)S(1)}, u32[]{:S(2)}, u32[]{:S(2)}) collective-permute-start(f32[104,128]{1,0:T(8,128)S(1)} %get-tuple-element.101), channel_id=1, source_target_pairs={{0,1},{2,3},{1,0},{3,2},{4,5},{6,7},{5,4},{7,6},{8,9},{10,11},{9,8... | collective-permute-start | bytes 159752 | tf_op jit(solution)/shard_map/ppermute | solution.py:840
  24.6 6.6 %collective-permute-start.7 = (f32[96,128]{1,0:T(8,128)S(1)}, f32[96,128]{1,0:T(8,128)S(1)}, u32[]{:S(2)}, u32[]{:S(2)}) collective-permute-start(f32[96,128]{1,0:T(8,128)S(1)} %maximum_dynamic-update-slice_fusion.3), channel_id=1, source_target_pairs={{0,4},{8,12},{16,20},{24,28},{4,0},{12,8},{20,16},{28,24},{1,5},{9... | collective-permute-start | bytes 147464 | tf_op jit(solution)/shard_map/ppermute | solution.py:840
  26.0 6.9 %collective-permute-start.6 = (f32[96,128]{1,0:T(8,128)S(1)}, f32[96,128]{1,0:T(8,128)S(1)}, u32[]{:S(2)}, u32[]{:S(2)}) collective-permute-start(f32[96,128]{1,0:T(8,128)S(1)} %maximum_dynamic-update-slice_fusion.2), channel_id=1, source_target_pairs={{4,8},{12,16},{20,24},{8,4},{16,12},{24,20},{5,9},{13,17},{21,25},... | collective-permute-start | bytes 147464 | tf_op jit(solution)/shard_map/ppermute | solution.py:840
  34.0 5.5 %collective-permute-start.8 = (f32[104,128]{1,0:T(8,128)S(1)}, f32[104,128]{1,0:T(8,128)S(1)}, u32[]{:S(2)}, u32[]{:S(2)}) collective-permute-start(f32[104,128]{1,0:T(8,128)S(1)} %get-tuple-element.122), channel_id=1, source_target_pairs={{1,2},{2,1},{5,6},{6,5},{9,10},{10,9},{13,14},{14,13},{17,18},{18,... | collective-permute-start | bytes 159752 | tf_op jit(solution)/shard_map/ppermute | solution.py:840
  36.4 3.1 %collective-permute-start.9 = (f32[104,128]{1,0:T(8,128)S(1)}, f32[104,128]{1,0:T(8,128)S(1)}, u32[]{:S(2)}, u32[]{:S(2)}) collective-permute-start(f32[104,128]{1,0:T(8,128)S(1)} %get-tuple-element.123), channel_id=1, source_target_pairs={{0,1},{2,3},{1,0},{3,2},{4,5},{6,7},{5,4},{7,6},{8,9},{10,11},{9,8... | collective-permute-start | bytes 159752 | tf_op jit(solution)/shard_map/ppermute | solution.py:840
  39.5 5.9 %collective-permute-start.11 = (f32[96,128]{1,0:T(8,128)S(1)}, f32[96,128]{1,0:T(8,128)S(1)}, u32[]{:S(2)}, u32[]{:S(2)}) collective-permute-start(f32[96,128]{1,0:T(8,128)S(1)} %maximum_dynamic-update-slice_fusion.5), channel_id=1, source_target_pairs={{0,4},{8,12},{16,20},{24,28},{4,0},{12,8},{20,16},{28,24},{1,5},{9... | collective-permute-start | bytes 147464 | tf_op jit(solution)/shard_map/ppermute | solution.py:840
  41.0 6.9 %collective-permute-start.10 = (f32[96,128]{1,0:T(8,128)S(1)}, f32[96,128]{1,0:T(8,128)S(1)}, u32[]{:S(2)}, u32[]{:S(2)}) collective-permute-start(f32[96,128]{1,0:T(8,128)S(1)} %maximum_dynamic-update-slice_fusion.4), channel_id=1, source_target_pairs={{4,8},{12,16},{20,24},{8,4},{16,12},{24,20},{5,9},{13,17},{21,25},... | collective-permute-start | bytes 147464 | tf_op jit(solution)/shard_map/ppermute | solution.py:840

commit v11 on v10

--- a/solution.py
+++ b/solution.py
@@ -134,12 +134,12 @@
                 results.append((k * g.plane + own, load_u(k, x, t) - hb * change))
         return results
 
-    turns, layer = layers
+    turns, layer, count = layers
 
     @pl.loop(0, turns)
     def _(turn):
         x = layer(turn)
-        for row, value in water_layer(x) + water_layer(x + 1):
+        for row, value in [result for step in range(count) for result in water_layer(x + step)]:
             water_out[aligned(row), :] = value
 
 
@@ -462,7 +462,7 @@
 
     water_velocity(
         g,
-        (nx // 2, lambda turn: 2 * turn),
+        (nx // 4, lambda turn: 4 * turn, 4),
         water_out,
         press,
         lambda t, x: bricks[ZZ * g.across + t, pl.ds(x, 1), :],
@@ -498,9 +498,9 @@
         layer = x - (x // (nx - SUB)) * (nx - 2 * SUB) + 1
         return ux[aligned(layer * ny + SUB * t), :]
 
-    water_layers((SUB, lambda turn: 2 * turn + (turn // (SUB // 2)) * (nx - 2 * SUB)), near_face)
+    water_layers((SUB, lambda turn: 2 * turn + (turn // (SUB // 2)) * (nx - 2 * SUB), 2), near_face)
     water_layers(
-        ((nx - 2 * SUB) // 2, lambda turn: SUB + 2 * turn),
+        ((nx - 2 * SUB) // 2, lambda turn: SUB + 2 * turn, 2),
         lambda x, t: water[aligned(plane + x * ny + SUB * t), :],
     )
 

time: 49.8 us -> 49.8 us (level)
  waiting for transfers between devices: 8.53 us -> 9.79 us
  Pallas kernels: 22.7 us -> 22.1 us
  starting transfers between devices: 17.2 us -> 16.6 us
    ppermute x12, waiting for transfers between devices: 8.53 us -> 9.79 us  [swap(): return lax.ppermute(value, axis, pairs + [(j, i) for i, j in pairs])]
    ppermute x12, starting transfers between devices: 17.2 us -> 16.6 us  [swap(): return lax.ppermute(value, axis, pairs + [(j, i) for i, j in pairs])]
    pallas_call x1, Pallas kernels: 3.5 us -> 2.91 us  [body(): pl.pallas_call(functools.partial(first_water_kernel, g), out_shape=[buffe...]
  transfers between devices with their start and end apart: 12 -> 12, of which waited for: 6 -> 6; matrix products, arithmetic and copies ran while one was open for 0% -> 0% of each run, Pallas kernels for 32% -> 31%
where the time goes in v11:
time: 49.8 us; the launch traced here: 49.5 us
  Pallas kernels  22.1 us (44%)
  starting transfers between devices  16.6 us (33%)
  waiting for transfers between devices  9.79 us (20%)
  between operations  0.84 us (2%)
    ppermute x12, starting transfers between devices, swap(): return lax.ppermute(value, axis, pairs + [(j, i) for i, j in pairs])  16.6 us
    ppermute x12, waiting for transfers between devices, swap(): return lax.ppermute(value, axis, pairs + [(j, i) for i, j in pairs])  9.79 us
    pallas_call x3, Pallas kernels, body(): pl.pallas_call(functools.partial(inner_kernel, g, first, last), out_shape...  9.1 us
    pallas_call x3, Pallas kernels, body(): pl.pallas_call(functools.partial(edge_kernel, g, first, last), out_shape=...  3.97 us
    pallas_call x2, Pallas kernels, body(): pl.pallas_call(functools.partial(edge_water_kernel, g), out_shape=[buffer...  3.3 us
    pallas_call x1, Pallas kernels, body(): pl.pallas_call(functools.partial(first_water_kernel, g), out_shape=[buffe...  2.91 us
    pallas_call x1, Pallas kernels, body(): pl.pallas_call(functools.partial(first_kernel, g), out_shape=[buffer(4 *...  2.83 us
  transfers between devices with their start and end apart: 12, of which 6 were waited for; matrix products, arithmetic and copies ran while one was open for 0% of the time, Pallas kernels for 31%

profile of v11, /device:TPU:10, one launch (start us, length us, event | category | flops | bytes accessed | tf_op | source)
XLA Modules:
  0.0 49.5 jit_solution(6953459111136278020)
XLA Ops:
  0.6 0.1 add_convert_fusion
  0.7 0.1 broadcast_in_dim.2.odd.refs_6_
  0.8 0.0 copy-start
  0.8 0.0 copy-start.1
  0.8 2.8 %first_bricks.1 = (f32[4096,128]{1,0:T(8,128)S(1)}, f32[36,32,128]{2,1,0:T(8,128)S(1)}, f32[36,32,128]{2,1,0:T(8,128)S(1)}, f32[8,8,128]{2,1,0:T(8,128)S(1)}, f3...) custom-call(s32[4]{0:T(128)} %live_hbm.1, ...), custom_call_target="tpu_custom_call" | custom-call | tf_op jit(solution)/shard_map/first_bricks/pallas_call | solution.py:897
  3.6 1.9 %collective-permute-start = (f32[136,128]{1,0:T(8,128)S(1)}, f32[136,128]{1,0:T(8,128)S(1)}, u32[]{:S(2)}, u32[]{:S(2)}) collective-permute-start(f32[136,128]{1,0:T(8,128)S(1)} %get-tuple-element.80), channel_id=1, source_target_pairs={{1,2},{2,1},{5,6},{6,5},{9,10},{10,9},{13,14},{14,13},{17,18},{18,... | collective-permute-start | bytes 208904 | tf_op jit(solution)/shard_map/ppermute | solution.py:840
  5.6 0.1 collective-permute-start.1
  5.6 0.0 copy-done
  5.6 0.0 copy-done.1
  5.7 2.9 %first_water.1 = (f32[4096,128]{1,0:T(8,128)S(1)}, f32[128,128]{1,0:T(8,128)S(1)}, f32[128,128]{1,0:T(8,128)S(1)}, f32[1024,128]{1,0:T(8,128)S(1)}, f32[1024,128]{1,0:T(8,128)S(1)}, /*index=5*/f32[72,32,128]{2,1,0:T(8,128)S(1)}) custom-call(f32[4096,128]{1,0:T(8,128)S(1)} %get-tuple-element.69.pressure, ...), custom_call_target="tpu_custom_call", output_to_operand_aliasing={{0}: (0, {}), {1}: (1, {}), {2}: (2, {})} | custom-call | flops 20000000 | bytes 8000000 | tf_op jit(solution)/shard_map/first_water/pallas_call | solution.py:932
  8.6 0.7 %collective-permute-done.refs_7_ = f32[136,128]{1,0:T(8,128)S(1)} collective-permute-done((f32[136,128]{1,0:T(8,128)S(1)}, f32[136,128]{1,0:T(8,128)S(1)}, u32[]{:S(2)}, u32[]{:S(2)}) %collective-permute-start) | collective-permute-done | bytes 69664 | tf_op jit(solution)/shard_map/ppermute | solution.py:840
  9.3 0.0 collective-permute-done.1.refs_8_
  9.3 1.6 %collective-permute-start.3 = (f32[128,128]{1,0:T(8,128)S(1)}, f32[128,128]{1,0:T(8,128)S(1)}, u32[]{:S(2)}, u32[]{:S(2)}) collective-permute-start(f32[128,128]{1,0:T(8,128)S(1)} %maximum_dynamic-update-slice_fusion.1), channel_id=1, source_target_pairs={{0,4},{8,12},{16,20},{24,28},{4,0},{12,8},{20,16},{28,24},{1,5},{9... | collective-permute-start | bytes 196616 | tf_op jit(solution)/shard_map/ppermute | solution.py:840
  10.9 2.3 %collective-permute-start.2 = (f32[128,128]{1,0:T(8,128)S(1)}, f32[128,128]{1,0:T(8,128)S(1)}, u32[]{:S(2)}, u32[]{:S(2)}) collective-permute-start(f32[128,128]{1,0:T(8,128)S(1)} %maximum_dynamic-update-slice_fusion), channel_id=1, source_target_pairs={{4,8},{12,16},{20,24},{8,4},{16,12},{24,20},{5,9},{13,17},{21,25},... | collective-permute-start | bytes 196616 | tf_op jit(solution)/shard_map/ppermute | solution.py:840
  13.2 3.4 %inner.3 = (f32[1536,128]{1,0:T(8,128)S(1)}, f32[18,48,128]{2,1,0:T(8,128)S(1)}, f32[4096,128]{1,0:T(8,128)S(1)}, f32[34,48,128]{2,1,0:T(8,128)S(1)}, f32[24,48,...) custom-call(f32[4096,128]{1,0:T(8,128)S(1)} %get-tuple-element.76.refs_0_.wat, ...), custom_call_target="tpu_custom_call" | custom-call | flops 20000000 | bytes 8000000 | tf_op jit(solution)/shard_map/inner/pallas_call | solution.py:964
  16.5 0.0 collective-permute-done.3.refs_10_
  16.6 1.4 %collective-permute-done.2.refs_9_ = f32[128,128]{1,0:T(8,128)S(1)} collective-permute-done((f32[128,128]{1,0:T(8,128)S(1)}, f32[128,128]{1,0:T(8,128)S(1)}, u32[]{:S(2)}, u32[]{:S(2)}) %collective-permute-start.2) | collective-permute-done | bytes 65568 | tf_op jit(solution)/shard_map/ppermute | solution.py:840
  17.9 1.2 %edges.3 = (f32[18,48,128]{2,1,0:T(8,128)S(1)}, f32[4096,128]{1,0:T(8,128)S(1)}, f32[34,48,128]{2,1,0:T(8,128)S(1)}, f32[24,48,128]{2,1,0:T(8,128)S(1)}, f32[36,...) custom-call(f32[4096,128]{1,0:T(8,128)S(1)} %get-tuple-element.76.re, ...), custom_call_target="tpu_custom_call", output_to_operand_aliasing={{0}: (12, {}), {1}: (13, {}), {2}: (14, {}), {3}: (15, {}),... | custom-call | tf_op jit(solution)/shard_map/edges/pallas_call | solution.py:991
  19.1 1.9 %collective-permute-start.4 = (f32[104,128]{1,0:T(8,128)S(1)}, f32[104,128]{1,0:T(8,128)S(1)}, u32[]{:S(2)}, u32[]{:S(2)}) collective-permute-start(f32[104,128]{1,0:T(8,128)S(1)} %get-tuple-element.100), channel_id=1, source_target_pairs={{1,2},{2,1},{5,6},{6,5},{9,10},{10,9},{13,14},{14,13},{17,18},{18,... | collective-permute-start | bytes 159752 | tf_op jit(solution)/shard_map/ppermute | solution.py:840
  21.0 0.1 collective-permute-start.5
  21.1 1.6 %edge_water.2 = (f32[4096,128]{1,0:T(8,128)S(1)}, f32[96,128]{1,0:T(8,128)S(1)}, f32[96,128]{1,0:T(8,128)S(1)}) custom-call(f32[4096,128]{1,0:T(8,128)S(1)} %get-tuple-element.91.same, f32[96,128]{1,0:T(8,128)S(1)} %get-tuple-element.92.row_first, ...), custom_call_target="tpu_custom_call", output_to_operand_aliasing={{0}: (0, {}), {1}: (1, {}), {2}: (2, {})} | custom-call | flops 20000000 | bytes 8000000 | tf_op jit(solution)/shard_map/edge_water/pallas_call | solution.py:1014
  22.7 1.8 %collective-permute-done.4.refs_7_ = f32[104,128]{1,0:T(8,128)S(1)} collective-permute-done((f32[104,128]{1,0:T(8,128)S(1)}, f32[104,128]{1,0:T(8,128)S(1)}, u32[]{:S(2)}, u32[]{:S(2)}) %collective-permute-start.4) | collective-permute-done | bytes 53280 | tf_op jit(solution)/shard_map/ppermute | solution.py:840
  24.6 0.0 collective-permute-done.5.refs_8_
  24.6 1.4 %collective-permute-start.7 = (f32[96,128]{1,0:T(8,128)S(1)}, f32[96,128]{1,0:T(8,128)S(1)}, u32[]{:S(2)}, u32[]{:S(2)}) collective-permute-start(f32[96,128]{1,0:T(8,128)S(1)} %maximum_dynamic-update-slice_fusion.3), channel_id=1, source_target_pairs={{0,4},{8,12},{16,20},{24,28},{4,0},{12,8},{20,16},{28,24},{1,5},{9... | collective-permute-start | bytes 147464 | tf_op jit(solution)/shard_map/ppermute | solution.py:840
  26.0 1.9 %collective-permute-start.6 = (f32[96,128]{1,0:T(8,128)S(1)}, f32[96,128]{1,0:T(8,128)S(1)}, u32[]{:S(2)}, u32[]{:S(2)}) collective-permute-start(f32[96,128]{1,0:T(8,128)S(1)} %maximum_dynamic-update-slice_fusion.2), channel_id=1, source_target_pairs={{4,8},{12,16},{20,24},{8,4},{16,12},{24,20},{5,9},{13,17},{21,25},... | collective-permute-start | bytes 147464 | tf_op jit(solution)/shard_map/ppermute | solution.py:840
  27.9 3.3 %inner.4 = (f32[1536,128]{1,0:T(8,128)S(1)}, f32[18,48,128]{2,1,0:T(8,128)S(1)}, f32[4096,128]{1,0:T(8,128)S(1)}, f32[34,48,128]{2,1,0:T(8,128)S(1)}, f32[24,48,...) custom-call(f32[4096,128]{1,0:T(8,128)S(1)} %get-tuple-element.97.refs_0_.water, ...), custom_call_target="tpu_custom_call" | custom-call | flops 20000000 | bytes 8000000 | tf_op jit(solution)/shard_map/inner/pallas_call | solution.py:964
  31.2 0.0 collective-permute-done.7.refs_10_
  31.2 1.6 %collective-permute-done.6.refs_9_ = f32[96,128]{1,0:T(8,128)S(1)} collective-permute-done((f32[96,128]{1,0:T(8,128)S(1)}, f32[96,128]{1,0:T(8,128)S(1)}, u32[]{:S(2)}, u32[]{:S(2)}) %collective-permute-start.6) | collective-permute-done | bytes 49184 | tf_op jit(solution)/shard_map/ppermute | solution.py:840
  32.9 1.2 %edges.4 = (f32[18,48,128]{2,1,0:T(8,128)S(1)}, f32[4096,128]{1,0:T(8,128)S(1)}, f32[34,48,128]{2,1,0:T(8,128)S(1)}, f32[24,48,128]{2,1,0:T(8,128)S(1)}, f32[36,...) custom-call(f32[4096,128]{1,0:T(8,128)S(1)} %get-tuple-element.97.re, ...), custom_call_target="tpu_custom_call", output_to_operand_aliasing={{0}: (13, {}), {1}: (14, {}), {2}: (15, {}), {3}: (16, {}),... | custom-call | tf_op jit(solution)/shard_map/edges/pallas_call | solution.py:991
  34.0 1.9 %collective-permute-start.8 = (f32[104,128]{1,0:T(8,128)S(1)}, f32[104,128]{1,0:T(8,128)S(1)}, u32[]{:S(2)}, u32[]{:S(2)}) collective-permute-start(f32[104,128]{1,0:T(8,128)S(1)} %get-tuple-element.122), channel_id=1, source_target_pairs={{1,2},{2,1},{5,6},{6,5},{9,10},{10,9},{13,14},{14,13},{17,18},{18,... | collective-permute-start | bytes 159752 | tf_op jit(solution)/shard_map/ppermute | solution.py:840
  36.0 0.1 collective-permute-start.9
  36.0 1.7 %edge_water.3 = (f32[4096,128]{1,0:T(8,128)S(1)}, f32[96,128]{1,0:T(8,128)S(1)}, f32[96,128]{1,0:T(8,128)S(1)}) custom-call(f32[4096,128]{1,0:T(8,128)S(1)} %get-tuple-element.113.same, f32[96,128]{1,0:T(8,128)S(1)} %get-tuple-element.114.row_first, ...), custom_call_target="tpu_custom_call", output_to_operand_aliasing={{0}: (0, {}), {1}: (1, {}), {2}: (2, {})} | custom-call | flops 20000000 | bytes 8000000 | tf_op jit(solution)/shard_map/edge_water/pallas_call | solution.py:1014
  37.7 1.8 %collective-permute-done.8.refs_7_ = f32[104,128]{1,0:T(8,128)S(1)} collective-permute-done((f32[104,128]{1,0:T(8,128)S(1)}, f32[104,128]{1,0:T(8,128)S(1)}, u32[]{:S(2)}, u32[]{:S(2)}) %collective-permute-start.8) | collective-permute-done | bytes 53280 | tf_op jit(solution)/shard_map/ppermute | solution.py:840
  39.5 0.0 collective-permute-done.9.refs_8_
  39.5 1.5 %collective-permute-start.11 = (f32[96,128]{1,0:T(8,128)S(1)}, f32[96,128]{1,0:T(8,128)S(1)}, u32[]{:S(2)}, u32[]{:S(2)}) collective-permute-start(f32[96,128]{1,0:T(8,128)S(1)} %maximum_dynamic-update-slice_fusion.5), channel_id=1, source_target_pairs={{0,4},{8,12},{16,20},{24,28},{4,0},{12,8},{20,16},{28,24},{1,5},{9... | collective-permute-start | bytes 147464 | tf_op jit(solution)/shard_map/ppermute | solution.py:840
  41.0 1.9 %collective-permute-start.10 = (f32[96,128]{1,0:T(8,128)S(1)}, f32[96,128]{1,0:T(8,128)S(1)}, u32[]{:S(2)}, u32[]{:S(2)}) collective-permute-start(f32[96,128]{1,0:T(8,128)S(1)} %maximum_dynamic-update-slice_fusion.4), channel_id=1, source_target_pairs={{4,8},{12,16},{20,24},{8,4},{16,12},{24,20},{5,9},{13,17},{21,25},... | collective-permute-start | bytes 147464 | tf_op jit(solution)/shard_map/ppermute | solution.py:840
  43.0 2.4 %inner.5 = (f32[1536,128]{1,0:T(8,128)S(1)}, f32[18,48,128]{2,1,0:T(8,128)S(1)}, f32[4096,128]{1,0:T(8,128)}, f32[1024,128]{1,0:T(8,128)S(1)}, f32[4,9,16,256]{3...) custom-call(f32[4096,128]{1,0:T(8,128)S(1)} %get-tuple-element.119.refs_0_, f32[36,32,128]{2,1,0:T(8,128)S(1)} %get-tuple-element.120.refs_1_, ...), custom_call_target="tpu_custom_call" | custom-call | flops 20000000 | bytes 8000000 | tf_op jit(solution)/shard_map/inner/pallas_call | solution.py:964
  45.4 0.0 collective-permute-done.11.refs_10_
  45.4 2.5 %collective-permute-done.10.refs_9_ = f32[96,128]{1,0:T(8,128)S(1)} collective-permute-done((f32[96,128]{1,0:T(8,128)S(1)}, f32[96,128]{1,0:T(8,128)S(1)}, u32[]{:S(2)}, u32[]{:S(2)}) %collective-permute-start.10) | collective-permute-done | bytes 49184 | tf_op jit(solution)/shard_map/ppermute | solution.py:840
  47.9 1.6 %edges.5 = (f32[18,48,128]{2,1,0:T(8,128)S(1)}, f32[4096,128]{1,0:T(8,128)}, f32[4,9,16,256]{3,2,1,0:T(8,128)}, f32[4,18,16,256]{3,2,1,0:T(8,128)}) custom-call(f32[4096,128]{1,0:T(8,128)S(1)} %get-tuple-element.119.refs_0_, f32[36,32,128]{2,1,0:T(8,128)S(1)} %get-tuple-element.120.refs_1_, ...), custom_call_target="tpu_custom_call", output_to_operand_aliasing={{0}: (16, {}), {1}: (17, {})} | custom-call | tf_op jit(solution)/shard_map/edges/pallas_call | solution.py:991
  (12 shorter events, 0.1 us)
Async XLA Ops:
  0.8 4.8 %copy-start = (f32[4,32,32,128]{3,2,1,0:T(8,128)S(1)}, f32[4,32,32,128]{3,2,1,0:T(8,128)}, u32[]{:S(2)}) copy-start(f32[4,32,32,128]{3,2,1,0:T(8,128)} %state.1) | copy-start | bytes 6291460
  0.8 4.9 %copy-start.1 = (s32[32,32,128]{2,1,0:T(8,128)S(1)}, s32[32,32,128]{2,1,0:T(8,128)}, u32[]{:S(2)}) copy-start(s32[32,32,128]{2,1,0:T(8,128)} %material.1) | copy-start | bytes 1572868
  3.6 5.6 %collective-permute-start = (f32[136,128]{1,0:T(8,128)S(1)}, f32[136,128]{1,0:T(8,128)S(1)}, u32[]{:S(2)}, u32[]{:S(2)}) collective-permute-start(f32[136,128]{1,0:T(8,128)S(1)} %get-tuple-element.80), channel_id=1, source_target_pairs={{1,2},{2,1},{5,6},{6,5},{9,10},{10,9},{13,14},{14,13},{17,18},{18,... | collective-permute-start | bytes 208904 | tf_op jit(solution)/shard_map/ppermute | solution.py:840
  5.6 3.7 %collective-permute-start.1 = (f32[136,128]{1,0:T(8,128)S(1)}, f32[136,128]{1,0:T(8,128)S(1)}, u32[]{:S(2)}, u32[]{:S(2)}) collective-permute-start(f32[136,128]{1,0:T(8,128)S(1)} %get-tuple-element.81), channel_id=1, source_target_pairs={{0,1},{2,3},{1,0},{3,2},{4,5},{6,7},{5,4},{7,6},{8,9},{10,11},{9,8... | collective-permute-start | bytes 208904 | tf_op jit(solution)/shard_map/ppermute | solution.py:840
  9.3 7.3 %collective-permute-start.3 = (f32[128,128]{1,0:T(8,128)S(1)}, f32[128,128]{1,0:T(8,128)S(1)}, u32[]{:S(2)}, u32[]{:S(2)}) collective-permute-start(f32[128,128]{1,0:T(8,128)S(1)} %maximum_dynamic-update-slice_fusion.1), channel_id=1, source_target_pairs={{0,4},{8,12},{16,20},{24,28},{4,0},{12,8},{20,16},{28,24},{1,5},{9... | collective-permute-start | bytes 196616 | tf_op jit(solution)/shard_map/ppermute | solution.py:840
  10.9 7.0 %collective-permute-start.2 = (f32[128,128]{1,0:T(8,128)S(1)}, f32[128,128]{1,0:T(8,128)S(1)}, u32[]{:S(2)}, u32[]{:S(2)}) collective-permute-start(f32[128,128]{1,0:T(8,128)S(1)} %maximum_dynamic-update-slice_fusion), channel_id=1, source_target_pairs={{4,8},{12,16},{20,24},{8,4},{16,12},{24,20},{5,9},{13,17},{21,25},... | collective-permute-start | bytes 196616 | tf_op jit(solution)/shard_map/ppermute | solution.py:840
  19.1 5.5 %collective-permute-start.4 = (f32[104,128]{1,0:T(8,128)S(1)}, f32[104,128]{1,0:T(8,128)S(1)}, u32[]{:S(2)}, u32[]{:S(2)}) collective-permute-start(f32[104,128]{1,0:T(8,128)S(1)} %get-tuple-element.100), channel_id=1, source_target_pairs={{1,2},{2,1},{5,6},{6,5},{9,10},{10,9},{13,14},{14,13},{17,18},{18,... | collective-permute-start | bytes 159752 | tf_op jit(solution)/shard_map/ppermute | solution.py:840
  21.0 3.5 %collective-permute-start.5 = (f32[104,128]{1,0:T(8,128)S(1)}, f32[104,128]{1,0:T(8,128)S(1)}, u32[]{:S(2)}, u32[]{:S(2)}) collective-permute-start(f32[104,128]{1,0:T(8,128)S(1)} %get-tuple-element.101), channel_id=1, source_target_pairs={{0,1},{2,3},{1,0},{3,2},{4,5},{6,7},{5,4},{7,6},{8,9},{10,11},{9,8... | collective-permute-start | bytes 159752 | tf_op jit(solution)/shard_map/ppermute | solution.py:840
  24.6 6.6 %collective-permute-start.7 = (f32[96,128]{1,0:T(8,128)S(1)}, f32[96,128]{1,0:T(8,128)S(1)}, u32[]{:S(2)}, u32[]{:S(2)}) collective-permute-start(f32[96,128]{1,0:T(8,128)S(1)} %maximum_dynamic-update-slice_fusion.3), channel_id=1, source_target_pairs={{0,4},{8,12},{16,20},{24,28},{4,0},{12,8},{20,16},{28,24},{1,5},{9... | collective-permute-start | bytes 147464 | tf_op jit(solution)/shard_map/ppermute | solution.py:840
  26.0 6.9 %collective-permute-start.6 = (f32[96,128]{1,0:T(8,128)S(1)}, f32[96,128]{1,0:T(8,128)S(1)}, u32[]{:S(2)}, u32[]{:S(2)}) collective-permute-start(f32[96,128]{1,0:T(8,128)S(1)} %maximum_dynamic-update-slice_fusion.2), channel_id=1, source_target_pairs={{4,8},{12,16},{20,24},{8,4},{16,12},{24,20},{5,9},{13,17},{21,25},... | collective-permute-start | bytes 147464 | tf_op jit(solution)/shard_map/ppermute | solution.py:840
  34.0 5.5 %collective-permute-start.8 = (f32[104,128]{1,0:T(8,128)S(1)}, f32[104,128]{1,0:T(8,128)S(1)}, u32[]{:S(2)}, u32[]{:S(2)}) collective-permute-start(f32[104,128]{1,0:T(8,128)S(1)} %get-tuple-element.122), channel_id=1, source_target_pairs={{1,2},{2,1},{5,6},{6,5},{9,10},{10,9},{13,14},{14,13},{17,18},{18,... | collective-permute-start | bytes 159752 | tf_op jit(solution)/shard_map/ppermute | solution.py:840
  36.0 3.5 %collective-permute-start.9 = (f32[104,128]{1,0:T(8,128)S(1)}, f32[104,128]{1,0:T(8,128)S(1)}, u32[]{:S(2)}, u32[]{:S(2)}) collective-permute-start(f32[104,128]{1,0:T(8,128)S(1)} %get-tuple-element.123), channel_id=1, source_target_pairs={{0,1},{2,3},{1,0},{3,2},{4,5},{6,7},{5,4},{7,6},{8,9},{10,11},{9,8... | collective-permute-start | bytes 159752 | tf_op jit(solution)/shard_map/ppermute | solution.py:840
  39.5 5.9 %collective-permute-start.11 = (f32[96,128]{1,0:T(8,128)S(1)}, f32[96,128]{1,0:T(8,128)S(1)}, u32[]{:S(2)}, u32[]{:S(2)}) collective-permute-start(f32[96,128]{1,0:T(8,128)S(1)} %maximum_dynamic-update-slice_fusion.5), channel_id=1, source_target_pairs={{0,4},{8,12},{16,20},{24,28},{4,0},{12,8},{20,16},{28,24},{1,5},{9... | collective-permute-start | bytes 147464 | tf_op jit(solution)/shard_map/ppermute | solution.py:840
  41.0 6.9 %collective-permute-start.10 = (f32[96,128]{1,0:T(8,128)S(1)}, f32[96,128]{1,0:T(8,128)S(1)}, u32[]{:S(2)}, u32[]{:S(2)}) collective-permute-start(f32[96,128]{1,0:T(8,128)S(1)} %maximum_dynamic-update-slice_fusion.4), channel_id=1, source_target_pairs={{4,8},{12,16},{20,24},{8,4},{16,12},{24,20},{5,9},{13,17},{21,25},... | collective-permute-start | bytes 147464 | tf_op jit(solution)/shard_map/ppermute | solution.py:840
